TPU v7x, 32 devices: a whole 2x2x4 slice. The times are simulated.
32 devices in a mesh: groups: 2 (over y), loop: 4 (over z), heads: 2 (over x), pair: 2 (over core).
Axes of the slice: x: 2, y: 2, z: 4, core: 2. Of those that a mesh axis runs over, the one named last changes fastest.
Arguments:
- queries: bfloat16 [5120, 2048], P(('groups', 'loop'), ('heads', 'pair')), parts along dimension 0, may hold values from -96 to 96
- suffix_kv: bfloat16 [5120, 2, 256], P(('groups', 'loop'), 'heads'), parts along dimension 0, may hold values from -4 to 4
- prompt_kv: bfloat16 [2048, 2, 256], P(('groups', 'loop'), 'heads'), parts along dimension 0, may hold values from -4 to 4
- lengths: int32 [16], P('groups'), parts along dimension 0, may hold values from 128 to 320, as said below
Outputs:
- attended: bfloat16 [5120, 2048], P(('groups', 'loop'), ('heads', 'pair')), parts along dimension 0
There are 2 independent parts, one for each index of `groups`. A program takes and returns all parts, laid end to end along the dimension named above; each array names one. Nothing has to cross between parts.
Inputs may be any that keep to these rules, and one draw needn't show every extreme that they name: Each agent's suffix has 128 to 320 tokens, and agents d * 2 to d * 2 + 1 belong to loop index d, so their lengths add up to at most 640 slots.
All inputs are finite; a program needn't handle non-finite values.
Results may differ from a plain program's by a relative error of at most 0.0065.
Values may be sent and summed in bfloat16 or wider, within the bound.
No kernel may reach another device: no remote copies, remote signals or barrier semaphores. Data moves between devices by JAX's collectives and lax.ppermute only.
A program may use at most 64 MiB of HBM per device.

v0:
```python
import math

import jax
import jax.numpy as jnp
from jax import lax
from jax.sharding import PartitionSpec as P

HD = 128
AG_DEV = 2
MAXLEN = 320
BLK = 128


very_negative = -1e30


def attend_segment(running, query_block, key_block, value_block, score_scale):
    row_best, row_total, weighted = running
    scores = (
        lax.dot_general(
            query_block, key_block, (((1,), (1,)), ((), ())), preferred_element_type=jnp.float32
        )
        * score_scale
    )
    new_best = jnp.maximum(row_best, jnp.max(scores, axis=1))
    factor = jnp.exp(row_best - new_best)
    weights = jnp.exp(scores - new_best[:, None])
    row_total = row_total * factor + jnp.sum(weights, axis=1)
    weighted = weighted * factor[:, None] + jnp.dot(
        weights.astype(jnp.bfloat16), value_block, preferred_element_type=jnp.float32
    )
    return (new_best, row_total, weighted)


def prompt_segments(key_piece):
    key_count = key_piece.shape[0]
    segment = key_count
    while segment > 1024 and segment % 2 == 0:
        segment = segment // 2
    key_blocks = key_piece[:, 0, :HD].reshape(key_count // segment, segment, HD)
    value_blocks = key_piece[:, 0, HD:].reshape(key_count // segment, segment, HD)
    return (key_blocks, value_blocks)


def fold_groups(carry_now, groups, first_block, stop_block, segments, score_scale):
    key_blocks, value_blocks = segments

    def visit_block(block_index, carry_in):
        row_best, row_total, weighted = carry_in
        query_block = groups[block_index]

        def through(running, pair_block):
            return (
                attend_segment(running, query_block, pair_block[0], pair_block[1], score_scale),
                None,
            )

        block_state, unused = lax.scan(
            through,
            (row_best[block_index], row_total[block_index], weighted[block_index]),
            (key_blocks, value_blocks),
        )
        return (
            row_best.at[block_index].set(block_state[0]),
            row_total.at[block_index].set(block_state[1]),
            weighted.at[block_index].set(block_state[2]),
        )

    return lax.fori_loop(first_block, stop_block, visit_block, carry_now)


def empty_carry(block_total, group_rows):
    return (
        jnp.full((block_total, group_rows), very_negative, jnp.float32),
        jnp.zeros((block_total, group_rows), jnp.float32),
        jnp.zeros((block_total, group_rows, HD), jnp.float32),
    )


def shards(queries, suffix_kv, prompt_kv, lengths):
    slot_rows = queries.shape[0]
    local_heads = queries.shape[1] // HD
    group_rows = BLK * local_heads
    block_count = slot_rows // BLK
    score_scale = 1.0 / math.sqrt(HD)
    loop_size = lax.axis_size("loop")
    position = lax.axis_index("loop")
    agent_lengths = lengths.reshape(loop_size, AG_DEV)
    live_counts = jnp.sum(agent_lengths, axis=1)
    live_blocks = (live_counts + BLK - 1) // BLK
    my_agents = agent_lengths[position]
    my_live = live_counts[position]
    my_blocks = live_blocks[position]
    groups = queries.reshape(block_count, group_rows, HD)
    own_state = fold_groups(
        empty_carry(block_count, group_rows),
        groups,
        0,
        my_blocks,
        prompt_segments(lax.all_gather(prompt_kv, "loop", axis=0, tiled=True)),
        score_scale,
    )
    window = BLK * ((MAXLEN + BLK - 2) // BLK) + BLK
    agent_ends = jnp.cumsum(my_agents)

    def agent_index(rows_at):
        return jnp.sum((rows_at[:, None] >= agent_ends[None, :]).astype(jnp.int32), axis=1)

    group_offsets = jnp.arange(group_rows, dtype=jnp.int32) // local_heads
    window_offsets = jnp.arange(window, dtype=jnp.int32)

    def suffix_block(block_index, carry_in):
        row_best, row_total, weighted = carry_in
        query_at = block_index * BLK + group_offsets
        window_start = jnp.clip((block_index + 1) * BLK - window, 0, slot_rows - window)
        key_at = window_start + window_offsets
        window_rows = lax.dynamic_slice_in_dim(suffix_kv, window_start, window, 0)[:, 0, :]
        allowed = (agent_index(query_at)[:, None] == agent_index(key_at)[None, :]) & (
            key_at[None, :] <= query_at[:, None]
        )
        scores = (
            lax.dot_general(
                groups[block_index],
                window_rows[:, :HD],
                (((1,), (1,)), ((), ())),
                preferred_element_type=jnp.float32,
            )
            * score_scale
        )
        scores = jnp.where(allowed, scores, very_negative)
        old_best = row_best[block_index]
        new_best = jnp.maximum(old_best, jnp.max(scores, axis=1))
        factor = jnp.exp(old_best - new_best)
        weights = jnp.where(allowed, jnp.exp(scores - new_best[:, None]), 0.0)
        new_total = row_total[block_index] * factor + jnp.sum(weights, axis=1)
        new_weighted = weighted[block_index] * factor[:, None] + jnp.dot(
            weights.astype(jnp.bfloat16), window_rows[:, HD:], preferred_element_type=jnp.float32
        )
        return (
            row_best.at[block_index].set(new_best),
            row_total.at[block_index].set(new_total),
            weighted.at[block_index].set(new_weighted),
        )

    row_best, row_total, weighted = lax.fori_loop(0, my_blocks, suffix_block, own_state)
    row_at = (
        jnp.arange(block_count * group_rows, dtype=jnp.int32).reshape(block_count, group_rows)
        // local_heads
    )
    live_mask = row_at < my_live
    safe_total = jnp.where(live_mask, row_total, 1.0)
    attended = jnp.where(live_mask[:, :, None], weighted / safe_total[:, :, None], 0.0)
    return attended.reshape(slot_rows, local_heads * HD).astype(jnp.bfloat16)


def solution(mesh):
    placed = (
        P(("groups", "loop"), ("heads", "pair")),
        P(("groups", "loop"), "heads", None),
        P(("groups", "loop"), "heads", None),
        P("groups"),
    )
    return jax.shard_map(
        shards,
        mesh=mesh,
        in_specs=placed,
        out_specs=P(("groups", "loop"), ("heads", "pair")),
        check_vma=False,
    )
```

profile of v0, /device:TPU:0, one launch (start us, length us, event | category | flops | bytes accessed | tf_op | source)
XLA Modules:
  0.0 101.9 jit_solution(12341792189640622242)
XLA Ops:
  1.6 2.2 %reshape.310 = bf16[5,512,128]{2,1,0:T(8,128)(2,1)} reshape(bf16[640,512]{1,0:T(8,128)(2,1)} %param.20) | data formatting | bytes 1310720 | tf_op jit(solution)/shard_map/reshape | solution.py:94
  3.8 17.3 %all_gather.3 = bf16[1024,1,256]{2,0,1:T(8,128)(2,1)S(1)} all-gather(bf16[256,1,256]{2,0,1:T(8,128)(2,1)S(1)} %copy-done), channel_id=1, replica_groups=mesh['groups'=2,'loop'=4,'heads'=2,'pair'=2] {'loop'}, dimensions={0}, use_global_device_ids=true | all-gather | bytes 655360 | tf_op jit(solution)/shard_map/all_gather | solution.py:100
  21.1 0.8 slice_bitcast_fusion
  22.1 38.4 %while.43 = (s32[]{:T(128)}, f32[5,512]{1,0:T(8,128)S(1)}, f32[5,512]{1,0:T(8,128)S(1)}, f32[5,512,128]{2,1,0:T(8,128)S(1)}, s32[]{:T(128)}, /*index=5*/bf16[5,5...) while((s32[]{:T(128)}, f32[5,512]{1,0:T(8,128)S(1)}, ...), condition=%wide.region_6.7_spmd, body=%wide.region_1.6_spmd.sunk | while | flops 272829984 | bytes 8041200 | solution.py:69
  23.5 1.5 %multiply_reduce_fusion.2 = (f32[512]{0:T(512)S(1)}, f32[512,1024]{1,0:T(8,128)S(1)}) fusion(bf16[1,1024,128]{2,1,0:T(8,128)(2,1)} %get-tuple-element.513, bf16[5,512,128]{2,1,0:T(8,128)(2,1)} %get-tuple-element.512, s32[]{:T(128)} %select_n.108), kind=kOutput, calls=%fused_computation.3.clone.1 | convolution fusion | flops 135265792 | bytes 2492928 | tf_op jit(solution)/shard_map/while/body/while/body/eval_jaxpr/dot_general | solution.py:20
  27.6 2.0 %fusion.67 = f32[5,512,128]{2,1,0:T(8,128)S(1)} fusion(f32[5,512,128]{2,1,0:T(8,128)S(1)} %get-tuple-element.496, s32[]{:T(128)} %select_n.108, f32[1,512,128]{2,1,0:T(8,128)S(1)} %constant_dynamic-slice_fusion.8, f32[512,1024]{1,0:T(8,128)S(1)} %get-tuple-element.457, f32[512]{0:T(512)S(1)} %get-tuple-element.459, ...), kind=kOutput, calls=%fused_computation.9.clone.1 | convolution fusion | flops 135987200 | bytes 2887685 | tf_op jit(solution)/shard_map/while/body/while/body/eval_jaxpr/dot_general | solution.py:29
  31.0 1.5 %multiply_reduce_fusion.2 = (f32[512]{0:T(512)S(1)}, f32[512,1024]{1,0:T(8,128)S(1)}) fusion(bf16[1,1024,128]{2,1,0:T(8,128)(2,1)} %get-tuple-element.513, bf16[5,512,128]{2,1,0:T(8,128)(2,1)} %get-tuple-element.512, s32[]{:T(128)} %select_n.108), kind=kOutput, calls=%fused_computation.3.clone.1 | convolution fusion | flops 135265792 | bytes 2492928 | tf_op jit(solution)/shard_map/while/body/while/body/eval_jaxpr/dot_general | solution.py:20
  35.1 2.0 %fusion.67 = f32[5,512,128]{2,1,0:T(8,128)S(1)} fusion(f32[5,512,128]{2,1,0:T(8,128)S(1)} %get-tuple-element.496, s32[]{:T(128)} %select_n.108, f32[1,512,128]{2,1,0:T(8,128)S(1)} %constant_dynamic-slice_fusion.8, f32[512,1024]{1,0:T(8,128)S(1)} %get-tuple-element.457, f32[512]{0:T(512)S(1)} %get-tuple-element.459, ...), kind=kOutput, calls=%fused_computation.9.clone.1 | convolution fusion | flops 135987200 | bytes 2887685 | tf_op jit(solution)/shard_map/while/body/while/body/eval_jaxpr/dot_general | solution.py:29
  38.6 1.5 %multiply_reduce_fusion.2 = (f32[512]{0:T(512)S(1)}, f32[512,1024]{1,0:T(8,128)S(1)}) fusion(bf16[1,1024,128]{2,1,0:T(8,128)(2,1)} %get-tuple-element.513, bf16[5,512,128]{2,1,0:T(8,128)(2,1)} %get-tuple-element.512, s32[]{:T(128)} %select_n.108), kind=kOutput, calls=%fused_computation.3.clone.1 | convolution fusion | flops 135265792 | bytes 2492928 | tf_op jit(solution)/shard_map/while/body/while/body/eval_jaxpr/dot_general | solution.py:20
  42.6 2.0 %fusion.67 = f32[5,512,128]{2,1,0:T(8,128)S(1)} fusion(f32[5,512,128]{2,1,0:T(8,128)S(1)} %get-tuple-element.496, s32[]{:T(128)} %select_n.108, f32[1,512,128]{2,1,0:T(8,128)S(1)} %constant_dynamic-slice_fusion.8, f32[512,1024]{1,0:T(8,128)S(1)} %get-tuple-element.457, f32[512]{0:T(512)S(1)} %get-tuple-element.459, ...), kind=kOutput, calls=%fused_computation.9.clone.1 | convolution fusion | flops 135987200 | bytes 2887685 | tf_op jit(solution)/shard_map/while/body/while/body/eval_jaxpr/dot_general | solution.py:29
  46.1 1.5 %multiply_reduce_fusion.2 = (f32[512]{0:T(512)S(1)}, f32[512,1024]{1,0:T(8,128)S(1)}) fusion(bf16[1,1024,128]{2,1,0:T(8,128)(2,1)} %get-tuple-element.513, bf16[5,512,128]{2,1,0:T(8,128)(2,1)} %get-tuple-element.512, s32[]{:T(128)} %select_n.108), kind=kOutput, calls=%fused_computation.3.clone.1 | convolution fusion | flops 135265792 | bytes 2492928 | tf_op jit(solution)/shard_map/while/body/while/body/eval_jaxpr/dot_general | solution.py:20
  50.2 2.0 %fusion.67 = f32[5,512,128]{2,1,0:T(8,128)S(1)} fusion(f32[5,512,128]{2,1,0:T(8,128)S(1)} %get-tuple-element.496, s32[]{:T(128)} %select_n.108, f32[1,512,128]{2,1,0:T(8,128)S(1)} %constant_dynamic-slice_fusion.8, f32[512,1024]{1,0:T(8,128)S(1)} %get-tuple-element.457, f32[512]{0:T(512)S(1)} %get-tuple-element.459, ...), kind=kOutput, calls=%fused_computation.9.clone.1 | convolution fusion | flops 135987200 | bytes 2887685 | tf_op jit(solution)/shard_map/while/body/while/body/eval_jaxpr/dot_general | solution.py:29
  53.7 1.5 %multiply_reduce_fusion.2 = (f32[512]{0:T(512)S(1)}, f32[512,1024]{1,0:T(8,128)S(1)}) fusion(bf16[1,1024,128]{2,1,0:T(8,128)(2,1)} %get-tuple-element.513, bf16[5,512,128]{2,1,0:T(8,128)(2,1)} %get-tuple-element.512, s32[]{:T(128)} %select_n.108), kind=kOutput, calls=%fused_computation.3.clone.1 | convolution fusion | flops 135265792 | bytes 2492928 | tf_op jit(solution)/shard_map/while/body/while/body/eval_jaxpr/dot_general | solution.py:20
  57.7 2.0 %fusion.67 = f32[5,512,128]{2,1,0:T(8,128)S(1)} fusion(f32[5,512,128]{2,1,0:T(8,128)S(1)} %get-tuple-element.496, s32[]{:T(128)} %select_n.108, f32[1,512,128]{2,1,0:T(8,128)S(1)} %constant_dynamic-slice_fusion.8, f32[512,1024]{1,0:T(8,128)S(1)} %get-tuple-element.457, f32[512]{0:T(512)S(1)} %get-tuple-element.459, ...), kind=kOutput, calls=%fused_computation.9.clone.1 | convolution fusion | flops 135987200 | bytes 2887685 | tf_op jit(solution)/shard_map/while/body/while/body/eval_jaxpr/dot_general | solution.py:29
  60.7 37.2 %while.44 = (s32[]{:T(128)}, f32[5,512]{1,0:T(8,128)S(1)}, f32[5,512]{1,0:T(8,128)S(1)}, f32[5,512,128]{2,1,0:T(8,128)S(1)}, s32[]{:T(128)}, /*index=5*/s32[2]{0...) while((s32[]{:T(128)}, f32[5,512]{1,0:T(8,128)S(1)}, ...), condition=%wide.region_15.16_spmd.clone, body=%wide.region_8.15_spmd.clone.sunk | while | flops 139146784 | bytes 5194576 | solution.py:145
  62.1 1.0 dynamic-slice_bitcast_fusion.3
  63.2 1.3 %fusion.72 = (f32[512]{0:T(512)S(1)}, f32[512,512]{0,1:T(8,128)S(1)}) fusion(bf16[512,256]{1,0:T(8,128)(2,1)S(1)} %dynamic-slice_bitcast_fusion.3, bf16[5,512,128]{2,1,0:T(8,128)(2,1)} %get-tuple-element.559, s32[]{:T(128)} %select_n.112, s32[512]{0:T(512)S(1)} %get-tuple-element.469, s32[512]{0:T(512)S(1)} %get-tuple-element.470, ...), kind=kOutput, calls=%fused_computation.96.clone.1 | convolution fusion | flops 68681216 | bytes 1321472 | tf_op jit(solution)/shard_map/while/body/dot_general | solution.py:122
  66.9 1.1 %fusion.74 = f32[5,512,128]{2,1,0:T(8,128)S(1)} fusion(f32[5,512,128]{2,1,0:T(8,128)S(1)} %get-tuple-element.540, s32[]{:T(128)} %select_n.112, f32[1,512,128]{2,1,0:T(8,128)S(1)} %constant_dynamic-slice_fusion.9, f32[512,512]{0,1:T(8,128)S(1)} %get-tuple-element.475, f32[512]{0:T(512)S(1)} %get-tuple-element.477, s32[512]{0:T(512)S(1)} %get-tuple-element.469, ...), kind=kOutput, calls=%fused_computation.35.clone.1 | convolution fusion | flops 68878336 | bytes 1716229 | tf_op jit(solution)/shard_map/while/body/dot_general | solution.py:136
  69.4 1.0 dynamic-slice_bitcast_fusion.3
  70.5 1.3 %fusion.72 = (f32[512]{0:T(512)S(1)}, f32[512,512]{0,1:T(8,128)S(1)}) fusion(bf16[512,256]{1,0:T(8,128)(2,1)S(1)} %dynamic-slice_bitcast_fusion.3, bf16[5,512,128]{2,1,0:T(8,128)(2,1)} %get-tuple-element.559, s32[]{:T(128)} %select_n.112, s32[512]{0:T(512)S(1)} %get-tuple-element.469, s32[512]{0:T(512)S(1)} %get-tuple-element.470, ...), kind=kOutput, calls=%fused_computation.96.clone.1 | convolution fusion | flops 68681216 | bytes 1321472 | tf_op jit(solution)/shard_map/while/body/dot_general | solution.py:122
  74.2 1.1 %fusion.74 = f32[5,512,128]{2,1,0:T(8,128)S(1)} fusion(f32[5,512,128]{2,1,0:T(8,128)S(1)} %get-tuple-element.540, s32[]{:T(128)} %select_n.112, f32[1,512,128]{2,1,0:T(8,128)S(1)} %constant_dynamic-slice_fusion.9, f32[512,512]{0,1:T(8,128)S(1)} %get-tuple-element.475, f32[512]{0:T(512)S(1)} %get-tuple-element.477, s32[512]{0:T(512)S(1)} %get-tuple-element.469, ...), kind=kOutput, calls=%fused_computation.35.clone.1 | convolution fusion | flops 68878336 | bytes 1716229 | tf_op jit(solution)/shard_map/while/body/dot_general | solution.py:136
  76.7 1.0 dynamic-slice_bitcast_fusion.3
  77.8 1.3 %fusion.72 = (f32[512]{0:T(512)S(1)}, f32[512,512]{0,1:T(8,128)S(1)}) fusion(bf16[512,256]{1,0:T(8,128)(2,1)S(1)} %dynamic-slice_bitcast_fusion.3, bf16[5,512,128]{2,1,0:T(8,128)(2,1)} %get-tuple-element.559, s32[]{:T(128)} %select_n.112, s32[512]{0:T(512)S(1)} %get-tuple-element.469, s32[512]{0:T(512)S(1)} %get-tuple-element.470, ...), kind=kOutput, calls=%fused_computation.96.clone.1 | convolution fusion | flops 68681216 | bytes 1321472 | tf_op jit(solution)/shard_map/while/body/dot_general | solution.py:122
  81.5 1.1 %fusion.74 = f32[5,512,128]{2,1,0:T(8,128)S(1)} fusion(f32[5,512,128]{2,1,0:T(8,128)S(1)} %get-tuple-element.540, s32[]{:T(128)} %select_n.112, f32[1,512,128]{2,1,0:T(8,128)S(1)} %constant_dynamic-slice_fusion.9, f32[512,512]{0,1:T(8,128)S(1)} %get-tuple-element.475, f32[512]{0:T(512)S(1)} %get-tuple-element.477, s32[512]{0:T(512)S(1)} %get-tuple-element.469, ...), kind=kOutput, calls=%fused_computation.35.clone.1 | convolution fusion | flops 68878336 | bytes 1716229 | tf_op jit(solution)/shard_map/while/body/dot_general | solution.py:136
  84.0 1.0 dynamic-slice_bitcast_fusion.3
  85.1 1.3 %fusion.72 = (f32[512]{0:T(512)S(1)}, f32[512,512]{0,1:T(8,128)S(1)}) fusion(bf16[512,256]{1,0:T(8,128)(2,1)S(1)} %dynamic-slice_bitcast_fusion.3, bf16[5,512,128]{2,1,0:T(8,128)(2,1)} %get-tuple-element.559, s32[]{:T(128)} %select_n.112, s32[512]{0:T(512)S(1)} %get-tuple-element.469, s32[512]{0:T(512)S(1)} %get-tuple-element.470, ...), kind=kOutput, calls=%fused_computation.96.clone.1 | convolution fusion | flops 68681216 | bytes 1321472 | tf_op jit(solution)/shard_map/while/body/dot_general | solution.py:122
  88.8 1.1 %fusion.74 = f32[5,512,128]{2,1,0:T(8,128)S(1)} fusion(f32[5,512,128]{2,1,0:T(8,128)S(1)} %get-tuple-element.540, s32[]{:T(128)} %select_n.112, f32[1,512,128]{2,1,0:T(8,128)S(1)} %constant_dynamic-slice_fusion.9, f32[512,512]{0,1:T(8,128)S(1)} %get-tuple-element.475, f32[512]{0:T(512)S(1)} %get-tuple-element.477, s32[512]{0:T(512)S(1)} %get-tuple-element.469, ...), kind=kOutput, calls=%fused_computation.35.clone.1 | convolution fusion | flops 68878336 | bytes 1716229 | tf_op jit(solution)/shard_map/while/body/dot_general | solution.py:136
  91.3 1.0 dynamic-slice_bitcast_fusion.3
  92.5 1.3 %fusion.72 = (f32[512]{0:T(512)S(1)}, f32[512,512]{0,1:T(8,128)S(1)}) fusion(bf16[512,256]{1,0:T(8,128)(2,1)S(1)} %dynamic-slice_bitcast_fusion.3, bf16[5,512,128]{2,1,0:T(8,128)(2,1)} %get-tuple-element.559, s32[]{:T(128)} %select_n.112, s32[512]{0:T(512)S(1)} %get-tuple-element.469, s32[512]{0:T(512)S(1)} %get-tuple-element.470, ...), kind=kOutput, calls=%fused_computation.96.clone.1 | convolution fusion | flops 68681216 | bytes 1321472 | tf_op jit(solution)/shard_map/while/body/dot_general | solution.py:122
  96.1 1.1 %fusion.74 = f32[5,512,128]{2,1,0:T(8,128)S(1)} fusion(f32[5,512,128]{2,1,0:T(8,128)S(1)} %get-tuple-element.540, s32[]{:T(128)} %select_n.112, f32[1,512,128]{2,1,0:T(8,128)S(1)} %constant_dynamic-slice_fusion.9, f32[512,512]{0,1:T(8,128)S(1)} %get-tuple-element.475, f32[512]{0:T(512)S(1)} %get-tuple-element.477, s32[512]{0:T(512)S(1)} %get-tuple-element.469, ...), kind=kOutput, calls=%fused_computation.35.clone.1 | convolution fusion | flops 68878336 | bytes 1716229 | tf_op jit(solution)/shard_map/while/body/dot_general | solution.py:136
  99.9 0.9 select_convert_fusion
  100.7 1.2 %convert_element_type.29 = bf16[640,512]{1,0:T(8,128)(2,1)} reshape(bf16[5,512,128]{2,1,0:T(8,128)(2,1)S(1)} %select_convert_fusion) | data formatting | bytes 1310720 | tf_op jit(solution)/shard_map/convert_element_type | solution.py:153
  (118 shorter events, 35.4 us)
Async XLA Ops:
  0.0 3.8 %copy-start = (bf16[256,1,256]{2,0,1:T(8,128)(2,1)S(1)}, bf16[256,1,256]{2,0,1:T(8,128)(2,1)}, u32[]{:S(2)}) copy-start(bf16[256,1,256]{2,0,1:T(8,128)(2,1)} %param.22) | copy-start | bytes 393220
  21.1 0.9 copy-start.1
  21.1 0.9 copy-start.2
where the time goes:
time: 103 us; the launch traced here: 102 us
  other arithmetic  32.6 us (32%)
  matrix products  29.9 us (29%)
  blocking collectives  17.3 us (17%)
  local copies, waits for them, and re-layouts  12.9 us (13%)
  loops' own time  9.11 us (9%)
    another operation x41, other arithmetic  25.6 us
    all_gather x1, blocking collectives, shards(): lax.all_gather(prompt_kv, 'loop', axis=0, tiled=True)  17.3 us
    dot_general x5, matrix products, attend_segment(): jnp.dot(weights.astype(jnp.bfloat16), value_block, preferred_element_type...  10.2 us
    dot_general x5, matrix products, attend_segment(): lax.dot_general(query_block, key_block, (((1,), (1,)), ((), ())), preferr...  7.67 us
    dot_general x5, matrix products, suffix_block(): lax.dot_general(groups[block_index], window_rows[:, :HD], (((1,), (1,)),...  6.47 us
    dot_general x5, matrix products, suffix_block(): jnp.dot(weights.astype(jnp.bfloat16), window_rows[:, HD:], preferred_elem...  5.54 us
    squeeze x5, local copies, waits for them, and re-layouts, suffix_block(): lax.dynamic_slice_in_dim(suffix_kv, window_start, window, 0)[:, 0, :]  5.07 us
    another operation x1, loops' own time, shards(): lax.fori_loop(0, my_blocks, suffix_block, own_state)  4.6 us

commit v1 on v0

v1 whole, which is shorter than its diff:
```python
import functools
import math

import jax
import jax.numpy as jnp
from jax import lax
from jax.experimental import pallas as pl
from jax.experimental.pallas import tpu as pltpu
from jax.sharding import PartitionSpec as P

HD = 128
AG_DEV = 2
MAXLEN = 320
BLK = 128

masked_score = -1e30
total_limit = 2.0**100
score_scale = math.log2(math.e) / math.sqrt(HD)


def scores_of(query_rows, key_rows):
    return lax.dot_general(
        query_rows, key_rows, (((1,), (1,)), ((), ())), preferred_element_type=jnp.float32
    )


def with_ones(value_rows):
    return jnp.concatenate([value_rows, jnp.ones_like(value_rows)], axis=1)


def stacked(ref, rows, head_count):
    return jnp.concatenate([ref[rows, h * HD : (h + 1) * HD] for h in range(head_count)], axis=0)


def unstack(ref, rows, head_count, value):
    count = value.shape[0] // head_count
    for h in range(head_count):
        ref[rows, h * HD : (h + 1) * HD] = value[h * count : (h + 1) * count]


def widen(row_value, width):
    return jnp.concatenate([row_value] * (width // HD), axis=1)


def local_stage(lengths_ref, query_ref, suffix_ref, own_ref, best_ref, total_ref, sum_ref):
    rows_all = query_ref.shape[0]
    heads = query_ref.shape[1] // HD
    position = lax.axis_index("loop")
    own_keys = own_ref[:, :HD]
    own_values = with_ones(own_ref[:, HD:])
    window = BLK * ((MAXLEN + BLK - 2) // BLK) + BLK
    for block in range(rows_all // BLK):
        stop = (block + 1) * BLK
        start = max(0, stop - window)
        rows = slice(block * BLK, stop)
        row_at = block * BLK + lax.broadcasted_iota(jnp.int32, (BLK, stop - start), 0)
        key_at = start + lax.broadcasted_iota(jnp.int32, (BLK, stop - start), 1)
        first = jnp.zeros_like(row_at)
        agent_end = 0
        for agent in range(AG_DEV):
            agent_end = agent_end + lengths_ref[position * AG_DEV + agent]
            first = jnp.where(row_at >= agent_end, agent_end, first)
        allowed = (key_at <= row_at) & (key_at >= first)
        queries = stacked(query_ref, rows, heads)
        suffix_values = with_ones(suffix_ref[start:stop, HD:])
        own_scores = scores_of(queries, own_keys) * score_scale
        suffix_scores = scores_of(queries, suffix_ref[start:stop, :HD]) * score_scale
        suffix_scores = jnp.where(
            jnp.concatenate([allowed] * heads, axis=0), suffix_scores, masked_score
        )
        best = jnp.maximum(
            jnp.max(own_scores, axis=1, keepdims=True),
            jnp.max(suffix_scores, axis=1, keepdims=True),
        )
        own_weights = jnp.exp2(own_scores - best).astype(jnp.bfloat16)
        suffix_weights = jnp.exp2(suffix_scores - best).astype(jnp.bfloat16)
        result = jnp.dot(own_weights, own_values, preferred_element_type=jnp.float32)
        result = result + jnp.dot(
            suffix_weights, suffix_values, preferred_element_type=jnp.float32
        )
        unstack(best_ref, rows, heads, jnp.broadcast_to(best, (heads * BLK, HD)))
        unstack(sum_ref, rows, heads, result[:, :HD])
        unstack(total_ref, rows, heads, result[:, HD:])


def remote_stage(shard_count, *refs):
    lengths_ref, query_ref, best_ref, total_ref, sum_ref = refs[:5]
    shard_refs = refs[5 : 5 + shard_count]
    out_ref = refs[5 + shard_count]
    rows_all = query_ref.shape[0]
    heads = query_ref.shape[1] // HD
    position = lax.axis_index("loop")
    live = 0
    for agent in range(AG_DEV):
        live = live + lengths_ref[position * AG_DEV + agent]

    def finish(rows, first_row, total, weighted):
        row_at = first_row + lax.broadcasted_iota(jnp.int32, (BLK, HD), 0)
        is_live = jnp.concatenate([row_at < live] * heads, axis=0)
        unstack(
            out_ref, rows, heads, jnp.where(is_live, weighted / total, 0.0).astype(jnp.bfloat16)
        )

    trusted = jnp.full((8, HD), True)
    keys = [ref[:, :HD] for ref in shard_refs]
    values = [with_ones(ref[:, HD:]) for ref in shard_refs]
    for block in range(rows_all // BLK):
        rows = slice(block * BLK, (block + 1) * BLK)
        queries = stacked(query_ref, rows, heads)
        best = stacked(best_ref, rows, heads)
        weighted = stacked(sum_ref, rows, heads)
        total = stacked(total_ref, rows, heads)
        for key_rows, value_rows in zip(keys, values):
            scores = scores_of(queries, key_rows) * score_scale
            weights = jnp.exp2(scores - widen(best, scores.shape[1])).astype(jnp.bfloat16)
            result = jnp.dot(weights, value_rows, preferred_element_type=jnp.float32)
            weighted = weighted + result[:, :HD]
            total = total + result[:, HD:]
        good = (total < total_limit).reshape(heads * BLK // 8, 8, HD)
        trusted = trusted & jnp.all(good, axis=0)
        finish(rows, block * BLK, total, weighted)

    @pl.when(jnp.logical_not(jnp.all(trusted)))
    def exact_maximum():
        def visit(block, unused):
            first_row = pl.multiple_of(block * BLK, BLK)
            rows = pl.ds(first_row, BLK)
            queries = stacked(query_ref, rows, heads)
            best = stacked(best_ref, rows, heads)
            weighted = stacked(sum_ref, rows, heads)
            total = stacked(total_ref, rows, heads)
            for key_rows, value_rows in zip(keys, values):
                scores = scores_of(queries, key_rows) * score_scale
                new_best = jnp.maximum(best, jnp.max(scores, axis=1, keepdims=True))
                factor = jnp.exp2(best - new_best)
                weights = jnp.exp2(scores - widen(new_best, scores.shape[1]))
                result = jnp.dot(
                    weights.astype(jnp.bfloat16), value_rows, preferred_element_type=jnp.float32
                )
                weighted = weighted * factor + result[:, :HD]
                total = total * factor + result[:, HD:]
                best = new_best
            finish(rows, first_row, total, weighted)
            return unused

        lax.fori_loop(0, rows_all // BLK, visit, 0)


def shards(queries, suffix_kv, prompt_kv, lengths):
    slots, width = queries.shape
    loop_size = lax.axis_size("loop")
    own = prompt_kv[:, 0, :]
    suffix = suffix_kv[:, 0, :]
    shard_rows = own.shape[0]
    arrived = []
    for step in range(1, loop_size):
        pairs = [(i, (i + step) % loop_size) for i in range(loop_size)]
        arrived.append(lax.ppermute(own, "loop", pairs))
    in_smem = pl.BlockSpec(memory_space=pltpu.SMEM)
    in_vmem = pl.BlockSpec(memory_space=pltpu.VMEM)
    state = jax.ShapeDtypeStruct((slots, width), jnp.float32)
    heads = width // HD
    local_pairs = slots * heads * (shard_rows + MAXLEN)
    best, total, weighted = pl.pallas_call(
        local_stage,
        name="local_stage",
        out_shape=[state] * 3,
        in_specs=[in_smem] + [in_vmem] * 3,
        out_specs=[in_vmem] * 3,
        compiler_params=pltpu.CompilerParams(vmem_limit_bytes=24 * 2**20),
        cost_estimate=pl.CostEstimate(
            flops=local_pairs * HD * 4,
            bytes_accessed=slots * width * 14,
            transcendentals=local_pairs,
        ),
    )(lengths, queries, suffix, own)
    remote_pairs = slots * heads * shard_rows * (loop_size - 1)
    return pl.pallas_call(
        functools.partial(remote_stage, loop_size - 1),
        name="remote_stage",
        out_shape=jax.ShapeDtypeStruct((slots, width), jnp.bfloat16),
        in_specs=[in_smem] + [in_vmem] * (3 + loop_size),
        out_specs=in_vmem,
        compiler_params=pltpu.CompilerParams(vmem_limit_bytes=32 * 2**20),
        cost_estimate=pl.CostEstimate(
            flops=remote_pairs * HD * 4,
            bytes_accessed=slots * width * 16,
            transcendentals=remote_pairs,
        ),
    )(lengths, queries, best, total, weighted, *arrived)


def solution(mesh):
    placed = (
        P(("groups", "loop"), ("heads", "pair")),
        P(("groups", "loop"), "heads", None),
        P(("groups", "loop"), "heads", None),
        P("groups"),
    )
    return jax.shard_map(
        shards,
        mesh=mesh,
        in_specs=placed,
        out_specs=P(("groups", "loop"), ("heads", "pair")),
        check_vma=False,
    )
```

time: 103 us -> 24.8 us (0.24)
  other arithmetic: 32.6 us -> 0 us
  matrix products: 29.9 us -> 0 us
  blocking collectives: 17.3 us -> 0 us
  Pallas kernels: 0 us -> 11.6 us
  local copies, waits for them, and re-layouts: 12.9 us -> 3.62 us
  loops' own time: 9.11 us -> 0 us
  starting transfers between devices: 0 us -> 6.06 us
  waiting for transfers between devices: 0 us -> 3.24 us
    dot_general x20 -> x0, matrix products: 29.9 us -> none  [the longest x5 10.2 us: attend_segment(): jnp.dot(weights.astype(jnp.bfloat16), value_block, preferred_element_type...]
    another operation x41 -> x0, other arithmetic: 25.6 us -> none
    all_gather x1 -> x0, blocking collectives: 17.3 us -> none  [shards(): lax.all_gather(prompt_kv, 'loop', axis=0, tiled=True)]
    pallas_call x0 -> x2, Pallas kernels: none -> 11.6 us  [the longest x1 8.09 us: shards(): pl.pallas_call(functools.partial(remote_stage, loop_size - 1), name='remo...]
    another operation x2 -> x0, loops' own time: 9.11 us -> none  [the longest x1 4.6 us: shards(): lax.fori_loop(0, my_blocks, suffix_block, own_state)]
    ppermute x0 -> x3, starting transfers between devices: none -> 6.06 us  [shards(): arrived.append(lax.ppermute(own, 'loop', pairs))]
    squeeze x5 -> x0, local copies, waits for them, and re-layouts: 5.07 us -> none  [suffix_block(): lax.dynamic_slice_in_dim(suffix_kv, window_start, window, 0)[:, 0, :]]
    reduce_sum x16 -> x0, other arithmetic: 4.67 us -> none  [the longest x5 2.52 us: attend_segment(): row_total = row_total * factor + jnp.sum(weights, axis=1)]
  transfers between devices with their start and end apart: 0 -> 3, of which waited for: 0 -> 1; matrix products, arithmetic and copies ran while one was open for 0% -> 0% of each run, Pallas kernels for 0% -> 14%
where the time goes in v1:
time: 24.8 us; the launch traced here: 24.6 us
  Pallas kernels  11.6 us (47%)
  starting transfers between devices  6.06 us (24%)
  local copies, waits for them, and re-layouts  3.62 us (15%)
  waiting for transfers between devices  3.24 us (13%)
    pallas_call x1, Pallas kernels, shards(): pl.pallas_call(functools.partial(remote_stage, loop_size - 1), name='remo...  8.09 us
    ppermute x3, starting transfers between devices, shards(): arrived.append(lax.ppermute(own, 'loop', pairs))  6.06 us
    unnamed x12, local copies, waits for them, and re-layouts  3.62 us
    pallas_call x1, Pallas kernels, shards(): pl.pallas_call(local_stage, name='local_stage', out_shape=[state] * 3, in...  3.53 us
    ppermute x3, waiting for transfers between devices, shards(): arrived.append(lax.ppermute(own, 'loop', pairs))  3.24 us
  transfers between devices with their start and end apart: 3, of which 1 were waited for; matrix products, arithmetic and copies ran while one was open for 0% of the time, Pallas kernels for 14%

profile of v1, /device:TPU:0, one launch (start us, length us, event | category | flops | bytes accessed | tf_op | source)
XLA Modules:
  0.0 24.6 jit_solution(3276514016052070352)
XLA Ops:
  0.0 5.0 %collective-permute-start.2 = (bf16[256,256]{1,0:T(8,128)(2,1)}, bf16[256,256]{1,0:T(8,128)(2,1)S(1)}, u32[]{:S(2)}, u32[]{:S(2)}) collective-permute-start(bf16[256,256]{1,0:T(8,128)(2,1)} %bitcast.3), channel_id=1, source_target_pairs={{0,12},{4,0},{8,4},{12,8},{1,13},{5,1},{9,5},{13,9},{2,14},{6,2},{... | collective-permute-start | bytes 393224 | tf_op jit(solution)/shard_map/ppermute | solution.py:158
  5.0 0.0 collective-permute-start.1
  5.1 1.0 %collective-permute-start = (bf16[256,256]{1,0:T(8,128)(2,1)}, bf16[256,256]{1,0:T(8,128)(2,1)S(1)}, u32[]{:S(2)}, u32[]{:S(2)}) collective-permute-start(bf16[256,256]{1,0:T(8,128)(2,1)} %bitcast.5), channel_id=1, source_target_pairs={{0,4},{4,8},{8,12},{12,0},{1,5},{5,9},{9,13},{13,1},{2,6},{6,10},{... | collective-permute-start | bytes 393224 | tf_op jit(solution)/shard_map/ppermute | solution.py:158
  6.1 0.0 copy-start
  6.1 1.1 %copy-done = bf16[640,512]{1,0:T(8,128)(2,1)S(1)} copy-done((bf16[640,512]{1,0:T(8,128)(2,1)S(1)}, bf16[640,512]{1,0:T(8,128)(2,1)}, u32[]{:S(2)}) %copy-start) | copy-done | bytes 655384
  7.2 0.0 copy-start.2
  7.2 0.7 %copy-done.2 = s32[8]{0:T(128)S(1)} copy-done((s32[8]{0:T(128)S(1)}, s32[8]{0:T(128)}, u32[]{:S(2)}) %copy-start.2) | copy-done | bytes 56
  7.8 0.0 copy-start.4
  7.8 1.0 %copy-done.4 = bf16[640,1,256]{2,0,1:T(8,128)(2,1)S(1)} copy-done((bf16[640,1,256]{2,0,1:T(8,128)(2,1)S(1)}, bf16[640,1,256]{2,0,1:T(8,128)(2,1)}, u32[]{:S(2)}) %copy-start.4) | copy-done | bytes 327704
  8.8 0.0 copy-start.5
  8.8 0.9 %copy-done.5 = bf16[256,1,256]{2,0,1:T(8,128)(2,1)S(1)} copy-done((bf16[256,1,256]{2,0,1:T(8,128)(2,1)S(1)}, bf16[256,1,256]{2,0,1:T(8,128)(2,1)}, u32[]{:S(2)}) %copy-start.5) | copy-done | bytes 131096
  9.7 0.0 copy-start.1
  9.7 0.0 copy-start.3
  9.7 3.5 %local_stage.1 = (f32[640,512]{1,0:T(8,128)S(1)}, f32[640,512]{1,0:T(8,128)S(1)}, f32[640,512]{1,0:T(8,128)S(1)}) custom-call(s32[8]{0:T(128)S(1)} %copy-done.2, bf16[640,512]{1,0:T(8,128)(2,1)S(1)} %copy-done, bf16[640,256]{1,0:T(8,128)(2,1)S(1)} %bitcast.2, bf16[256,256]{1,0:T(8,128)(2,1)S(1)} %bitcast.6), custom_call_target="tpu_custom_call" | custom-call | flops 754974720 | bytes 4587520 | tf_op jit(solution)/shard_map/local_stage/pallas_call | solution.py:164
  13.2 0.0 collective-permute-done.2.refs_7_
  13.2 3.2 %collective-permute-done.1.refs_6_ = bf16[256,256]{1,0:T(8,128)(2,1)S(1)} collective-permute-done((bf16[256,256]{1,0:T(8,128)(2,1)}, bf16[256,256]{1,0:T(8,128)(2,1)S(1)}, u32[]{:S(2)}, u32[]{:S(2)}) %collective-permute-start.1) | collective-permute-done | bytes 131104 | tf_op jit(solution)/shard_map/ppermute | solution.py:158
  16.5 0.0 collective-permute-done.refs_5_
  16.5 0.0 copy-done.1
  16.5 0.0 copy-done.3
  16.5 8.1 %remote_stage.1 = bf16[640,512]{1,0:T(8,128)(2,1)} custom-call(s32[8]{0:T(128)S(1)} %copy-done.3, bf16[640,512]{1,0:T(8,128)(2,1)S(1)} %copy-done.1, f32[640,512]{1,0:T(8,128)S(1)} %get-tuple-element.8.refs_2_, f32[640,512]{1,0:T(8,128)S(1)} %get-tuple-element.9.refs_3_, f32[640,512]{1,0:T(8,128)S(1)} %get-tuple-element.10.refs_4_, ...), custom_call_target="tpu_custom_call" | custom-call | flops 1006632960 | bytes 5242880 | tf_op jit(solution)/shard_map/remote_stage/pallas_call | solution.py:178
Async XLA Ops:
  0.0 13.2 %collective-permute-start.2 = (bf16[256,256]{1,0:T(8,128)(2,1)}, bf16[256,256]{1,0:T(8,128)(2,1)S(1)}, u32[]{:S(2)}, u32[]{:S(2)}) collective-permute-start(bf16[256,256]{1,0:T(8,128)(2,1)} %bitcast.3), channel_id=1, source_target_pairs={{0,12},{4,0},{8,4},{12,8},{1,13},{5,1},{9,5},{13,9},{2,14},{6,2},{... | collective-permute-start | bytes 393224 | tf_op jit(solution)/shard_map/ppermute | solution.py:158
  5.0 11.4 %collective-permute-start.1 = (bf16[256,256]{1,0:T(8,128)(2,1)}, bf16[256,256]{1,0:T(8,128)(2,1)S(1)}, u32[]{:S(2)}, u32[]{:S(2)}) collective-permute-start(bf16[256,256]{1,0:T(8,128)(2,1)} %bitcast.4), channel_id=1, source_target_pairs={{0,8},{4,12},{8,0},{12,4},{1,9},{5,13},{9,1},{13,5},{2,10},{6,14},... | collective-permute-start | bytes 393224 | tf_op jit(solution)/shard_map/ppermute | solution.py:158
  5.1 11.4 %collective-permute-start = (bf16[256,256]{1,0:T(8,128)(2,1)}, bf16[256,256]{1,0:T(8,128)(2,1)S(1)}, u32[]{:S(2)}, u32[]{:S(2)}) collective-permute-start(bf16[256,256]{1,0:T(8,128)(2,1)} %bitcast.5), channel_id=1, source_target_pairs={{0,4},{4,8},{8,12},{12,0},{1,5},{5,9},{9,13},{13,1},{2,6},{6,10},{... | collective-permute-start | bytes 393224 | tf_op jit(solution)/shard_map/ppermute | solution.py:158
  6.1 1.1 %copy-start = (bf16[640,512]{1,0:T(8,128)(2,1)S(1)}, bf16[640,512]{1,0:T(8,128)(2,1)}, u32[]{:S(2)}) copy-start(bf16[640,512]{1,0:T(8,128)(2,1)} %refs_1_.1) | copy-start | bytes 1966084
  7.2 0.7 %copy-start.2 = (s32[8]{0:T(128)S(1)}, s32[8]{0:T(128)}, u32[]{:S(2)}) copy-start(s32[8]{0:T(128)} %refs_0_.1) | copy-start | bytes 100
  7.8 1.0 %copy-start.4 = (bf16[640,1,256]{2,0,1:T(8,128)(2,1)S(1)}, bf16[640,1,256]{2,0,1:T(8,128)(2,1)}, u32[]{:S(2)}) copy-start(bf16[640,1,256]{2,0,1:T(8,128)(2,1)} %param.5) | copy-start | bytes 983044
  8.8 0.9 %copy-start.5 = (bf16[256,1,256]{2,0,1:T(8,128)(2,1)S(1)}, bf16[256,1,256]{2,0,1:T(8,128)(2,1)}, u32[]{:S(2)}) copy-start(bf16[256,1,256]{2,0,1:T(8,128)(2,1)} %param.6) | copy-start | bytes 393220
  9.7 6.8 %copy-start.1 = (bf16[640,512]{1,0:T(8,128)(2,1)S(1)}, bf16[640,512]{1,0:T(8,128)(2,1)}, u32[]{:S(2)}) copy-start(bf16[640,512]{1,0:T(8,128)(2,1)} %refs_1_.1) | copy-start | bytes 1966084
  9.7 6.8 %copy-start.3 = (s32[8]{0:T(128)S(1)}, s32[8]{0:T(128)}, u32[]{:S(2)}) copy-start(s32[8]{0:T(128)} %refs_0_.1) | copy-start | bytes 100

commit v2 on v1

v2 whole, which is shorter than its diff:
```python
import functools
import math

import jax
import jax.numpy as jnp
from jax import lax
from jax.experimental import pallas as pl
from jax.experimental.pallas import tpu as pltpu
from jax.sharding import PartitionSpec as P

HD = 128
AG_DEV = 2
MAXLEN = 320
BLK = 128

masked_score = -1e30
empty_best = 1e30
total_limit = 2.0**100
score_scale = math.log2(math.e) / math.sqrt(HD)


def scores_of(query_rows, key_rows):
    return (
        lax.dot_general(
            query_rows, key_rows, (((1,), (1,)), ((), ())), preferred_element_type=jnp.float32
        )
        * score_scale
    )


def with_ones(value_rows):
    return jnp.concatenate([value_rows, jnp.ones_like(value_rows)], axis=1)


def stacked(ref, rows, head_count):
    return jnp.concatenate([ref[rows, h * HD : (h + 1) * HD] for h in range(head_count)], axis=0)


def unstack(ref, rows, head_count, value):
    count = value.shape[0] // head_count
    for h in range(head_count):
        ref[rows, h * HD : (h + 1) * HD] = value[h * count : (h + 1) * count]


def widen(row_value, width):
    return jnp.concatenate([row_value] * (width // HD), axis=1)


def local_stage(
    lengths_hbm,
    query_hbm,
    suffix_hbm,
    own_hbm,
    best_ref,
    total_ref,
    sum_ref,
    query_ref,
    lengths_ref,
    suffix_ref,
    own_ref,
    whole_sems,
    block_sems,
):
    rows_all = query_ref.shape[0]
    heads = query_ref.shape[1] // HD
    blocks = rows_all // BLK
    whole = [
        pltpu.make_async_copy(source, target, whole_sems.at[i])
        for i, (source, target) in enumerate(
            [(lengths_hbm, lengths_ref), (own_hbm, own_ref), (suffix_hbm, suffix_ref)]
        )
    ]
    pieces = [
        pltpu.make_async_copy(
            query_hbm.at[pl.ds(block * BLK, BLK)],
            query_ref.at[pl.ds(block * BLK, BLK)],
            block_sems.at[block],
        )
        for block in range(blocks)
    ]
    for copy in whole + pieces:
        copy.start()
    for copy in whole:
        copy.wait()
    position = lax.axis_index("loop")
    own_keys = own_ref[:, :HD]
    own_values = with_ones(own_ref[:, HD:])
    window = BLK * ((MAXLEN + BLK - 2) // BLK) + BLK
    for block in range(blocks):
        stop = (block + 1) * BLK
        start = max(0, stop - window)
        rows = slice(block * BLK, stop)
        row_at = block * BLK + lax.broadcasted_iota(jnp.int32, (BLK, stop - start), 0)
        key_at = start + lax.broadcasted_iota(jnp.int32, (BLK, stop - start), 1)
        first = jnp.zeros_like(row_at)
        agent_end = 0
        for agent in range(AG_DEV):
            agent_end = agent_end + lengths_ref[position * AG_DEV + agent]
            first = jnp.where(row_at >= agent_end, agent_end, first)
        allowed = (key_at <= row_at) & (key_at >= first)
        pieces[block].wait()
        queries = stacked(query_ref, rows, heads)
        own_scores = scores_of(queries, own_keys)
        suffix_scores = jnp.where(
            jnp.concatenate([allowed] * heads, axis=0),
            scores_of(queries, suffix_ref[start:stop, :HD]),
            masked_score,
        )
        best = jnp.maximum(
            jnp.max(own_scores, axis=1, keepdims=True),
            jnp.max(suffix_scores, axis=1, keepdims=True),
        )
        own_weights = jnp.exp2(own_scores - best).astype(jnp.bfloat16)
        suffix_weights = jnp.exp2(suffix_scores - best).astype(jnp.bfloat16)
        result = jnp.dot(own_weights, own_values, preferred_element_type=jnp.float32)
        result = result + jnp.dot(
            suffix_weights,
            with_ones(suffix_ref[start:stop, HD:]),
            preferred_element_type=jnp.float32,
        )
        row_at = block * BLK + lax.broadcasted_iota(jnp.int32, (BLK, HD), 0)
        live = jnp.concatenate([row_at < agent_end] * heads, axis=0)
        unstack(best_ref, rows, heads, jnp.where(live, best, empty_best))
        unstack(sum_ref, rows, heads, jnp.where(live, result[:, :HD], 0.0))
        unstack(total_ref, rows, heads, jnp.where(live, result[:, HD:], 1.0))


def add_pieces(query_ref, best_ref, rows, heads, pieces, total, weighted):
    queries = stacked(query_ref, rows, heads)
    best = stacked(best_ref, rows, heads)
    for key_rows, value_rows in pieces:
        scores = scores_of(queries, key_rows)
        weights = jnp.exp2(scores - widen(best, scores.shape[1])).astype(jnp.bfloat16)
        result = jnp.dot(weights, value_rows, preferred_element_type=jnp.float32)
        weighted = weighted + result[:, :HD]
        total = total + result[:, HD:]
    return total, weighted


def loaded(piece_refs):
    return [(ref[:, :HD], with_ones(ref[:, HD:])) for ref in piece_refs]


def first_half_stage(*refs):
    query_ref, best_ref, total_ref, sum_ref = refs[:4]
    piece_refs = refs[4:-2]
    total_out, sum_out = refs[-2:]
    heads = query_ref.shape[1] // HD
    pieces = loaded(piece_refs)
    for block in range(query_ref.shape[0] // BLK):
        rows = slice(block * BLK, (block + 1) * BLK)
        total, weighted = add_pieces(
            query_ref,
            best_ref,
            rows,
            heads,
            pieces,
            stacked(total_ref, rows, heads),
            stacked(sum_ref, rows, heads),
        )
        unstack(total_out, rows, heads, total)
        unstack(sum_out, rows, heads, weighted)


def second_half_stage(count, *refs):
    query_ref, best_ref, old_total_ref, old_sum_ref, total_ref, sum_ref = refs[:6]
    early_refs = refs[6 : 6 + count]
    late_refs = refs[6 + count : 6 + 2 * count]
    out_hbm, out_ref, out_sems = refs[6 + 2 * count :]
    heads = query_ref.shape[1] // HD
    blocks = query_ref.shape[0] // BLK

    def out_copy(block):
        rows = pl.ds(block * BLK, BLK)
        return pltpu.make_async_copy(out_ref.at[rows], out_hbm.at[rows], out_sems.at[block])

    def finish(rows, total, weighted):
        unstack(out_ref, rows, heads, (weighted / total).astype(jnp.bfloat16))

    trusted = jnp.full((8, HD), True)
    late = loaded(late_refs)
    for block in range(blocks):
        rows = slice(block * BLK, (block + 1) * BLK)
        total, weighted = add_pieces(
            query_ref,
            best_ref,
            rows,
            heads,
            late,
            stacked(total_ref, rows, heads),
            stacked(sum_ref, rows, heads),
        )
        good = (total < total_limit).reshape(heads * BLK // 8, 8, HD)
        trusted = trusted & jnp.all(good, axis=0)
        finish(rows, total, weighted)
        out_copy(block).start()
    for block in range(blocks):
        out_copy(block).wait()

    @pl.when(jnp.logical_not(jnp.all(trusted)))
    def exact_maximum():
        def visit(block, unused):
            rows = pl.ds(pl.multiple_of(block * BLK, BLK), BLK)
            queries = stacked(query_ref, rows, heads)
            best = stacked(best_ref, rows, heads)
            weighted = stacked(old_sum_ref, rows, heads)
            total = stacked(old_total_ref, rows, heads)
            for key_rows, value_rows in loaded(early_refs + late_refs):
                scores = scores_of(queries, key_rows)
                new_best = jnp.maximum(best, jnp.max(scores, axis=1, keepdims=True))
                factor = jnp.exp2(best - new_best)
                weights = jnp.exp2(scores - widen(new_best, scores.shape[1]))
                result = jnp.dot(
                    weights.astype(jnp.bfloat16), value_rows, preferred_element_type=jnp.float32
                )
                weighted = weighted * factor + result[:, :HD]
                total = total * factor + result[:, HD:]
                best = new_best
            finish(rows, total, weighted)
            copy = out_copy(block)
            copy.start()
            copy.wait()
            return unused

        lax.fori_loop(0, blocks, visit, 0)


def shards(queries, suffix_kv, prompt_kv, lengths):
    slots, width = queries.shape
    heads = width // HD
    loop_size = lax.axis_size("loop")
    pair_size = lax.axis_size("pair")
    own = prompt_kv[:, 0, :]
    suffix = suffix_kv[:, 0, :]
    shard_rows = own.shape[0]
    half_rows = shard_rows // pair_size
    half = lax.dynamic_slice_in_dim(own, lax.axis_index("pair") * half_rows, half_rows, 0)
    early, late = [], []
    for step in range(1, loop_size):
        around = [(i, (i + step) % loop_size) for i in range(loop_size)]
        early.append(lax.ppermute(half, "loop", around))
    in_hbm = pl.BlockSpec(memory_space=pltpu.HBM)
    in_vmem = pl.BlockSpec(memory_space=pltpu.VMEM)
    state = jax.ShapeDtypeStruct((slots, width), jnp.float32)

    def cost(keys):
        return pl.CostEstimate(
            flops=slots * heads * keys * HD * 4,
            bytes_accessed=slots * width * 14,
            transcendentals=slots * heads * keys,
        )

    best, total, weighted, queries = pl.pallas_call(
        local_stage,
        name="local_stage",
        out_shape=[state] * 3 + [jax.ShapeDtypeStruct((slots, width), queries.dtype)],
        in_specs=[in_hbm] * 4,
        out_specs=[in_vmem] * 4,
        scratch_shapes=[
            pltpu.SMEM(lengths.shape, lengths.dtype),
            pltpu.VMEM(suffix.shape, suffix.dtype),
            pltpu.VMEM(own.shape, own.dtype),
            pltpu.SemaphoreType.DMA((3,)),
            pltpu.SemaphoreType.DMA((slots // BLK,)),
        ],
        compiler_params=pltpu.CompilerParams(vmem_limit_bytes=24 * 2**20),
        cost_estimate=cost(shard_rows + MAXLEN),
    )(*(pltpu.with_memory_space_constraint(x, pltpu.HBM) for x in (lengths, queries, suffix, own)))
    early, best = lax.optimization_barrier((early, best))
    for piece in early:
        for turn in range(1, pair_size):
            across = [(i, (i + turn) % pair_size) for i in range(pair_size)]
            late.append(lax.ppermute(piece, "pair", across))
    early_total, early_weighted = pl.pallas_call(
        first_half_stage,
        name="first_half_stage",
        out_shape=[state] * 2,
        in_specs=[in_vmem] * (4 + len(early)),
        out_specs=[in_vmem] * 2,
        compiler_params=pltpu.CompilerParams(vmem_limit_bytes=24 * 2**20),
        cost_estimate=cost(half_rows * len(early)),
    )(queries, best, total, weighted, *early)
    return pl.pallas_call(
        functools.partial(second_half_stage, len(early)),
        name="second_half_stage",
        out_shape=jax.ShapeDtypeStruct((slots, width), jnp.bfloat16),
        in_specs=[in_vmem] * (6 + len(early) + len(late)),
        out_specs=in_hbm,
        scratch_shapes=[
            pltpu.VMEM((slots, width), jnp.bfloat16),
            pltpu.SemaphoreType.DMA((slots // BLK,)),
        ],
        compiler_params=pltpu.CompilerParams(vmem_limit_bytes=24 * 2**20),
        cost_estimate=cost(half_rows * len(late)),
    )(queries, best, total, weighted, early_total, early_weighted, *early, *late)


def solution(mesh):
    placed = (
        P(("groups", "loop"), ("heads", "pair")),
        P(("groups", "loop"), "heads", None),
        P(("groups", "loop"), "heads", None),
        P("groups"),
    )
    return jax.shard_map(
        shards,
        mesh=mesh,
        in_specs=placed,
        out_specs=P(("groups", "loop"), ("heads", "pair")),
        check_vma=False,
    )
```

time: 24.8 us -> 30.3 us (1.22)
  Pallas kernels: 11.6 us -> 22.4 us
  waiting for transfers between devices: 3.24 us -> 0.02 us
  local copies, waits for them, and re-layouts: 3.62 us -> 0.84 us
  starting transfers between devices: 6.06 us -> 6.71 us
    pallas_call x2 -> x3, Pallas kernels: 11.6 us -> 22.4 us  [the longest x1 14 us: shards(): pl.pallas_call(functools.partial(second_half_stage, len(early)), name='se...]
    unnamed x12 -> x0, local copies, waits for them, and re-layouts: 3.62 us -> none
    ppermute x3 -> x6, waiting for transfers between devices: 3.24 us -> 0.02 us  [the longest x3 0.01 us: shards(): early.append(lax.ppermute(half, 'loop', around))]
    dynamic_slice x0 -> x1, local copies, waits for them, and re-layouts: none -> 0.84 us  [shards(): lax.dynamic_slice_in_dim(own, lax.axis_index('pair') * half_rows, half_ro...]
    ppermute x3 -> x6, starting transfers between devices: 6.06 us -> 6.71 us  [the longest x3 6.06 us: shards(): early.append(lax.ppermute(half, 'loop', around))]
  transfers between devices with their start and end apart: 3 -> 6, of which waited for: 1 -> 0; matrix products, arithmetic and copies ran while one was open for 0% -> 0% of each run, Pallas kernels for 14% -> 28%
where the time goes in v2:
time: 30.3 us; the launch traced here: 30 us
  Pallas kernels  22.4 us (74%)
  starting transfers between devices  6.71 us (22%)
  local copies, waits for them, and re-layouts  0.84 us (3%)
    pallas_call x1, Pallas kernels, shards(): pl.pallas_call(functools.partial(second_half_stage, len(early)), name='se...  14 us
    ppermute x3, starting transfers between devices, shards(): early.append(lax.ppermute(half, 'loop', around))  6.06 us
    pallas_call x1, Pallas kernels, shards(): pl.pallas_call(local_stage, name='local_stage', out_shape=[state] * 3 + [...  6.06 us
    pallas_call x1, Pallas kernels, shards(): pl.pallas_call(first_half_stage, name='first_half_stage', out_shape=[stat...  2.35 us
    dynamic_slice x1, local copies, waits for them, and re-layouts, shards(): lax.dynamic_slice_in_dim(own, lax.axis_index('pair') * half_rows, half_ro...  0.84 us
    ppermute x3, starting transfers between devices, shards(): late.append(lax.ppermute(piece, 'pair', across))  0.65 us
  transfers between devices with their start and end apart: 6, of which 0 were waited for; matrix products, arithmetic and copies ran while one was open for 0% of the time, Pallas kernels for 28%

profile of v2, /device:TPU:0, one launch (start us, length us, event | category | flops | bytes accessed | tf_op | source)
XLA Modules:
  0.0 30.0 jit_solution(2686885034759192724)
XLA Ops:
  0.0 0.8 %dynamic-slice_bitcast_fusion = bf16[128,256]{1,0:T(8,128)(2,1)S(1)} fusion(bf16[256,1,256]{2,0,1:T(8,128)(2,1)} %param.6, s32[]{:T(128)S(6)} %select_n.3), kind=kLoop, calls=%fused_computation | loop fusion | bytes 131076 | tf_op jit(solution)/shard_map/dynamic_slice | solution.py:237
  0.8 5.0 %collective-permute-start.2 = (bf16[128,256]{1,0:T(8,128)(2,1)S(1)}, bf16[128,256]{1,0:T(8,128)(2,1)S(1)}, u32[]{:S(2)}, u32[]{:S(2)}) collective-permute-start(bf16[128,256]{1,0:T(8,128)(2,1)S(1)} %dynamic-slice_bitcast_fusion), channel_id=1, source_target_pairs={{0,12},{4,0},{8,4},{12,8},{1,13},{5,1},{9,5},{13,9},{2,14},{6,2},{... | collective-permute-start | bytes 196616 | tf_op jit(solution)/shard_map/ppermute | solution.py:241
  5.9 0.0 collective-permute-start.1
  5.9 1.0 %collective-permute-start = (bf16[128,256]{1,0:T(8,128)(2,1)S(1)}, bf16[128,256]{1,0:T(8,128)(2,1)S(1)}, u32[]{:S(2)}, u32[]{:S(2)}) collective-permute-start(bf16[128,256]{1,0:T(8,128)(2,1)S(1)} %dynamic-slice_bitcast_fusion), channel_id=1, source_target_pairs={{0,4},{4,8},{8,12},{12,0},{1,5},{5,9},{9,13},{13,1},{2,6},{6,10},{... | collective-permute-start | bytes 196616 | tf_op jit(solution)/shard_map/ppermute | solution.py:241
  6.9 6.1 %local_stage.1 = (f32[640,512]{1,0:T(8,128)S(1)}, f32[640,512]{1,0:T(8,128)S(1)}, f32[640,512]{1,0:T(8,128)S(1)}, bf16[640,512]{1,0:T(8,128)(2,1)S(1)}) custom-call(s32[8]{0:T(128)} %lengths_hbm.1, bf16[640,512]{1,0:T(8,128)(2,1)} %query_hbm.1, bf16[640,256]{1,0:T(8,128)(2,1)} %bitcast.5, bf16[256,256]{1,0:T(8,128)(2,1)} %bitcast.4), custom_call_target="tpu_custom_call" | custom-call | flops 754974720 | bytes 4587520 | tf_op jit(solution)/shard_map/local_stage/pallas_call | solution.py:253
  13.0 0.0 collective-permute-done.2.refs_6_.refs_8_
  13.0 0.0 collective-permute-done.1.refs_5_.refs_7_
  13.0 0.0 collective-permute-done.refs_4_.refs_6_
  13.0 0.1 collective-permute-start.3
  13.1 0.5 %collective-permute-start.4 = (bf16[128,256]{1,0:T(8,128)(2,1)S(1)}, bf16[128,256]{1,0:T(8,128)(2,1)S(1)}, u32[]{:S(2)}, u32[]{:S(2)}) collective-permute-start(bf16[128,256]{1,0:T(8,128)(2,1)S(1)} %collective-permute-done.1.refs_5_.refs_7_), channel_id=1, source_target_pairs={{0,1},{1,0},{2,3},{3,2},{4,5},{5,4},{6,7},{7,6},{8,9},{9,8},{10,11... | collective-permute-start | bytes 196616 | tf_op jit(solution)/shard_map/ppermute | solution.py:273
  13.6 0.1 collective-permute-start.5
  13.7 2.3 %first_half_stage.1 = (f32[640,512]{1,0:T(8,128)S(1)}, f32[640,512]{1,0:T(8,128)S(1)}) custom-call(bf16[640,512]{1,0:T(8,128)(2,1)S(1)} %get-tuple-element.15.refs_0_, f32[640,512]{1,0:T(8,128)S(1)} %get-tuple-element.17.refs_1_, f32[640,512]{1,0:T(8,128)S(1)} %get-tuple-element.18.refs_2_, f32[640,512]{1,0:T(8,128)S(1)} %get-tuple-element.19.refs_3_, ...), custom_call_target="tpu_custom_call" | custom-call | flops 503316480 | bytes 4587520 | tf_op jit(solution)/shard_map/first_half_stage/pallas_call | solution.py:274
  16.0 0.0 collective-permute-done.3.refs_9_
  16.0 0.0 collective-permute-done.4.refs_10_
  16.0 0.0 collective-permute-done.5.refs_11_
  16.0 14.0 %second_half_stage.1 = bf16[640,512]{1,0:T(8,128)(2,1)} custom-call(bf16[640,512]{1,0:T(8,128)(2,1)S(1)} %get-tuple-element.15.refs_0_, f32[640,512]{1,0:T(8,128)S(1)} %get-tuple-element.17.refs_1_, f32[640,512]{1,0:T(8,128)S(1)} %get-tuple-element.18.refs_2_, f32[640,512]{1,0:T(8,128)S(1)} %get-tuple-element.19.refs_3_, ...), custom_call_target="tpu_custom_call" | custom-call | flops 503316480 | bytes 4587520 | tf_op jit(solution)/shard_map/second_half_stage/pallas_call | solution.py:283
Async XLA Ops:
  0.8 12.1 %collective-permute-start.2 = (bf16[128,256]{1,0:T(8,128)(2,1)S(1)}, bf16[128,256]{1,0:T(8,128)(2,1)S(1)}, u32[]{:S(2)}, u32[]{:S(2)}) collective-permute-start(bf16[128,256]{1,0:T(8,128)(2,1)S(1)} %dynamic-slice_bitcast_fusion), channel_id=1, source_target_pairs={{0,12},{4,0},{8,4},{12,8},{1,13},{5,1},{9,5},{13,9},{2,14},{6,2},{... | collective-permute-start | bytes 196616 | tf_op jit(solution)/shard_map/ppermute | solution.py:241
  5.9 7.1 %collective-permute-start.1 = (bf16[128,256]{1,0:T(8,128)(2,1)S(1)}, bf16[128,256]{1,0:T(8,128)(2,1)S(1)}, u32[]{:S(2)}, u32[]{:S(2)}) collective-permute-start(bf16[128,256]{1,0:T(8,128)(2,1)S(1)} %dynamic-slice_bitcast_fusion), channel_id=1, source_target_pairs={{0,8},{4,12},{8,0},{12,4},{1,9},{5,13},{9,1},{13,5},{2,10},{6,14},... | collective-permute-start | bytes 196616 | tf_op jit(solution)/shard_map/ppermute | solution.py:241
  5.9 7.1 %collective-permute-start = (bf16[128,256]{1,0:T(8,128)(2,1)S(1)}, bf16[128,256]{1,0:T(8,128)(2,1)S(1)}, u32[]{:S(2)}, u32[]{:S(2)}) collective-permute-start(bf16[128,256]{1,0:T(8,128)(2,1)S(1)} %dynamic-slice_bitcast_fusion), channel_id=1, source_target_pairs={{0,4},{4,8},{8,12},{12,0},{1,5},{5,9},{9,13},{13,1},{2,6},{6,10},{... | collective-permute-start | bytes 196616 | tf_op jit(solution)/shard_map/ppermute | solution.py:241
  13.0 3.0 %collective-permute-start.3 = (bf16[128,256]{1,0:T(8,128)(2,1)S(1)}, bf16[128,256]{1,0:T(8,128)(2,1)S(1)}, u32[]{:S(2)}, u32[]{:S(2)}) collective-permute-start(bf16[128,256]{1,0:T(8,128)(2,1)S(1)} %collective-permute-done.refs_4_.refs_6_), channel_id=1, source_target_pairs={{0,1},{1,0},{2,3},{3,2},{4,5},{5,4},{6,7},{7,6},{8,9},{9,8},{10,11... | collective-permute-start | bytes 196616 | tf_op jit(solution)/shard_map/ppermute | solution.py:273
  13.1 2.9 %collective-permute-start.4 = (bf16[128,256]{1,0:T(8,128)(2,1)S(1)}, bf16[128,256]{1,0:T(8,128)(2,1)S(1)}, u32[]{:S(2)}, u32[]{:S(2)}) collective-permute-start(bf16[128,256]{1,0:T(8,128)(2,1)S(1)} %collective-permute-done.1.refs_5_.refs_7_), channel_id=1, source_target_pairs={{0,1},{1,0},{2,3},{3,2},{4,5},{5,4},{6,7},{7,6},{8,9},{9,8},{10,11... | collective-permute-start | bytes 196616 | tf_op jit(solution)/shard_map/ppermute | solution.py:273
  13.6 2.5 %collective-permute-start.5 = (bf16[128,256]{1,0:T(8,128)(2,1)S(1)}, bf16[128,256]{1,0:T(8,128)(2,1)S(1)}, u32[]{:S(2)}, u32[]{:S(2)}) collective-permute-start(bf16[128,256]{1,0:T(8,128)(2,1)S(1)} %collective-permute-done.2.refs_6_.refs_8_), channel_id=1, source_target_pairs={{0,1},{1,0},{2,3},{3,2},{4,5},{5,4},{6,7},{7,6},{8,9},{9,8},{10,11... | collective-permute-start | bytes 196616 | tf_op jit(solution)/shard_map/ppermute | solution.py:273

commit v3 on v2

--- a/solution.py
+++ b/solution.py
@@ -80,7 +80,7 @@
     ]
     for copy in whole + pieces:
         copy.start()
-    for copy in whole:
+    for copy in whole + pieces:
         copy.wait()
     position = lax.axis_index("loop")
     own_keys = own_ref[:, :HD]
@@ -98,7 +98,6 @@
             agent_end = agent_end + lengths_ref[position * AG_DEV + agent]
             first = jnp.where(row_at >= agent_end, agent_end, first)
         allowed = (key_at <= row_at) & (key_at >= first)
-        pieces[block].wait()
         queries = stacked(query_ref, rows, heads)
         own_scores = scores_of(queries, own_keys)
         suffix_scores = jnp.where(
@@ -125,87 +124,86 @@
         unstack(total_ref, rows, heads, jnp.where(live, result[:, HD:], 1.0))
 
 
-def add_pieces(query_ref, best_ref, rows, heads, pieces, total, weighted):
-    queries = stacked(query_ref, rows, heads)
-    best = stacked(best_ref, rows, heads)
-    for key_rows, value_rows in pieces:
-        scores = scores_of(queries, key_rows)
-        weights = jnp.exp2(scores - widen(best, scores.shape[1])).astype(jnp.bfloat16)
-        result = jnp.dot(weights, value_rows, preferred_element_type=jnp.float32)
-        weighted = weighted + result[:, :HD]
-        total = total + result[:, HD:]
-    return total, weighted
-
-
-def loaded(piece_refs):
-    return [(ref[:, :HD], with_ones(ref[:, HD:])) for ref in piece_refs]
-
-
-def first_half_stage(*refs):
+def add_shard(queries, best, key_rows, value_rows, total, weighted):
+    scores = scores_of(queries, key_rows)
+    weights = jnp.exp2(scores - widen(best, scores.shape[1])).astype(jnp.bfloat16)
+    result = jnp.dot(weights, value_rows, preferred_element_type=jnp.float32)
+    return total + result[:, HD:], weighted + result[:, :HD]
+
+
+def row_blocks(count):
+    step = next(size for size in (160, 128, count) if count % size == 0)
+    return [slice(first, first + step) for first in range(0, count, step)]
+
+
+def early_stage(*refs):
     query_ref, best_ref, total_ref, sum_ref = refs[:4]
-    piece_refs = refs[4:-2]
+    shard_refs = refs[4:-2]
     total_out, sum_out = refs[-2:]
     heads = query_ref.shape[1] // HD
-    pieces = loaded(piece_refs)
-    for block in range(query_ref.shape[0] // BLK):
-        rows = slice(block * BLK, (block + 1) * BLK)
-        total, weighted = add_pieces(
-            query_ref,
-            best_ref,
-            rows,
-            heads,
-            pieces,
-            stacked(total_ref, rows, heads),
-            stacked(sum_ref, rows, heads),
-        )
+    shards_here = [(ref[:, :HD], with_ones(ref[:, HD:])) for ref in shard_refs]
+    for rows in row_blocks(query_ref.shape[0]):
+        queries = stacked(query_ref, rows, heads)
+        best = stacked(best_ref, rows, heads)
+        total = stacked(total_ref, rows, heads)
+        weighted = stacked(sum_ref, rows, heads)
+        for key_rows, value_rows in shards_here:
+            total, weighted = add_shard(queries, best, key_rows, value_rows, total, weighted)
         unstack(total_out, rows, heads, total)
         unstack(sum_out, rows, heads, weighted)
 
 
-def second_half_stage(count, *refs):
+def late_stage(early_count, late_count, half_count, *refs):
     query_ref, best_ref, old_total_ref, old_sum_ref, total_ref, sum_ref = refs[:6]
-    early_refs = refs[6 : 6 + count]
-    late_refs = refs[6 + count : 6 + 2 * count]
-    out_hbm, out_ref, out_sems = refs[6 + 2 * count :]
+    refs = refs[6:]
+    early_refs, refs = refs[:early_count], refs[early_count:]
+    late_refs, refs = refs[:late_count], refs[late_count:]
+    direct_refs, refs = refs[:half_count], refs[half_count:]
+    passed_refs, refs = refs[:half_count], refs[half_count:]
+    out_hbm, out_ref, out_sems = refs
     heads = query_ref.shape[1] // HD
-    blocks = query_ref.shape[0] // BLK
-
-    def out_copy(block):
-        rows = pl.ds(block * BLK, BLK)
-        return pltpu.make_async_copy(out_ref.at[rows], out_hbm.at[rows], out_sems.at[block])
+    blocks = row_blocks(query_ref.shape[0])
+    is_direct = lax.axis_index("pair") == 0
+
+    def load(early):
+        loaded = [ref[...] for ref in early + late_refs]
+        for direct_ref, passed_ref in zip(direct_refs, passed_refs):
+            loaded.append(jnp.where(is_direct, direct_ref[...], passed_ref[...]))
+        return [(shard[:, :HD], with_ones(shard[:, HD:])) for shard in loaded]
+
+    def out_copy(index, rows):
+        return pltpu.make_async_copy(out_ref.at[rows], out_hbm.at[rows], out_sems.at[index])
 
     def finish(rows, total, weighted):
         unstack(out_ref, rows, heads, (weighted / total).astype(jnp.bfloat16))
 
     trusted = jnp.full((8, HD), True)
-    late = loaded(late_refs)
-    for block in range(blocks):
-        rows = slice(block * BLK, (block + 1) * BLK)
-        total, weighted = add_pieces(
-            query_ref,
-            best_ref,
-            rows,
-            heads,
-            late,
-            stacked(total_ref, rows, heads),
-            stacked(sum_ref, rows, heads),
-        )
-        good = (total < total_limit).reshape(heads * BLK // 8, 8, HD)
+    shards_here = load(())
+    for index, rows in enumerate(blocks):
+        queries = stacked(query_ref, rows, heads)
+        best = stacked(best_ref, rows, heads)
+        total = stacked(total_ref, rows, heads)
+        weighted = stacked(sum_ref, rows, heads)
+        for key_rows, value_rows in shards_here:
+            total, weighted = add_shard(queries, best, key_rows, value_rows, total, weighted)
+        good = (total < total_limit).reshape(total.shape[0] // 8, 8, HD)
         trusted = trusted & jnp.all(good, axis=0)
         finish(rows, total, weighted)
-        out_copy(block).start()
-    for block in range(blocks):
-        out_copy(block).wait()
+        out_copy(index, rows).start()
+    for index, rows in enumerate(blocks):
+        out_copy(index, rows).wait()
 
     @pl.when(jnp.logical_not(jnp.all(trusted)))
     def exact_maximum():
-        def visit(block, unused):
-            rows = pl.ds(pl.multiple_of(block * BLK, BLK), BLK)
+        size = query_ref.shape[0] // len(blocks)
+
+        def visit(index, unused):
+            rows = pl.ds(pl.multiple_of(index * size, size), size)
             queries = stacked(query_ref, rows, heads)
             best = stacked(best_ref, rows, heads)
             weighted = stacked(old_sum_ref, rows, heads)
             total = stacked(old_total_ref, rows, heads)
-            for key_rows, value_rows in loaded(early_refs + late_refs):
+            for key_rows, value_rows in load(early_refs):
                 scores = scores_of(queries, key_rows)
                 new_best = jnp.maximum(best, jnp.max(scores, axis=1, keepdims=True))
                 factor = jnp.exp2(best - new_best)
@@ -217,28 +215,33 @@
                 total = total * factor + result[:, HD:]
                 best = new_best
             finish(rows, total, weighted)
-            copy = out_copy(block)
+            copy = out_copy(index, rows)
             copy.start()
             copy.wait()
             return unused
 
-        lax.fori_loop(0, blocks, visit, 0)
+        lax.fori_loop(0, len(blocks), visit, 0)
 
 
 def shards(queries, suffix_kv, prompt_kv, lengths):
     slots, width = queries.shape
     heads = width // HD
     loop_size = lax.axis_size("loop")
-    pair_size = lax.axis_size("pair")
     own = prompt_kv[:, 0, :]
     suffix = suffix_kv[:, 0, :]
     shard_rows = own.shape[0]
-    half_rows = shard_rows // pair_size
-    half = lax.dynamic_slice_in_dim(own, lax.axis_index("pair") * half_rows, half_rows, 0)
-    early, late = [], []
-    for step in range(1, loop_size):
-        around = [(i, (i + step) % loop_size) for i in range(loop_size)]
-        early.append(lax.ppermute(half, "loop", around))
+
+    def place(loop_index, pair_index):
+        return loop_index % loop_size * 2 + pair_index
+
+    early, direct = [], []
+    for step in range(1, (loop_size + 1) // 2):
+        hops = [(place(i, 0), place(i + step, 0)) for i in range(loop_size)]
+        hops += [(place(i, 1), place(i - step, 1)) for i in range(loop_size)]
+        early.append(lax.ppermute(own, ("loop", "pair"), hops))
+    if loop_size % 2 == 0:
+        hops = [(place(i, 0), place(i + loop_size // 2, 0)) for i in range(loop_size)]
+        direct.append(lax.ppermute(own, ("loop", "pair"), hops))
     in_hbm = pl.BlockSpec(memory_space=pltpu.HBM)
     in_vmem = pl.BlockSpec(memory_space=pltpu.VMEM)
     state = jax.ShapeDtypeStruct((slots, width), jnp.float32)
@@ -266,33 +269,41 @@
         compiler_params=pltpu.CompilerParams(vmem_limit_bytes=24 * 2**20),
         cost_estimate=cost(shard_rows + MAXLEN),
     )(*(pltpu.with_memory_space_constraint(x, pltpu.HBM) for x in (lengths, queries, suffix, own)))
-    early, best = lax.optimization_barrier((early, best))
-    for piece in early:
-        for turn in range(1, pair_size):
-            across = [(i, (i + turn) % pair_size) for i in range(pair_size)]
-            late.append(lax.ppermute(piece, "pair", across))
-    early_total, early_weighted = pl.pallas_call(
-        first_half_stage,
-        name="first_half_stage",
-        out_shape=[state] * 2,
-        in_specs=[in_vmem] * (4 + len(early)),
-        out_specs=[in_vmem] * 2,
-        compiler_params=pltpu.CompilerParams(vmem_limit_bytes=24 * 2**20),
-        cost_estimate=cost(half_rows * len(early)),
-    )(queries, best, total, weighted, *early)
+    early, direct, best = lax.optimization_barrier((early, direct, best))
+    late = [
+        lax.ppermute(shard, ("loop", "pair"), [(p, p ^ 1) for p in range(2 * loop_size)])
+        for shard in early
+    ]
+    passed = [
+        lax.ppermute(shard, ("loop", "pair"), [(2 * i, 2 * i + 1) for i in range(loop_size)])
+        for shard in direct
+    ]
+    early_total, early_weighted = total, weighted
+    if early:
+        early_total, early_weighted = pl.pallas_call(
+            early_stage,
+            name="early_stage",
+            out_shape=[state] * 2,
+            in_specs=[in_vmem] * (4 + len(early)),
+            out_specs=[in_vmem] * 2,
+            compiler_params=pltpu.CompilerParams(vmem_limit_bytes=24 * 2**20),
+            cost_estimate=cost(shard_rows * len(early)),
+        )(queries, best, total, weighted, *early)
+    last_inputs = (queries, best, total, weighted, early_total, early_weighted)
+    last_inputs += (*early, *late, *direct, *passed)
     return pl.pallas_call(
-        functools.partial(second_half_stage, len(early)),
-        name="second_half_stage",
+        functools.partial(late_stage, len(early), len(late), len(direct)),
+        name="late_stage",
         out_shape=jax.ShapeDtypeStruct((slots, width), jnp.bfloat16),
-        in_specs=[in_vmem] * (6 + len(early) + len(late)),
+        in_specs=[in_vmem] * len(last_inputs),
         out_specs=in_hbm,
         scratch_shapes=[
             pltpu.VMEM((slots, width), jnp.bfloat16),
-            pltpu.SemaphoreType.DMA((slots // BLK,)),
+            pltpu.SemaphoreType.DMA((len(row_blocks(slots)),)),
         ],
-        compiler_params=pltpu.CompilerParams(vmem_limit_bytes=24 * 2**20),
-        cost_estimate=cost(half_rows * len(late)),
-    )(queries, best, total, weighted, early_total, early_weighted, *early, *late)
+        compiler_params=pltpu.CompilerParams(vmem_limit_bytes=32 * 2**20),
+        cost_estimate=cost(shard_rows * (len(late) + len(direct))),
+    )(*last_inputs)
 
 
 def solution(mesh):

time: 30.3 us -> 24.8 us (0.82)
  Pallas kernels: 22.4 us -> 14.2 us
  starting transfers between devices: 6.71 us -> 8.92 us
  waiting for transfers between devices: 0.02 us -> 1.44 us
  local copies, waits for them, and re-layouts: 0.84 us -> 0 us
    pallas_call x2, Pallas kernels: 16.3 us -> 9.88 us  [the longest x1 8.92 us: shards(): pl.pallas_call(functools.partial(late_stage, len(early), len(late), len(d...]
    ppermute x6 -> x4, starting transfers between devices: 6.71 us -> 8.92 us  [the longest x1 5.93 us: shards(): direct.append(lax.ppermute(own, ('loop', 'pair'), hops))]
    pallas_call x1, Pallas kernels: 6.06 us -> 4.31 us  [shards(): pl.pallas_call(local_stage, name='local_stage', out_shape=[state] * 3 + [...]
    ppermute x6 -> x4, waiting for transfers between devices: 0.02 us -> 1.44 us  [the longest x1 1.07 us: shards(): early.append(lax.ppermute(own, ('loop', 'pair'), hops))]
    dynamic_slice x1 -> x0, local copies, waits for them, and re-layouts: 0.84 us -> none  [shards(): lax.dynamic_slice_in_dim(own, lax.axis_index('pair') * half_rows, half_ro...]
  transfers between devices with their start and end apart: 6 -> 4, of which waited for: 0 -> 2; matrix products, arithmetic and copies ran while one was open for 0% -> 0% of each run, Pallas kernels for 28% -> 21%
where the time goes in v3:
time: 24.8 us; the launch traced here: 24.6 us
  Pallas kernels  14.2 us (57%)
  starting transfers between devices  8.92 us (36%)
  waiting for transfers between devices  1.44 us (6%)
    pallas_call x1, Pallas kernels, shards(): pl.pallas_call(functools.partial(late_stage, len(early), len(late), len(d...  8.92 us
    ppermute x1, starting transfers between devices, shards(): direct.append(lax.ppermute(own, ('loop', 'pair'), hops))  5.93 us
    pallas_call x1, Pallas kernels, shards(): pl.pallas_call(local_stage, name='local_stage', out_shape=[state] * 3 + [...  4.31 us
    ppermute x1, starting transfers between devices, shards(): early.append(lax.ppermute(own, ('loop', 'pair'), hops))  1.63 us
    ppermute x1, starting transfers between devices, shards(): lax.ppermute(shard, ('loop', 'pair'), [(2 * i, 2 * i + 1) for i in range(...  1.29 us
    ppermute x1, waiting for transfers between devices, shards(): early.append(lax.ppermute(own, ('loop', 'pair'), hops))  1.07 us
    pallas_call x1, Pallas kernels, shards(): pl.pallas_call(early_stage, name='early_stage', out_shape=[state] * 2, in...  0.96 us
  transfers between devices with their start and end apart: 4, of which 2 were waited for; matrix products, arithmetic and copies ran while one was open for 0% of the time, Pallas kernels for 21%

profile of v3, /device:TPU:0, one launch (start us, length us, event | category | flops | bytes accessed | tf_op | source)
XLA Modules:
  0.0 24.6 jit_solution(4486217614724045388)
XLA Ops:
  0.0 5.9 %collective-permute-start.1 = (bf16[256,256]{1,0:T(8,128)(2,1)}, bf16[256,256]{1,0:T(8,128)(2,1)S(1)}, u32[]{:S(2)}, u32[]{:S(2)}) collective-permute-start(bf16[256,256]{1,0:T(8,128)(2,1)} %bitcast.3), channel_id=1, source_target_pairs={{0,8},{4,12},{8,0},{12,4},{2,10},{6,14},{10,2},{14,6},{16,24},{20,... | collective-permute-start | bytes 393224 | tf_op jit(solution)/shard_map/ppermute | solution.py:244
  5.9 1.6 %collective-permute-start = (bf16[256,256]{1,0:T(8,128)(2,1)}, bf16[256,256]{1,0:T(8,128)(2,1)S(1)}, u32[]{:S(2)}, u32[]{:S(2)}) collective-permute-start(bf16[256,256]{1,0:T(8,128)(2,1)} %bitcast.4), channel_id=1, source_target_pairs={{0,4},{4,8},{8,12},{12,0},{1,13},{5,1},{9,5},{13,9},{2,6},{6,10},{... | collective-permute-start | bytes 393224 | tf_op jit(solution)/shard_map/ppermute | solution.py:241
  7.6 4.3 %local_stage.1 = (f32[640,512]{1,0:T(8,128)S(1)}, f32[640,512]{1,0:T(8,128)S(1)}, f32[640,512]{1,0:T(8,128)S(1)}, bf16[640,512]{1,0:T(8,128)(2,1)S(1)}) custom-call(s32[8]{0:T(128)} %lengths_hbm.1, bf16[640,512]{1,0:T(8,128)(2,1)} %query_hbm.1, bf16[640,256]{1,0:T(8,128)(2,1)} %bitcast.2, bf16[256,256]{1,0:T(8,128)(2,1)} %bitcast.5), custom_call_target="tpu_custom_call" | custom-call | flops 754974720 | bytes 4587520 | tf_op jit(solution)/shard_map/local_stage/pallas_call | solution.py:256
  11.9 0.0 collective-permute-done.1.refs_8_
  11.9 1.1 %collective-permute-done.refs_4_.refs_6_ = bf16[256,256]{1,0:T(8,128)(2,1)S(1)} collective-permute-done((bf16[256,256]{1,0:T(8,128)(2,1)}, bf16[256,256]{1,0:T(8,128)(2,1)S(1)}, u32[]{:S(2)}, u32[]{:S(2)}) %collective-permute-start) | collective-permute-done | bytes 131104 | tf_op jit(solution)/shard_map/ppermute | solution.py:241
  13.0 1.3 %collective-permute-start.3 = (bf16[256,256]{1,0:T(8,128)(2,1)S(1)}, bf16[256,256]{1,0:T(8,128)(2,1)S(1)}, u32[]{:S(2)}, u32[]{:S(2)}) collective-permute-start(bf16[256,256]{1,0:T(8,128)(2,1)S(1)} %collective-permute-done.1.refs_8_), channel_id=1, source_target_pairs={{0,1},{4,5},{8,9},{12,13},{2,3},{6,7},{10,11},{14,15},{16,17},{20,... | collective-permute-start | bytes 393224 | tf_op jit(solution)/shard_map/ppermute | solution.py:278
  14.3 0.1 collective-permute-start.2
  14.3 1.0 %early_stage.1 = (f32[640,512]{1,0:T(8,128)S(1)}, f32[640,512]{1,0:T(8,128)S(1)}) custom-call(bf16[640,512]{1,0:T(8,128)(2,1)S(1)} %get-tuple-element.14.refs_0_, f32[640,512]{1,0:T(8,128)S(1)} %get-tuple-element.16.refs_1_, f32[640,512]{1,0:T(8,128)S(1)} %get-tuple-element.17.refs_2_, f32[640,512]{1,0:T(8,128)S(1)} %get-tuple-element.18.refs_3_, ...), custom_call_target="tpu_custom_call" | custom-call | flops 335544320 | bytes 4587520 | tf_op jit(solution)/shard_map/early_stage/pallas_call | solution.py:283
  15.3 0.0 collective-permute-done.3.refs_9_
  15.3 0.4 %collective-permute-done.2.refs_7_ = bf16[256,256]{1,0:T(8,128)(2,1)S(1)} collective-permute-done((bf16[256,256]{1,0:T(8,128)(2,1)S(1)}, bf16[256,256]{1,0:T(8,128)(2,1)S(1)}, u32[]{:S(2)}, u32[]{:S(2)}) %collective-permute-start.2) | collective-permute-done | bytes 131104 | tf_op jit(solution)/shard_map/ppermute | solution.py:274
  15.7 8.9 %late_stage.1 = bf16[640,512]{1,0:T(8,128)(2,1)} custom-call(bf16[640,512]{1,0:T(8,128)(2,1)S(1)} %get-tuple-element.14.refs_0_, f32[640,512]{1,0:T(8,128)S(1)} %get-tuple-element.16.refs_1_, f32[640,512]{1,0:T(8,128)S(1)} %get-tuple-element.17.refs_2_, f32[640,512]{1,0:T(8,128)S(1)} %get-tuple-element.18.refs_3_, f32[640,512]{1,0:T(8,128)S(1)} %get-tuple-element.20.refs_4_, ...), custom_call_target="tpu_custom_call" | custom-call | flops 671088640 | bytes 4587520 | tf_op jit(solution)/shard_map/late_stage/pallas_call | solution.py:294
Async XLA Ops:
  0.0 11.9 %collective-permute-start.1 = (bf16[256,256]{1,0:T(8,128)(2,1)}, bf16[256,256]{1,0:T(8,128)(2,1)S(1)}, u32[]{:S(2)}, u32[]{:S(2)}) collective-permute-start(bf16[256,256]{1,0:T(8,128)(2,1)} %bitcast.3), channel_id=1, source_target_pairs={{0,8},{4,12},{8,0},{12,4},{2,10},{6,14},{10,2},{14,6},{16,24},{20,... | collective-permute-start | bytes 393224 | tf_op jit(solution)/shard_map/ppermute | solution.py:244
  5.9 7.0 %collective-permute-start = (bf16[256,256]{1,0:T(8,128)(2,1)}, bf16[256,256]{1,0:T(8,128)(2,1)S(1)}, u32[]{:S(2)}, u32[]{:S(2)}) collective-permute-start(bf16[256,256]{1,0:T(8,128)(2,1)} %bitcast.4), channel_id=1, source_target_pairs={{0,4},{4,8},{8,12},{12,0},{1,13},{5,1},{9,5},{13,9},{2,6},{6,10},{... | collective-permute-start | bytes 393224 | tf_op jit(solution)/shard_map/ppermute | solution.py:241
  13.0 2.3 %collective-permute-start.3 = (bf16[256,256]{1,0:T(8,128)(2,1)S(1)}, bf16[256,256]{1,0:T(8,128)(2,1)S(1)}, u32[]{:S(2)}, u32[]{:S(2)}) collective-permute-start(bf16[256,256]{1,0:T(8,128)(2,1)S(1)} %collective-permute-done.1.refs_8_), channel_id=1, source_target_pairs={{0,1},{4,5},{8,9},{12,13},{2,3},{6,7},{10,11},{14,15},{16,17},{20,... | collective-permute-start | bytes 393224 | tf_op jit(solution)/shard_map/ppermute | solution.py:278
  14.3 1.4 %collective-permute-start.2 = (bf16[256,256]{1,0:T(8,128)(2,1)S(1)}, bf16[256,256]{1,0:T(8,128)(2,1)S(1)}, u32[]{:S(2)}, u32[]{:S(2)}) collective-permute-start(bf16[256,256]{1,0:T(8,128)(2,1)S(1)} %collective-permute-done.refs_4_.refs_6_), channel_id=1, source_target_pairs={{0,1},{1,0},{4,5},{5,4},{8,9},{9,8},{12,13},{13,12},{2,3},{3,2},{6... | collective-permute-start | bytes 393224 | tf_op jit(solution)/shard_map/ppermute | solution.py:274

commit v4 on v3

--- a/solution.py
+++ b/solution.py
@@ -235,13 +235,14 @@
         return loop_index % loop_size * 2 + pair_index
 
     early, direct = [], []
-    for step in range(1, (loop_size + 1) // 2):
+    if loop_size % 2 == 0:
+        hops = [(place(i, 0), place(i + loop_size // 2, 0)) for i in range(loop_size)]
+        hops += [(place(i, 1), place(i, 1)) for i in range(loop_size)]
+        direct.append(lax.ppermute(own, ("loop", "pair"), hops))
+    for step in reversed(range(1, (loop_size + 1) // 2)):
         hops = [(place(i, 0), place(i + step, 0)) for i in range(loop_size)]
         hops += [(place(i, 1), place(i - step, 1)) for i in range(loop_size)]
         early.append(lax.ppermute(own, ("loop", "pair"), hops))
-    if loop_size % 2 == 0:
-        hops = [(place(i, 0), place(i + loop_size // 2, 0)) for i in range(loop_size)]
-        direct.append(lax.ppermute(own, ("loop", "pair"), hops))
     in_hbm = pl.BlockSpec(memory_space=pltpu.HBM)
     in_vmem = pl.BlockSpec(memory_space=pltpu.VMEM)
     state = jax.ShapeDtypeStruct((slots, width), jnp.float32)
@@ -270,14 +271,9 @@
         cost_estimate=cost(shard_rows + MAXLEN),
     )(*(pltpu.with_memory_space_constraint(x, pltpu.HBM) for x in (lengths, queries, suffix, own)))
     early, direct, best = lax.optimization_barrier((early, direct, best))
-    late = [
-        lax.ppermute(shard, ("loop", "pair"), [(p, p ^ 1) for p in range(2 * loop_size)])
-        for shard in early
-    ]
-    passed = [
-        lax.ppermute(shard, ("loop", "pair"), [(2 * i, 2 * i + 1) for i in range(loop_size)])
-        for shard in direct
-    ]
+    swap = [(p, p ^ 1) for p in range(2 * loop_size)]
+    late = [lax.ppermute(shard, ("loop", "pair"), swap) for shard in early]
+    passed = [lax.ppermute(shard, ("loop", "pair"), swap) for shard in direct]
     early_total, early_weighted = total, weighted
     if early:
         early_total, early_weighted = pl.pallas_call(

time: 24.8 us -> 23.6 us (0.952)
  starting transfers between devices: 8.92 us -> 8.07 us
  waiting for transfers between devices: 1.44 us -> 1.13 us
    ppermute x2, starting transfers between devices: 1.36 us -> 0.51 us  [the longest x1 0.51 us: shards(): late = [lax.ppermute(shard, ('loop', 'pair'), swap) for shard in early]]
    ppermute x2, waiting for transfers between devices: 0.36 us -> 0.06 us  [the longest x1 0.05 us: shards(): late = [lax.ppermute(shard, ('loop', 'pair'), swap) for shard in early]]
  transfers between devices with their start and end apart: 4 -> 4, of which waited for: 2 -> 2; matrix products, arithmetic and copies ran while one was open for 0% -> 0% of each run, Pallas kernels for 21% -> 22%
where the time goes in v4:
time: 23.6 us; the launch traced here: 23.4 us
  Pallas kernels  14.2 us (60%)
  starting transfers between devices  8.07 us (34%)
  waiting for transfers between devices  1.13 us (5%)
    pallas_call x1, Pallas kernels, shards(): pl.pallas_call(functools.partial(late_stage, len(early), len(late), len(d...  8.92 us
    ppermute x1, starting transfers between devices, shards(): direct.append(lax.ppermute(own, ('loop', 'pair'), hops))  5.93 us
    pallas_call x1, Pallas kernels, shards(): pl.pallas_call(local_stage, name='local_stage', out_shape=[state] * 3 + [...  4.31 us
    ppermute x1, starting transfers between devices, shards(): early.append(lax.ppermute(own, ('loop', 'pair'), hops))  1.63 us
    ppermute x1, waiting for transfers between devices, shards(): early.append(lax.ppermute(own, ('loop', 'pair'), hops))  1.07 us
    pallas_call x1, Pallas kernels, shards(): pl.pallas_call(early_stage, name='early_stage', out_shape=[state] * 2, in...  0.95 us
    ppermute x1, starting transfers between devices, shards(): late = [lax.ppermute(shard, ('loop', 'pair'), swap) for shard in early]  0.51 us
  transfers between devices with their start and end apart: 4, of which 2 were waited for; matrix products, arithmetic and copies ran while one was open for 0% of the time, Pallas kernels for 22%

profile of v4, /device:TPU:0, one launch (start us, length us, event | category | flops | bytes accessed | tf_op | source)
XLA Modules:
  0.0 23.4 jit_solution(14710700735883272278)
XLA Ops:
  0.0 5.9 %collective-permute-start.1 = (bf16[256,256]{1,0:T(8,128)(2,1)}, bf16[256,256]{1,0:T(8,128)(2,1)S(1)}, u32[]{:S(2)}, u32[]{:S(2)}) collective-permute-start(bf16[256,256]{1,0:T(8,128)(2,1)} %bitcast.3), channel_id=1, source_target_pairs={{0,8},{4,12},{8,0},{12,4},{1,1},{5,5},{9,9},{13,13},{2,10},{6,14},... | collective-permute-start | bytes 393224 | tf_op jit(solution)/shard_map/ppermute | solution.py:241
  5.9 1.6 %collective-permute-start = (bf16[256,256]{1,0:T(8,128)(2,1)}, bf16[256,256]{1,0:T(8,128)(2,1)S(1)}, u32[]{:S(2)}, u32[]{:S(2)}) collective-permute-start(bf16[256,256]{1,0:T(8,128)(2,1)} %bitcast.4), channel_id=1, source_target_pairs={{0,4},{4,8},{8,12},{12,0},{1,13},{5,1},{9,5},{13,9},{2,6},{6,10},{... | collective-permute-start | bytes 393224 | tf_op jit(solution)/shard_map/ppermute | solution.py:245
  7.6 4.3 %local_stage.1 = (f32[640,512]{1,0:T(8,128)S(1)}, f32[640,512]{1,0:T(8,128)S(1)}, f32[640,512]{1,0:T(8,128)S(1)}, bf16[640,512]{1,0:T(8,128)(2,1)S(1)}) custom-call(s32[8]{0:T(128)} %lengths_hbm.1, bf16[640,512]{1,0:T(8,128)(2,1)} %query_hbm.1, bf16[640,256]{1,0:T(8,128)(2,1)} %bitcast.2, bf16[256,256]{1,0:T(8,128)(2,1)} %bitcast.5), custom_call_target="tpu_custom_call" | custom-call | flops 754974720 | bytes 4587520 | tf_op jit(solution)/shard_map/local_stage/pallas_call | solution.py:257
  11.9 0.0 collective-permute-done.1.refs_8_
  11.9 1.1 %collective-permute-done.refs_4_.refs_6_ = bf16[256,256]{1,0:T(8,128)(2,1)S(1)} collective-permute-done((bf16[256,256]{1,0:T(8,128)(2,1)}, bf16[256,256]{1,0:T(8,128)(2,1)S(1)}, u32[]{:S(2)}, u32[]{:S(2)}) %collective-permute-start) | collective-permute-done | bytes 131104 | tf_op jit(solution)/shard_map/ppermute | solution.py:245
  13.0 0.0 collective-permute-start.3
  13.0 0.5 %collective-permute-start.2 = (bf16[256,256]{1,0:T(8,128)(2,1)S(1)}, bf16[256,256]{1,0:T(8,128)(2,1)S(1)}, u32[]{:S(2)}, u32[]{:S(2)}) collective-permute-start(bf16[256,256]{1,0:T(8,128)(2,1)S(1)} %collective-permute-done.refs_4_.refs_6_), channel_id=1, source_target_pairs={{0,1},{1,0},{4,5},{5,4},{8,9},{9,8},{12,13},{13,12},{2,3},{3,2},{6... | collective-permute-start | bytes 393224 | tf_op jit(solution)/shard_map/ppermute | solution.py:275
  13.5 1.0 %early_stage.1 = (f32[640,512]{1,0:T(8,128)S(1)}, f32[640,512]{1,0:T(8,128)S(1)}) custom-call(bf16[640,512]{1,0:T(8,128)(2,1)S(1)} %get-tuple-element.14.refs_0_, f32[640,512]{1,0:T(8,128)S(1)} %get-tuple-element.16.refs_1_, f32[640,512]{1,0:T(8,128)S(1)} %get-tuple-element.17.refs_2_, f32[640,512]{1,0:T(8,128)S(1)} %get-tuple-element.18.refs_3_, ...), custom_call_target="tpu_custom_call" | custom-call | flops 335544320 | bytes 4587520 | tf_op jit(solution)/shard_map/early_stage/pallas_call | solution.py:279
  14.4 0.0 collective-permute-done.3.refs_9_
  14.5 0.1 collective-permute-done.2.refs_7_
  14.5 8.9 %late_stage.1 = bf16[640,512]{1,0:T(8,128)(2,1)} custom-call(bf16[640,512]{1,0:T(8,128)(2,1)S(1)} %get-tuple-element.14.refs_0_, f32[640,512]{1,0:T(8,128)S(1)} %get-tuple-element.16.refs_1_, f32[640,512]{1,0:T(8,128)S(1)} %get-tuple-element.17.refs_2_, f32[640,512]{1,0:T(8,128)S(1)} %get-tuple-element.18.refs_3_, f32[640,512]{1,0:T(8,128)S(1)} %get-tuple-element.20.refs_4_, ...), custom_call_target="tpu_custom_call" | custom-call | flops 671088640 | bytes 4587520 | tf_op jit(solution)/shard_map/late_stage/pallas_call | solution.py:290
Async XLA Ops:
  0.0 11.9 %collective-permute-start.1 = (bf16[256,256]{1,0:T(8,128)(2,1)}, bf16[256,256]{1,0:T(8,128)(2,1)S(1)}, u32[]{:S(2)}, u32[]{:S(2)}) collective-permute-start(bf16[256,256]{1,0:T(8,128)(2,1)} %bitcast.3), channel_id=1, source_target_pairs={{0,8},{4,12},{8,0},{12,4},{1,1},{5,5},{9,9},{13,13},{2,10},{6,14},... | collective-permute-start | bytes 393224 | tf_op jit(solution)/shard_map/ppermute | solution.py:241
  5.9 7.0 %collective-permute-start = (bf16[256,256]{1,0:T(8,128)(2,1)}, bf16[256,256]{1,0:T(8,128)(2,1)S(1)}, u32[]{:S(2)}, u32[]{:S(2)}) collective-permute-start(bf16[256,256]{1,0:T(8,128)(2,1)} %bitcast.4), channel_id=1, source_target_pairs={{0,4},{4,8},{8,12},{12,0},{1,13},{5,1},{9,5},{13,9},{2,6},{6,10},{... | collective-permute-start | bytes 393224 | tf_op jit(solution)/shard_map/ppermute | solution.py:245
  13.0 1.5 %collective-permute-start.3 = (bf16[256,256]{1,0:T(8,128)(2,1)S(1)}, bf16[256,256]{1,0:T(8,128)(2,1)S(1)}, u32[]{:S(2)}, u32[]{:S(2)}) collective-permute-start(bf16[256,256]{1,0:T(8,128)(2,1)S(1)} %collective-permute-done.1.refs_8_), channel_id=1, source_target_pairs={{0,1},{1,0},{4,5},{5,4},{8,9},{9,8},{12,13},{13,12},{2,3},{3,2},{6... | collective-permute-start | bytes 393224 | tf_op jit(solution)/shard_map/ppermute | solution.py:276
  13.0 1.5 %collective-permute-start.2 = (bf16[256,256]{1,0:T(8,128)(2,1)S(1)}, bf16[256,256]{1,0:T(8,128)(2,1)S(1)}, u32[]{:S(2)}, u32[]{:S(2)}) collective-permute-start(bf16[256,256]{1,0:T(8,128)(2,1)S(1)} %collective-permute-done.refs_4_.refs_6_), channel_id=1, source_target_pairs={{0,1},{1,0},{4,5},{5,4},{8,9},{9,8},{12,13},{13,12},{2,3},{3,2},{6... | collective-permute-start | bytes 393224 | tf_op jit(solution)/shard_map/ppermute | solution.py:275

commit v5 on v4

--- a/solution.py
+++ b/solution.py
@@ -136,39 +136,17 @@
     return [slice(first, first + step) for first in range(0, count, step)]
 
 
-def early_stage(*refs):
-    query_ref, best_ref, total_ref, sum_ref = refs[:4]
-    shard_refs = refs[4:-2]
-    total_out, sum_out = refs[-2:]
-    heads = query_ref.shape[1] // HD
-    shards_here = [(ref[:, :HD], with_ones(ref[:, HD:])) for ref in shard_refs]
-    for rows in row_blocks(query_ref.shape[0]):
-        queries = stacked(query_ref, rows, heads)
-        best = stacked(best_ref, rows, heads)
-        total = stacked(total_ref, rows, heads)
-        weighted = stacked(sum_ref, rows, heads)
-        for key_rows, value_rows in shards_here:
-            total, weighted = add_shard(queries, best, key_rows, value_rows, total, weighted)
-        unstack(total_out, rows, heads, total)
-        unstack(sum_out, rows, heads, weighted)
-
-
-def late_stage(early_count, late_count, half_count, *refs):
-    query_ref, best_ref, old_total_ref, old_sum_ref, total_ref, sum_ref = refs[:6]
-    refs = refs[6:]
-    early_refs, refs = refs[:early_count], refs[early_count:]
-    late_refs, refs = refs[:late_count], refs[late_count:]
-    direct_refs, refs = refs[:half_count], refs[half_count:]
-    passed_refs, refs = refs[:half_count], refs[half_count:]
-    out_hbm, out_ref, out_sems = refs
+def late_stage(
+    query_ref, best_ref, total_ref, sum_ref, gathered_ref, out_hbm, out_ref, out_sems
+):
+    old_total_ref, old_sum_ref = total_ref, sum_ref
     heads = query_ref.shape[1] // HD
     blocks = row_blocks(query_ref.shape[0])
-    is_direct = lax.axis_index("pair") == 0
-
-    def load(early):
-        loaded = [ref[...] for ref in early + late_refs]
-        for direct_ref, passed_ref in zip(direct_refs, passed_refs):
-            loaded.append(jnp.where(is_direct, direct_ref[...], passed_ref[...]))
+    loop_size = gathered_ref.shape[0]
+    position = lax.axis_index("loop")
+
+    def load(unused):
+        loaded = [gathered_ref[lax.rem(position + i, loop_size)] for i in range(1, loop_size)]
         return [(shard[:, :HD], with_ones(shard[:, HD:])) for shard in loaded]
 
     def out_copy(index, rows):
@@ -203,7 +181,7 @@
             best = stacked(best_ref, rows, heads)
             weighted = stacked(old_sum_ref, rows, heads)
             total = stacked(old_total_ref, rows, heads)
-            for key_rows, value_rows in load(early_refs):
+            for key_rows, value_rows in load(()):
                 scores = scores_of(queries, key_rows)
                 new_best = jnp.maximum(best, jnp.max(scores, axis=1, keepdims=True))
                 factor = jnp.exp2(best - new_best)
@@ -231,18 +209,7 @@
     suffix = suffix_kv[:, 0, :]
     shard_rows = own.shape[0]
 
-    def place(loop_index, pair_index):
-        return loop_index % loop_size * 2 + pair_index
-
-    early, direct = [], []
-    if loop_size % 2 == 0:
-        hops = [(place(i, 0), place(i + loop_size // 2, 0)) for i in range(loop_size)]
-        hops += [(place(i, 1), place(i, 1)) for i in range(loop_size)]
-        direct.append(lax.ppermute(own, ("loop", "pair"), hops))
-    for step in reversed(range(1, (loop_size + 1) // 2)):
-        hops = [(place(i, 0), place(i + step, 0)) for i in range(loop_size)]
-        hops += [(place(i, 1), place(i - step, 1)) for i in range(loop_size)]
-        early.append(lax.ppermute(own, ("loop", "pair"), hops))
+    gathered = lax.all_gather(own, "loop", axis=0, tiled=False)
     in_hbm = pl.BlockSpec(memory_space=pltpu.HBM)
     in_vmem = pl.BlockSpec(memory_space=pltpu.VMEM)
     state = jax.ShapeDtypeStruct((slots, width), jnp.float32)
@@ -270,36 +237,19 @@
         compiler_params=pltpu.CompilerParams(vmem_limit_bytes=24 * 2**20),
         cost_estimate=cost(shard_rows + MAXLEN),
     )(*(pltpu.with_memory_space_constraint(x, pltpu.HBM) for x in (lengths, queries, suffix, own)))
-    early, direct, best = lax.optimization_barrier((early, direct, best))
-    swap = [(p, p ^ 1) for p in range(2 * loop_size)]
-    late = [lax.ppermute(shard, ("loop", "pair"), swap) for shard in early]
-    passed = [lax.ppermute(shard, ("loop", "pair"), swap) for shard in direct]
-    early_total, early_weighted = total, weighted
-    if early:
-        early_total, early_weighted = pl.pallas_call(
-            early_stage,
-            name="early_stage",
-            out_shape=[state] * 2,
-            in_specs=[in_vmem] * (4 + len(early)),
-            out_specs=[in_vmem] * 2,
-            compiler_params=pltpu.CompilerParams(vmem_limit_bytes=24 * 2**20),
-            cost_estimate=cost(shard_rows * len(early)),
-        )(queries, best, total, weighted, *early)
-    last_inputs = (queries, best, total, weighted, early_total, early_weighted)
-    last_inputs += (*early, *late, *direct, *passed)
     return pl.pallas_call(
-        functools.partial(late_stage, len(early), len(late), len(direct)),
+        late_stage,
         name="late_stage",
         out_shape=jax.ShapeDtypeStruct((slots, width), jnp.bfloat16),
-        in_specs=[in_vmem] * len(last_inputs),
+        in_specs=[in_vmem] * 5,
         out_specs=in_hbm,
         scratch_shapes=[
             pltpu.VMEM((slots, width), jnp.bfloat16),
             pltpu.SemaphoreType.DMA((len(row_blocks(slots)),)),
         ],
         compiler_params=pltpu.CompilerParams(vmem_limit_bytes=32 * 2**20),
-        cost_estimate=cost(shard_rows * (len(late) + len(direct))),
-    )(*last_inputs)
+        cost_estimate=cost(shard_rows * (loop_size - 1)),
+    )(queries, best, total, weighted, gathered)
 
 
 def solution(mesh):

time: 23.6 us -> 31.6 us (1.34)
  blocking collectives: 0 us -> 17.6 us
  starting transfers between devices: 8.07 us -> 0 us
  waiting for transfers between devices: 1.13 us -> 0 us
    all_gather x0 -> x1, blocking collectives: none -> 17.6 us  [shards(): gathered = lax.all_gather(own, 'loop', axis=0, tiled=False)]
    ppermute x4 -> x0, starting transfers between devices: 8.07 us -> none  [the longest x1 5.93 us: shards(): direct.append(lax.ppermute(own, ('loop', 'pair'), hops))]
    ppermute x4 -> x0, waiting for transfers between devices: 1.13 us -> none  [the longest x1 1.07 us: shards(): early.append(lax.ppermute(own, ('loop', 'pair'), hops))]
    pallas_call x2 -> x1, Pallas kernels: 9.87 us -> 9.6 us  [shards(): pl.pallas_call(late_stage, name='late_stage', out_shape=jax.ShapeDtypeStr...]
  transfers between devices with their start and end apart: 4 -> 0, of which waited for: 2 -> 0; matrix products, arithmetic and copies ran while one was open for 0% -> 0% of each run, Pallas kernels for 22% -> 0%
where the time goes in v5:
time: 31.6 us; the launch traced here: 31.5 us
  blocking collectives  17.6 us (56%)
  Pallas kernels  13.9 us (44%)
    all_gather x1, blocking collectives, shards(): gathered = lax.all_gather(own, 'loop', axis=0, tiled=False)  17.6 us
    pallas_call x1, Pallas kernels, shards(): pl.pallas_call(late_stage, name='late_stage', out_shape=jax.ShapeDtypeStr...  9.6 us
    pallas_call x1, Pallas kernels, shards(): pl.pallas_call(local_stage, name='local_stage', out_shape=[state] * 3 + [...  4.31 us

profile of v5, /device:TPU:0, one launch (start us, length us, event | category | flops | bytes accessed | tf_op | source)
XLA Modules:
  0.0 31.5 jit_solution(16350400745927422450)
XLA Ops:
  0.0 17.6 %all-gather = bf16[1024,1,256]{2,0,1:T(8,128)(2,1)S(1)} all-gather(bf16[256,1,256]{2,0,1:T(8,128)(2,1)} %param.6), channel_id=2, replica_groups=mesh['groups'=2,'loop'=4,'heads'=2,'pair'=2] {'loop'}, dimensions={0}, use_global_device_ids=true | all-gather | bytes 655360 | tf_op jit(solution)/shard_map/all_gather | solution.py:212
  17.6 4.3 %local_stage.1 = (f32[640,512]{1,0:T(8,128)S(1)}, f32[640,512]{1,0:T(8,128)S(1)}, f32[640,512]{1,0:T(8,128)S(1)}, bf16[640,512]{1,0:T(8,128)(2,1)S(1)}) custom-call(s32[8]{0:T(128)} %lengths_hbm.1, bf16[640,512]{1,0:T(8,128)(2,1)} %query_hbm.1, bf16[640,256]{1,0:T(8,128)(2,1)} %bitcast.5, bf16[256,256]{1,0:T(8,128)(2,1)} %bitcast.4), custom_call_target="tpu_custom_call" | custom-call | flops 754974720 | bytes 4587520 | tf_op jit(solution)/shard_map/local_stage/pallas_call | solution.py:224
  21.9 9.6 %late_stage.1 = bf16[640,512]{1,0:T(8,128)(2,1)} custom-call(bf16[640,512]{1,0:T(8,128)(2,1)S(1)} %get-tuple-element.9.query_ref, f32[640,512]{1,0:T(8,128)S(1)} %get-tuple-element.10.best_ref, f32[640,512]{1,0:T(8,128)S(1)} %get-tuple-element.11.total_ref, f32[640,512]{1,0:T(8,128)S(1)} %get-tuple-element.12.sum_ref, bf16[4,256,256]{2,1,0:T(8,128)(2,1)S(1)} %bitcast.3), custom_call_target="tpu_custom_call" | custom-call | flops 1006632960 | bytes 4587520 | tf_op jit(solution)/shard_map/late_stage/pallas_call | solution.py:240

commit v6 on v4

--- a/solution.py
+++ b/solution.py
@@ -46,58 +46,63 @@
     return jnp.concatenate([row_value] * (width // HD), axis=1)
 
 
-def local_stage(
+def load_stage(
     lengths_hbm,
     query_hbm,
     suffix_hbm,
     own_hbm,
-    best_ref,
-    total_ref,
-    sum_ref,
     query_ref,
-    lengths_ref,
     suffix_ref,
     own_ref,
-    whole_sems,
-    block_sems,
+    half_ref,
+    first_ref,
+    lengths_ref,
+    sems,
 ):
-    rows_all = query_ref.shape[0]
+    half_rows = half_ref.shape[0]
+    half_start = pl.multiple_of(lax.axis_index("pair") * half_rows, half_rows)
+    copies = [
+        pltpu.make_async_copy(source, target, sems.at[i])
+        for i, (source, target) in enumerate(
+            [
+                (lengths_hbm, lengths_ref),
+                (own_hbm.at[pl.ds(half_start, half_rows)], half_ref),
+                (own_hbm, own_ref),
+                (suffix_hbm, suffix_ref),
+                (query_hbm, query_ref),
+            ]
+        )
+    ]
+    for copy in copies:
+        copy.start()
+    copies[0].wait()
+    slots = query_ref.shape[0]
+    position = lax.axis_index("loop")
+    row_at = lax.broadcasted_iota(jnp.int32, first_ref.shape, 0)
+    first = jnp.zeros_like(row_at)
+    agent_end = 0
+    for agent in range(AG_DEV):
+        agent_end = agent_end + lengths_ref[position * AG_DEV + agent]
+        first = jnp.where(row_at >= agent_end, agent_end if agent + 1 < AG_DEV else slots, first)
+    first_ref[...] = first
+    for copy in copies[1:]:
+        copy.wait()
+
+
+def local_stage(query_ref, suffix_ref, own_ref, first_ref, best_ref, total_ref, sum_ref):
+    slots = query_ref.shape[0]
     heads = query_ref.shape[1] // HD
-    blocks = rows_all // BLK
-    whole = [
-        pltpu.make_async_copy(source, target, whole_sems.at[i])
-        for i, (source, target) in enumerate(
-            [(lengths_hbm, lengths_ref), (own_hbm, own_ref), (suffix_hbm, suffix_ref)]
-        )
-    ]
-    pieces = [
-        pltpu.make_async_copy(
-            query_hbm.at[pl.ds(block * BLK, BLK)],
-            query_ref.at[pl.ds(block * BLK, BLK)],
-            block_sems.at[block],
-        )
-        for block in range(blocks)
-    ]
-    for copy in whole + pieces:
-        copy.start()
-    for copy in whole + pieces:
-        copy.wait()
-    position = lax.axis_index("loop")
     own_keys = own_ref[:, :HD]
     own_values = with_ones(own_ref[:, HD:])
     window = BLK * ((MAXLEN + BLK - 2) // BLK) + BLK
-    for block in range(blocks):
+    for block in range(slots // BLK):
         stop = (block + 1) * BLK
         start = max(0, stop - window)
         rows = slice(block * BLK, stop)
         row_at = block * BLK + lax.broadcasted_iota(jnp.int32, (BLK, stop - start), 0)
         key_at = start + lax.broadcasted_iota(jnp.int32, (BLK, stop - start), 1)
-        first = jnp.zeros_like(row_at)
-        agent_end = 0
-        for agent in range(AG_DEV):
-            agent_end = agent_end + lengths_ref[position * AG_DEV + agent]
-            first = jnp.where(row_at >= agent_end, agent_end, first)
-        allowed = (key_at <= row_at) & (key_at >= first)
+        first = first_ref[rows]
+        allowed = (key_at <= row_at) & (key_at >= widen(first, stop - start))
         queries = stacked(query_ref, rows, heads)
         own_scores = scores_of(queries, own_keys)
         suffix_scores = jnp.where(
@@ -117,8 +122,7 @@
             with_ones(suffix_ref[start:stop, HD:]),
             preferred_element_type=jnp.float32,
         )
-        row_at = block * BLK + lax.broadcasted_iota(jnp.int32, (BLK, HD), 0)
-        live = jnp.concatenate([row_at < agent_end] * heads, axis=0)
+        live = jnp.concatenate([first < slots] * heads, axis=0)
         unstack(best_ref, rows, heads, jnp.where(live, best, empty_best))
         unstack(sum_ref, rows, heads, jnp.where(live, result[:, :HD], 0.0))
         unstack(total_ref, rows, heads, jnp.where(live, result[:, HD:], 1.0))
@@ -156,19 +160,18 @@
 def late_stage(early_count, late_count, half_count, *refs):
     query_ref, best_ref, old_total_ref, old_sum_ref, total_ref, sum_ref = refs[:6]
     refs = refs[6:]
+    half_refs, refs = refs[:half_count], refs[half_count:]
+    other_half_refs, refs = refs[:half_count], refs[half_count:]
     early_refs, refs = refs[:early_count], refs[early_count:]
     late_refs, refs = refs[:late_count], refs[late_count:]
-    direct_refs, refs = refs[:half_count], refs[half_count:]
-    passed_refs, refs = refs[:half_count], refs[half_count:]
     out_hbm, out_ref, out_sems = refs
     heads = query_ref.shape[1] // HD
     blocks = row_blocks(query_ref.shape[0])
-    is_direct = lax.axis_index("pair") == 0
 
     def load(early):
         loaded = [ref[...] for ref in early + late_refs]
-        for direct_ref, passed_ref in zip(direct_refs, passed_refs):
-            loaded.append(jnp.where(is_direct, direct_ref[...], passed_ref[...]))
+        for half_ref, other_ref in zip(half_refs, other_half_refs):
+            loaded.append(jnp.concatenate([half_ref[...], other_ref[...]], axis=0))
         return [(shard[:, :HD], with_ones(shard[:, HD:])) for shard in loaded]
 
     def out_copy(index, rows):
@@ -234,15 +237,6 @@
     def place(loop_index, pair_index):
         return loop_index % loop_size * 2 + pair_index
 
-    early, direct = [], []
-    if loop_size % 2 == 0:
-        hops = [(place(i, 0), place(i + loop_size // 2, 0)) for i in range(loop_size)]
-        hops += [(place(i, 1), place(i, 1)) for i in range(loop_size)]
-        direct.append(lax.ppermute(own, ("loop", "pair"), hops))
-    for step in reversed(range(1, (loop_size + 1) // 2)):
-        hops = [(place(i, 0), place(i + step, 0)) for i in range(loop_size)]
-        hops += [(place(i, 1), place(i - step, 1)) for i in range(loop_size)]
-        early.append(lax.ppermute(own, ("loop", "pair"), hops))
     in_hbm = pl.BlockSpec(memory_space=pltpu.HBM)
     in_vmem = pl.BlockSpec(memory_space=pltpu.VMEM)
     state = jax.ShapeDtypeStruct((slots, width), jnp.float32)
@@ -254,26 +248,50 @@
             transcendentals=slots * heads * keys,
         )
 
-    best, total, weighted, queries = pl.pallas_call(
+    early = []
+    for step in range(1, (loop_size + 1) // 2):
+        hops = [(place(i, 0), place(i + step, 0)) for i in range(loop_size)]
+        hops += [(place(i, 1), place(i - step, 1)) for i in range(loop_size)]
+        early.append(lax.ppermute(own, ("loop", "pair"), hops))
+    half_rows = shard_rows // 2
+    queries, suffix, own, half, first = pl.pallas_call(
+        load_stage,
+        name="load_stage",
+        out_shape=[
+            jax.ShapeDtypeStruct(queries.shape, queries.dtype),
+            jax.ShapeDtypeStruct(suffix.shape, suffix.dtype),
+            jax.ShapeDtypeStruct(own.shape, own.dtype),
+            jax.ShapeDtypeStruct((half_rows, own.shape[1]), own.dtype),
+            jax.ShapeDtypeStruct((slots, HD), jnp.int32),
+        ],
+        in_specs=[in_hbm] * 4,
+        out_specs=[in_vmem] * 5,
+        scratch_shapes=[
+            pltpu.SMEM(lengths.shape, lengths.dtype),
+            pltpu.SemaphoreType.DMA((5,)),
+        ],
+        compiler_params=pltpu.CompilerParams(vmem_limit_bytes=8 * 2**20),
+        cost_estimate=pl.CostEstimate(
+            flops=0, bytes_accessed=slots * width * 6, transcendentals=0
+        ),
+    )(*(pltpu.with_memory_space_constraint(x, pltpu.HBM) for x in (lengths, queries, suffix, own)))
+    halves = []
+    if loop_size % 2 == 0:
+        across = [(i, (i + loop_size // 2) % loop_size) for i in range(loop_size)]
+        halves.append(lax.ppermute(half, "loop", across))
+    best, total, weighted = pl.pallas_call(
         local_stage,
         name="local_stage",
-        out_shape=[state] * 3 + [jax.ShapeDtypeStruct((slots, width), queries.dtype)],
-        in_specs=[in_hbm] * 4,
-        out_specs=[in_vmem] * 4,
-        scratch_shapes=[
-            pltpu.SMEM(lengths.shape, lengths.dtype),
-            pltpu.VMEM(suffix.shape, suffix.dtype),
-            pltpu.VMEM(own.shape, own.dtype),
-            pltpu.SemaphoreType.DMA((3,)),
-            pltpu.SemaphoreType.DMA((slots // BLK,)),
-        ],
+        out_shape=[state] * 3,
+        in_specs=[in_vmem] * 4,
+        out_specs=[in_vmem] * 3,
         compiler_params=pltpu.CompilerParams(vmem_limit_bytes=24 * 2**20),
         cost_estimate=cost(shard_rows + MAXLEN),
-    )(*(pltpu.with_memory_space_constraint(x, pltpu.HBM) for x in (lengths, queries, suffix, own)))
-    early, direct, best = lax.optimization_barrier((early, direct, best))
+    )(queries, suffix, own, first)
+    halves, early, best = lax.optimization_barrier((halves, early, best))
     swap = [(p, p ^ 1) for p in range(2 * loop_size)]
+    other_halves = [lax.ppermute(half, ("loop", "pair"), swap) for half in halves]
     late = [lax.ppermute(shard, ("loop", "pair"), swap) for shard in early]
-    passed = [lax.ppermute(shard, ("loop", "pair"), swap) for shard in direct]
     early_total, early_weighted = total, weighted
     if early:
         early_total, early_weighted = pl.pallas_call(
@@ -286,9 +304,9 @@
             cost_estimate=cost(shard_rows * len(early)),
         )(queries, best, total, weighted, *early)
     last_inputs = (queries, best, total, weighted, early_total, early_weighted)
-    last_inputs += (*early, *late, *direct, *passed)
+    last_inputs += (*halves, *other_halves, *early, *late)
     return pl.pallas_call(
-        functools.partial(late_stage, len(early), len(late), len(direct)),
+        functools.partial(late_stage, len(early), len(late), len(halves)),
         name="late_stage",
         out_shape=jax.ShapeDtypeStruct((slots, width), jnp.bfloat16),
         in_specs=[in_vmem] * len(last_inputs),
@@ -298,7 +316,7 @@
             pltpu.SemaphoreType.DMA((len(row_blocks(slots)),)),
         ],
         compiler_params=pltpu.CompilerParams(vmem_limit_bytes=32 * 2**20),
-        cost_estimate=cost(shard_rows * (len(late) + len(direct))),
+        cost_estimate=cost(shard_rows * (len(late) + len(halves))),
     )(*last_inputs)
 
 

time: 23.6 us -> 22.2 us (0.941)
  starting transfers between devices: 8.07 us -> 6.19 us
  waiting for transfers between devices: 1.13 us -> 1.73 us
    ppermute x2, starting transfers between devices: 5.93 us -> 3.05 us  [the longest x1 2.65 us: shards(): halves.append(lax.ppermute(half, 'loop', across))]
    ppermute x2, waiting for transfers between devices: 0.01 us -> 1.73 us  [the longest x1 1.72 us: shards(): halves.append(lax.ppermute(half, 'loop', across))]
    ppermute x1, starting transfers between devices: 1.63 us -> 3.02 us  [shards(): early.append(lax.ppermute(own, ('loop', 'pair'), hops))]
    ppermute x1, waiting for transfers between devices: 1.07 us -> 0.01 us  [shards(): early.append(lax.ppermute(own, ('loop', 'pair'), hops))]
    ppermute x1, starting transfers between devices: 0.51 us -> 0.12 us  [shards(): late = [lax.ppermute(shard, ('loop', 'pair'), swap) for shard in early]]
    pallas_call x2 -> x3, Pallas kernels: 13.2 us -> 13.2 us  [the longest x1 8.91 us: shards(): pl.pallas_call(functools.partial(late_stage, len(early), len(late), len(h...]
  transfers between devices with their start and end apart: 4 -> 4, of which waited for: 2 -> 1; matrix products, arithmetic and copies ran while one was open for 0% -> 0% of each run, Pallas kernels for 22% -> 24%
where the time goes in v6:
time: 22.2 us; the launch traced here: 22.1 us
  Pallas kernels  14.1 us (64%)
  starting transfers between devices  6.19 us (28%)
  waiting for transfers between devices  1.73 us (8%)
    pallas_call x1, Pallas kernels, shards(): pl.pallas_call(functools.partial(late_stage, len(early), len(late), len(h...  8.91 us
    ppermute x1, starting transfers between devices, shards(): early.append(lax.ppermute(own, ('loop', 'pair'), hops))  3.02 us
    pallas_call x1, Pallas kernels, shards(): pl.pallas_call(local_stage, name='local_stage', out_shape=[state] * 3, in...  2.92 us
    ppermute x1, starting transfers between devices, shards(): halves.append(lax.ppermute(half, 'loop', across))  2.65 us
    ppermute x1, waiting for transfers between devices, shards(): halves.append(lax.ppermute(half, 'loop', across))  1.72 us
    pallas_call x1, Pallas kernels, shards(): pl.pallas_call(load_stage, name='load_stage', out_shape=[jax.ShapeDtypeSt...  1.33 us
    pallas_call x1, Pallas kernels, shards(): pl.pallas_call(early_stage, name='early_stage', out_shape=[state] * 2, in...  0.95 us
  transfers between devices with their start and end apart: 4, of which 1 were waited for; matrix products, arithmetic and copies ran while one was open for 0% of the time, Pallas kernels for 24%

profile of v6, /device:TPU:0, one launch (start us, length us, event | category | flops | bytes accessed | tf_op | source)
XLA Modules:
  0.0 22.1 jit_solution(17597893875488898973)
XLA Ops:
  0.0 3.0 %collective-permute-start.1 = (bf16[256,256]{1,0:T(8,128)(2,1)}, bf16[256,256]{1,0:T(8,128)(2,1)S(1)}, u32[]{:S(2)}, u32[]{:S(2)}) collective-permute-start(bf16[256,256]{1,0:T(8,128)(2,1)} %bitcast.3), channel_id=1, source_target_pairs={{0,4},{4,8},{8,12},{12,0},{1,13},{5,1},{9,5},{13,9},{2,6},{6,10},{... | collective-permute-start | bytes 393224 | tf_op jit(solution)/shard_map/ppermute | solution.py:255
  3.0 1.3 %load_stage.1 = (bf16[640,512]{1,0:T(8,128)(2,1)S(1)}, bf16[640,256]{1,0:T(8,128)(2,1)S(1)}, bf16[256,256]{1,0:T(8,128)(2,1)S(1)}, bf16[128,256]{1,0:T(8,128)(2,1)S(1)}, s32[640,128]{1,0:T(8,128)S(1)}) custom-call(s32[8]{0:T(128)} %lengths_hbm.1, bf16[640,512]{1,0:T(8,128)(2,1)} %query_hbm.1, bf16[640,256]{1,0:T(8,128)(2,1)} %bitcast.2, bf16[256,256]{1,0:T(8,128)(2,1)} %bitcast.4), custom_call_target="tpu_custom_call" | custom-call | bytes 1966080 | tf_op jit(solution)/shard_map/load_stage/pallas_call | solution.py:257
  4.4 2.7 %collective-permute-start = (bf16[128,256]{1,0:T(8,128)(2,1)S(1)}, bf16[128,256]{1,0:T(8,128)(2,1)S(1)}, u32[]{:S(2)}, u32[]{:S(2)}) collective-permute-start(bf16[128,256]{1,0:T(8,128)(2,1)S(1)} %get-tuple-element.19), channel_id=1, source_target_pairs={{0,8},{4,12},{8,0},{12,4},{1,9},{5,13},{9,1},{13,5},{2,10},{6,14},... | collective-permute-start | bytes 196616 | tf_op jit(solution)/shard_map/ppermute | solution.py:281
  7.0 2.9 %local_stage.1 = (f32[640,512]{1,0:T(8,128)S(1)}, f32[640,512]{1,0:T(8,128)S(1)}, f32[640,512]{1,0:T(8,128)S(1)}) custom-call(bf16[640,512]{1,0:T(8,128)(2,1)S(1)} %get-tuple-element.18.query_ref.refs_0_, bf16[640,256]{1,0:T(8,128)(2,1)S(1)} %get-tuple-element.20.suffix_ref, bf16[256,256]{1,0:T(8,128)(2,1)S(1)} %get-tuple-element.21.own_ref, ...), custom_call_target="tpu_custom_call" | custom-call | flops 754974720 | bytes 4587520 | tf_op jit(solution)/shard_map/local_stage/pallas_call | solution.py:282
  9.9 1.7 %collective-permute-done.refs_6_ = bf16[128,256]{1,0:T(8,128)(2,1)S(1)} collective-permute-done((bf16[128,256]{1,0:T(8,128)(2,1)S(1)}, bf16[128,256]{1,0:T(8,128)(2,1)S(1)}, u32[]{:S(2)}, u32[]{:S(2)}) %collective-permute-start) | collective-permute-done | bytes 65568 | tf_op jit(solution)/shard_map/ppermute | solution.py:281
  11.7 0.0 collective-permute-done.1.refs_4_.refs_8_
  11.7 0.1 collective-permute-start.3
  11.8 0.4 %collective-permute-start.2 = (bf16[128,256]{1,0:T(8,128)(2,1)S(1)}, bf16[128,256]{1,0:T(8,128)(2,1)S(1)}, u32[]{:S(2)}, u32[]{:S(2)}) collective-permute-start(bf16[128,256]{1,0:T(8,128)(2,1)S(1)} %collective-permute-done.refs_6_), channel_id=1, source_target_pairs={{0,1},{1,0},{4,5},{5,4},{8,9},{9,8},{12,13},{13,12},{2,3},{3,2},{6... | collective-permute-start | bytes 196616 | tf_op jit(solution)/shard_map/ppermute | solution.py:293
  12.2 1.0 %early_stage.1 = (f32[640,512]{1,0:T(8,128)S(1)}, f32[640,512]{1,0:T(8,128)S(1)}) custom-call(bf16[640,512]{1,0:T(8,128)(2,1)S(1)} %get-tuple-element.18.query_ref.refs_0_, f32[640,512]{1,0:T(8,128)S(1)} %get-tuple-element.24.refs_1_, f32[640,512]{1,0:T(8,128)S(1)} %get-tuple-element.25.refs_2_, f32[640,512]{1,0:T(8,128)S(1)} %get-tuple-element.26.refs_3_, ...), custom_call_target="tpu_custom_call" | custom-call | flops 335544320 | bytes 4587520 | tf_op jit(solution)/shard_map/early_stage/pallas_call | solution.py:297
  13.1 0.0 collective-permute-done.2.refs_7_
  13.2 0.0 collective-permute-done.3.refs_9_
  13.2 8.9 %late_stage.1 = bf16[640,512]{1,0:T(8,128)(2,1)} custom-call(bf16[640,512]{1,0:T(8,128)(2,1)S(1)} %get-tuple-element.18.query_ref.refs_0_, f32[640,512]{1,0:T(8,128)S(1)} %get-tuple-element.24.refs_1_, f32[640,512]{1,0:T(8,128)S(1)} %get-tuple-element.25.refs_2_, f32[640,512]{1,0:T(8,128)S(1)} %get-tuple-element.26.refs_3_, ...), custom_call_target="tpu_custom_call" | custom-call | flops 671088640 | bytes 4587520 | tf_op jit(solution)/shard_map/late_stage/pallas_call | solution.py:308
Async XLA Ops:
  0.0 11.7 %collective-permute-start.1 = (bf16[256,256]{1,0:T(8,128)(2,1)}, bf16[256,256]{1,0:T(8,128)(2,1)S(1)}, u32[]{:S(2)}, u32[]{:S(2)}) collective-permute-start(bf16[256,256]{1,0:T(8,128)(2,1)} %bitcast.3), channel_id=1, source_target_pairs={{0,4},{4,8},{8,12},{12,0},{1,13},{5,1},{9,5},{13,9},{2,6},{6,10},{... | collective-permute-start | bytes 393224 | tf_op jit(solution)/shard_map/ppermute | solution.py:255
  4.4 7.3 %collective-permute-start = (bf16[128,256]{1,0:T(8,128)(2,1)S(1)}, bf16[128,256]{1,0:T(8,128)(2,1)S(1)}, u32[]{:S(2)}, u32[]{:S(2)}) collective-permute-start(bf16[128,256]{1,0:T(8,128)(2,1)S(1)} %get-tuple-element.19), channel_id=1, source_target_pairs={{0,8},{4,12},{8,0},{12,4},{1,9},{5,13},{9,1},{13,5},{2,10},{6,14},... | collective-permute-start | bytes 196616 | tf_op jit(solution)/shard_map/ppermute | solution.py:281
  11.7 1.5 %collective-permute-start.3 = (bf16[256,256]{1,0:T(8,128)(2,1)S(1)}, bf16[256,256]{1,0:T(8,128)(2,1)S(1)}, u32[]{:S(2)}, u32[]{:S(2)}) collective-permute-start(bf16[256,256]{1,0:T(8,128)(2,1)S(1)} %collective-permute-done.1.refs_4_.refs_8_), channel_id=1, source_target_pairs={{0,1},{1,0},{4,5},{5,4},{8,9},{9,8},{12,13},{13,12},{2,3},{3,2},{6... | collective-permute-start | bytes 393224 | tf_op jit(solution)/shard_map/ppermute | solution.py:294
  11.8 1.4 %collective-permute-start.2 = (bf16[128,256]{1,0:T(8,128)(2,1)S(1)}, bf16[128,256]{1,0:T(8,128)(2,1)S(1)}, u32[]{:S(2)}, u32[]{:S(2)}) collective-permute-start(bf16[128,256]{1,0:T(8,128)(2,1)S(1)} %collective-permute-done.refs_6_), channel_id=1, source_target_pairs={{0,1},{1,0},{4,5},{5,4},{8,9},{9,8},{12,13},{13,12},{2,3},{3,2},{6... | collective-permute-start | bytes 196616 | tf_op jit(solution)/shard_map/ppermute | solution.py:293

commit v7 on v5

--- a/solution.py
+++ b/solution.py
@@ -136,18 +136,33 @@
     return [slice(first, first + step) for first in range(0, count, step)]
 
 
-def late_stage(
-    query_ref, best_ref, total_ref, sum_ref, gathered_ref, out_hbm, out_ref, out_sems
-):
-    old_total_ref, old_sum_ref = total_ref, sum_ref
+def add_stage(*refs):
+    query_ref, best_ref, total_ref, sum_ref = refs[:4]
+    shard_refs = refs[4:-2]
+    total_out, sum_out = refs[-2:]
+    heads = query_ref.shape[1] // HD
+    shards_here = [(ref[:, :HD], with_ones(ref[:, HD:])) for ref in shard_refs]
+    for rows in row_blocks(query_ref.shape[0]):
+        queries = stacked(query_ref, rows, heads)
+        best = stacked(best_ref, rows, heads)
+        total = stacked(total_ref, rows, heads)
+        weighted = stacked(sum_ref, rows, heads)
+        for key_rows, value_rows in shards_here:
+            total, weighted = add_shard(queries, best, key_rows, value_rows, total, weighted)
+        unstack(total_out, rows, heads, total)
+        unstack(sum_out, rows, heads, weighted)
+
+
+def last_stage(earlier_count, last_count, *refs):
+    query_ref, best_ref, old_total_ref, old_sum_ref, total_ref, sum_ref = refs[:6]
+    earlier_refs = refs[6 : 6 + earlier_count]
+    last_refs = refs[6 + earlier_count : 6 + earlier_count + last_count]
+    out_hbm, out_ref, out_sems = refs[6 + earlier_count + last_count :]
     heads = query_ref.shape[1] // HD
     blocks = row_blocks(query_ref.shape[0])
-    loop_size = gathered_ref.shape[0]
-    position = lax.axis_index("loop")
-
-    def load(unused):
-        loaded = [gathered_ref[lax.rem(position + i, loop_size)] for i in range(1, loop_size)]
-        return [(shard[:, :HD], with_ones(shard[:, HD:])) for shard in loaded]
+
+    def load(shard_refs):
+        return [(ref[:, :HD], with_ones(ref[:, HD:])) for ref in shard_refs]
 
     def out_copy(index, rows):
         return pltpu.make_async_copy(out_ref.at[rows], out_hbm.at[rows], out_sems.at[index])
@@ -156,7 +171,7 @@
         unstack(out_ref, rows, heads, (weighted / total).astype(jnp.bfloat16))
 
     trusted = jnp.full((8, HD), True)
-    shards_here = load(())
+    shards_here = load(last_refs)
     for index, rows in enumerate(blocks):
         queries = stacked(query_ref, rows, heads)
         best = stacked(best_ref, rows, heads)
@@ -181,7 +196,7 @@
             best = stacked(best_ref, rows, heads)
             weighted = stacked(old_sum_ref, rows, heads)
             total = stacked(old_total_ref, rows, heads)
-            for key_rows, value_rows in load(()):
+            for key_rows, value_rows in load(earlier_refs + last_refs):
                 scores = scores_of(queries, key_rows)
                 new_best = jnp.maximum(best, jnp.max(scores, axis=1, keepdims=True))
                 factor = jnp.exp2(best - new_best)
@@ -209,17 +224,24 @@
     suffix = suffix_kv[:, 0, :]
     shard_rows = own.shape[0]
 
-    gathered = lax.all_gather(own, "loop", axis=0, tiled=False)
+    power_of_two = loop_size & (loop_size - 1) == 0
+
+    def exchange(shard, step_of_core):
+        hops = []
+        for core, step in enumerate(step_of_core):
+            for i in range(loop_size):
+                to = i ^ step if power_of_two else (i + step) % loop_size
+                hops.append((2 * i + core, 2 * to + core))
+        return lax.ppermute(shard, ("loop", "pair"), hops)
+
+    to_both = 1 - loop_size % 2
+    early = [exchange(own, (1, 1))] * to_both
+    middle = [exchange(own, (step, step + 1)) for step in range(1 + to_both, loop_size, 2)]
     in_hbm = pl.BlockSpec(memory_space=pltpu.HBM)
     in_vmem = pl.BlockSpec(memory_space=pltpu.VMEM)
     state = jax.ShapeDtypeStruct((slots, width), jnp.float32)
 
-    def cost(keys):
-        return pl.CostEstimate(
-            flops=slots * heads * keys * HD * 4,
-            bytes_accessed=slots * width * 14,
-            transcendentals=slots * heads * keys,
-        )
+    cost = pl.CostEstimate(flops=1, bytes_accessed=1, transcendentals=0)
 
     best, total, weighted, queries = pl.pallas_call(
         local_stage,
@@ -235,21 +257,41 @@
             pltpu.SemaphoreType.DMA((slots // BLK,)),
         ],
         compiler_params=pltpu.CompilerParams(vmem_limit_bytes=24 * 2**20),
-        cost_estimate=cost(shard_rows + MAXLEN),
+        cost_estimate=cost,
     )(*(pltpu.with_memory_space_constraint(x, pltpu.HBM) for x in (lengths, queries, suffix, own)))
+    def add_shards(total, weighted, shards_now):
+        if not shards_now:
+            return total, weighted
+        return pl.pallas_call(
+            add_stage,
+            name="add_stage",
+            out_shape=[state] * 2,
+            in_specs=[in_vmem] * (4 + len(shards_now)),
+            out_specs=[in_vmem] * 2,
+            compiler_params=pltpu.CompilerParams(vmem_limit_bytes=24 * 2**20),
+            cost_estimate=cost,
+        )(queries, best, total, weighted, *shards_now)
+
+    new_total, new_weighted = add_shards(total, weighted, early)
+    middle, new_total = lax.optimization_barrier((middle, new_total))
+    swap = [(p, p ^ 1) for p in range(2 * loop_size)]
+    last = [lax.ppermute(shard, ("loop", "pair"), swap) for shard in middle]
+    new_total, new_weighted = add_shards(new_total, new_weighted, middle)
+    last_inputs = (queries, best, total, weighted, new_total, new_weighted)
+    last_inputs += (*early, *middle, *last)
     return pl.pallas_call(
-        late_stage,
-        name="late_stage",
+        functools.partial(last_stage, len(early) + len(middle), len(last)),
+        name="last_stage",
         out_shape=jax.ShapeDtypeStruct((slots, width), jnp.bfloat16),
-        in_specs=[in_vmem] * 5,
+        in_specs=[in_vmem] * len(last_inputs),
         out_specs=in_hbm,
         scratch_shapes=[
             pltpu.VMEM((slots, width), jnp.bfloat16),
             pltpu.SemaphoreType.DMA((len(row_blocks(slots)),)),
         ],
         compiler_params=pltpu.CompilerParams(vmem_limit_bytes=32 * 2**20),
-        cost_estimate=cost(shard_rows * (loop_size - 1)),
-    )(queries, best, total, weighted, gathered)
+        cost_estimate=cost,
+    )(*last_inputs)
 
 
 def solution(mesh):

time: 31.6 us -> 21.6 us (0.68)
  blocking collectives: 17.6 us -> 0 us
  starting transfers between devices: 0 us -> 5.62 us
  waiting for transfers between devices: 0 us -> 1.4 us
  Pallas kernels: 13.9 us -> 14.5 us
    all_gather x1 -> x0, blocking collectives: 17.6 us -> none  [shards(): gathered = lax.all_gather(own, 'loop', axis=0, tiled=False)]
    ppermute x0 -> x3, starting transfers between devices: none -> 5.62 us  [the longest x2 5.61 us: exchange(): return lax.ppermute(shard, ('loop', 'pair'), hops)]
    ppermute x0 -> x3, waiting for transfers between devices: none -> 1.4 us  [the longest x2 1.02 us: exchange(): return lax.ppermute(shard, ('loop', 'pair'), hops)]
    pallas_call x1 -> x3, Pallas kernels: 9.6 us -> 10.1 us  [the longest x1 8.24 us: shards(): pl.pallas_call(functools.partial(last_stage, len(early) + len(middle), le...]
  transfers between devices with their start and end apart: 0 -> 3, of which waited for: 0 -> 2; matrix products, arithmetic and copies ran while one was open for 0% -> 0% of each run, Pallas kernels for 0% -> 29%
where the time goes in v7:
time: 21.6 us; the launch traced here: 21.5 us
  Pallas kernels  14.5 us (67%)
  starting transfers between devices  5.62 us (26%)
  waiting for transfers between devices  1.4 us (6%)
    pallas_call x1, Pallas kernels, shards(): pl.pallas_call(functools.partial(last_stage, len(early) + len(middle), le...  8.24 us
    ppermute x2, starting transfers between devices, exchange(): return lax.ppermute(shard, ('loop', 'pair'), hops)  5.61 us
    pallas_call x1, Pallas kernels, shards(): pl.pallas_call(local_stage, name='local_stage', out_shape=[state] * 3 + [...  4.3 us
    pallas_call x2, Pallas kernels, add_shards(): pl.pallas_call(add_stage, name='add_stage', out_shape=[state] * 2, in_spe...  1.91 us
    ppermute x2, waiting for transfers between devices, exchange(): return lax.ppermute(shard, ('loop', 'pair'), hops)  1.02 us
  transfers between devices with their start and end apart: 3, of which 2 were waited for; matrix products, arithmetic and copies ran while one was open for 0% of the time, Pallas kernels for 29%

profile of v7, /device:TPU:0, one launch (start us, length us, event | category | flops | bytes accessed | tf_op | source)
XLA Modules:
  0.0 21.5 jit_solution(2174653420726734867)
XLA Ops:
  0.0 3.0 %collective-permute-start.1 = (bf16[256,256]{1,0:T(8,128)(2,1)}, bf16[256,256]{1,0:T(8,128)(2,1)S(1)}, u32[]{:S(2)}, u32[]{:S(2)}) collective-permute-start(bf16[256,256]{1,0:T(8,128)(2,1)} %bitcast.3), channel_id=1, source_target_pairs={{0,4},{4,0},{8,12},{12,8},{1,5},{5,1},{9,13},{13,9},{2,6},{6,2},{1... | collective-permute-start | bytes 393224 | tf_op jit(solution)/shard_map/ppermute | solution.py:235
  3.0 2.6 %collective-permute-start = (bf16[256,256]{1,0:T(8,128)(2,1)}, bf16[256,256]{1,0:T(8,128)(2,1)S(1)}, u32[]{:S(2)}, u32[]{:S(2)}) collective-permute-start(bf16[256,256]{1,0:T(8,128)(2,1)} %bitcast.4), channel_id=1, source_target_pairs={{0,8},{4,12},{8,0},{12,4},{1,13},{5,9},{9,5},{13,1},{2,10},{6,14},... | collective-permute-start | bytes 393224 | tf_op jit(solution)/shard_map/ppermute | solution.py:235
  5.6 4.3 %local_stage.1 = (f32[640,512]{1,0:T(8,128)S(1)}, f32[640,512]{1,0:T(8,128)S(1)}, f32[640,512]{1,0:T(8,128)S(1)}, bf16[640,512]{1,0:T(8,128)(2,1)S(1)}) custom-call(s32[8]{0:T(128)} %lengths_hbm.1, bf16[640,512]{1,0:T(8,128)(2,1)} %query_hbm.1, bf16[640,256]{1,0:T(8,128)(2,1)} %bitcast.2, bf16[256,256]{1,0:T(8,128)(2,1)} %bitcast.5), custom_call_target="tpu_custom_call" | custom-call | flops 1 | bytes 1 | tf_op jit(solution)/shard_map/local_stage/pallas_call | solution.py:246
  9.9 0.0 collective-permute-done.1.refs_4_.refs_6_
  9.9 1.0 %add_stage.2 = (f32[640,512]{1,0:T(8,128)S(1)}, f32[640,512]{1,0:T(8,128)S(1)}) custom-call(bf16[640,512]{1,0:T(8,128)(2,1)S(1)} %get-tuple-element.15.refs_0_, f32[640,512]{1,0:T(8,128)S(1)} %get-tuple-element.16.refs_1_, f32[640,512]{1,0:T(8,128)S(1)} %get-tuple-element.17.refs_2_, f32[640,512]{1,0:T(8,128)S(1)} %get-tuple-element.18.refs_3_, ...), custom_call_target="tpu_custom_call" | custom-call | flops 1 | bytes 1 | tf_op jit(solution)/shard_map/add_stage/pallas_call | solution.py:265
  10.9 1.0 %collective-permute-done.refs_4_.refs_7_ = bf16[256,256]{1,0:T(8,128)(2,1)S(1)} collective-permute-done((bf16[256,256]{1,0:T(8,128)(2,1)}, bf16[256,256]{1,0:T(8,128)(2,1)S(1)}, u32[]{:S(2)}, u32[]{:S(2)}) %collective-permute-start) | collective-permute-done | bytes 131104 | tf_op jit(solution)/shard_map/ppermute | solution.py:235
  11.9 0.0 collective-permute-start.2
  11.9 1.0 %add_stage.3 = (f32[640,512]{1,0:T(8,128)S(1)}, f32[640,512]{1,0:T(8,128)S(1)}) custom-call(bf16[640,512]{1,0:T(8,128)(2,1)S(1)} %get-tuple-element.15.refs_0_, f32[640,512]{1,0:T(8,128)S(1)} %get-tuple-element.16.refs_1_, f32[640,512]{1,0:T(8,128)S(1)} %get-tuple-element.20.refs_2_, f32[640,512]{1,0:T(8,128)S(1)} %get-tuple-element.21.refs_3_, ...), custom_call_target="tpu_custom_call" | custom-call | flops 1 | bytes 1 | tf_op jit(solution)/shard_map/add_stage/pallas_call | solution.py:265
  12.9 0.4 %collective-permute-done.2.refs_8_ = bf16[256,256]{1,0:T(8,128)(2,1)S(1)} collective-permute-done((bf16[256,256]{1,0:T(8,128)(2,1)S(1)}, bf16[256,256]{1,0:T(8,128)(2,1)S(1)}, u32[]{:S(2)}, u32[]{:S(2)}) %collective-permute-start.2) | collective-permute-done | bytes 131104 | tf_op jit(solution)/shard_map/ppermute | solution.py:278
  13.3 8.2 %last_stage.1 = bf16[640,512]{1,0:T(8,128)(2,1)} custom-call(bf16[640,512]{1,0:T(8,128)(2,1)S(1)} %get-tuple-element.15.refs_0_, f32[640,512]{1,0:T(8,128)S(1)} %get-tuple-element.16.refs_1_, f32[640,512]{1,0:T(8,128)S(1)} %get-tuple-element.17.refs_2_, f32[640,512]{1,0:T(8,128)S(1)} %get-tuple-element.18.refs_3_, f32[640,512]{1,0:T(8,128)S(1)} %get-tuple-element.23.refs_4_, ...), custom_call_target="tpu_custom_call" | custom-call | flops 1 | bytes 1 | tf_op jit(solution)/shard_map/last_stage/pallas_call | solution.py:282
Async XLA Ops:
  0.0 9.9 %collective-permute-start.1 = (bf16[256,256]{1,0:T(8,128)(2,1)}, bf16[256,256]{1,0:T(8,128)(2,1)S(1)}, u32[]{:S(2)}, u32[]{:S(2)}) collective-permute-start(bf16[256,256]{1,0:T(8,128)(2,1)} %bitcast.3), channel_id=1, source_target_pairs={{0,4},{4,0},{8,12},{12,8},{1,5},{5,1},{9,13},{13,9},{2,6},{6,2},{1... | collective-permute-start | bytes 393224 | tf_op jit(solution)/shard_map/ppermute | solution.py:235
  3.0 8.9 %collective-permute-start = (bf16[256,256]{1,0:T(8,128)(2,1)}, bf16[256,256]{1,0:T(8,128)(2,1)S(1)}, u32[]{:S(2)}, u32[]{:S(2)}) collective-permute-start(bf16[256,256]{1,0:T(8,128)(2,1)} %bitcast.4), channel_id=1, source_target_pairs={{0,8},{4,12},{8,0},{12,4},{1,13},{5,9},{9,5},{13,1},{2,10},{6,14},... | collective-permute-start | bytes 393224 | tf_op jit(solution)/shard_map/ppermute | solution.py:235
  11.9 1.3 %collective-permute-start.2 = (bf16[256,256]{1,0:T(8,128)(2,1)S(1)}, bf16[256,256]{1,0:T(8,128)(2,1)S(1)}, u32[]{:S(2)}, u32[]{:S(2)}) collective-permute-start(bf16[256,256]{1,0:T(8,128)(2,1)S(1)} %collective-permute-done.refs_4_.refs_7_), channel_id=1, source_target_pairs={{0,1},{1,0},{4,5},{5,4},{8,9},{9,8},{12,13},{13,12},{2,3},{3,2},{6... | collective-permute-start | bytes 393224 | tf_op jit(solution)/shard_map/ppermute | solution.py:278

commit v8 on v7

--- a/solution.py
+++ b/solution.py
@@ -272,13 +272,12 @@
             cost_estimate=cost,
         )(queries, best, total, weighted, *shards_now)
 
-    new_total, new_weighted = add_shards(total, weighted, early)
-    middle, new_total = lax.optimization_barrier((middle, new_total))
+    middle, best = lax.optimization_barrier((middle, best))
     swap = [(p, p ^ 1) for p in range(2 * loop_size)]
     last = [lax.ppermute(shard, ("loop", "pair"), swap) for shard in middle]
-    new_total, new_weighted = add_shards(new_total, new_weighted, middle)
+    new_total, new_weighted = add_shards(total, weighted, middle + early)
     last_inputs = (queries, best, total, weighted, new_total, new_weighted)
-    last_inputs += (*early, *middle, *last)
+    last_inputs += (*middle, *early, *last)
     return pl.pallas_call(
         functools.partial(last_stage, len(early) + len(middle), len(last)),
         name="last_stage",

time: 21.6 us -> 21.6 us (level)
  Pallas kernels: 14.5 us -> 14.2 us
  waiting for transfers between devices: 1.4 us -> 1.69 us
    ppermute x2, waiting for transfers between devices: 1.02 us -> 1.68 us  [exchange(): return lax.ppermute(shard, ('loop', 'pair'), hops)]
    ppermute x1, waiting for transfers between devices: 0.38 us -> 0.01 us  [shards(): last = [lax.ppermute(shard, ('loop', 'pair'), swap) for shard in middle]]
    pallas_call x2 -> x1, Pallas kernels: 1.91 us -> 1.64 us  [add_shards(): pl.pallas_call(add_stage, name='add_stage', out_shape=[state] * 2, in_spe...]
  transfers between devices with their start and end apart: 3 -> 3, of which waited for: 2 -> 2; matrix products, arithmetic and copies ran while one was open for 0% -> 0% of each run, Pallas kernels for 29% -> 28%
where the time goes in v8:
time: 21.6 us; the launch traced here: 21.5 us
  Pallas kernels  14.2 us (66%)
  starting transfers between devices  5.62 us (26%)
  waiting for transfers between devices  1.69 us (8%)
    pallas_call x1, Pallas kernels, shards(): pl.pallas_call(functools.partial(last_stage, len(early) + len(middle), le...  8.24 us
    ppermute x2, starting transfers between devices, exchange(): return lax.ppermute(shard, ('loop', 'pair'), hops)  5.61 us
    pallas_call x1, Pallas kernels, shards(): pl.pallas_call(local_stage, name='local_stage', out_shape=[state] * 3 + [...  4.3 us
    ppermute x2, waiting for transfers between devices, exchange(): return lax.ppermute(shard, ('loop', 'pair'), hops)  1.68 us
    pallas_call x1, Pallas kernels, add_shards(): pl.pallas_call(add_stage, name='add_stage', out_shape=[state] * 2, in_spe...  1.64 us
  transfers between devices with their start and end apart: 3, of which 2 were waited for; matrix products, arithmetic and copies ran while one was open for 0% of the time, Pallas kernels for 28%

profile of v8, /device:TPU:0, one launch (start us, length us, event | category | flops | bytes accessed | tf_op | source)
XLA Modules:
  0.0 21.5 jit_solution(237531175579835372)
XLA Ops:
  0.0 4.0 %collective-permute-start = (bf16[256,256]{1,0:T(8,128)(2,1)}, bf16[256,256]{1,0:T(8,128)(2,1)S(1)}, u32[]{:S(2)}, u32[]{:S(2)}) collective-permute-start(bf16[256,256]{1,0:T(8,128)(2,1)} %bitcast.3), channel_id=1, source_target_pairs={{0,8},{4,12},{8,0},{12,4},{1,13},{5,9},{9,5},{13,1},{2,10},{6,14},... | collective-permute-start | bytes 393224 | tf_op jit(solution)/shard_map/ppermute | solution.py:235
  4.0 1.6 %collective-permute-start.1 = (bf16[256,256]{1,0:T(8,128)(2,1)}, bf16[256,256]{1,0:T(8,128)(2,1)S(1)}, u32[]{:S(2)}, u32[]{:S(2)}) collective-permute-start(bf16[256,256]{1,0:T(8,128)(2,1)} %bitcast.4), channel_id=1, source_target_pairs={{0,4},{4,0},{8,12},{12,8},{1,5},{5,1},{9,13},{13,9},{2,6},{6,2},{1... | collective-permute-start | bytes 393224 | tf_op jit(solution)/shard_map/ppermute | solution.py:235
  5.6 4.3 %local_stage.1 = (f32[640,512]{1,0:T(8,128)S(1)}, f32[640,512]{1,0:T(8,128)S(1)}, f32[640,512]{1,0:T(8,128)S(1)}, bf16[640,512]{1,0:T(8,128)(2,1)S(1)}) custom-call(s32[8]{0:T(128)} %lengths_hbm.1, bf16[640,512]{1,0:T(8,128)(2,1)} %query_hbm.1, bf16[640,256]{1,0:T(8,128)(2,1)} %bitcast.2, bf16[256,256]{1,0:T(8,128)(2,1)} %bitcast.5), custom_call_target="tpu_custom_call" | custom-call | flops 1 | bytes 1 | tf_op jit(solution)/shard_map/local_stage/pallas_call | solution.py:246
  9.9 0.9 %collective-permute-done.refs_4_.refs_6_ = bf16[256,256]{1,0:T(8,128)(2,1)S(1)} collective-permute-done((bf16[256,256]{1,0:T(8,128)(2,1)}, bf16[256,256]{1,0:T(8,128)(2,1)S(1)}, u32[]{:S(2)}, u32[]{:S(2)}) %collective-permute-start) | collective-permute-done | bytes 131104 | tf_op jit(solution)/shard_map/ppermute | solution.py:235
  10.8 0.0 collective-permute-start.2
  10.8 0.8 %collective-permute-done.1.refs_5_.refs_7_ = bf16[256,256]{1,0:T(8,128)(2,1)S(1)} collective-permute-done((bf16[256,256]{1,0:T(8,128)(2,1)}, bf16[256,256]{1,0:T(8,128)(2,1)S(1)}, u32[]{:S(2)}, u32[]{:S(2)}) %collective-permute-start.1) | collective-permute-done | bytes 131104 | tf_op jit(solution)/shard_map/ppermute | solution.py:235
  11.6 1.6 %add_stage.1 = (f32[640,512]{1,0:T(8,128)S(1)}, f32[640,512]{1,0:T(8,128)S(1)}) custom-call(bf16[640,512]{1,0:T(8,128)(2,1)S(1)} %get-tuple-element.13.refs_0_, f32[640,512]{1,0:T(8,128)S(1)} %get-tuple-element.15.refs_1_, f32[640,512]{1,0:T(8,128)S(1)} %get-tuple-element.16.refs_2_, f32[640,512]{1,0:T(8,128)S(1)} %get-tuple-element.17.refs_3_, ...), custom_call_target="tpu_custom_call" | custom-call | flops 1 | bytes 1 | tf_op jit(solution)/shard_map/add_stage/pallas_call | solution.py:265
  13.3 0.0 collective-permute-done.2.refs_8_
  13.3 8.2 %last_stage.1 = bf16[640,512]{1,0:T(8,128)(2,1)} custom-call(bf16[640,512]{1,0:T(8,128)(2,1)S(1)} %get-tuple-element.13.refs_0_, f32[640,512]{1,0:T(8,128)S(1)} %get-tuple-element.15.refs_1_, f32[640,512]{1,0:T(8,128)S(1)} %get-tuple-element.16.refs_2_, f32[640,512]{1,0:T(8,128)S(1)} %get-tuple-element.17.refs_3_, f32[640,512]{1,0:T(8,128)S(1)} %get-tuple-element.19.refs_4_, ...), custom_call_target="tpu_custom_call" | custom-call | flops 1 | bytes 1 | tf_op jit(solution)/shard_map/last_stage/pallas_call | solution.py:281
Async XLA Ops:
  0.0 10.8 %collective-permute-start = (bf16[256,256]{1,0:T(8,128)(2,1)}, bf16[256,256]{1,0:T(8,128)(2,1)S(1)}, u32[]{:S(2)}, u32[]{:S(2)}) collective-permute-start(bf16[256,256]{1,0:T(8,128)(2,1)} %bitcast.3), channel_id=1, source_target_pairs={{0,8},{4,12},{8,0},{12,4},{1,13},{5,9},{9,5},{13,1},{2,10},{6,14},... | collective-permute-start | bytes 393224 | tf_op jit(solution)/shard_map/ppermute | solution.py:235
  4.0 7.6 %collective-permute-start.1 = (bf16[256,256]{1,0:T(8,128)(2,1)}, bf16[256,256]{1,0:T(8,128)(2,1)S(1)}, u32[]{:S(2)}, u32[]{:S(2)}) collective-permute-start(bf16[256,256]{1,0:T(8,128)(2,1)} %bitcast.4), channel_id=1, source_target_pairs={{0,4},{4,0},{8,12},{12,8},{1,5},{5,1},{9,13},{13,9},{2,6},{6,2},{1... | collective-permute-start | bytes 393224 | tf_op jit(solution)/shard_map/ppermute | solution.py:235
  10.8 2.4 %collective-permute-start.2 = (bf16[256,256]{1,0:T(8,128)(2,1)S(1)}, bf16[256,256]{1,0:T(8,128)(2,1)S(1)}, u32[]{:S(2)}, u32[]{:S(2)}) collective-permute-start(bf16[256,256]{1,0:T(8,128)(2,1)S(1)} %collective-permute-done.refs_4_.refs_6_), channel_id=1, source_target_pairs={{0,1},{1,0},{4,5},{5,4},{8,9},{9,8},{12,13},{13,12},{2,3},{3,2},{6... | collective-permute-start | bytes 393224 | tf_op jit(solution)/shard_map/ppermute | solution.py:277

commit v9 on v8

--- a/solution.py
+++ b/solution.py
@@ -235,7 +235,7 @@
         return lax.ppermute(shard, ("loop", "pair"), hops)
 
     to_both = 1 - loop_size % 2
-    early = [exchange(own, (1, 1))] * to_both
+    both = [exchange(own, (1, 1))] * to_both
     middle = [exchange(own, (step, step + 1)) for step in range(1 + to_both, loop_size, 2)]
     in_hbm = pl.BlockSpec(memory_space=pltpu.HBM)
     in_vmem = pl.BlockSpec(memory_space=pltpu.VMEM)
@@ -275,11 +275,11 @@
     middle, best = lax.optimization_barrier((middle, best))
     swap = [(p, p ^ 1) for p in range(2 * loop_size)]
     last = [lax.ppermute(shard, ("loop", "pair"), swap) for shard in middle]
-    new_total, new_weighted = add_shards(total, weighted, middle + early)
+    new_total, new_weighted = add_shards(total, weighted, middle)
     last_inputs = (queries, best, total, weighted, new_total, new_weighted)
-    last_inputs += (*middle, *early, *last)
+    last_inputs += (*middle, *last, *both)
     return pl.pallas_call(
-        functools.partial(last_stage, len(early) + len(middle), len(last)),
+        functools.partial(last_stage, len(middle), len(last) + len(both)),
         name="last_stage",
         out_shape=jax.ShapeDtypeStruct((slots, width), jnp.bfloat16),
         in_specs=[in_vmem] * len(last_inputs),

time: 21.6 us -> 21.2 us (0.981)
  waiting for transfers between devices: 1.69 us -> 1.27 us
    ppermute x2, waiting for transfers between devices: 1.68 us -> 0.9 us  [exchange(): return lax.ppermute(shard, ('loop', 'pair'), hops)]
    pallas_call x1, Pallas kernels: 8.24 us -> 8.92 us  [shards(): pl.pallas_call(functools.partial(last_stage, len(middle), len(last) + len...]
    pallas_call x1, Pallas kernels: 1.64 us -> 0.96 us  [add_shards(): pl.pallas_call(add_stage, name='add_stage', out_shape=[state] * 2, in_spe...]
    ppermute x1, waiting for transfers between devices: 0.01 us -> 0.37 us  [shards(): last = [lax.ppermute(shard, ('loop', 'pair'), swap) for shard in middle]]
  transfers between devices with their start and end apart: 3 -> 3, of which waited for: 2 -> 2; matrix products, arithmetic and copies ran while one was open for 0% -> 0% of each run, Pallas kernels for 28% -> 25%
where the time goes in v9:
time: 21.2 us; the launch traced here: 21.1 us
  Pallas kernels  14.2 us (67%)
  starting transfers between devices  5.62 us (27%)
  waiting for transfers between devices  1.27 us (6%)
    pallas_call x1, Pallas kernels, shards(): pl.pallas_call(functools.partial(last_stage, len(middle), len(last) + len...  8.92 us
    ppermute x2, starting transfers between devices, exchange(): return lax.ppermute(shard, ('loop', 'pair'), hops)  5.61 us
    pallas_call x1, Pallas kernels, shards(): pl.pallas_call(local_stage, name='local_stage', out_shape=[state] * 3 + [...  4.3 us
    pallas_call x1, Pallas kernels, add_shards(): pl.pallas_call(add_stage, name='add_stage', out_shape=[state] * 2, in_spe...  0.96 us
    ppermute x2, waiting for transfers between devices, exchange(): return lax.ppermute(shard, ('loop', 'pair'), hops)  0.9 us
  transfers between devices with their start and end apart: 3, of which 2 were waited for; matrix products, arithmetic and copies ran while one was open for 0% of the time, Pallas kernels for 25%

profile of v9, /device:TPU:0, one launch (start us, length us, event | category | flops | bytes accessed | tf_op | source)
XLA Modules:
  0.0 21.1 jit_solution(13317904566258442307)
XLA Ops:
  0.0 4.0 %collective-permute-start = (bf16[256,256]{1,0:T(8,128)(2,1)}, bf16[256,256]{1,0:T(8,128)(2,1)S(1)}, u32[]{:S(2)}, u32[]{:S(2)}) collective-permute-start(bf16[256,256]{1,0:T(8,128)(2,1)} %bitcast.3), channel_id=1, source_target_pairs={{0,8},{4,12},{8,0},{12,4},{1,13},{5,9},{9,5},{13,1},{2,10},{6,14},... | collective-permute-start | bytes 393224 | tf_op jit(solution)/shard_map/ppermute | solution.py:235
  4.0 1.6 %collective-permute-start.2 = (bf16[256,256]{1,0:T(8,128)(2,1)}, bf16[256,256]{1,0:T(8,128)(2,1)S(1)}, u32[]{:S(2)}, u32[]{:S(2)}) collective-permute-start(bf16[256,256]{1,0:T(8,128)(2,1)} %bitcast.4), channel_id=1, source_target_pairs={{0,4},{4,0},{8,12},{12,8},{1,5},{5,1},{9,13},{13,9},{2,6},{6,2},{1... | collective-permute-start | bytes 393224 | tf_op jit(solution)/shard_map/ppermute | solution.py:235
  5.6 4.3 %local_stage.1 = (f32[640,512]{1,0:T(8,128)S(1)}, f32[640,512]{1,0:T(8,128)S(1)}, f32[640,512]{1,0:T(8,128)S(1)}, bf16[640,512]{1,0:T(8,128)(2,1)S(1)}) custom-call(s32[8]{0:T(128)} %lengths_hbm.1, bf16[640,512]{1,0:T(8,128)(2,1)} %query_hbm.1, bf16[640,256]{1,0:T(8,128)(2,1)} %bitcast.2, bf16[256,256]{1,0:T(8,128)(2,1)} %bitcast.5), custom_call_target="tpu_custom_call" | custom-call | flops 1 | bytes 1 | tf_op jit(solution)/shard_map/local_stage/pallas_call | solution.py:246
  9.9 0.9 %collective-permute-done.refs_4_.refs_6_ = bf16[256,256]{1,0:T(8,128)(2,1)S(1)} collective-permute-done((bf16[256,256]{1,0:T(8,128)(2,1)}, bf16[256,256]{1,0:T(8,128)(2,1)S(1)}, u32[]{:S(2)}, u32[]{:S(2)}) %collective-permute-start) | collective-permute-done | bytes 131104 | tf_op jit(solution)/shard_map/ppermute | solution.py:235
  10.8 0.0 collective-permute-start.1
  10.8 1.0 %add_stage.1 = (f32[640,512]{1,0:T(8,128)S(1)}, f32[640,512]{1,0:T(8,128)S(1)}) custom-call(bf16[640,512]{1,0:T(8,128)(2,1)S(1)} %get-tuple-element.13.refs_0_, f32[640,512]{1,0:T(8,128)S(1)} %get-tuple-element.15.refs_1_, f32[640,512]{1,0:T(8,128)S(1)} %get-tuple-element.16.refs_2_, f32[640,512]{1,0:T(8,128)S(1)} %get-tuple-element.17.refs_3_, ...), custom_call_target="tpu_custom_call" | custom-call | flops 1 | bytes 1 | tf_op jit(solution)/shard_map/add_stage/pallas_call | solution.py:265
  11.8 0.0 collective-permute-done.2.refs_8_
  11.8 0.4 %collective-permute-done.1.refs_7_ = bf16[256,256]{1,0:T(8,128)(2,1)S(1)} collective-permute-done((bf16[256,256]{1,0:T(8,128)(2,1)S(1)}, bf16[256,256]{1,0:T(8,128)(2,1)S(1)}, u32[]{:S(2)}, u32[]{:S(2)}) %collective-permute-start.1) | collective-permute-done | bytes 131104 | tf_op jit(solution)/shard_map/ppermute | solution.py:277
  12.2 8.9 %last_stage.1 = bf16[640,512]{1,0:T(8,128)(2,1)} custom-call(bf16[640,512]{1,0:T(8,128)(2,1)S(1)} %get-tuple-element.13.refs_0_, f32[640,512]{1,0:T(8,128)S(1)} %get-tuple-element.15.refs_1_, f32[640,512]{1,0:T(8,128)S(1)} %get-tuple-element.16.refs_2_, f32[640,512]{1,0:T(8,128)S(1)} %get-tuple-element.17.refs_3_, f32[640,512]{1,0:T(8,128)S(1)} %get-tuple-element.19.refs_4_, ...), custom_call_target="tpu_custom_call" | custom-call | flops 1 | bytes 1 | tf_op jit(solution)/shard_map/last_stage/pallas_call | solution.py:281
Async XLA Ops:
  0.0 10.8 %collective-permute-start = (bf16[256,256]{1,0:T(8,128)(2,1)}, bf16[256,256]{1,0:T(8,128)(2,1)S(1)}, u32[]{:S(2)}, u32[]{:S(2)}) collective-permute-start(bf16[256,256]{1,0:T(8,128)(2,1)} %bitcast.3), channel_id=1, source_target_pairs={{0,8},{4,12},{8,0},{12,4},{1,13},{5,9},{9,5},{13,1},{2,10},{6,14},... | collective-permute-start | bytes 393224 | tf_op jit(solution)/shard_map/ppermute | solution.py:235
  4.0 7.8 %collective-permute-start.2 = (bf16[256,256]{1,0:T(8,128)(2,1)}, bf16[256,256]{1,0:T(8,128)(2,1)S(1)}, u32[]{:S(2)}, u32[]{:S(2)}) collective-permute-start(bf16[256,256]{1,0:T(8,128)(2,1)} %bitcast.4), channel_id=1, source_target_pairs={{0,4},{4,0},{8,12},{12,8},{1,5},{5,1},{9,13},{13,9},{2,6},{6,2},{1... | collective-permute-start | bytes 393224 | tf_op jit(solution)/shard_map/ppermute | solution.py:235
  10.8 1.3 %collective-permute-start.1 = (bf16[256,256]{1,0:T(8,128)(2,1)S(1)}, bf16[256,256]{1,0:T(8,128)(2,1)S(1)}, u32[]{:S(2)}, u32[]{:S(2)}) collective-permute-start(bf16[256,256]{1,0:T(8,128)(2,1)S(1)} %collective-permute-done.refs_4_.refs_6_), channel_id=1, source_target_pairs={{0,1},{1,0},{4,5},{5,4},{8,9},{9,8},{12,13},{13,12},{2,3},{3,2},{6... | collective-permute-start | bytes 393224 | tf_op jit(solution)/shard_map/ppermute | solution.py:277

commit v10 on v9

--- a/solution.py
+++ b/solution.py
@@ -83,8 +83,6 @@
     for copy in whole + pieces:
         copy.wait()
     position = lax.axis_index("loop")
-    own_keys = own_ref[:, :HD]
-    own_values = with_ones(own_ref[:, HD:])
     window = BLK * ((MAXLEN + BLK - 2) // BLK) + BLK
     for block in range(blocks):
         stop = (block + 1) * BLK
@@ -99,24 +97,16 @@
             first = jnp.where(row_at >= agent_end, agent_end, first)
         allowed = (key_at <= row_at) & (key_at >= first)
         queries = stacked(query_ref, rows, heads)
-        own_scores = scores_of(queries, own_keys)
+        shard = jnp.concatenate([own_ref[...], suffix_ref[start:stop]], axis=0)
+        scores = scores_of(queries, shard[:, :HD])
+        own_scores = scores[:, : own_ref.shape[0]]
         suffix_scores = jnp.where(
-            jnp.concatenate([allowed] * heads, axis=0),
-            scores_of(queries, suffix_ref[start:stop, :HD]),
-            masked_score,
-        )
-        best = jnp.maximum(
-            jnp.max(own_scores, axis=1, keepdims=True),
-            jnp.max(suffix_scores, axis=1, keepdims=True),
-        )
-        own_weights = jnp.exp2(own_scores - best).astype(jnp.bfloat16)
-        suffix_weights = jnp.exp2(suffix_scores - best).astype(jnp.bfloat16)
-        result = jnp.dot(own_weights, own_values, preferred_element_type=jnp.float32)
-        result = result + jnp.dot(
-            suffix_weights,
-            with_ones(suffix_ref[start:stop, HD:]),
-            preferred_element_type=jnp.float32,
-        )
+            jnp.concatenate([allowed] * heads, axis=0), scores[:, own_ref.shape[0] :], masked_score
+        )
+        scores = jnp.concatenate([own_scores, suffix_scores], axis=1)
+        best = jnp.max(scores, axis=1, keepdims=True)
+        weights = jnp.exp2(scores - best).astype(jnp.bfloat16)
+        result = jnp.dot(weights, with_ones(shard[:, HD:]), preferred_element_type=jnp.float32)
         row_at = block * BLK + lax.broadcasted_iota(jnp.int32, (BLK, HD), 0)
         live = jnp.concatenate([row_at < agent_end] * heads, axis=0)
         unstack(best_ref, rows, heads, jnp.where(live, best, empty_best))
@@ -131,8 +121,8 @@
     return total + result[:, HD:], weighted + result[:, :HD]
 
 
-def row_blocks(count):
-    step = next(size for size in (160, 128, count) if count % size == 0)
+def row_blocks(count, largest):
+    step = next(size for size in (largest, 128, 16, count) if count % size == 0)
     return [slice(first, first + step) for first in range(0, count, step)]
 
 
@@ -142,7 +132,7 @@
     total_out, sum_out = refs[-2:]
     heads = query_ref.shape[1] // HD
     shards_here = [(ref[:, :HD], with_ones(ref[:, HD:])) for ref in shard_refs]
-    for rows in row_blocks(query_ref.shape[0]):
+    for rows in row_blocks(query_ref.shape[0], 80):
         queries = stacked(query_ref, rows, heads)
         best = stacked(best_ref, rows, heads)
         total = stacked(total_ref, rows, heads)
@@ -159,10 +149,7 @@
     last_refs = refs[6 + earlier_count : 6 + earlier_count + last_count]
     out_hbm, out_ref, out_sems = refs[6 + earlier_count + last_count :]
     heads = query_ref.shape[1] // HD
-    blocks = row_blocks(query_ref.shape[0])
-
-    def load(shard_refs):
-        return [(ref[:, :HD], with_ones(ref[:, HD:])) for ref in shard_refs]
+    blocks = row_blocks(query_ref.shape[0], 160)
 
     def out_copy(index, rows):
         return pltpu.make_async_copy(out_ref.at[rows], out_hbm.at[rows], out_sems.at[index])
@@ -171,14 +158,14 @@
         unstack(out_ref, rows, heads, (weighted / total).astype(jnp.bfloat16))
 
     trusted = jnp.full((8, HD), True)
-    shards_here = load(last_refs)
+    shard = jnp.concatenate([ref[...] for ref in last_refs], axis=0)
+    key_rows, value_rows = shard[:, :HD], with_ones(shard[:, HD:])
     for index, rows in enumerate(blocks):
         queries = stacked(query_ref, rows, heads)
         best = stacked(best_ref, rows, heads)
         total = stacked(total_ref, rows, heads)
         weighted = stacked(sum_ref, rows, heads)
-        for key_rows, value_rows in shards_here:
-            total, weighted = add_shard(queries, best, key_rows, value_rows, total, weighted)
+        total, weighted = add_shard(queries, best, key_rows, value_rows, total, weighted)
         good = (total < total_limit).reshape(total.shape[0] // 8, 8, HD)
         trusted = trusted & jnp.all(good, axis=0)
         finish(rows, total, weighted)
@@ -196,7 +183,8 @@
             best = stacked(best_ref, rows, heads)
             weighted = stacked(old_sum_ref, rows, heads)
             total = stacked(old_total_ref, rows, heads)
-            for key_rows, value_rows in load(earlier_refs + last_refs):
+            for shard_ref in earlier_refs + last_refs:
+                key_rows, value_rows = shard_ref[:, :HD], with_ones(shard_ref[:, HD:])
                 scores = scores_of(queries, key_rows)
                 new_best = jnp.maximum(best, jnp.max(scores, axis=1, keepdims=True))
                 factor = jnp.exp2(best - new_best)
@@ -286,7 +274,7 @@
         out_specs=in_hbm,
         scratch_shapes=[
             pltpu.VMEM((slots, width), jnp.bfloat16),
-            pltpu.SemaphoreType.DMA((len(row_blocks(slots)),)),
+            pltpu.SemaphoreType.DMA((len(row_blocks(slots, 160)),)),
         ],
         compiler_params=pltpu.CompilerParams(vmem_limit_bytes=32 * 2**20),
         cost_estimate=cost,

time: 21.2 us -> 21.2 us (level)
  no operation moved by 1% of the time
where the time goes in v10:
time: 21.2 us; the launch traced here: 21.1 us
  Pallas kernels  14.2 us (67%)
  starting transfers between devices  5.62 us (27%)
  waiting for transfers between devices  1.26 us (6%)
    pallas_call x1, Pallas kernels, shards(): pl.pallas_call(functools.partial(last_stage, len(middle), len(last) + len...  8.92 us
    ppermute x2, starting transfers between devices, exchange(): return lax.ppermute(shard, ('loop', 'pair'), hops)  5.61 us
    pallas_call x1, Pallas kernels, shards(): pl.pallas_call(local_stage, name='local_stage', out_shape=[state] * 3 + [...  4.31 us
    pallas_call x1, Pallas kernels, add_shards(): pl.pallas_call(add_stage, name='add_stage', out_shape=[state] * 2, in_spe...  0.96 us
    ppermute x2, waiting for transfers between devices, exchange(): return lax.ppermute(shard, ('loop', 'pair'), hops)  0.89 us
  transfers between devices with their start and end apart: 3, of which 2 were waited for; matrix products, arithmetic and copies ran while one was open for 0% of the time, Pallas kernels for 25%

profile of v10, /device:TPU:0, one launch (start us, length us, event | category | flops | bytes accessed | tf_op | source)
XLA Modules:
  0.0 21.1 jit_solution(7460170183061851695)
XLA Ops:
  0.0 4.0 %collective-permute-start = (bf16[256,256]{1,0:T(8,128)(2,1)}, bf16[256,256]{1,0:T(8,128)(2,1)S(1)}, u32[]{:S(2)}, u32[]{:S(2)}) collective-permute-start(bf16[256,256]{1,0:T(8,128)(2,1)} %bitcast.3), channel_id=1, source_target_pairs={{0,8},{4,12},{8,0},{12,4},{1,13},{5,9},{9,5},{13,1},{2,10},{6,14},... | collective-permute-start | bytes 393224 | tf_op jit(solution)/shard_map/ppermute | solution.py:223
  4.0 1.6 %collective-permute-start.2 = (bf16[256,256]{1,0:T(8,128)(2,1)}, bf16[256,256]{1,0:T(8,128)(2,1)S(1)}, u32[]{:S(2)}, u32[]{:S(2)}) collective-permute-start(bf16[256,256]{1,0:T(8,128)(2,1)} %bitcast.4), channel_id=1, source_target_pairs={{0,4},{4,0},{8,12},{12,8},{1,5},{5,1},{9,13},{13,9},{2,6},{6,2},{1... | collective-permute-start | bytes 393224 | tf_op jit(solution)/shard_map/ppermute | solution.py:223
  5.6 4.3 %local_stage.1 = (f32[640,512]{1,0:T(8,128)S(1)}, f32[640,512]{1,0:T(8,128)S(1)}, f32[640,512]{1,0:T(8,128)S(1)}, bf16[640,512]{1,0:T(8,128)(2,1)S(1)}) custom-call(s32[8]{0:T(128)} %lengths_hbm.1, bf16[640,512]{1,0:T(8,128)(2,1)} %query_hbm.1, bf16[640,256]{1,0:T(8,128)(2,1)} %bitcast.2, bf16[256,256]{1,0:T(8,128)(2,1)} %bitcast.5), custom_call_target="tpu_custom_call" | custom-call | flops 1 | bytes 1 | tf_op jit(solution)/shard_map/local_stage/pallas_call | solution.py:234
  9.9 0.9 %collective-permute-done.refs_4_.refs_6_ = bf16[256,256]{1,0:T(8,128)(2,1)S(1)} collective-permute-done((bf16[256,256]{1,0:T(8,128)(2,1)}, bf16[256,256]{1,0:T(8,128)(2,1)S(1)}, u32[]{:S(2)}, u32[]{:S(2)}) %collective-permute-start) | collective-permute-done | bytes 131104 | tf_op jit(solution)/shard_map/ppermute | solution.py:223
  10.8 0.0 collective-permute-start.1
  10.8 1.0 %add_stage.1 = (f32[640,512]{1,0:T(8,128)S(1)}, f32[640,512]{1,0:T(8,128)S(1)}) custom-call(bf16[640,512]{1,0:T(8,128)(2,1)S(1)} %get-tuple-element.13.refs_0_, f32[640,512]{1,0:T(8,128)S(1)} %get-tuple-element.15.refs_1_, f32[640,512]{1,0:T(8,128)S(1)} %get-tuple-element.16.refs_2_, f32[640,512]{1,0:T(8,128)S(1)} %get-tuple-element.17.refs_3_, ...), custom_call_target="tpu_custom_call" | custom-call | flops 1 | bytes 1 | tf_op jit(solution)/shard_map/add_stage/pallas_call | solution.py:253
  11.8 0.0 collective-permute-done.2.refs_8_
  11.8 0.4 %collective-permute-done.1.refs_7_ = bf16[256,256]{1,0:T(8,128)(2,1)S(1)} collective-permute-done((bf16[256,256]{1,0:T(8,128)(2,1)S(1)}, bf16[256,256]{1,0:T(8,128)(2,1)S(1)}, u32[]{:S(2)}, u32[]{:S(2)}) %collective-permute-start.1) | collective-permute-done | bytes 131104 | tf_op jit(solution)/shard_map/ppermute | solution.py:265
  12.2 8.9 %last_stage.1 = bf16[640,512]{1,0:T(8,128)(2,1)} custom-call(bf16[640,512]{1,0:T(8,128)(2,1)S(1)} %get-tuple-element.13.refs_0_, f32[640,512]{1,0:T(8,128)S(1)} %get-tuple-element.15.refs_1_, f32[640,512]{1,0:T(8,128)S(1)} %get-tuple-element.16.refs_2_, f32[640,512]{1,0:T(8,128)S(1)} %get-tuple-element.17.refs_3_, f32[640,512]{1,0:T(8,128)S(1)} %get-tuple-element.19.refs_4_, ...), custom_call_target="tpu_custom_call" | custom-call | flops 1 | bytes 1 | tf_op jit(solution)/shard_map/last_stage/pallas_call | solution.py:269
Async XLA Ops:
  0.0 10.8 %collective-permute-start = (bf16[256,256]{1,0:T(8,128)(2,1)}, bf16[256,256]{1,0:T(8,128)(2,1)S(1)}, u32[]{:S(2)}, u32[]{:S(2)}) collective-permute-start(bf16[256,256]{1,0:T(8,128)(2,1)} %bitcast.3), channel_id=1, source_target_pairs={{0,8},{4,12},{8,0},{12,4},{1,13},{5,9},{9,5},{13,1},{2,10},{6,14},... | collective-permute-start | bytes 393224 | tf_op jit(solution)/shard_map/ppermute | solution.py:223
  4.0 7.8 %collective-permute-start.2 = (bf16[256,256]{1,0:T(8,128)(2,1)}, bf16[256,256]{1,0:T(8,128)(2,1)S(1)}, u32[]{:S(2)}, u32[]{:S(2)}) collective-permute-start(bf16[256,256]{1,0:T(8,128)(2,1)} %bitcast.4), channel_id=1, source_target_pairs={{0,4},{4,0},{8,12},{12,8},{1,5},{5,1},{9,13},{13,9},{2,6},{6,2},{1... | collective-permute-start | bytes 393224 | tf_op jit(solution)/shard_map/ppermute | solution.py:223
  10.8 1.3 %collective-permute-start.1 = (bf16[256,256]{1,0:T(8,128)(2,1)S(1)}, bf16[256,256]{1,0:T(8,128)(2,1)S(1)}, u32[]{:S(2)}, u32[]{:S(2)}) collective-permute-start(bf16[256,256]{1,0:T(8,128)(2,1)S(1)} %collective-permute-done.refs_4_.refs_6_), channel_id=1, source_target_pairs={{0,1},{1,0},{4,5},{5,4},{8,9},{9,8},{12,13},{13,12},{2,3},{3,2},{6... | collective-permute-start | bytes 393224 | tf_op jit(solution)/shard_map/ppermute | solution.py:265

commit v11 on v10

--- a/solution.py
+++ b/solution.py
@@ -55,6 +55,7 @@
     total_ref,
     sum_ref,
     query_ref,
+    wide_ref,
     lengths_ref,
     suffix_ref,
     own_ref,
@@ -104,12 +105,19 @@
             jnp.concatenate([allowed] * heads, axis=0), scores[:, own_ref.shape[0] :], masked_score
         )
         scores = jnp.concatenate([own_scores, suffix_scores], axis=1)
-        best = jnp.max(scores, axis=1, keepdims=True)
-        weights = jnp.exp2(scores - best).astype(jnp.bfloat16)
+        best = jnp.max(scores, axis=1, keepdims=True) / score_scale
+        best = best.astype(jnp.bfloat16).astype(jnp.float32)
+        weights = jnp.exp2(scores - best * score_scale).astype(jnp.bfloat16)
         result = jnp.dot(weights, with_ones(shard[:, HD:]), preferred_element_type=jnp.float32)
         row_at = block * BLK + lax.broadcasted_iota(jnp.int32, (BLK, HD), 0)
         live = jnp.concatenate([row_at < agent_end] * heads, axis=0)
-        unstack(best_ref, rows, heads, jnp.where(live, best, empty_best))
+        best = jnp.where(live, best, empty_best)
+        unstack(best_ref, rows, heads, best * score_scale)
+        lane = lax.broadcasted_iota(jnp.int32, best.shape, 1)
+        point = jnp.where(lane == 0, -best, 0.0).astype(jnp.bfloat16)
+        for h in range(heads):
+            wide_ref[rows, 2 * h * HD : (2 * h + 1) * HD] = queries[h * BLK : (h + 1) * BLK]
+            wide_ref[rows, (2 * h + 1) * HD : (2 * h + 2) * HD] = point[h * BLK : (h + 1) * BLK]
         unstack(sum_ref, rows, heads, jnp.where(live, result[:, :HD], 0.0))
         unstack(total_ref, rows, heads, jnp.where(live, result[:, HD:], 1.0))
 
@@ -127,20 +135,20 @@
 
 
 def add_stage(*refs):
-    query_ref, best_ref, total_ref, sum_ref = refs[:4]
-    shard_refs = refs[4:-2]
+    wide_ref, total_ref, sum_ref = refs[:3]
+    shard_refs = refs[3:-2]
     total_out, sum_out = refs[-2:]
-    heads = query_ref.shape[1] // HD
-    shards_here = [(ref[:, :HD], with_ones(ref[:, HD:])) for ref in shard_refs]
-    for rows in row_blocks(query_ref.shape[0], 80):
-        queries = stacked(query_ref, rows, heads)
-        best = stacked(best_ref, rows, heads)
-        total = stacked(total_ref, rows, heads)
-        weighted = stacked(sum_ref, rows, heads)
-        for key_rows, value_rows in shards_here:
-            total, weighted = add_shard(queries, best, key_rows, value_rows, total, weighted)
-        unstack(total_out, rows, heads, total)
-        unstack(sum_out, rows, heads, weighted)
+    heads = sum_ref.shape[1] // HD
+    shard = jnp.concatenate([ref[...] for ref in shard_refs], axis=0)
+    key_rows, value_rows = with_ones(shard[:, :HD]), with_ones(shard[:, HD:])
+    for rows in row_blocks(wide_ref.shape[0], 160):
+        queries = jnp.concatenate(
+            [wide_ref[rows, 2 * h * HD : (2 * h + 2) * HD] for h in range(heads)], axis=0
+        )
+        weights = jnp.exp2(scores_of(queries, key_rows)).astype(jnp.bfloat16)
+        result = jnp.dot(weights, value_rows, preferred_element_type=jnp.float32)
+        unstack(total_out, rows, heads, stacked(total_ref, rows, heads) + result[:, HD:])
+        unstack(sum_out, rows, heads, stacked(sum_ref, rows, heads) + result[:, :HD])
 
 
 def last_stage(earlier_count, last_count, *refs):
@@ -231,12 +239,16 @@
 
     cost = pl.CostEstimate(flops=1, bytes_accessed=1, transcendentals=0)
 
-    best, total, weighted, queries = pl.pallas_call(
+    best, total, weighted, queries, wide = pl.pallas_call(
         local_stage,
         name="local_stage",
-        out_shape=[state] * 3 + [jax.ShapeDtypeStruct((slots, width), queries.dtype)],
+        out_shape=[state] * 3
+        + [
+            jax.ShapeDtypeStruct((slots, width), queries.dtype),
+            jax.ShapeDtypeStruct((slots, 2 * width), queries.dtype),
+        ],
         in_specs=[in_hbm] * 4,
-        out_specs=[in_vmem] * 4,
+        out_specs=[in_vmem] * 5,
         scratch_shapes=[
             pltpu.SMEM(lengths.shape, lengths.dtype),
             pltpu.VMEM(suffix.shape, suffix.dtype),
@@ -254,11 +266,11 @@
             add_stage,
             name="add_stage",
             out_shape=[state] * 2,
-            in_specs=[in_vmem] * (4 + len(shards_now)),
+            in_specs=[in_vmem] * (3 + len(shards_now)),
             out_specs=[in_vmem] * 2,
             compiler_params=pltpu.CompilerParams(vmem_limit_bytes=24 * 2**20),
             cost_estimate=cost,
-        )(queries, best, total, weighted, *shards_now)
+        )(wide, total, weighted, *shards_now)
 
     middle, best = lax.optimization_barrier((middle, best))
     swap = [(p, p ^ 1) for p in range(2 * loop_size)]

time: 21.2 us -> 21.2 us (level)
  Pallas kernels: 14.2 us -> 14.6 us
  waiting for transfers between devices: 1.26 us -> 0.88 us
    pallas_call x1, Pallas kernels: 4.31 us -> 4.54 us  [shards(): pl.pallas_call(local_stage, name='local_stage', out_shape=[state] * 3 + [...]
    ppermute x2, waiting for transfers between devices: 0.89 us -> 0.67 us  [exchange(): return lax.ppermute(shard, ('loop', 'pair'), hops)]
  transfers between devices with their start and end apart: 3 -> 3, of which waited for: 2 -> 2; matrix products, arithmetic and copies ran while one was open for 0% -> 0% of each run, Pallas kernels for 25% -> 27%
where the time goes in v11:
time: 21.2 us; the launch traced here: 21.1 us
  Pallas kernels  14.6 us (69%)
  starting transfers between devices  5.62 us (27%)
  waiting for transfers between devices  0.88 us (4%)
    pallas_call x1, Pallas kernels, shards(): pl.pallas_call(functools.partial(last_stage, len(middle), len(last) + len...  8.92 us
    ppermute x2, starting transfers between devices, exchange(): return lax.ppermute(shard, ('loop', 'pair'), hops)  5.61 us
    pallas_call x1, Pallas kernels, shards(): pl.pallas_call(local_stage, name='local_stage', out_shape=[state] * 3 + [...  4.54 us
    pallas_call x1, Pallas kernels, add_shards(): pl.pallas_call(add_stage, name='add_stage', out_shape=[state] * 2, in_spe...  1.11 us
    ppermute x2, waiting for transfers between devices, exchange(): return lax.ppermute(shard, ('loop', 'pair'), hops)  0.67 us
  transfers between devices with their start and end apart: 3, of which 2 were waited for; matrix products, arithmetic and copies ran while one was open for 0% of the time, Pallas kernels for 27%

profile of v11, /device:TPU:0, one launch (start us, length us, event | category | flops | bytes accessed | tf_op | source)
XLA Modules:
  0.0 21.1 jit_solution(7345200230728594843)
XLA Ops:
  0.0 4.0 %collective-permute-start = (bf16[256,256]{1,0:T(8,128)(2,1)}, bf16[256,256]{1,0:T(8,128)(2,1)S(1)}, u32[]{:S(2)}, u32[]{:S(2)}) collective-permute-start(bf16[256,256]{1,0:T(8,128)(2,1)} %bitcast.3), channel_id=1, source_target_pairs={{0,8},{4,12},{8,0},{12,4},{1,13},{5,9},{9,5},{13,1},{2,10},{6,14},... | collective-permute-start | bytes 393224 | tf_op jit(solution)/shard_map/ppermute | solution.py:231
  4.0 1.6 %collective-permute-start.2 = (bf16[256,256]{1,0:T(8,128)(2,1)}, bf16[256,256]{1,0:T(8,128)(2,1)S(1)}, u32[]{:S(2)}, u32[]{:S(2)}) collective-permute-start(bf16[256,256]{1,0:T(8,128)(2,1)} %bitcast.4), channel_id=1, source_target_pairs={{0,4},{4,0},{8,12},{12,8},{1,5},{5,1},{9,13},{13,9},{2,6},{6,2},{1... | collective-permute-start | bytes 393224 | tf_op jit(solution)/shard_map/ppermute | solution.py:231
  5.6 4.5 %local_stage.1 = (f32[640,512]{1,0:T(8,128)S(1)}, f32[640,512]{1,0:T(8,128)S(1)}, f32[640,512]{1,0:T(8,128)S(1)}, bf16[640,512]{1,0:T(8,128)(2,1)S(1)}, bf16[640,1024]{1,0:T(8,128)(2,1)S(1)}) custom-call(s32[8]{0:T(128)} %lengths_hbm.1, bf16[640,512]{1,0:T(8,128)(2,1)} %query_hbm.1, bf16[640,256]{1,0:T(8,128)(2,1)} %bitcast.2, bf16[256,256]{1,0:T(8,128)(2,1)} %bitcast.5), custom_call_target="tpu_custom_call" | custom-call | flops 1 | bytes 1 | tf_op jit(solution)/shard_map/local_stage/pallas_call | solution.py:242
  10.2 0.7 %collective-permute-done.refs_3_.refs_6_ = bf16[256,256]{1,0:T(8,128)(2,1)S(1)} collective-permute-done((bf16[256,256]{1,0:T(8,128)(2,1)}, bf16[256,256]{1,0:T(8,128)(2,1)S(1)}, u32[]{:S(2)}, u32[]{:S(2)}) %collective-permute-start) | collective-permute-done | bytes 131104 | tf_op jit(solution)/shard_map/ppermute | solution.py:231
  10.8 0.0 collective-permute-start.1
  10.8 1.1 %add_stage.1 = (f32[640,512]{1,0:T(8,128)S(1)}, f32[640,512]{1,0:T(8,128)S(1)}) custom-call(bf16[640,1024]{1,0:T(8,128)(2,1)S(1)} %get-tuple-element.19.refs_0_, f32[640,512]{1,0:T(8,128)S(1)} %get-tuple-element.17.refs_1_.refs_2_, f32[640,512]{1,0:T(8,128)S(1)} %get-tuple-element.18.refs_2_.refs_3_, bf16[256,256]{1,0:T(8,128)(2,1)S(1)} %collective-permute-done.refs_3_.refs_6_), custom_call_target="tpu_custom_call" | custom-call | flops 1 | bytes 1 | tf_op jit(solution)/shard_map/add_stage/pallas_call | solution.py:265
  11.9 0.0 collective-permute-done.2.refs_8_
  12.0 0.2 %collective-permute-done.1.refs_7_ = bf16[256,256]{1,0:T(8,128)(2,1)S(1)} collective-permute-done((bf16[256,256]{1,0:T(8,128)(2,1)S(1)}, bf16[256,256]{1,0:T(8,128)(2,1)S(1)}, u32[]{:S(2)}, u32[]{:S(2)}) %collective-permute-start.1) | collective-permute-done | bytes 131104 | tf_op jit(solution)/shard_map/ppermute | solution.py:277
  12.2 8.9 %last_stage.1 = bf16[640,512]{1,0:T(8,128)(2,1)} custom-call(bf16[640,512]{1,0:T(8,128)(2,1)S(1)} %get-tuple-element.14.refs_0_, f32[640,512]{1,0:T(8,128)S(1)} %get-tuple-element.16.refs_1_, f32[640,512]{1,0:T(8,128)S(1)} %get-tuple-element.17.refs_1_.refs_2_, f32[640,512]{1,0:T(8,128)S(1)} %get-tuple-element.18.refs_2_.refs_3_, ...), custom_call_target="tpu_custom_call" | custom-call | flops 1 | bytes 1 | tf_op jit(solution)/shard_map/last_stage/pallas_call | solution.py:281
Async XLA Ops:
  0.0 10.8 %collective-permute-start = (bf16[256,256]{1,0:T(8,128)(2,1)}, bf16[256,256]{1,0:T(8,128)(2,1)S(1)}, u32[]{:S(2)}, u32[]{:S(2)}) collective-permute-start(bf16[256,256]{1,0:T(8,128)(2,1)} %bitcast.3), channel_id=1, source_target_pairs={{0,8},{4,12},{8,0},{12,4},{1,13},{5,9},{9,5},{13,1},{2,10},{6,14},... | collective-permute-start | bytes 393224 | tf_op jit(solution)/shard_map/ppermute | solution.py:231
  4.0 7.9 %collective-permute-start.2 = (bf16[256,256]{1,0:T(8,128)(2,1)}, bf16[256,256]{1,0:T(8,128)(2,1)S(1)}, u32[]{:S(2)}, u32[]{:S(2)}) collective-permute-start(bf16[256,256]{1,0:T(8,128)(2,1)} %bitcast.4), channel_id=1, source_target_pairs={{0,4},{4,0},{8,12},{12,8},{1,5},{5,1},{9,13},{13,9},{2,6},{6,2},{1... | collective-permute-start | bytes 393224 | tf_op jit(solution)/shard_map/ppermute | solution.py:231
  10.8 1.3 %collective-permute-start.1 = (bf16[256,256]{1,0:T(8,128)(2,1)S(1)}, bf16[256,256]{1,0:T(8,128)(2,1)S(1)}, u32[]{:S(2)}, u32[]{:S(2)}) collective-permute-start(bf16[256,256]{1,0:T(8,128)(2,1)S(1)} %collective-permute-done.refs_3_.refs_6_), channel_id=1, source_target_pairs={{0,1},{1,0},{4,5},{5,4},{8,9},{9,8},{12,13},{13,12},{2,3},{3,2},{6... | collective-permute-start | bytes 393224 | tf_op jit(solution)/shard_map/ppermute | solution.py:277

commit v12 on v10

--- a/solution.py
+++ b/solution.py
@@ -114,11 +114,13 @@
         unstack(total_ref, rows, heads, jnp.where(live, result[:, HD:], 1.0))
 
 
-def add_shard(queries, best, key_rows, value_rows, total, weighted):
-    scores = scores_of(queries, key_rows)
-    weights = jnp.exp2(scores - widen(best, scores.shape[1])).astype(jnp.bfloat16)
-    result = jnp.dot(weights, value_rows, preferred_element_type=jnp.float32)
-    return total + result[:, HD:], weighted + result[:, :HD]
+def staged(blocks, start, finish):
+    coming = start(blocks[0])
+    for index, rows in enumerate(blocks):
+        now = coming
+        if index + 1 < len(blocks):
+            coming = start(blocks[index + 1])
+        finish(index, rows, now)
 
 
 def row_blocks(count, largest):
@@ -131,16 +133,20 @@
     shard_refs = refs[4:-2]
     total_out, sum_out = refs[-2:]
     heads = query_ref.shape[1] // HD
-    shards_here = [(ref[:, :HD], with_ones(ref[:, HD:])) for ref in shard_refs]
-    for rows in row_blocks(query_ref.shape[0], 80):
-        queries = stacked(query_ref, rows, heads)
+    shard = jnp.concatenate([ref[...] for ref in shard_refs], axis=0)
+    key_rows, value_rows = shard[:, :HD], with_ones(shard[:, HD:])
+
+    def start(rows):
+        return scores_of(stacked(query_ref, rows, heads), key_rows)
+
+    def finish(index, rows, scores):
         best = stacked(best_ref, rows, heads)
-        total = stacked(total_ref, rows, heads)
-        weighted = stacked(sum_ref, rows, heads)
-        for key_rows, value_rows in shards_here:
-            total, weighted = add_shard(queries, best, key_rows, value_rows, total, weighted)
-        unstack(total_out, rows, heads, total)
-        unstack(sum_out, rows, heads, weighted)
+        weights = jnp.exp2(scores - widen(best, scores.shape[1])).astype(jnp.bfloat16)
+        result = jnp.dot(weights, value_rows, preferred_element_type=jnp.float32)
+        unstack(total_out, rows, heads, stacked(total_ref, rows, heads) + result[:, HD:])
+        unstack(sum_out, rows, heads, stacked(sum_ref, rows, heads) + result[:, :HD])
+
+    staged(row_blocks(query_ref.shape[0], 80), start, finish)
 
 
 def last_stage(earlier_count, last_count, *refs):
@@ -149,31 +155,38 @@
     last_refs = refs[6 + earlier_count : 6 + earlier_count + last_count]
     out_hbm, out_ref, out_sems = refs[6 + earlier_count + last_count :]
     heads = query_ref.shape[1] // HD
-    blocks = row_blocks(query_ref.shape[0], 160)
+    blocks = row_blocks(query_ref.shape[0], 80)
 
     def out_copy(index, rows):
         return pltpu.make_async_copy(out_ref.at[rows], out_hbm.at[rows], out_sems.at[index])
 
-    def finish(rows, total, weighted):
+    def write(rows, total, weighted):
         unstack(out_ref, rows, heads, (weighted / total).astype(jnp.bfloat16))
 
-    trusted = jnp.full((8, HD), True)
     shard = jnp.concatenate([ref[...] for ref in last_refs], axis=0)
-    key_rows, value_rows = shard[:, :HD], with_ones(shard[:, HD:])
-    for index, rows in enumerate(blocks):
-        queries = stacked(query_ref, rows, heads)
+    trusted = [jnp.full((8, HD), True)]
+
+    def start(rows):
+        return scores_of(stacked(query_ref, rows, heads), shard[:, :HD])
+
+    def finish(index, rows, scores):
         best = stacked(best_ref, rows, heads)
-        total = stacked(total_ref, rows, heads)
-        weighted = stacked(sum_ref, rows, heads)
-        total, weighted = add_shard(queries, best, key_rows, value_rows, total, weighted)
+        weights = jnp.exp2(scores - widen(best, scores.shape[1]))
+        lanes = sum(weights[:, i : i + HD] for i in range(0, scores.shape[1], HD))
+        total = stacked(total_ref, rows, heads) + jnp.sum(lanes, axis=1, keepdims=True)
+        weighted = stacked(sum_ref, rows, heads) + jnp.dot(
+            weights.astype(jnp.bfloat16), shard[:, HD:], preferred_element_type=jnp.float32
+        )
         good = (total < total_limit).reshape(total.shape[0] // 8, 8, HD)
-        trusted = trusted & jnp.all(good, axis=0)
-        finish(rows, total, weighted)
+        trusted[0] = trusted[0] & jnp.all(good, axis=0)
+        write(rows, total, weighted)
         out_copy(index, rows).start()
+
+    staged(blocks, start, finish)
     for index, rows in enumerate(blocks):
         out_copy(index, rows).wait()
 
-    @pl.when(jnp.logical_not(jnp.all(trusted)))
+    @pl.when(jnp.logical_not(jnp.all(trusted[0])))
     def exact_maximum():
         size = query_ref.shape[0] // len(blocks)
 
@@ -195,7 +208,7 @@
                 weighted = weighted * factor + result[:, :HD]
                 total = total * factor + result[:, HD:]
                 best = new_best
-            finish(rows, total, weighted)
+            write(rows, total, weighted)
             copy = out_copy(index, rows)
             copy.start()
             copy.wait()
@@ -274,7 +287,7 @@
         out_specs=in_hbm,
         scratch_shapes=[
             pltpu.VMEM((slots, width), jnp.bfloat16),
-            pltpu.SemaphoreType.DMA((len(row_blocks(slots, 160)),)),
+            pltpu.SemaphoreType.DMA((len(row_blocks(slots, 80)),)),
         ],
         compiler_params=pltpu.CompilerParams(vmem_limit_bytes=32 * 2**20),
         cost_estimate=cost,

time: 21.2 us -> 24.8 us (1.17)
  Pallas kernels: 14.2 us -> 17.7 us
    pallas_call x1, Pallas kernels: 8.92 us -> 12.5 us  [shards(): pl.pallas_call(functools.partial(last_stage, len(middle), len(last) + len...]
  transfers between devices with their start and end apart: 3 -> 3, of which waited for: 2 -> 2; matrix products, arithmetic and copies ran while one was open for 0% -> 0% of each run, Pallas kernels for 25% -> 21%
where the time goes in v12:
time: 24.8 us; the launch traced here: 24.7 us
  Pallas kernels  17.7 us (71%)
  starting transfers between devices  5.62 us (23%)
  waiting for transfers between devices  1.32 us (5%)
    pallas_call x1, Pallas kernels, shards(): pl.pallas_call(functools.partial(last_stage, len(middle), len(last) + len...  12.5 us
    ppermute x2, starting transfers between devices, exchange(): return lax.ppermute(shard, ('loop', 'pair'), hops)  5.61 us
    pallas_call x1, Pallas kernels, shards(): pl.pallas_call(local_stage, name='local_stage', out_shape=[state] * 3 + [...  4.31 us
    pallas_call x1, Pallas kernels, add_shards(): pl.pallas_call(add_stage, name='add_stage', out_shape=[state] * 2, in_spe...  0.9 us
    ppermute x2, waiting for transfers between devices, exchange(): return lax.ppermute(shard, ('loop', 'pair'), hops)  0.89 us
  transfers between devices with their start and end apart: 3, of which 2 were waited for; matrix products, arithmetic and copies ran while one was open for 0% of the time, Pallas kernels for 21%

profile of v12, /device:TPU:0, one launch (start us, length us, event | category | flops | bytes accessed | tf_op | source)
XLA Modules:
  0.0 24.7 jit_solution(234993055129347590)
XLA Ops:
  0.0 4.0 %collective-permute-start = (bf16[256,256]{1,0:T(8,128)(2,1)}, bf16[256,256]{1,0:T(8,128)(2,1)S(1)}, u32[]{:S(2)}, u32[]{:S(2)}) collective-permute-start(bf16[256,256]{1,0:T(8,128)(2,1)} %bitcast.3), channel_id=1, source_target_pairs={{0,8},{4,12},{8,0},{12,4},{1,13},{5,9},{9,5},{13,1},{2,10},{6,14},... | collective-permute-start | bytes 393224 | tf_op jit(solution)/shard_map/ppermute | solution.py:236
  4.0 1.6 %collective-permute-start.2 = (bf16[256,256]{1,0:T(8,128)(2,1)}, bf16[256,256]{1,0:T(8,128)(2,1)S(1)}, u32[]{:S(2)}, u32[]{:S(2)}) collective-permute-start(bf16[256,256]{1,0:T(8,128)(2,1)} %bitcast.4), channel_id=1, source_target_pairs={{0,4},{4,0},{8,12},{12,8},{1,5},{5,1},{9,13},{13,9},{2,6},{6,2},{1... | collective-permute-start | bytes 393224 | tf_op jit(solution)/shard_map/ppermute | solution.py:236
  5.6 4.3 %local_stage.1 = (f32[640,512]{1,0:T(8,128)S(1)}, f32[640,512]{1,0:T(8,128)S(1)}, f32[640,512]{1,0:T(8,128)S(1)}, bf16[640,512]{1,0:T(8,128)(2,1)S(1)}) custom-call(s32[8]{0:T(128)} %lengths_hbm.1, bf16[640,512]{1,0:T(8,128)(2,1)} %query_hbm.1, bf16[640,256]{1,0:T(8,128)(2,1)} %bitcast.2, bf16[256,256]{1,0:T(8,128)(2,1)} %bitcast.5), custom_call_target="tpu_custom_call" | custom-call | flops 1 | bytes 1 | tf_op jit(solution)/shard_map/local_stage/pallas_call | solution.py:247
  9.9 0.9 %collective-permute-done.refs_4_.refs_6_ = bf16[256,256]{1,0:T(8,128)(2,1)S(1)} collective-permute-done((bf16[256,256]{1,0:T(8,128)(2,1)}, bf16[256,256]{1,0:T(8,128)(2,1)S(1)}, u32[]{:S(2)}, u32[]{:S(2)}) %collective-permute-start) | collective-permute-done | bytes 131104 | tf_op jit(solution)/shard_map/ppermute | solution.py:236
  10.8 0.0 collective-permute-start.1
  10.8 0.9 %add_stage.1 = (f32[640,512]{1,0:T(8,128)S(1)}, f32[640,512]{1,0:T(8,128)S(1)}) custom-call(bf16[640,512]{1,0:T(8,128)(2,1)S(1)} %get-tuple-element.13.refs_0_, f32[640,512]{1,0:T(8,128)S(1)} %get-tuple-element.15.refs_1_, f32[640,512]{1,0:T(8,128)S(1)} %get-tuple-element.16.refs_2_, f32[640,512]{1,0:T(8,128)S(1)} %get-tuple-element.17.refs_3_, ...), custom_call_target="tpu_custom_call" | custom-call | flops 1 | bytes 1 | tf_op jit(solution)/shard_map/add_stage/pallas_call | solution.py:266
  11.7 0.0 collective-permute-done.2.refs_8_
  11.7 0.4 %collective-permute-done.1.refs_7_ = bf16[256,256]{1,0:T(8,128)(2,1)S(1)} collective-permute-done((bf16[256,256]{1,0:T(8,128)(2,1)S(1)}, bf16[256,256]{1,0:T(8,128)(2,1)S(1)}, u32[]{:S(2)}, u32[]{:S(2)}) %collective-permute-start.1) | collective-permute-done | bytes 131104 | tf_op jit(solution)/shard_map/ppermute | solution.py:278
  12.2 12.5 %last_stage.1 = bf16[640,512]{1,0:T(8,128)(2,1)} custom-call(bf16[640,512]{1,0:T(8,128)(2,1)S(1)} %get-tuple-element.13.refs_0_, f32[640,512]{1,0:T(8,128)S(1)} %get-tuple-element.15.refs_1_, f32[640,512]{1,0:T(8,128)S(1)} %get-tuple-element.16.refs_2_, f32[640,512]{1,0:T(8,128)S(1)} %get-tuple-element.17.refs_3_, f32[640,512]{1,0:T(8,128)S(1)} %get-tuple-element.19.refs_4_, ...), custom_call_target="tpu_custom_call" | custom-call | flops 1 | bytes 1 | tf_op jit(solution)/shard_map/last_stage/pallas_call | solution.py:282
Async XLA Ops:
  0.0 10.8 %collective-permute-start = (bf16[256,256]{1,0:T(8,128)(2,1)}, bf16[256,256]{1,0:T(8,128)(2,1)S(1)}, u32[]{:S(2)}, u32[]{:S(2)}) collective-permute-start(bf16[256,256]{1,0:T(8,128)(2,1)} %bitcast.3), channel_id=1, source_target_pairs={{0,8},{4,12},{8,0},{12,4},{1,13},{5,9},{9,5},{13,1},{2,10},{6,14},... | collective-permute-start | bytes 393224 | tf_op jit(solution)/shard_map/ppermute | solution.py:236
  4.0 7.7 %collective-permute-start.2 = (bf16[256,256]{1,0:T(8,128)(2,1)}, bf16[256,256]{1,0:T(8,128)(2,1)S(1)}, u32[]{:S(2)}, u32[]{:S(2)}) collective-permute-start(bf16[256,256]{1,0:T(8,128)(2,1)} %bitcast.4), channel_id=1, source_target_pairs={{0,4},{4,0},{8,12},{12,8},{1,5},{5,1},{9,13},{13,9},{2,6},{6,2},{1... | collective-permute-start | bytes 393224 | tf_op jit(solution)/shard_map/ppermute | solution.py:236
  10.8 1.3 %collective-permute-start.1 = (bf16[256,256]{1,0:T(8,128)(2,1)S(1)}, bf16[256,256]{1,0:T(8,128)(2,1)S(1)}, u32[]{:S(2)}, u32[]{:S(2)}) collective-permute-start(bf16[256,256]{1,0:T(8,128)(2,1)S(1)} %collective-permute-done.refs_4_.refs_6_), channel_id=1, source_target_pairs={{0,1},{1,0},{4,5},{5,4},{8,9},{9,8},{12,13},{13,12},{2,3},{3,2},{6... | collective-permute-start | bytes 393224 | tf_op jit(solution)/shard_map/ppermute | solution.py:278

commit v13 on v12

--- a/solution.py
+++ b/solution.py
@@ -149,11 +149,14 @@
     staged(row_blocks(query_ref.shape[0], 80), start, finish)
 
 
-def last_stage(earlier_count, last_count, *refs):
+def last_stage(far_count, near_count, *refs):
     query_ref, best_ref, old_total_ref, old_sum_ref, total_ref, sum_ref = refs[:6]
-    earlier_refs = refs[6 : 6 + earlier_count]
-    last_refs = refs[6 + earlier_count : 6 + earlier_count + last_count]
-    out_hbm, out_ref, out_sems = refs[6 + earlier_count + last_count :]
+    refs = refs[6:]
+    far_refs, refs = refs[:far_count], refs[far_count:]
+    swapped_refs, refs = refs[:far_count], refs[far_count:]
+    by_swap_refs, refs = refs[:near_count], refs[near_count:]
+    direct_refs, refs = refs[:near_count], refs[near_count:]
+    out_hbm, out_ref, out_sems = refs
     heads = query_ref.shape[1] // HD
     blocks = row_blocks(query_ref.shape[0], 80)
 
@@ -163,7 +166,15 @@
     def write(rows, total, weighted):
         unstack(out_ref, rows, heads, (weighted / total).astype(jnp.bfloat16))
 
-    shard = jnp.concatenate([ref[...] for ref in last_refs], axis=0)
+    is_direct = lax.axis_index("pair") == 1
+
+    def last_shards():
+        shards_here = [ref[...] for ref in swapped_refs]
+        for by_swap, direct in zip(by_swap_refs, direct_refs):
+            shards_here.append(jnp.where(is_direct, direct[...], by_swap[...]))
+        return shards_here
+
+    shard = jnp.concatenate(last_shards(), axis=0)
     trusted = [jnp.full((8, HD), True)]
 
     def start(rows):
@@ -183,10 +194,11 @@
         out_copy(index, rows).start()
 
     staged(blocks, start, finish)
+    is_trusted = jnp.all(trusted[0])
     for index, rows in enumerate(blocks):
         out_copy(index, rows).wait()
 
-    @pl.when(jnp.logical_not(jnp.all(trusted[0])))
+    @pl.when(jnp.logical_not(is_trusted))
     def exact_maximum():
         size = query_ref.shape[0] // len(blocks)
 
@@ -196,8 +208,8 @@
             best = stacked(best_ref, rows, heads)
             weighted = stacked(old_sum_ref, rows, heads)
             total = stacked(old_total_ref, rows, heads)
-            for shard_ref in earlier_refs + last_refs:
-                key_rows, value_rows = shard_ref[:, :HD], with_ones(shard_ref[:, HD:])
+            for shard in [ref[...] for ref in far_refs] + last_shards():
+                key_rows, value_rows = shard[:, :HD], with_ones(shard[:, HD:])
                 scores = scores_of(queries, key_rows)
                 new_best = jnp.maximum(best, jnp.max(scores, axis=1, keepdims=True))
                 factor = jnp.exp2(best - new_best)
@@ -227,17 +239,24 @@
 
     power_of_two = loop_size & (loop_size - 1) == 0
 
-    def exchange(shard, step_of_core):
-        hops = []
-        for core, step in enumerate(step_of_core):
-            for i in range(loop_size):
-                to = i ^ step if power_of_two else (i + step) % loop_size
-                hops.append((2 * i + core, 2 * to + core))
-        return lax.ppermute(shard, ("loop", "pair"), hops)
-
-    to_both = 1 - loop_size % 2
-    both = [exchange(own, (1, 1))] * to_both
-    middle = [exchange(own, (step, step + 1)) for step in range(1 + to_both, loop_size, 2)]
+    def partner(i, step):
+        return i ^ step if power_of_two else (i + step) % loop_size
+
+    single = [1] * (1 - loop_size % 2)
+    single_hops = [
+        hop
+        for i in range(loop_size)
+        for hop in ((2 * i, 2 * partner(i, 1) + 1), (2 * i + 1, 2 * i))
+    ]
+    near = [lax.ppermute(own, ("loop", "pair"), single_hops) for step in single]
+    far = []
+    for step in range(1 + len(single), loop_size, 2):
+        hops = [
+            (2 * i + core, 2 * partner(i, step + core) + core)
+            for core in range(2)
+            for i in range(loop_size)
+        ]
+        far.append(lax.ppermute(own, ("loop", "pair"), hops))
     in_hbm = pl.BlockSpec(memory_space=pltpu.HBM)
     in_vmem = pl.BlockSpec(memory_space=pltpu.VMEM)
     state = jax.ShapeDtypeStruct((slots, width), jnp.float32)
@@ -273,14 +292,15 @@
             cost_estimate=cost,
         )(queries, best, total, weighted, *shards_now)
 
-    middle, best = lax.optimization_barrier((middle, best))
+    near, far, best = lax.optimization_barrier((near, far, best))
     swap = [(p, p ^ 1) for p in range(2 * loop_size)]
-    last = [lax.ppermute(shard, ("loop", "pair"), swap) for shard in middle]
-    new_total, new_weighted = add_shards(total, weighted, middle)
+    far_swapped = [lax.ppermute(shard, ("loop", "pair"), swap) for shard in far]
+    near_swapped = [lax.ppermute(shard, ("loop", "pair"), swap) for shard in near]
+    new_total, new_weighted = add_shards(total, weighted, far)
     last_inputs = (queries, best, total, weighted, new_total, new_weighted)
-    last_inputs += (*middle, *last, *both)
+    last_inputs += (*far, *far_swapped, *near_swapped, *near)
     return pl.pallas_call(
-        functools.partial(last_stage, len(middle), len(last) + len(both)),
+        functools.partial(last_stage, len(far), len(near)),
         name="last_stage",
         out_shape=jax.ShapeDtypeStruct((slots, width), jnp.bfloat16),
         in_specs=[in_vmem] * len(last_inputs),

time: 24.8 us -> 24.8 us (level)
  waiting for transfers between devices: 1.32 us -> 2.47 us
  starting transfers between devices: 5.62 us -> 4.55 us
    ppermute x3 -> x4, waiting for transfers between devices: 1.32 us -> 2.47 us  [the longest x1 2.36 us: shards(): far.append(lax.ppermute(own, ('loop', 'pair'), hops))]
    ppermute x3 -> x4, starting transfers between devices: 5.62 us -> 4.55 us  [the longest x1 4.04 us: shards(): far.append(lax.ppermute(own, ('loop', 'pair'), hops))]
  transfers between devices with their start and end apart: 3 -> 4, of which waited for: 2 -> 2; matrix products, arithmetic and copies ran while one was open for 0% -> 0% of each run, Pallas kernels for 21% -> 21%
where the time goes in v13:
time: 24.8 us; the launch traced here: 24.6 us
  Pallas kernels  17.6 us (71%)
  starting transfers between devices  4.55 us (18%)
  waiting for transfers between devices  2.47 us (10%)
    pallas_call x1, Pallas kernels, shards(): pl.pallas_call(functools.partial(last_stage, len(far), len(near)), name='...  12.4 us
    pallas_call x1, Pallas kernels, shards(): pl.pallas_call(local_stage, name='local_stage', out_shape=[state] * 3 + [...  4.31 us
    ppermute x1, starting transfers between devices, shards(): far.append(lax.ppermute(own, ('loop', 'pair'), hops))  4.04 us
    ppermute x1, waiting for transfers between devices, shards(): far.append(lax.ppermute(own, ('loop', 'pair'), hops))  2.36 us
    pallas_call x1, Pallas kernels, add_shards(): pl.pallas_call(add_stage, name='add_stage', out_shape=[state] * 2, in_spe...  0.9 us
    ppermute x1, starting transfers between devices, shards(): far_swapped = [lax.ppermute(shard, ('loop', 'pair'), swap) for shard in far]  0.51 us
  transfers between devices with their start and end apart: 4, of which 2 were waited for; matrix products, arithmetic and copies ran while one was open for 0% of the time, Pallas kernels for 21%

profile of v13, /device:TPU:0, one launch (start us, length us, event | category | flops | bytes accessed | tf_op | source)
XLA Modules:
  0.0 24.6 jit_solution(5722825651043407446)
XLA Ops:
  0.0 4.0 %collective-permute-start.1 = (bf16[256,256]{1,0:T(8,128)(2,1)}, bf16[256,256]{1,0:T(8,128)(2,1)S(1)}, u32[]{:S(2)}, u32[]{:S(2)}) collective-permute-start(bf16[256,256]{1,0:T(8,128)(2,1)} %bitcast.3), channel_id=1, source_target_pairs={{0,8},{4,12},{8,0},{12,4},{1,13},{5,9},{9,5},{13,1},{2,10},{6,14},... | collective-permute-start | bytes 393224 | tf_op jit(solution)/shard_map/ppermute | solution.py:259
  4.0 0.0 collective-permute-start
  4.0 4.3 %local_stage.1 = (f32[640,512]{1,0:T(8,128)S(1)}, f32[640,512]{1,0:T(8,128)S(1)}, f32[640,512]{1,0:T(8,128)S(1)}, bf16[640,512]{1,0:T(8,128)(2,1)S(1)}) custom-call(s32[8]{0:T(128)} %lengths_hbm.1, bf16[640,512]{1,0:T(8,128)(2,1)} %query_hbm.1, bf16[640,256]{1,0:T(8,128)(2,1)} %bitcast.2, bf16[256,256]{1,0:T(8,128)(2,1)} %bitcast.5), custom_call_target="tpu_custom_call" | custom-call | flops 1 | bytes 1 | tf_op jit(solution)/shard_map/local_stage/pallas_call | solution.py:266
  8.4 2.4 %collective-permute-done.1.refs_4_.refs_6_ = bf16[256,256]{1,0:T(8,128)(2,1)S(1)} collective-permute-done((bf16[256,256]{1,0:T(8,128)(2,1)}, bf16[256,256]{1,0:T(8,128)(2,1)S(1)}, u32[]{:S(2)}, u32[]{:S(2)}) %collective-permute-start.1) | collective-permute-done | bytes 131104 | tf_op jit(solution)/shard_map/ppermute | solution.py:259
  10.7 0.0 collective-permute-done.refs_9_
  10.7 0.0 collective-permute-start.3
  10.7 0.5 %collective-permute-start.2 = (bf16[256,256]{1,0:T(8,128)(2,1)S(1)}, bf16[256,256]{1,0:T(8,128)(2,1)S(1)}, u32[]{:S(2)}, u32[]{:S(2)}) collective-permute-start(bf16[256,256]{1,0:T(8,128)(2,1)S(1)} %collective-permute-done.1.refs_4_.refs_6_), channel_id=1, source_target_pairs={{0,1},{1,0},{4,5},{5,4},{8,9},{9,8},{12,13},{13,12},{2,3},{3,2},{6... | collective-permute-start | bytes 393224 | tf_op jit(solution)/shard_map/ppermute | solution.py:297
  11.2 0.9 %add_stage.1 = (f32[640,512]{1,0:T(8,128)S(1)}, f32[640,512]{1,0:T(8,128)S(1)}) custom-call(bf16[640,512]{1,0:T(8,128)(2,1)S(1)} %get-tuple-element.14.refs_0_, f32[640,512]{1,0:T(8,128)S(1)} %get-tuple-element.16.refs_1_, f32[640,512]{1,0:T(8,128)S(1)} %get-tuple-element.17.refs_2_, f32[640,512]{1,0:T(8,128)S(1)} %get-tuple-element.18.refs_3_, ...), custom_call_target="tpu_custom_call" | custom-call | flops 1 | bytes 1 | tf_op jit(solution)/shard_map/add_stage/pallas_call | solution.py:285
  12.1 0.0 collective-permute-done.3.refs_8_
  12.2 0.1 collective-permute-done.2.refs_7_
  12.3 12.4 %last_stage.1 = bf16[640,512]{1,0:T(8,128)(2,1)} custom-call(bf16[640,512]{1,0:T(8,128)(2,1)S(1)} %get-tuple-element.14.refs_0_, f32[640,512]{1,0:T(8,128)S(1)} %get-tuple-element.16.refs_1_, f32[640,512]{1,0:T(8,128)S(1)} %get-tuple-element.17.refs_2_, f32[640,512]{1,0:T(8,128)S(1)} %get-tuple-element.18.refs_3_, f32[640,512]{1,0:T(8,128)S(1)} %get-tuple-element.20.refs_4_, ...), custom_call_target="tpu_custom_call" | custom-call | flops 1 | bytes 1 | tf_op jit(solution)/shard_map/last_stage/pallas_call | solution.py:302
Async XLA Ops:
  0.0 10.7 %collective-permute-start.1 = (bf16[256,256]{1,0:T(8,128)(2,1)}, bf16[256,256]{1,0:T(8,128)(2,1)S(1)}, u32[]{:S(2)}, u32[]{:S(2)}) collective-permute-start(bf16[256,256]{1,0:T(8,128)(2,1)} %bitcast.3), channel_id=1, source_target_pairs={{0,8},{4,12},{8,0},{12,4},{1,13},{5,9},{9,5},{13,1},{2,10},{6,14},... | collective-permute-start | bytes 393224 | tf_op jit(solution)/shard_map/ppermute | solution.py:259
  4.0 6.7 %collective-permute-start = (bf16[256,256]{1,0:T(8,128)(2,1)}, bf16[256,256]{1,0:T(8,128)(2,1)S(1)}, u32[]{:S(2)}, u32[]{:S(2)}) collective-permute-start(bf16[256,256]{1,0:T(8,128)(2,1)} %bitcast.4), channel_id=1, source_target_pairs={{0,5},{1,0},{4,1},{5,4},{8,13},{9,8},{12,9},{13,12},{2,7},{3,2},{6... | collective-permute-start | bytes 393224 | tf_op jit(solution)/shard_map/ppermute | solution.py:251
  10.7 1.4 %collective-permute-start.3 = (bf16[256,256]{1,0:T(8,128)(2,1)S(1)}, bf16[256,256]{1,0:T(8,128)(2,1)S(1)}, u32[]{:S(2)}, u32[]{:S(2)}) collective-permute-start(bf16[256,256]{1,0:T(8,128)(2,1)S(1)} %collective-permute-done.refs_9_), channel_id=1, source_target_pairs={{0,1},{1,0},{4,5},{5,4},{8,9},{9,8},{12,13},{13,12},{2,3},{3,2},{6... | collective-permute-start | bytes 393224 | tf_op jit(solution)/shard_map/ppermute | solution.py:298
  10.7 1.5 %collective-permute-start.2 = (bf16[256,256]{1,0:T(8,128)(2,1)S(1)}, bf16[256,256]{1,0:T(8,128)(2,1)S(1)}, u32[]{:S(2)}, u32[]{:S(2)}) collective-permute-start(bf16[256,256]{1,0:T(8,128)(2,1)S(1)} %collective-permute-done.1.refs_4_.refs_6_), channel_id=1, source_target_pairs={{0,1},{1,0},{4,5},{5,4},{8,9},{9,8},{12,13},{13,12},{2,3},{3,2},{6... | collective-permute-start | bytes 393224 | tf_op jit(solution)/shard_map/ppermute | solution.py:297

commit v14 on v13

--- a/solution.py
+++ b/solution.py
@@ -149,13 +149,13 @@
     staged(row_blocks(query_ref.shape[0], 80), start, finish)
 
 
-def last_stage(far_count, near_count, *refs):
+def last_stage(paired_count, single_count, *refs):
     query_ref, best_ref, old_total_ref, old_sum_ref, total_ref, sum_ref = refs[:6]
     refs = refs[6:]
-    far_refs, refs = refs[:far_count], refs[far_count:]
-    swapped_refs, refs = refs[:far_count], refs[far_count:]
-    by_swap_refs, refs = refs[:near_count], refs[near_count:]
-    direct_refs, refs = refs[:near_count], refs[near_count:]
+    paired_refs, refs = refs[:paired_count], refs[paired_count:]
+    swapped_refs, refs = refs[:paired_count], refs[paired_count:]
+    by_swap_refs, refs = refs[:single_count], refs[single_count:]
+    direct_refs, refs = refs[:single_count], refs[single_count:]
     out_hbm, out_ref, out_sems = refs
     heads = query_ref.shape[1] // HD
     blocks = row_blocks(query_ref.shape[0], 80)
@@ -166,7 +166,7 @@
     def write(rows, total, weighted):
         unstack(out_ref, rows, heads, (weighted / total).astype(jnp.bfloat16))
 
-    is_direct = lax.axis_index("pair") == 1
+    is_direct = lax.axis_index("pair") == 0
 
     def last_shards():
         shards_here = [ref[...] for ref in swapped_refs]
@@ -208,7 +208,7 @@
             best = stacked(best_ref, rows, heads)
             weighted = stacked(old_sum_ref, rows, heads)
             total = stacked(old_total_ref, rows, heads)
-            for shard in [ref[...] for ref in far_refs] + last_shards():
+            for shard in [ref[...] for ref in paired_refs] + last_shards():
                 key_rows, value_rows = shard[:, :HD], with_ones(shard[:, HD:])
                 scores = scores_of(queries, key_rows)
                 new_best = jnp.maximum(best, jnp.max(scores, axis=1, keepdims=True))
@@ -242,21 +242,25 @@
     def partner(i, step):
         return i ^ step if power_of_two else (i + step) % loop_size
 
-    single = [1] * (1 - loop_size % 2)
-    single_hops = [
-        hop
-        for i in range(loop_size)
-        for hop in ((2 * i, 2 * partner(i, 1) + 1), (2 * i + 1, 2 * i))
-    ]
-    near = [lax.ppermute(own, ("loop", "pair"), single_hops) for step in single]
-    far = []
-    for step in range(1 + len(single), loop_size, 2):
+    paired = []
+    for step in range(1, loop_size - 1, 2):
         hops = [
-            (2 * i + core, 2 * partner(i, step + core) + core)
-            for core in range(2)
+            hop
             for i in range(loop_size)
+            for hop in (
+                (2 * i, 2 * partner(i, step) + 1),
+                (2 * i + 1, 2 * partner(i, step + 1)),
+            )
         ]
-        far.append(lax.ppermute(own, ("loop", "pair"), hops))
+        paired.append(lax.ppermute(own, ("loop", "pair"), hops))
+    single = []
+    if loop_size % 2 == 0:
+        hops = [
+            hop
+            for i in range(loop_size)
+            for hop in ((2 * i, 2 * i + 1), (2 * i + 1, 2 * partner(i, loop_size - 1)))
+        ]
+        single.append(lax.ppermute(own, ("loop", "pair"), hops))
     in_hbm = pl.BlockSpec(memory_space=pltpu.HBM)
     in_vmem = pl.BlockSpec(memory_space=pltpu.VMEM)
     state = jax.ShapeDtypeStruct((slots, width), jnp.float32)
@@ -292,15 +296,15 @@
             cost_estimate=cost,
         )(queries, best, total, weighted, *shards_now)
 
-    near, far, best = lax.optimization_barrier((near, far, best))
+    single, paired, best = lax.optimization_barrier((single, paired, best))
     swap = [(p, p ^ 1) for p in range(2 * loop_size)]
-    far_swapped = [lax.ppermute(shard, ("loop", "pair"), swap) for shard in far]
-    near_swapped = [lax.ppermute(shard, ("loop", "pair"), swap) for shard in near]
-    new_total, new_weighted = add_shards(total, weighted, far)
+    paired_swapped = [lax.ppermute(shard, ("loop", "pair"), swap) for shard in paired]
+    single_swapped = [lax.ppermute(shard, ("loop", "pair"), swap) for shard in single]
+    new_total, new_weighted = add_shards(total, weighted, paired)
     last_inputs = (queries, best, total, weighted, new_total, new_weighted)
-    last_inputs += (*far, *far_swapped, *near_swapped, *near)
+    last_inputs += (*paired, *paired_swapped, *single_swapped, *single)
     return pl.pallas_call(
-        functools.partial(last_stage, len(far), len(near)),
+        functools.partial(last_stage, len(paired), len(single)),
         name="last_stage",
         out_shape=jax.ShapeDtypeStruct((slots, width), jnp.bfloat16),
         in_specs=[in_vmem] * len(last_inputs),

time: 24.8 us -> 24.8 us (level)
    ppermute x1 -> x2, starting transfers between devices: 0.01 us -> 0.51 us  [shards(): lax.ppermute(shard, ('loop', 'pair'), swap)]
    ppermute x3 -> x2, starting transfers between devices: 4.55 us -> 4.15 us  [the longest x1 2.46 us: shards(): paired.append(lax.ppermute(own, ('loop', 'pair'), hops))]
    ppermute x3 -> x2, waiting for transfers between devices: 2.46 us -> 2.29 us  [the longest x1 2.29 us: shards(): single.append(lax.ppermute(own, ('loop', 'pair'), hops))]
where the time goes in v14:
time: 24.8 us; the launch traced here: 24.7 us
  Pallas kernels  17.6 us (71%)
  starting transfers between devices  4.66 us (19%)
  waiting for transfers between devices  2.4 us (10%)
    pallas_call x1, Pallas kernels, shards(): pl.pallas_call(functools.partial(last_stage, len(paired), len(single)), n...  12.4 us
    pallas_call x1, Pallas kernels, shards(): pl.pallas_call(local_stage, name='local_stage', out_shape=[state] * 3 + [...  4.31 us
    ppermute x1, starting transfers between devices, shards(): paired.append(lax.ppermute(own, ('loop', 'pair'), hops))  2.46 us
    ppermute x1, waiting for transfers between devices, shards(): single.append(lax.ppermute(own, ('loop', 'pair'), hops))  2.29 us
    ppermute x1, starting transfers between devices, shards(): single.append(lax.ppermute(own, ('loop', 'pair'), hops))  1.69 us
    pallas_call x1, Pallas kernels, add_shards(): pl.pallas_call(add_stage, name='add_stage', out_shape=[state] * 2, in_spe...  0.9 us
    ppermute x2, starting transfers between devices, shards(): lax.ppermute(shard, ('loop', 'pair'), swap)  0.51 us
  transfers between devices with their start and end apart: 4, of which 2 were waited for; matrix products, arithmetic and copies ran while one was open for 0% of the time, Pallas kernels for 21%

profile of v14, /device:TPU:0, one launch (start us, length us, event | category | flops | bytes accessed | tf_op | source)
XLA Modules:
  0.0 24.7 jit_solution(10638286538438692993)
XLA Ops:
  0.0 2.5 %collective-permute-start.1 = (bf16[256,256]{1,0:T(8,128)(2,1)}, bf16[256,256]{1,0:T(8,128)(2,1)S(1)}, u32[]{:S(2)}, u32[]{:S(2)}) collective-permute-start(bf16[256,256]{1,0:T(8,128)(2,1)} %bitcast.3), channel_id=1, source_target_pairs={{0,5},{1,8},{4,1},{5,12},{8,13},{9,0},{12,9},{13,4},{2,7},{3,10},{... | collective-permute-start | bytes 393224 | tf_op jit(solution)/shard_map/ppermute | solution.py:255
  2.5 1.7 %collective-permute-start = (bf16[256,256]{1,0:T(8,128)(2,1)}, bf16[256,256]{1,0:T(8,128)(2,1)S(1)}, u32[]{:S(2)}, u32[]{:S(2)}) collective-permute-start(bf16[256,256]{1,0:T(8,128)(2,1)} %bitcast.4), channel_id=1, source_target_pairs={{0,1},{1,12},{4,5},{5,8},{8,9},{9,4},{12,13},{13,0},{2,3},{3,14},{... | collective-permute-start | bytes 393224 | tf_op jit(solution)/shard_map/ppermute | solution.py:263
  4.2 4.3 %local_stage.1 = (f32[640,512]{1,0:T(8,128)S(1)}, f32[640,512]{1,0:T(8,128)S(1)}, f32[640,512]{1,0:T(8,128)S(1)}, bf16[640,512]{1,0:T(8,128)(2,1)S(1)}) custom-call(s32[8]{0:T(128)} %lengths_hbm.1, bf16[640,512]{1,0:T(8,128)(2,1)} %query_hbm.1, bf16[640,256]{1,0:T(8,128)(2,1)} %bitcast.2, bf16[256,256]{1,0:T(8,128)(2,1)} %bitcast.5), custom_call_target="tpu_custom_call" | custom-call | flops 1 | bytes 1 | tf_op jit(solution)/shard_map/local_stage/pallas_call | solution.py:270
  8.5 0.0 collective-permute-done.1.refs_4_.refs_6_
  8.5 2.3 %collective-permute-done.refs_9_ = bf16[256,256]{1,0:T(8,128)(2,1)S(1)} collective-permute-done((bf16[256,256]{1,0:T(8,128)(2,1)}, bf16[256,256]{1,0:T(8,128)(2,1)S(1)}, u32[]{:S(2)}, u32[]{:S(2)}) %collective-permute-start) | collective-permute-done | bytes 131104 | tf_op jit(solution)/shard_map/ppermute | solution.py:263
  10.8 0.0 collective-permute-start.3
  10.8 0.5 %collective-permute-start.2 = (bf16[256,256]{1,0:T(8,128)(2,1)S(1)}, bf16[256,256]{1,0:T(8,128)(2,1)S(1)}, u32[]{:S(2)}, u32[]{:S(2)}) collective-permute-start(bf16[256,256]{1,0:T(8,128)(2,1)S(1)} %collective-permute-done.1.refs_4_.refs_6_), channel_id=1, source_target_pairs={{0,1},{1,0},{4,5},{5,4},{8,9},{9,8},{12,13},{13,12},{2,3},{3,2},{6... | collective-permute-start | bytes 393224 | tf_op jit(solution)/shard_map/ppermute | solution.py:301
  11.3 0.9 %add_stage.1 = (f32[640,512]{1,0:T(8,128)S(1)}, f32[640,512]{1,0:T(8,128)S(1)}) custom-call(bf16[640,512]{1,0:T(8,128)(2,1)S(1)} %get-tuple-element.14.refs_0_, f32[640,512]{1,0:T(8,128)S(1)} %get-tuple-element.16.refs_1_, f32[640,512]{1,0:T(8,128)S(1)} %get-tuple-element.17.refs_2_, f32[640,512]{1,0:T(8,128)S(1)} %get-tuple-element.18.refs_3_, ...), custom_call_target="tpu_custom_call" | custom-call | flops 1 | bytes 1 | tf_op jit(solution)/shard_map/add_stage/pallas_call | solution.py:289
  12.2 0.0 collective-permute-done.3.refs_8_
  12.2 0.1 collective-permute-done.2.refs_7_
  12.3 12.4 %last_stage.1 = bf16[640,512]{1,0:T(8,128)(2,1)} custom-call(bf16[640,512]{1,0:T(8,128)(2,1)S(1)} %get-tuple-element.14.refs_0_, f32[640,512]{1,0:T(8,128)S(1)} %get-tuple-element.16.refs_1_, f32[640,512]{1,0:T(8,128)S(1)} %get-tuple-element.17.refs_2_, f32[640,512]{1,0:T(8,128)S(1)} %get-tuple-element.18.refs_3_, f32[640,512]{1,0:T(8,128)S(1)} %get-tuple-element.20.refs_4_, ...), custom_call_target="tpu_custom_call" | custom-call | flops 1 | bytes 1 | tf_op jit(solution)/shard_map/last_stage/pallas_call | solution.py:306
Async XLA Ops:
  0.0 8.5 %collective-permute-start.1 = (bf16[256,256]{1,0:T(8,128)(2,1)}, bf16[256,256]{1,0:T(8,128)(2,1)S(1)}, u32[]{:S(2)}, u32[]{:S(2)}) collective-permute-start(bf16[256,256]{1,0:T(8,128)(2,1)} %bitcast.3), channel_id=1, source_target_pairs={{0,5},{1,8},{4,1},{5,12},{8,13},{9,0},{12,9},{13,4},{2,7},{3,10},{... | collective-permute-start | bytes 393224 | tf_op jit(solution)/shard_map/ppermute | solution.py:255
  2.5 8.3 %collective-permute-start = (bf16[256,256]{1,0:T(8,128)(2,1)}, bf16[256,256]{1,0:T(8,128)(2,1)S(1)}, u32[]{:S(2)}, u32[]{:S(2)}) collective-permute-start(bf16[256,256]{1,0:T(8,128)(2,1)} %bitcast.4), channel_id=1, source_target_pairs={{0,1},{1,12},{4,5},{5,8},{8,9},{9,4},{12,13},{13,0},{2,3},{3,14},{... | collective-permute-start | bytes 393224 | tf_op jit(solution)/shard_map/ppermute | solution.py:263
  10.8 1.4 %collective-permute-start.3 = (bf16[256,256]{1,0:T(8,128)(2,1)S(1)}, bf16[256,256]{1,0:T(8,128)(2,1)S(1)}, u32[]{:S(2)}, u32[]{:S(2)}) collective-permute-start(bf16[256,256]{1,0:T(8,128)(2,1)S(1)} %collective-permute-done.refs_9_), channel_id=1, source_target_pairs={{0,1},{1,0},{4,5},{5,4},{8,9},{9,8},{12,13},{13,12},{2,3},{3,2},{6... | collective-permute-start | bytes 393224 | tf_op jit(solution)/shard_map/ppermute | solution.py:302
  10.8 1.5 %collective-permute-start.2 = (bf16[256,256]{1,0:T(8,128)(2,1)S(1)}, bf16[256,256]{1,0:T(8,128)(2,1)S(1)}, u32[]{:S(2)}, u32[]{:S(2)}) collective-permute-start(bf16[256,256]{1,0:T(8,128)(2,1)S(1)} %collective-permute-done.1.refs_4_.refs_6_), channel_id=1, source_target_pairs={{0,1},{1,0},{4,5},{5,4},{8,9},{9,8},{12,13},{13,12},{2,3},{3,2},{6... | collective-permute-start | bytes 393224 | tf_op jit(solution)/shard_map/ppermute | solution.py:301

commit v15 on v14

--- a/solution.py
+++ b/solution.py
@@ -169,10 +169,10 @@
     is_direct = lax.axis_index("pair") == 0
 
     def last_shards():
-        shards_here = [ref[...] for ref in swapped_refs]
-        for by_swap, direct in zip(by_swap_refs, direct_refs):
-            shards_here.append(jnp.where(is_direct, direct[...], by_swap[...]))
-        return shards_here
+        return [
+            jnp.where(is_direct, direct[...], by_swap[...])
+            for by_swap, direct in zip(by_swap_refs, direct_refs)
+        ]
 
     shard = jnp.concatenate(last_shards(), axis=0)
     trusted = [jnp.full((8, HD), True)]
@@ -208,7 +208,7 @@
             best = stacked(best_ref, rows, heads)
             weighted = stacked(old_sum_ref, rows, heads)
             total = stacked(old_total_ref, rows, heads)
-            for shard in [ref[...] for ref in paired_refs] + last_shards():
+            for shard in [ref[...] for ref in paired_refs + swapped_refs] + last_shards():
                 key_rows, value_rows = shard[:, :HD], with_ones(shard[:, HD:])
                 scores = scores_of(queries, key_rows)
                 new_best = jnp.maximum(best, jnp.max(scores, axis=1, keepdims=True))
@@ -296,11 +296,19 @@
             cost_estimate=cost,
         )(queries, best, total, weighted, *shards_now)
 
-    single, paired, best = lax.optimization_barrier((single, paired, best))
     swap = [(p, p ^ 1) for p in range(2 * loop_size)]
-    paired_swapped = [lax.ppermute(shard, ("loop", "pair"), swap) for shard in paired]
-    single_swapped = [lax.ppermute(shard, ("loop", "pair"), swap) for shard in single]
+
+    def swapped(shards_now):
+        return [lax.ppermute(shard, ("loop", "pair"), swap) for shard in shards_now]
+
+    paired, best = lax.optimization_barrier((paired, best))
+    paired_swapped = swapped(paired)
     new_total, new_weighted = add_shards(total, weighted, paired)
+    single, new_total = lax.optimization_barrier((single, new_total))
+    single_swapped = swapped(single)
+    if not single:
+        single = single_swapped = [paired_swapped.pop()]
+    new_total, new_weighted = add_shards(new_total, new_weighted, paired_swapped)
     last_inputs = (queries, best, total, weighted, new_total, new_weighted)
     last_inputs += (*paired, *paired_swapped, *single_swapped, *single)
     return pl.pallas_call(

time: 24.8 us -> 24 us (0.968)
  waiting for transfers between devices: 2.4 us -> 0.73 us
  starting transfers between devices: 4.66 us -> 5.23 us
  Pallas kernels: 17.6 us -> 17.9 us
    ppermute x1, waiting for transfers between devices: 2.29 us -> 0.3 us  [shards(): single.append(lax.ppermute(own, ('loop', 'pair'), hops))]
    pallas_call x1 -> x2, Pallas kernels: 0.9 us -> 1.81 us  [add_shards(): pl.pallas_call(add_stage, name='add_stage', out_shape=[state] * 2, in_spe...]
    pallas_call x1, Pallas kernels: 12.4 us -> 11.7 us  [shards(): pl.pallas_call(functools.partial(last_stage, len(paired), len(single)), n...]
    ppermute x2, starting transfers between devices: 0.51 us -> 1.08 us  [swapped(): return [lax.ppermute(shard, ('loop', 'pair'), swap) for shard in shards_now]]
    ppermute x2, waiting for transfers between devices: 0.1 us -> 0.43 us  [swapped(): return [lax.ppermute(shard, ('loop', 'pair'), swap) for shard in shards_now]]
  transfers between devices with their start and end apart: 4 -> 4, of which waited for: 2 -> 2; matrix products, arithmetic and copies ran while one was open for 0% -> 0% of each run, Pallas kernels for 21% -> 26%
where the time goes in v15:
time: 24 us; the launch traced here: 23.9 us
  Pallas kernels  17.9 us (75%)
  starting transfers between devices  5.23 us (22%)
  waiting for transfers between devices  0.73 us (3%)
    pallas_call x1, Pallas kernels, shards(): pl.pallas_call(functools.partial(last_stage, len(paired), len(single)), n...  11.7 us
    pallas_call x1, Pallas kernels, shards(): pl.pallas_call(local_stage, name='local_stage', out_shape=[state] * 3 + [...  4.31 us
    ppermute x1, starting transfers between devices, shards(): paired.append(lax.ppermute(own, ('loop', 'pair'), hops))  2.46 us
    pallas_call x2, Pallas kernels, add_shards(): pl.pallas_call(add_stage, name='add_stage', out_shape=[state] * 2, in_spe...  1.81 us
    ppermute x1, starting transfers between devices, shards(): single.append(lax.ppermute(own, ('loop', 'pair'), hops))  1.69 us
    ppermute x2, starting transfers between devices, swapped(): return [lax.ppermute(shard, ('loop', 'pair'), swap) for shard in shards_now]  1.08 us
  transfers between devices with their start and end apart: 4, of which 2 were waited for; matrix products, arithmetic and copies ran while one was open for 0% of the time, Pallas kernels for 26%

profile of v15, /device:TPU:0, one launch (start us, length us, event | category | flops | bytes accessed | tf_op | source)
XLA Modules:
  0.0 23.9 jit_solution(9314510530841815812)
XLA Ops:
  0.0 2.5 %collective-permute-start = (bf16[256,256]{1,0:T(8,128)(2,1)}, bf16[256,256]{1,0:T(8,128)(2,1)S(1)}, u32[]{:S(2)}, u32[]{:S(2)}) collective-permute-start(bf16[256,256]{1,0:T(8,128)(2,1)} %bitcast.3), channel_id=1, source_target_pairs={{0,5},{1,8},{4,1},{5,12},{8,13},{9,0},{12,9},{13,4},{2,7},{3,10},{... | collective-permute-start | bytes 393224 | tf_op jit(solution)/shard_map/ppermute | solution.py:255
  2.5 1.7 %collective-permute-start.1 = (bf16[256,256]{1,0:T(8,128)(2,1)}, bf16[256,256]{1,0:T(8,128)(2,1)S(1)}, u32[]{:S(2)}, u32[]{:S(2)}) collective-permute-start(bf16[256,256]{1,0:T(8,128)(2,1)} %bitcast.4), channel_id=1, source_target_pairs={{0,1},{1,12},{4,5},{5,8},{8,9},{9,4},{12,13},{13,0},{2,3},{3,14},{... | collective-permute-start | bytes 393224 | tf_op jit(solution)/shard_map/ppermute | solution.py:263
  4.2 4.3 %local_stage.1 = (f32[640,512]{1,0:T(8,128)S(1)}, f32[640,512]{1,0:T(8,128)S(1)}, f32[640,512]{1,0:T(8,128)S(1)}, bf16[640,512]{1,0:T(8,128)(2,1)S(1)}) custom-call(s32[8]{0:T(128)} %lengths_hbm.1, bf16[640,512]{1,0:T(8,128)(2,1)} %query_hbm.1, bf16[640,256]{1,0:T(8,128)(2,1)} %bitcast.2, bf16[256,256]{1,0:T(8,128)(2,1)} %bitcast.5), custom_call_target="tpu_custom_call" | custom-call | flops 1 | bytes 1 | tf_op jit(solution)/shard_map/local_stage/pallas_call | solution.py:270
  8.5 0.0 collective-permute-done.refs_4_.refs_6_
  8.5 1.1 %collective-permute-start.2 = (bf16[256,256]{1,0:T(8,128)(2,1)S(1)}, bf16[256,256]{1,0:T(8,128)(2,1)S(1)}, u32[]{:S(2)}, u32[]{:S(2)}) collective-permute-start(bf16[256,256]{1,0:T(8,128)(2,1)S(1)} %collective-permute-done.refs_4_.refs_6_), channel_id=1, source_target_pairs={{0,1},{1,0},{4,5},{5,4},{8,9},{9,8},{12,13},{13,12},{2,3},{3,2},{6... | collective-permute-start | bytes 393224 | tf_op jit(solution)/shard_map/ppermute | solution.py:302
  9.6 0.9 %add_stage.2 = (f32[640,512]{1,0:T(8,128)S(1)}, f32[640,512]{1,0:T(8,128)S(1)}) custom-call(bf16[640,512]{1,0:T(8,128)(2,1)S(1)} %get-tuple-element.17.refs_0_, f32[640,512]{1,0:T(8,128)S(1)} %get-tuple-element.19.refs_1_, f32[640,512]{1,0:T(8,128)S(1)} %get-tuple-element.20.refs_2_, f32[640,512]{1,0:T(8,128)S(1)} %get-tuple-element.21.refs_3_, ...), custom_call_target="tpu_custom_call" | custom-call | flops 1 | bytes 1 | tf_op jit(solution)/shard_map/add_stage/pallas_call | solution.py:289
  10.5 0.3 %collective-permute-done.1.refs_9_ = bf16[256,256]{1,0:T(8,128)(2,1)S(1)} collective-permute-done((bf16[256,256]{1,0:T(8,128)(2,1)}, bf16[256,256]{1,0:T(8,128)(2,1)S(1)}, u32[]{:S(2)}, u32[]{:S(2)}) %collective-permute-start.1) | collective-permute-done | bytes 131104 | tf_op jit(solution)/shard_map/ppermute | solution.py:263
  10.8 0.0 collective-permute-start.3
  10.8 0.0 collective-permute-done.2.refs_4_.refs_7_
  10.8 0.9 %add_stage.3 = (f32[640,512]{1,0:T(8,128)S(1)}, f32[640,512]{1,0:T(8,128)S(1)}) custom-call(bf16[640,512]{1,0:T(8,128)(2,1)S(1)} %get-tuple-element.17.refs_0_, f32[640,512]{1,0:T(8,128)S(1)} %get-tuple-element.19.refs_1_, f32[640,512]{1,0:T(8,128)S(1)} %get-tuple-element.24.refs_2_, f32[640,512]{1,0:T(8,128)S(1)} %get-tuple-element.25.refs_3_, ...), custom_call_target="tpu_custom_call" | custom-call | flops 1 | bytes 1 | tf_op jit(solution)/shard_map/add_stage/pallas_call | solution.py:289
  11.7 0.4 %collective-permute-done.3.refs_8_ = bf16[256,256]{1,0:T(8,128)(2,1)S(1)} collective-permute-done((bf16[256,256]{1,0:T(8,128)(2,1)S(1)}, bf16[256,256]{1,0:T(8,128)(2,1)S(1)}, u32[]{:S(2)}, u32[]{:S(2)}) %collective-permute-start.3) | collective-permute-done | bytes 131104 | tf_op jit(solution)/shard_map/ppermute | solution.py:302
  12.1 11.7 %last_stage.1 = bf16[640,512]{1,0:T(8,128)(2,1)} custom-call(bf16[640,512]{1,0:T(8,128)(2,1)S(1)} %get-tuple-element.17.refs_0_, f32[640,512]{1,0:T(8,128)S(1)} %get-tuple-element.19.refs_1_, f32[640,512]{1,0:T(8,128)S(1)} %get-tuple-element.20.refs_2_, f32[640,512]{1,0:T(8,128)S(1)} %get-tuple-element.21.refs_3_, f32[640,512]{1,0:T(8,128)S(1)} %get-tuple-element.26.refs_4_, ...), custom_call_target="tpu_custom_call" | custom-call | flops 1 | bytes 1 | tf_op jit(solution)/shard_map/last_stage/pallas_call | solution.py:314
Async XLA Ops:
  0.0 8.5 %collective-permute-start = (bf16[256,256]{1,0:T(8,128)(2,1)}, bf16[256,256]{1,0:T(8,128)(2,1)S(1)}, u32[]{:S(2)}, u32[]{:S(2)}) collective-permute-start(bf16[256,256]{1,0:T(8,128)(2,1)} %bitcast.3), channel_id=1, source_target_pairs={{0,5},{1,8},{4,1},{5,12},{8,13},{9,0},{12,9},{13,4},{2,7},{3,10},{... | collective-permute-start | bytes 393224 | tf_op jit(solution)/shard_map/ppermute | solution.py:255
  2.5 8.3 %collective-permute-start.1 = (bf16[256,256]{1,0:T(8,128)(2,1)}, bf16[256,256]{1,0:T(8,128)(2,1)S(1)}, u32[]{:S(2)}, u32[]{:S(2)}) collective-permute-start(bf16[256,256]{1,0:T(8,128)(2,1)} %bitcast.4), channel_id=1, source_target_pairs={{0,1},{1,12},{4,5},{5,8},{8,9},{9,4},{12,13},{13,0},{2,3},{3,14},{... | collective-permute-start | bytes 393224 | tf_op jit(solution)/shard_map/ppermute | solution.py:263
  8.5 2.3 %collective-permute-start.2 = (bf16[256,256]{1,0:T(8,128)(2,1)S(1)}, bf16[256,256]{1,0:T(8,128)(2,1)S(1)}, u32[]{:S(2)}, u32[]{:S(2)}) collective-permute-start(bf16[256,256]{1,0:T(8,128)(2,1)S(1)} %collective-permute-done.refs_4_.refs_6_), channel_id=1, source_target_pairs={{0,1},{1,0},{4,5},{5,4},{8,9},{9,8},{12,13},{13,12},{2,3},{3,2},{6... | collective-permute-start | bytes 393224 | tf_op jit(solution)/shard_map/ppermute | solution.py:302
  10.8 1.3 %collective-permute-start.3 = (bf16[256,256]{1,0:T(8,128)(2,1)S(1)}, bf16[256,256]{1,0:T(8,128)(2,1)S(1)}, u32[]{:S(2)}, u32[]{:S(2)}) collective-permute-start(bf16[256,256]{1,0:T(8,128)(2,1)S(1)} %collective-permute-done.1.refs_9_), channel_id=1, source_target_pairs={{0,1},{1,0},{4,5},{5,4},{8,9},{9,8},{12,13},{13,12},{2,3},{3,2},{6... | collective-permute-start | bytes 393224 | tf_op jit(solution)/shard_map/ppermute | solution.py:302

commit v16 on v15

--- a/solution.py
+++ b/solution.py
@@ -243,13 +243,13 @@
         return i ^ step if power_of_two else (i + step) % loop_size
 
     paired = []
-    for step in range(1, loop_size - 1, 2):
+    for step in range(1, (loop_size + 1) // 2):
         hops = [
             hop
             for i in range(loop_size)
             for hop in (
                 (2 * i, 2 * partner(i, step) + 1),
-                (2 * i + 1, 2 * partner(i, step + 1)),
+                (2 * i + 1, 2 * partner(i, loop_size - step)),
             )
         ]
         paired.append(lax.ppermute(own, ("loop", "pair"), hops))
@@ -258,7 +258,7 @@
         hops = [
             hop
             for i in range(loop_size)
-            for hop in ((2 * i, 2 * i + 1), (2 * i + 1, 2 * partner(i, loop_size - 1)))
+            for hop in ((2 * i, 2 * i + 1), (2 * i + 1, 2 * partner(i, loop_size // 2)))
         ]
         single.append(lax.ppermute(own, ("loop", "pair"), hops))
     in_hbm = pl.BlockSpec(memory_space=pltpu.HBM)

time: 24 us -> 24.5 us (1.021)
  waiting for transfers between devices: 0.73 us -> 1.22 us
    ppermute x1, starting transfers between devices: 1.69 us -> 2.7 us  [shards(): single.append(lax.ppermute(own, ('loop', 'pair'), hops))]
    ppermute x2, starting transfers between devices: 1.08 us -> 0.07 us  [swapped(): return [lax.ppermute(shard, ('loop', 'pair'), swap) for shard in shards_now]]
    ppermute x1, waiting for transfers between devices: 0.3 us -> 0.79 us  [shards(): single.append(lax.ppermute(own, ('loop', 'pair'), hops))]
  transfers between devices with their start and end apart: 4 -> 4, of which waited for: 2 -> 2; matrix products, arithmetic and copies ran while one was open for 0% -> 0% of each run, Pallas kernels for 26% -> 25%
where the time goes in v16:
time: 24.5 us; the launch traced here: 24.4 us
  Pallas kernels  17.9 us (73%)
  starting transfers between devices  5.24 us (21%)
  waiting for transfers between devices  1.22 us (5%)
    pallas_call x1, Pallas kernels, shards(): pl.pallas_call(functools.partial(last_stage, len(paired), len(single)), n...  11.7 us
    pallas_call x1, Pallas kernels, shards(): pl.pallas_call(local_stage, name='local_stage', out_shape=[state] * 3 + [...  4.31 us
    ppermute x1, starting transfers between devices, shards(): single.append(lax.ppermute(own, ('loop', 'pair'), hops))  2.7 us
    ppermute x1, starting transfers between devices, shards(): paired.append(lax.ppermute(own, ('loop', 'pair'), hops))  2.46 us
    pallas_call x2, Pallas kernels, add_shards(): pl.pallas_call(add_stage, name='add_stage', out_shape=[state] * 2, in_spe...  1.81 us
    ppermute x1, waiting for transfers between devices, shards(): single.append(lax.ppermute(own, ('loop', 'pair'), hops))  0.79 us
  transfers between devices with their start and end apart: 4, of which 2 were waited for; matrix products, arithmetic and copies ran while one was open for 0% of the time, Pallas kernels for 25%

profile of v16, /device:TPU:0, one launch (start us, length us, event | category | flops | bytes accessed | tf_op | source)
XLA Modules:
  0.0 24.4 jit_solution(8960588250804156350)
XLA Ops:
  0.0 2.5 %collective-permute-start = (bf16[256,256]{1,0:T(8,128)(2,1)}, bf16[256,256]{1,0:T(8,128)(2,1)S(1)}, u32[]{:S(2)}, u32[]{:S(2)}) collective-permute-start(bf16[256,256]{1,0:T(8,128)(2,1)} %bitcast.3), channel_id=1, source_target_pairs={{0,5},{1,12},{4,1},{5,8},{8,13},{9,4},{12,9},{13,0},{2,7},{3,14},{... | collective-permute-start | bytes 393224 | tf_op jit(solution)/shard_map/ppermute | solution.py:255
  2.5 2.7 %collective-permute-start.1 = (bf16[256,256]{1,0:T(8,128)(2,1)}, bf16[256,256]{1,0:T(8,128)(2,1)S(1)}, u32[]{:S(2)}, u32[]{:S(2)}) collective-permute-start(bf16[256,256]{1,0:T(8,128)(2,1)} %bitcast.4), channel_id=1, source_target_pairs={{0,1},{1,8},{4,5},{5,12},{8,9},{9,0},{12,13},{13,4},{2,3},{3,10},{... | collective-permute-start | bytes 393224 | tf_op jit(solution)/shard_map/ppermute | solution.py:263
  5.2 4.3 %local_stage.1 = (f32[640,512]{1,0:T(8,128)S(1)}, f32[640,512]{1,0:T(8,128)S(1)}, f32[640,512]{1,0:T(8,128)S(1)}, bf16[640,512]{1,0:T(8,128)(2,1)S(1)}) custom-call(s32[8]{0:T(128)} %lengths_hbm.1, bf16[640,512]{1,0:T(8,128)(2,1)} %query_hbm.1, bf16[640,256]{1,0:T(8,128)(2,1)} %bitcast.2, bf16[256,256]{1,0:T(8,128)(2,1)} %bitcast.5), custom_call_target="tpu_custom_call" | custom-call | flops 1 | bytes 1 | tf_op jit(solution)/shard_map/local_stage/pallas_call | solution.py:270
  9.5 0.0 collective-permute-done.refs_4_.refs_6_
  9.5 0.1 collective-permute-start.2
  9.6 0.9 %add_stage.2 = (f32[640,512]{1,0:T(8,128)S(1)}, f32[640,512]{1,0:T(8,128)S(1)}) custom-call(bf16[640,512]{1,0:T(8,128)(2,1)S(1)} %get-tuple-element.17.refs_0_, f32[640,512]{1,0:T(8,128)S(1)} %get-tuple-element.19.refs_1_, f32[640,512]{1,0:T(8,128)S(1)} %get-tuple-element.20.refs_2_, f32[640,512]{1,0:T(8,128)S(1)} %get-tuple-element.21.refs_3_, ...), custom_call_target="tpu_custom_call" | custom-call | flops 1 | bytes 1 | tf_op jit(solution)/shard_map/add_stage/pallas_call | solution.py:289
  10.5 0.8 %collective-permute-done.1.refs_9_ = bf16[256,256]{1,0:T(8,128)(2,1)S(1)} collective-permute-done((bf16[256,256]{1,0:T(8,128)(2,1)}, bf16[256,256]{1,0:T(8,128)(2,1)S(1)}, u32[]{:S(2)}, u32[]{:S(2)}) %collective-permute-start.1) | collective-permute-done | bytes 131104 | tf_op jit(solution)/shard_map/ppermute | solution.py:263
  11.3 0.0 collective-permute-start.3
  11.3 0.0 collective-permute-done.2.refs_4_.refs_7_
  11.3 0.9 %add_stage.3 = (f32[640,512]{1,0:T(8,128)S(1)}, f32[640,512]{1,0:T(8,128)S(1)}) custom-call(bf16[640,512]{1,0:T(8,128)(2,1)S(1)} %get-tuple-element.17.refs_0_, f32[640,512]{1,0:T(8,128)S(1)} %get-tuple-element.19.refs_1_, f32[640,512]{1,0:T(8,128)S(1)} %get-tuple-element.24.refs_2_, f32[640,512]{1,0:T(8,128)S(1)} %get-tuple-element.25.refs_3_, ...), custom_call_target="tpu_custom_call" | custom-call | flops 1 | bytes 1 | tf_op jit(solution)/shard_map/add_stage/pallas_call | solution.py:289
  12.2 0.4 %collective-permute-done.3.refs_8_ = bf16[256,256]{1,0:T(8,128)(2,1)S(1)} collective-permute-done((bf16[256,256]{1,0:T(8,128)(2,1)S(1)}, bf16[256,256]{1,0:T(8,128)(2,1)S(1)}, u32[]{:S(2)}, u32[]{:S(2)}) %collective-permute-start.3) | collective-permute-done | bytes 131104 | tf_op jit(solution)/shard_map/ppermute | solution.py:302
  12.6 11.7 %last_stage.1 = bf16[640,512]{1,0:T(8,128)(2,1)} custom-call(bf16[640,512]{1,0:T(8,128)(2,1)S(1)} %get-tuple-element.17.refs_0_, f32[640,512]{1,0:T(8,128)S(1)} %get-tuple-element.19.refs_1_, f32[640,512]{1,0:T(8,128)S(1)} %get-tuple-element.20.refs_2_, f32[640,512]{1,0:T(8,128)S(1)} %get-tuple-element.21.refs_3_, f32[640,512]{1,0:T(8,128)S(1)} %get-tuple-element.26.refs_4_, ...), custom_call_target="tpu_custom_call" | custom-call | flops 1 | bytes 1 | tf_op jit(solution)/shard_map/last_stage/pallas_call | solution.py:314
Async XLA Ops:
  0.0 9.5 %collective-permute-start = (bf16[256,256]{1,0:T(8,128)(2,1)}, bf16[256,256]{1,0:T(8,128)(2,1)S(1)}, u32[]{:S(2)}, u32[]{:S(2)}) collective-permute-start(bf16[256,256]{1,0:T(8,128)(2,1)} %bitcast.3), channel_id=1, source_target_pairs={{0,5},{1,12},{4,1},{5,8},{8,13},{9,4},{12,9},{13,0},{2,7},{3,14},{... | collective-permute-start | bytes 393224 | tf_op jit(solution)/shard_map/ppermute | solution.py:255
  2.5 8.8 %collective-permute-start.1 = (bf16[256,256]{1,0:T(8,128)(2,1)}, bf16[256,256]{1,0:T(8,128)(2,1)S(1)}, u32[]{:S(2)}, u32[]{:S(2)}) collective-permute-start(bf16[256,256]{1,0:T(8,128)(2,1)} %bitcast.4), channel_id=1, source_target_pairs={{0,1},{1,8},{4,5},{5,12},{8,9},{9,0},{12,13},{13,4},{2,3},{3,10},{... | collective-permute-start | bytes 393224 | tf_op jit(solution)/shard_map/ppermute | solution.py:263
  9.5 1.8 %collective-permute-start.2 = (bf16[256,256]{1,0:T(8,128)(2,1)S(1)}, bf16[256,256]{1,0:T(8,128)(2,1)S(1)}, u32[]{:S(2)}, u32[]{:S(2)}) collective-permute-start(bf16[256,256]{1,0:T(8,128)(2,1)S(1)} %collective-permute-done.refs_4_.refs_6_), channel_id=1, source_target_pairs={{0,1},{1,0},{4,5},{5,4},{8,9},{9,8},{12,13},{13,12},{2,3},{3,2},{6... | collective-permute-start | bytes 393224 | tf_op jit(solution)/shard_map/ppermute | solution.py:302
  11.3 1.3 %collective-permute-start.3 = (bf16[256,256]{1,0:T(8,128)(2,1)S(1)}, bf16[256,256]{1,0:T(8,128)(2,1)S(1)}, u32[]{:S(2)}, u32[]{:S(2)}) collective-permute-start(bf16[256,256]{1,0:T(8,128)(2,1)S(1)} %collective-permute-done.1.refs_9_), channel_id=1, source_target_pairs={{0,1},{1,0},{4,5},{5,4},{8,9},{9,8},{12,13},{13,12},{2,3},{3,2},{6... | collective-permute-start | bytes 393224 | tf_op jit(solution)/shard_map/ppermute | solution.py:302

commit v17 on v12

--- a/solution.py
+++ b/solution.py
@@ -12,6 +12,7 @@
 AG_DEV = 2
 MAXLEN = 320
 BLK = 128
+FOUR = 4
 
 masked_score = -1e30
 empty_best = 1e30
@@ -128,20 +129,38 @@
     return [slice(first, first + step) for first in range(0, count, step)]
 
 
-def add_stage(*refs):
+def place():
+    return lax.rem(lax.axis_index("loop"), FOUR), lax.axis_index("pair")
+
+
+def penalty(is_there):
+    return jnp.where(is_there, 0.0, empty_best)
+
+
+def add_stage(by_swap, *refs):
     query_ref, best_ref, total_ref, sum_ref = refs[:4]
     shard_refs = refs[4:-2]
     total_out, sum_out = refs[-2:]
     heads = query_ref.shape[1] // HD
     shard = jnp.concatenate([ref[...] for ref in shard_refs], axis=0)
     key_rows, value_rows = shard[:, :HD], with_ones(shard[:, HD:])
+    extra = None
+    if by_swap is not None:
+        position, core = place()
+        extra = penalty((position != 1) | (core == int(by_swap)))
 
     def start(rows):
         return scores_of(stacked(query_ref, rows, heads), key_rows)
 
     def finish(index, rows, scores):
         best = stacked(best_ref, rows, heads)
-        weights = jnp.exp2(scores - widen(best, scores.shape[1])).astype(jnp.bfloat16)
+        if extra is None:
+            points = widen(best, scores.shape[1])
+        else:
+            held = shard_refs[-1].shape[0]
+            points = [best] * ((scores.shape[1] - held) // HD) + [best + extra] * (held // HD)
+            points = jnp.concatenate(points, axis=1)
+        weights = jnp.exp2(scores - points).astype(jnp.bfloat16)
         result = jnp.dot(weights, value_rows, preferred_element_type=jnp.float32)
         unstack(total_out, rows, heads, stacked(total_ref, rows, heads) + result[:, HD:])
         unstack(sum_out, rows, heads, stacked(sum_ref, rows, heads) + result[:, :HD])
@@ -149,13 +168,14 @@
     staged(row_blocks(query_ref.shape[0], 80), start, finish)
 
 
-def last_stage(earlier_count, last_count, *refs):
+def last_stage(routed, *refs):
     query_ref, best_ref, old_total_ref, old_sum_ref, total_ref, sum_ref = refs[:6]
-    earlier_refs = refs[6 : 6 + earlier_count]
-    last_refs = refs[6 + earlier_count : 6 + earlier_count + last_count]
-    out_hbm, out_ref, out_sems = refs[6 + earlier_count + last_count :]
+    earlier_refs, refs = refs[6:-6], refs[-6:]
+    direct_ref, swapped_ref, out_hbm, out_ref, trusted_ref, out_sems = refs
     heads = query_ref.shape[1] // HD
     blocks = row_blocks(query_ref.shape[0], 80)
+    position, core = place()
+    takes_both = (position == 1) & routed
 
     def out_copy(index, rows):
         return pltpu.make_async_copy(out_ref.at[rows], out_hbm.at[rows], out_sems.at[index])
@@ -163,32 +183,51 @@
     def write(rows, total, weighted):
         unstack(out_ref, rows, heads, (weighted / total).astype(jnp.bfloat16))
 
-    shard = jnp.concatenate([ref[...] for ref in last_refs], axis=0)
-    trusted = [jnp.full((8, HD), True)]
-
-    def start(rows):
-        return scores_of(stacked(query_ref, rows, heads), shard[:, :HD])
-
-    def finish(index, rows, scores):
-        best = stacked(best_ref, rows, heads)
-        weights = jnp.exp2(scores - widen(best, scores.shape[1]))
-        lanes = sum(weights[:, i : i + HD] for i in range(0, scores.shape[1], HD))
-        total = stacked(total_ref, rows, heads) + jnp.sum(lanes, axis=1, keepdims=True)
-        weighted = stacked(sum_ref, rows, heads) + jnp.dot(
-            weights.astype(jnp.bfloat16), shard[:, HD:], preferred_element_type=jnp.float32
-        )
-        good = (total < total_limit).reshape(total.shape[0] // 8, 8, HD)
-        trusted[0] = trusted[0] & jnp.all(good, axis=0)
-        write(rows, total, weighted)
-        out_copy(index, rows).start()
-
-    staged(blocks, start, finish)
-    for index, rows in enumerate(blocks):
-        out_copy(index, rows).wait()
-
-    @pl.when(jnp.logical_not(jnp.all(trusted[0])))
+    def process(shard):
+        trusted = [jnp.full((8, HD), True)]
+
+        def start(rows):
+            return scores_of(stacked(query_ref, rows, heads), shard[:, :HD])
+
+        def finish(index, rows, scores):
+            best = stacked(best_ref, rows, heads)
+            weights = jnp.exp2(scores - widen(best, scores.shape[1]))
+            lanes = sum(weights[:, i : i + HD] for i in range(0, scores.shape[1], HD))
+            total = stacked(total_ref, rows, heads) + jnp.sum(lanes, axis=1, keepdims=True)
+            weighted = stacked(sum_ref, rows, heads) + jnp.dot(
+                weights.astype(jnp.bfloat16), shard[:, HD:], preferred_element_type=jnp.float32
+            )
+            good = (total < total_limit).reshape(total.shape[0] // 8, 8, HD)
+            trusted[0] = trusted[0] & jnp.all(good, axis=0)
+            write(rows, total, weighted)
+            out_copy(index, rows).start()
+
+        staged(blocks, start, finish)
+        trusted_ref[0] = jnp.all(trusted[0]).astype(jnp.int32)
+        for index, rows in enumerate(blocks):
+            out_copy(index, rows).wait()
+
+    @pl.when(jnp.logical_not(takes_both))
+    def one_shard():
+        process(jnp.where(core == 0, direct_ref[...], swapped_ref[...]))
+
+    @pl.when(takes_both)
+    def two_shards():
+        process(jnp.concatenate([direct_ref[...], swapped_ref[...]], axis=0))
+
+    @pl.when(trusted_ref[0] == 0)
     def exact_maximum():
         size = query_ref.shape[0] // len(blocks)
+        counted = [(ref, 0.0) for ref in earlier_refs]
+        if routed:
+            counted[-2:] = [
+                (ref, penalty((position != 1) | (core == by_swap)))
+                for by_swap, ref in enumerate(earlier_refs[-2:])
+            ]
+        counted += [
+            (ref, penalty(takes_both | (core == by_swap)))
+            for by_swap, ref in enumerate([direct_ref, swapped_ref])
+        ]
 
         def visit(index, unused):
             rows = pl.ds(pl.multiple_of(index * size, size), size)
@@ -196,9 +235,9 @@
             best = stacked(best_ref, rows, heads)
             weighted = stacked(old_sum_ref, rows, heads)
             total = stacked(old_total_ref, rows, heads)
-            for shard_ref in earlier_refs + last_refs:
+            for shard_ref, extra in counted:
                 key_rows, value_rows = shard_ref[:, :HD], with_ones(shard_ref[:, HD:])
-                scores = scores_of(queries, key_rows)
+                scores = scores_of(queries, key_rows) - extra
                 new_best = jnp.maximum(best, jnp.max(scores, axis=1, keepdims=True))
                 factor = jnp.exp2(best - new_best)
                 weights = jnp.exp2(scores - widen(new_best, scores.shape[1]))
@@ -225,19 +264,41 @@
     suffix = suffix_kv[:, 0, :]
     shard_rows = own.shape[0]
 
-    power_of_two = loop_size & (loop_size - 1) == 0
-
-    def exchange(shard, step_of_core):
+    routed = loop_size >= FOUR and loop_size & (loop_size - 1) == 0
+
+    def send(shard, route):
         hops = []
-        for core, step in enumerate(step_of_core):
-            for i in range(loop_size):
-                to = i ^ step if power_of_two else (i + step) % loop_size
-                hops.append((2 * i + core, 2 * to + core))
+        for i in range(loop_size):
+            for core in range(2):
+                to, to_core = route(i, core)
+                hops.append((2 * i + core, 2 * to + to_core))
         return lax.ppermute(shard, ("loop", "pair"), hops)
 
-    to_both = 1 - loop_size % 2
-    both = [exchange(own, (1, 1))] * to_both
-    middle = [exchange(own, (step, step + 1)) for step in range(1 + to_both, loop_size, 2)]
+    def first_route(i, core):
+        position, base = i % FOUR, i - i % FOUR
+        if core == 0:
+            return {0: (i + 1, 0), 1: (i, 1)}.get(position, (i ^ 1, 1))
+        return {2: (base, 0), 3: (base, 1)}.get(position, (i ^ 3, 0))
+
+    def second_route(i, core):
+        position, base = i % FOUR, i - i % FOUR
+        if core == 0:
+            return (base, 0) if position == 1 else (i, 1)
+        return {2: (base + 1, 0), 3: (base + 1, 1)}.get(position, (i ^ 2, 0))
+
+    if routed:
+        early = [
+            send(own, lambda i, core, step=step: (i ^ (step + core), 1 - core))
+            for step in range(FOUR, loop_size, 2)
+        ]
+        early.append(send(own, first_route))
+        final = send(own, second_route)
+    else:
+        early = [
+            send(own, lambda i, core, step=step: ((i + step) % loop_size, core))
+            for step in range(1, loop_size)
+        ]
+        final = early.pop()
     in_hbm = pl.BlockSpec(memory_space=pltpu.HBM)
     in_vmem = pl.BlockSpec(memory_space=pltpu.VMEM)
     state = jax.ShapeDtypeStruct((slots, width), jnp.float32)
@@ -260,11 +321,11 @@
         compiler_params=pltpu.CompilerParams(vmem_limit_bytes=24 * 2**20),
         cost_estimate=cost,
     )(*(pltpu.with_memory_space_constraint(x, pltpu.HBM) for x in (lengths, queries, suffix, own)))
-    def add_shards(total, weighted, shards_now):
+    def add_shards(total, weighted, shards_now, by_swap):
         if not shards_now:
             return total, weighted
         return pl.pallas_call(
-            add_stage,
+            functools.partial(add_stage, by_swap if routed else None),
             name="add_stage",
             out_shape=[state] * 2,
             in_specs=[in_vmem] * (4 + len(shards_now)),
@@ -273,20 +334,27 @@
             cost_estimate=cost,
         )(queries, best, total, weighted, *shards_now)
 
-    middle, best = lax.optimization_barrier((middle, best))
-    swap = [(p, p ^ 1) for p in range(2 * loop_size)]
-    last = [lax.ppermute(shard, ("loop", "pair"), swap) for shard in middle]
-    new_total, new_weighted = add_shards(total, weighted, middle)
+    def swapped(shard):
+        return send(shard, lambda i, core: (i, 1 - core))
+
+    early, best = lax.optimization_barrier((early, best))
+    early_swapped = [swapped(shard) for shard in early] if routed else []
+    new_total, new_weighted = add_shards(total, weighted, early, False)
+    final, new_total = lax.optimization_barrier((final, new_total))
+    final_swapped = swapped(final) if routed else final
+    new_total, new_weighted = add_shards(new_total, new_weighted, early_swapped, True)
     last_inputs = (queries, best, total, weighted, new_total, new_weighted)
-    last_inputs += (*middle, *last, *both)
+    last_inputs += (*early[:-1], *early_swapped[:-1], *early[-1:], *early_swapped[-1:])
+    last_inputs += (final, final_swapped)
     return pl.pallas_call(
-        functools.partial(last_stage, len(middle), len(last) + len(both)),
+        functools.partial(last_stage, routed),
         name="last_stage",
         out_shape=jax.ShapeDtypeStruct((slots, width), jnp.bfloat16),
         in_specs=[in_vmem] * len(last_inputs),
         out_specs=in_hbm,
         scratch_shapes=[
             pltpu.VMEM((slots, width), jnp.bfloat16),
+            pltpu.SMEM((1,), jnp.int32),
             pltpu.SemaphoreType.DMA((len(row_blocks(slots, 80)),)),
         ],
         compiler_params=pltpu.CompilerParams(vmem_limit_bytes=32 * 2**20),

time: 24.8 us -> 24.6 us (level)
  waiting for transfers between devices: 1.32 us -> 0.09 us
  Pallas kernels: 17.7 us -> 18.5 us
    ppermute x3 -> x4, waiting for transfers between devices: 1.32 us -> 0.09 us  [send(): return lax.ppermute(shard, ('loop', 'pair'), hops)]
    pallas_call x2 -> x3, Pallas kernels: 13.4 us -> 14.2 us  [the longest x1 12.4 us: shards(): pl.pallas_call(functools.partial(last_stage, routed), name='last_stage',...]
    ppermute x3 -> x4, starting transfers between devices: 5.62 us -> 5.79 us  [send(): return lax.ppermute(shard, ('loop', 'pair'), hops)]
  transfers between devices with their start and end apart: 3 -> 4, of which waited for: 2 -> 1; matrix products, arithmetic and copies ran while one was open for 0% -> 0% of each run, Pallas kernels for 21% -> 25%
where the time goes in v17:
time: 24.6 us; the launch traced here: 24.4 us
  Pallas kernels  18.5 us (75%)
  starting transfers between devices  5.79 us (24%)
    pallas_call x1, Pallas kernels, shards(): pl.pallas_call(functools.partial(last_stage, routed), name='last_stage',...  12.4 us
    ppermute x4, starting transfers between devices, send(): return lax.ppermute(shard, ('loop', 'pair'), hops)  5.79 us
    pallas_call x1, Pallas kernels, shards(): pl.pallas_call(local_stage, name='local_stage', out_shape=[state] * 3 + [...  4.31 us
    pallas_call x2, Pallas kernels, add_shards(): pl.pallas_call(functools.partial(add_stage, by_swap if routed else None),...  1.8 us
  transfers between devices with their start and end apart: 4, of which 1 were waited for; matrix products, arithmetic and copies ran while one was open for 0% of the time, Pallas kernels for 25%

profile of v17, /device:TPU:0, one launch (start us, length us, event | category | flops | bytes accessed | tf_op | source)
XLA Modules:
  0.0 24.4 jit_solution(2047277502288315532)
XLA Ops:
  0.0 3.0 %collective-permute-start = (bf16[256,256]{1,0:T(8,128)(2,1)}, bf16[256,256]{1,0:T(8,128)(2,1)S(1)}, u32[]{:S(2)}, u32[]{:S(2)}) collective-permute-start(bf16[256,256]{1,0:T(8,128)(2,1)} %bitcast.3), channel_id=1, source_target_pairs={{0,4},{1,12},{4,5},{5,8},{8,13},{9,0},{12,9},{13,1},{2,6},{3,14},{... | collective-permute-start | bytes 393224 | tf_op jit(solution)/shard_map/ppermute | solution.py:275
  3.0 2.1 %collective-permute-start.1 = (bf16[256,256]{1,0:T(8,128)(2,1)}, bf16[256,256]{1,0:T(8,128)(2,1)S(1)}, u32[]{:S(2)}, u32[]{:S(2)}) collective-permute-start(bf16[256,256]{1,0:T(8,128)(2,1)} %bitcast.4), channel_id=1, source_target_pairs={{0,1},{1,8},{4,0},{5,12},{8,9},{9,4},{12,13},{13,5},{2,3},{3,10},{... | collective-permute-start | bytes 393224 | tf_op jit(solution)/shard_map/ppermute | solution.py:275
  5.2 4.3 %local_stage.1 = (f32[640,512]{1,0:T(8,128)S(1)}, f32[640,512]{1,0:T(8,128)S(1)}, f32[640,512]{1,0:T(8,128)S(1)}, bf16[640,512]{1,0:T(8,128)(2,1)S(1)}) custom-call(s32[8]{0:T(128)} %lengths_hbm.1, bf16[640,512]{1,0:T(8,128)(2,1)} %query_hbm.1, bf16[640,256]{1,0:T(8,128)(2,1)} %bitcast.2, bf16[256,256]{1,0:T(8,128)(2,1)} %bitcast.5), custom_call_target="tpu_custom_call" | custom-call | flops 1 | bytes 1 | tf_op jit(solution)/shard_map/local_stage/pallas_call | solution.py:308
  9.5 0.0 collective-permute-done.refs_4_.refs_6_
  9.5 0.1 collective-permute-start.2
  9.6 0.9 %add_stage.2 = (f32[640,512]{1,0:T(8,128)S(1)}, f32[640,512]{1,0:T(8,128)S(1)}) custom-call(bf16[640,512]{1,0:T(8,128)(2,1)S(1)} %get-tuple-element.17.refs_0_, f32[640,512]{1,0:T(8,128)S(1)} %get-tuple-element.19.refs_1_, f32[640,512]{1,0:T(8,128)S(1)} %get-tuple-element.20.refs_2_, f32[640,512]{1,0:T(8,128)S(1)} %get-tuple-element.21.refs_3_, ...), custom_call_target="tpu_custom_call" | custom-call | flops 1 | bytes 1 | tf_op jit(solution)/shard_map/add_stage/pallas_call | solution.py:327
  10.5 0.0 collective-permute-done.1.refs_8_
  10.5 0.6 %collective-permute-start.3 = (bf16[256,256]{1,0:T(8,128)(2,1)S(1)}, bf16[256,256]{1,0:T(8,128)(2,1)S(1)}, u32[]{:S(2)}, u32[]{:S(2)}) collective-permute-start(bf16[256,256]{1,0:T(8,128)(2,1)S(1)} %collective-permute-done.1.refs_8_), channel_id=1, source_target_pairs={{0,1},{1,0},{4,5},{5,4},{8,9},{9,8},{12,13},{13,12},{2,3},{3,2},{6... | collective-permute-start | bytes 393224 | tf_op jit(solution)/shard_map/ppermute | solution.py:275
  11.1 0.0 collective-permute-done.2.refs_4_.refs_7_
  11.1 0.9 %add_stage.3 = (f32[640,512]{1,0:T(8,128)S(1)}, f32[640,512]{1,0:T(8,128)S(1)}) custom-call(bf16[640,512]{1,0:T(8,128)(2,1)S(1)} %get-tuple-element.17.refs_0_, f32[640,512]{1,0:T(8,128)S(1)} %get-tuple-element.19.refs_1_, f32[640,512]{1,0:T(8,128)S(1)} %get-tuple-element.24.refs_2_, f32[640,512]{1,0:T(8,128)S(1)} %get-tuple-element.25.refs_3_, ...), custom_call_target="tpu_custom_call" | custom-call | flops 1 | bytes 1 | tf_op jit(solution)/shard_map/add_stage/pallas_call | solution.py:327
  12.0 0.1 collective-permute-done.3.refs_9_
  12.0 12.4 %last_stage.1 = bf16[640,512]{1,0:T(8,128)(2,1)} custom-call(bf16[640,512]{1,0:T(8,128)(2,1)S(1)} %get-tuple-element.17.refs_0_, f32[640,512]{1,0:T(8,128)S(1)} %get-tuple-element.19.refs_1_, f32[640,512]{1,0:T(8,128)S(1)} %get-tuple-element.20.refs_2_, f32[640,512]{1,0:T(8,128)S(1)} %get-tuple-element.21.refs_3_, f32[640,512]{1,0:T(8,128)S(1)} %get-tuple-element.26.refs_4_, ...), custom_call_target="tpu_custom_call" | custom-call | flops 1 | bytes 1 | tf_op jit(solution)/shard_map/last_stage/pallas_call | solution.py:349
Async XLA Ops:
  0.0 9.5 %collective-permute-start = (bf16[256,256]{1,0:T(8,128)(2,1)}, bf16[256,256]{1,0:T(8,128)(2,1)S(1)}, u32[]{:S(2)}, u32[]{:S(2)}) collective-permute-start(bf16[256,256]{1,0:T(8,128)(2,1)} %bitcast.3), channel_id=1, source_target_pairs={{0,4},{1,12},{4,5},{5,8},{8,13},{9,0},{12,9},{13,1},{2,6},{3,14},{... | collective-permute-start | bytes 393224 | tf_op jit(solution)/shard_map/ppermute | solution.py:275
  3.0 7.5 %collective-permute-start.1 = (bf16[256,256]{1,0:T(8,128)(2,1)}, bf16[256,256]{1,0:T(8,128)(2,1)S(1)}, u32[]{:S(2)}, u32[]{:S(2)}) collective-permute-start(bf16[256,256]{1,0:T(8,128)(2,1)} %bitcast.4), channel_id=1, source_target_pairs={{0,1},{1,8},{4,0},{5,12},{8,9},{9,4},{12,13},{13,5},{2,3},{3,10},{... | collective-permute-start | bytes 393224 | tf_op jit(solution)/shard_map/ppermute | solution.py:275
  9.5 1.6 %collective-permute-start.2 = (bf16[256,256]{1,0:T(8,128)(2,1)S(1)}, bf16[256,256]{1,0:T(8,128)(2,1)S(1)}, u32[]{:S(2)}, u32[]{:S(2)}) collective-permute-start(bf16[256,256]{1,0:T(8,128)(2,1)S(1)} %collective-permute-done.refs_4_.refs_6_), channel_id=1, source_target_pairs={{0,1},{1,0},{4,5},{5,4},{8,9},{9,8},{12,13},{13,12},{2,3},{3,2},{6... | collective-permute-start | bytes 393224 | tf_op jit(solution)/shard_map/ppermute | solution.py:275
  10.5 1.5 %collective-permute-start.3 = (bf16[256,256]{1,0:T(8,128)(2,1)S(1)}, bf16[256,256]{1,0:T(8,128)(2,1)S(1)}, u32[]{:S(2)}, u32[]{:S(2)}) collective-permute-start(bf16[256,256]{1,0:T(8,128)(2,1)S(1)} %collective-permute-done.1.refs_8_), channel_id=1, source_target_pairs={{0,1},{1,0},{4,5},{5,4},{8,9},{9,8},{12,13},{13,12},{2,3},{3,2},{6... | collective-permute-start | bytes 393224 | tf_op jit(solution)/shard_map/ppermute | solution.py:275

commit v18 on v17

--- a/solution.py
+++ b/solution.py
@@ -47,69 +47,80 @@
     return jnp.concatenate([row_value] * (width // HD), axis=1)
 
 
-def local_stage(
+def load_blocks(count):
+    return [pl.ds(first, BLK) for first in range(0, count, BLK)]
+
+
+def load_stage(
     lengths_hbm,
     query_hbm,
     suffix_hbm,
     own_hbm,
-    best_ref,
-    total_ref,
-    sum_ref,
     query_ref,
-    lengths_ref,
     suffix_ref,
     own_ref,
-    whole_sems,
-    block_sems,
+    first_ref,
+    lengths_ref,
+    sems,
 ):
-    rows_all = query_ref.shape[0]
+    pairs = [(lengths_hbm, lengths_ref), (own_hbm, own_ref)]
+    for source, target in ((query_hbm, query_ref), (suffix_hbm, suffix_ref)):
+        for rows in load_blocks(target.shape[0]):
+            pairs.append((source.at[rows], target.at[rows]))
+    copies = [
+        pltpu.make_async_copy(source, target, sems.at[i])
+        for i, (source, target) in enumerate(pairs)
+    ]
+    for copy in copies:
+        copy.start()
+    copies[0].wait()
+    slots = query_ref.shape[0]
+    position = lax.axis_index("loop")
+    row_at = lax.broadcasted_iota(jnp.int32, first_ref.shape, 0)
+    first = jnp.zeros_like(row_at)
+    agent_end = 0
+    for agent in range(AG_DEV):
+        agent_end = agent_end + lengths_ref[position * AG_DEV + agent]
+        first = jnp.where(row_at >= agent_end, agent_end if agent + 1 < AG_DEV else slots, first)
+    first_ref[...] = first
+    for copy in copies[1:]:
+        copy.wait()
+
+
+def local_stage(query_ref, suffix_ref, own_ref, first_ref, best_ref, total_ref, sum_ref):
+    slots = query_ref.shape[0]
     heads = query_ref.shape[1] // HD
-    blocks = rows_all // BLK
-    whole = [
-        pltpu.make_async_copy(source, target, whole_sems.at[i])
-        for i, (source, target) in enumerate(
-            [(lengths_hbm, lengths_ref), (own_hbm, own_ref), (suffix_hbm, suffix_ref)]
-        )
-    ]
-    pieces = [
-        pltpu.make_async_copy(
-            query_hbm.at[pl.ds(block * BLK, BLK)],
-            query_ref.at[pl.ds(block * BLK, BLK)],
-            block_sems.at[block],
-        )
-        for block in range(blocks)
-    ]
-    for copy in whole + pieces:
-        copy.start()
-    for copy in whole + pieces:
-        copy.wait()
-    position = lax.axis_index("loop")
+    own_keys = own_ref[:, :HD]
+    own_values = with_ones(own_ref[:, HD:])
     window = BLK * ((MAXLEN + BLK - 2) // BLK) + BLK
-    for block in range(blocks):
+    for block in range(slots // BLK):
         stop = (block + 1) * BLK
         start = max(0, stop - window)
         rows = slice(block * BLK, stop)
         row_at = block * BLK + lax.broadcasted_iota(jnp.int32, (BLK, stop - start), 0)
         key_at = start + lax.broadcasted_iota(jnp.int32, (BLK, stop - start), 1)
-        first = jnp.zeros_like(row_at)
-        agent_end = 0
-        for agent in range(AG_DEV):
-            agent_end = agent_end + lengths_ref[position * AG_DEV + agent]
-            first = jnp.where(row_at >= agent_end, agent_end, first)
-        allowed = (key_at <= row_at) & (key_at >= first)
+        first = first_ref[rows]
+        allowed = (key_at <= row_at) & (key_at >= widen(first, stop - start))
         queries = stacked(query_ref, rows, heads)
-        shard = jnp.concatenate([own_ref[...], suffix_ref[start:stop]], axis=0)
-        scores = scores_of(queries, shard[:, :HD])
-        own_scores = scores[:, : own_ref.shape[0]]
+        own_scores = scores_of(queries, own_keys)
         suffix_scores = jnp.where(
-            jnp.concatenate([allowed] * heads, axis=0), scores[:, own_ref.shape[0] :], masked_score
+            jnp.concatenate([allowed] * heads, axis=0),
+            scores_of(queries, suffix_ref[start:stop, :HD]),
+            masked_score,
         )
-        scores = jnp.concatenate([own_scores, suffix_scores], axis=1)
-        best = jnp.max(scores, axis=1, keepdims=True)
-        weights = jnp.exp2(scores - best).astype(jnp.bfloat16)
-        result = jnp.dot(weights, with_ones(shard[:, HD:]), preferred_element_type=jnp.float32)
-        row_at = block * BLK + lax.broadcasted_iota(jnp.int32, (BLK, HD), 0)
-        live = jnp.concatenate([row_at < agent_end] * heads, axis=0)
+        best = jnp.maximum(
+            jnp.max(own_scores, axis=1, keepdims=True),
+            jnp.max(suffix_scores, axis=1, keepdims=True),
+        )
+        own_weights = jnp.exp2(own_scores - best).astype(jnp.bfloat16)
+        suffix_weights = jnp.exp2(suffix_scores - best).astype(jnp.bfloat16)
+        result = jnp.dot(own_weights, own_values, preferred_element_type=jnp.float32)
+        result = result + jnp.dot(
+            suffix_weights,
+            with_ones(suffix_ref[start:stop, HD:]),
+            preferred_element_type=jnp.float32,
+        )
+        live = jnp.concatenate([first < slots] * heads, axis=0)
         unstack(best_ref, rows, heads, jnp.where(live, best, empty_best))
         unstack(sum_ref, rows, heads, jnp.where(live, result[:, :HD], 0.0))
         unstack(total_ref, rows, heads, jnp.where(live, result[:, HD:], 1.0))
@@ -130,7 +141,7 @@
 
 
 def place():
-    return lax.rem(lax.axis_index("loop"), FOUR), lax.axis_index("pair")
+    return lax.rem(lax.axis_index("loop"), 2) == 1, lax.axis_index("pair")
 
 
 def penalty(is_there):
@@ -146,8 +157,8 @@
     key_rows, value_rows = shard[:, :HD], with_ones(shard[:, HD:])
     extra = None
     if by_swap is not None:
-        position, core = place()
-        extra = penalty((position != 1) | (core == int(by_swap)))
+        is_odd, core = place()
+        extra = penalty(jnp.logical_not(is_odd) | (core == int(by_swap)))
 
     def start(rows):
         return scores_of(stacked(query_ref, rows, heads), key_rows)
@@ -174,8 +185,8 @@
     direct_ref, swapped_ref, out_hbm, out_ref, trusted_ref, out_sems = refs
     heads = query_ref.shape[1] // HD
     blocks = row_blocks(query_ref.shape[0], 80)
-    position, core = place()
-    takes_both = (position == 1) & routed
+    is_odd, core = place()
+    takes_both = is_odd & routed
 
     def out_copy(index, rows):
         return pltpu.make_async_copy(out_ref.at[rows], out_hbm.at[rows], out_sems.at[index])
@@ -221,7 +232,7 @@
         counted = [(ref, 0.0) for ref in earlier_refs]
         if routed:
             counted[-2:] = [
-                (ref, penalty((position != 1) | (core == by_swap)))
+                (ref, penalty(jnp.logical_not(is_odd) | (core == by_swap)))
                 for by_swap, ref in enumerate(earlier_refs[-2:])
             ]
         counted += [
@@ -275,23 +286,47 @@
         return lax.ppermute(shard, ("loop", "pair"), hops)
 
     def first_route(i, core):
-        position, base = i % FOUR, i - i % FOUR
-        if core == 0:
-            return {0: (i + 1, 0), 1: (i, 1)}.get(position, (i ^ 1, 1))
-        return {2: (base, 0), 3: (base, 1)}.get(position, (i ^ 3, 0))
+        if core == 1:
+            return (i ^ 2) & ~1, i & 1
+        return (i, 1) if i & 1 else (i + 1, 0)
 
     def second_route(i, core):
-        position, base = i % FOUR, i - i % FOUR
-        if core == 0:
-            return (base, 0) if position == 1 else (i, 1)
-        return {2: (base + 1, 0), 3: (base + 1, 1)}.get(position, (i ^ 2, 0))
-
+        if core == 1:
+            return (i ^ 2) | 1, i & 1
+        return (i - 1, 0) if i & 1 else (i, 1)
+
+    early = []
     if routed:
         early = [
             send(own, lambda i, core, step=step: (i ^ (step + core), 1 - core))
             for step in range(FOUR, loop_size, 2)
         ]
         early.append(send(own, first_route))
+    in_hbm = pl.BlockSpec(memory_space=pltpu.HBM)
+    in_vmem = pl.BlockSpec(memory_space=pltpu.VMEM)
+    state = jax.ShapeDtypeStruct((slots, width), jnp.float32)
+
+    cost = pl.CostEstimate(flops=1, bytes_accessed=1, transcendentals=0)
+
+    queries, suffix, own, first = pl.pallas_call(
+        load_stage,
+        name="load_stage",
+        out_shape=[
+            jax.ShapeDtypeStruct(queries.shape, queries.dtype),
+            jax.ShapeDtypeStruct(suffix.shape, suffix.dtype),
+            jax.ShapeDtypeStruct(own.shape, own.dtype),
+            jax.ShapeDtypeStruct((slots, HD), jnp.int32),
+        ],
+        in_specs=[in_hbm] * 4,
+        out_specs=[in_vmem] * 4,
+        scratch_shapes=[
+            pltpu.SMEM(lengths.shape, lengths.dtype),
+            pltpu.SemaphoreType.DMA((2 + 2 * len(load_blocks(slots)),)),
+        ],
+        compiler_params=pltpu.CompilerParams(vmem_limit_bytes=8 * 2**20),
+        cost_estimate=cost,
+    )(*(pltpu.with_memory_space_constraint(x, pltpu.HBM) for x in (lengths, queries, suffix, own)))
+    if routed:
         final = send(own, second_route)
     else:
         early = [
@@ -299,28 +334,16 @@
             for step in range(1, loop_size)
         ]
         final = early.pop()
-    in_hbm = pl.BlockSpec(memory_space=pltpu.HBM)
-    in_vmem = pl.BlockSpec(memory_space=pltpu.VMEM)
-    state = jax.ShapeDtypeStruct((slots, width), jnp.float32)
-
-    cost = pl.CostEstimate(flops=1, bytes_accessed=1, transcendentals=0)
-
-    best, total, weighted, queries = pl.pallas_call(
+    best, total, weighted = pl.pallas_call(
         local_stage,
         name="local_stage",
-        out_shape=[state] * 3 + [jax.ShapeDtypeStruct((slots, width), queries.dtype)],
-        in_specs=[in_hbm] * 4,
-        out_specs=[in_vmem] * 4,
-        scratch_shapes=[
-            pltpu.SMEM(lengths.shape, lengths.dtype),
-            pltpu.VMEM(suffix.shape, suffix.dtype),
-            pltpu.VMEM(own.shape, own.dtype),
-            pltpu.SemaphoreType.DMA((3,)),
-            pltpu.SemaphoreType.DMA((slots // BLK,)),
-        ],
+        out_shape=[state] * 3,
+        in_specs=[in_vmem] * 4,
+        out_specs=[in_vmem] * 3,
         compiler_params=pltpu.CompilerParams(vmem_limit_bytes=24 * 2**20),
         cost_estimate=cost,
-    )(*(pltpu.with_memory_space_constraint(x, pltpu.HBM) for x in (lengths, queries, suffix, own)))
+    )(queries, suffix, own, first)
+
     def add_shards(total, weighted, shards_now, by_swap):
         if not shards_now:
             return total, weighted

time: 24.6 us -> 24.5 us (level)
  starting transfers between devices: 5.79 us -> 5.37 us
  waiting for transfers between devices: 0.09 us -> 0.43 us
    ppermute x4, starting transfers between devices: 5.79 us -> 5.37 us  [send(): return lax.ppermute(shard, ('loop', 'pair'), hops)]
    ppermute x4, waiting for transfers between devices: 0.09 us -> 0.43 us  [send(): return lax.ppermute(shard, ('loop', 'pair'), hops)]
    pallas_call x1 -> x2, Pallas kernels: 4.31 us -> 4.28 us  [the longest x1 2.93 us: shards(): pl.pallas_call(local_stage, name='local_stage', out_shape=[state] * 3, in...]
where the time goes in v18:
time: 24.5 us; the launch traced here: 24.3 us
  Pallas kernels  18.5 us (76%)
  starting transfers between devices  5.37 us (22%)
  waiting for transfers between devices  0.43 us (2%)
    pallas_call x1, Pallas kernels, shards(): pl.pallas_call(functools.partial(last_stage, routed), name='last_stage',...  12.4 us
    ppermute x4, starting transfers between devices, send(): return lax.ppermute(shard, ('loop', 'pair'), hops)  5.37 us
    pallas_call x1, Pallas kernels, shards(): pl.pallas_call(local_stage, name='local_stage', out_shape=[state] * 3, in...  2.93 us
    pallas_call x2, Pallas kernels, add_shards(): pl.pallas_call(functools.partial(add_stage, by_swap if routed else None),...  1.79 us
    pallas_call x1, Pallas kernels, shards(): pl.pallas_call(load_stage, name='load_stage', out_shape=[jax.ShapeDtypeSt...  1.35 us
  transfers between devices with their start and end apart: 4, of which 1 were waited for; matrix products, arithmetic and copies ran while one was open for 0% of the time, Pallas kernels for 25%

profile of v18, /device:TPU:0, one launch (start us, length us, event | category | flops | bytes accessed | tf_op | source)
XLA Modules:
  0.0 24.3 jit_solution(9640148107290287057)
XLA Ops:
  0.0 3.0 %collective-permute-start = (bf16[256,256]{1,0:T(8,128)(2,1)}, bf16[256,256]{1,0:T(8,128)(2,1)S(1)}, u32[]{:S(2)}, u32[]{:S(2)}) collective-permute-start(bf16[256,256]{1,0:T(8,128)(2,1)} %bitcast.3), channel_id=1, source_target_pairs={{0,4},{1,8},{4,5},{5,9},{8,12},{9,0},{12,13},{13,1},{2,6},{3,10},{... | collective-permute-start | bytes 393224 | tf_op jit(solution)/shard_map/ppermute | solution.py:286
  3.0 1.4 %load_stage.1 = (bf16[640,512]{1,0:T(8,128)(2,1)S(1)}, bf16[640,256]{1,0:T(8,128)(2,1)S(1)}, bf16[256,256]{1,0:T(8,128)(2,1)S(1)}, s32[640,128]{1,0:T(8,128)S(1)}) custom-call(s32[8]{0:T(128)} %lengths_hbm.1, bf16[640,512]{1,0:T(8,128)(2,1)} %query_hbm.1, bf16[640,256]{1,0:T(8,128)(2,1)} %bitcast.2, bf16[256,256]{1,0:T(8,128)(2,1)} %bitcast.4), custom_call_target="tpu_custom_call" | custom-call | flops 1 | bytes 1 | tf_op jit(solution)/shard_map/load_stage/pallas_call | solution.py:311
  4.4 1.2 %collective-permute-start.1 = (bf16[256,256]{1,0:T(8,128)(2,1)S(1)}, bf16[256,256]{1,0:T(8,128)(2,1)S(1)}, u32[]{:S(2)}, u32[]{:S(2)}) collective-permute-start(bf16[256,256]{1,0:T(8,128)(2,1)S(1)} %get-tuple-element.22.own_ref), channel_id=1, source_target_pairs={{0,1},{1,12},{4,0},{5,13},{8,9},{9,4},{12,8},{13,5},{2,3},{3,14},{... | collective-permute-start | bytes 393224 | tf_op jit(solution)/shard_map/ppermute | solution.py:286
  5.6 2.9 %local_stage.1 = (f32[640,512]{1,0:T(8,128)S(1)}, f32[640,512]{1,0:T(8,128)S(1)}, f32[640,512]{1,0:T(8,128)S(1)}) custom-call(bf16[640,512]{1,0:T(8,128)(2,1)S(1)} %get-tuple-element.20.query_ref.refs_0_, bf16[640,256]{1,0:T(8,128)(2,1)S(1)} %get-tuple-element.21.suffix_ref, bf16[256,256]{1,0:T(8,128)(2,1)S(1)} %get-tuple-element.22.own_ref, ...), custom_call_target="tpu_custom_call" | custom-call | flops 1 | bytes 1 | tf_op jit(solution)/shard_map/local_stage/pallas_call | solution.py:337
  8.5 0.0 collective-permute-done.refs_4_.refs_6_
  8.5 1.1 %collective-permute-start.2 = (bf16[256,256]{1,0:T(8,128)(2,1)S(1)}, bf16[256,256]{1,0:T(8,128)(2,1)S(1)}, u32[]{:S(2)}, u32[]{:S(2)}) collective-permute-start(bf16[256,256]{1,0:T(8,128)(2,1)S(1)} %collective-permute-done.refs_4_.refs_6_), channel_id=1, source_target_pairs={{0,1},{1,0},{4,5},{5,4},{8,9},{9,8},{12,13},{13,12},{2,3},{3,2},{6... | collective-permute-start | bytes 393224 | tf_op jit(solution)/shard_map/ppermute | solution.py:286
  9.6 0.9 %add_stage.2 = (f32[640,512]{1,0:T(8,128)S(1)}, f32[640,512]{1,0:T(8,128)S(1)}) custom-call(bf16[640,512]{1,0:T(8,128)(2,1)S(1)} %get-tuple-element.20.query_ref.refs_0_, f32[640,512]{1,0:T(8,128)S(1)} %get-tuple-element.25.refs_1_, f32[640,512]{1,0:T(8,128)S(1)} %get-tuple-element.26.refs_2_, f32[640,512]{1,0:T(8,128)S(1)} %get-tuple-element.27.refs_3_, ...), custom_call_target="tpu_custom_call" | custom-call | flops 1 | bytes 1 | tf_op jit(solution)/shard_map/add_stage/pallas_call | solution.py:350
  10.5 0.0 collective-permute-done.1.refs_8_
  10.5 0.1 collective-permute-start.3
  10.6 0.0 collective-permute-done.2.refs_4_.refs_7_
  10.6 0.9 %add_stage.3 = (f32[640,512]{1,0:T(8,128)S(1)}, f32[640,512]{1,0:T(8,128)S(1)}) custom-call(bf16[640,512]{1,0:T(8,128)(2,1)S(1)} %get-tuple-element.20.query_ref.refs_0_, f32[640,512]{1,0:T(8,128)S(1)} %get-tuple-element.25.refs_1_, f32[640,512]{1,0:T(8,128)S(1)} %get-tuple-element.30.refs_2_, f32[640,512]{1,0:T(8,128)S(1)} %get-tuple-element.31.refs_3_, ...), custom_call_target="tpu_custom_call" | custom-call | flops 1 | bytes 1 | tf_op jit(solution)/shard_map/add_stage/pallas_call | solution.py:350
  11.5 0.4 %collective-permute-done.3.refs_9_ = bf16[256,256]{1,0:T(8,128)(2,1)S(1)} collective-permute-done((bf16[256,256]{1,0:T(8,128)(2,1)S(1)}, bf16[256,256]{1,0:T(8,128)(2,1)S(1)}, u32[]{:S(2)}, u32[]{:S(2)}) %collective-permute-start.3) | collective-permute-done | bytes 131104 | tf_op jit(solution)/shard_map/ppermute | solution.py:286
  11.9 12.4 %last_stage.1 = bf16[640,512]{1,0:T(8,128)(2,1)} custom-call(bf16[640,512]{1,0:T(8,128)(2,1)S(1)} %get-tuple-element.20.query_ref.refs_0_, f32[640,512]{1,0:T(8,128)S(1)} %get-tuple-element.25.refs_1_, f32[640,512]{1,0:T(8,128)S(1)} %get-tuple-element.26.refs_2_, f32[640,512]{1,0:T(8,128)S(1)} %get-tuple-element.27.refs_3_, ...), custom_call_target="tpu_custom_call" | custom-call | flops 1 | bytes 1 | tf_op jit(solution)/shard_map/last_stage/pallas_call | solution.py:372
Async XLA Ops:
  0.0 8.5 %collective-permute-start = (bf16[256,256]{1,0:T(8,128)(2,1)}, bf16[256,256]{1,0:T(8,128)(2,1)S(1)}, u32[]{:S(2)}, u32[]{:S(2)}) collective-permute-start(bf16[256,256]{1,0:T(8,128)(2,1)} %bitcast.3), channel_id=1, source_target_pairs={{0,4},{1,8},{4,5},{5,9},{8,12},{9,0},{12,13},{13,1},{2,6},{3,10},{... | collective-permute-start | bytes 393224 | tf_op jit(solution)/shard_map/ppermute | solution.py:286
  4.4 6.1 %collective-permute-start.1 = (bf16[256,256]{1,0:T(8,128)(2,1)S(1)}, bf16[256,256]{1,0:T(8,128)(2,1)S(1)}, u32[]{:S(2)}, u32[]{:S(2)}) collective-permute-start(bf16[256,256]{1,0:T(8,128)(2,1)S(1)} %get-tuple-element.22.own_ref), channel_id=1, source_target_pairs={{0,1},{1,12},{4,0},{5,13},{8,9},{9,4},{12,8},{13,5},{2,3},{3,14},{... | collective-permute-start | bytes 393224 | tf_op jit(solution)/shard_map/ppermute | solution.py:286
  8.5 2.1 %collective-permute-start.2 = (bf16[256,256]{1,0:T(8,128)(2,1)S(1)}, bf16[256,256]{1,0:T(8,128)(2,1)S(1)}, u32[]{:S(2)}, u32[]{:S(2)}) collective-permute-start(bf16[256,256]{1,0:T(8,128)(2,1)S(1)} %collective-permute-done.refs_4_.refs_6_), channel_id=1, source_target_pairs={{0,1},{1,0},{4,5},{5,4},{8,9},{9,8},{12,13},{13,12},{2,3},{3,2},{6... | collective-permute-start | bytes 393224 | tf_op jit(solution)/shard_map/ppermute | solution.py:286
  10.5 1.4 %collective-permute-start.3 = (bf16[256,256]{1,0:T(8,128)(2,1)S(1)}, bf16[256,256]{1,0:T(8,128)(2,1)S(1)}, u32[]{:S(2)}, u32[]{:S(2)}) collective-permute-start(bf16[256,256]{1,0:T(8,128)(2,1)S(1)} %collective-permute-done.1.refs_8_), channel_id=1, source_target_pairs={{0,1},{1,0},{4,5},{5,4},{8,9},{9,8},{12,13},{13,12},{2,3},{3,2},{6... | collective-permute-start | bytes 393224 | tf_op jit(solution)/shard_map/ppermute | solution.py:286

commit v19 on v17

--- a/solution.py
+++ b/solution.py
@@ -176,6 +176,7 @@
     blocks = row_blocks(query_ref.shape[0], 80)
     position, core = place()
     takes_both = (position == 1) & routed
+    is_direct = core == jnp.where(position == 0, 0, 1)
 
     def out_copy(index, rows):
         return pltpu.make_async_copy(out_ref.at[rows], out_hbm.at[rows], out_sems.at[index])
@@ -209,7 +210,7 @@
 
     @pl.when(jnp.logical_not(takes_both))
     def one_shard():
-        process(jnp.where(core == 0, direct_ref[...], swapped_ref[...]))
+        process(jnp.where(is_direct, direct_ref[...], swapped_ref[...]))
 
     @pl.when(takes_both)
     def two_shards():
@@ -225,8 +226,8 @@
                 for by_swap, ref in enumerate(earlier_refs[-2:])
             ]
         counted += [
-            (ref, penalty(takes_both | (core == by_swap)))
-            for by_swap, ref in enumerate([direct_ref, swapped_ref])
+            (direct_ref, penalty(takes_both | is_direct)),
+            (swapped_ref, penalty(takes_both | jnp.logical_not(is_direct))),
         ]
 
         def visit(index, unused):
@@ -275,16 +276,18 @@
         return lax.ppermute(shard, ("loop", "pair"), hops)
 
     def first_route(i, core):
-        position, base = i % FOUR, i - i % FOUR
-        if core == 0:
-            return {0: (i + 1, 0), 1: (i, 1)}.get(position, (i ^ 1, 1))
-        return {2: (base, 0), 3: (base, 1)}.get(position, (i ^ 3, 0))
+        base = i - i % FOUR
+        to, to_core = [((1, 0), (3, 1)), ((1, 1), (2, 0)), ((3, 0), (0, 0)), ((2, 1), (0, 1))][
+            i % FOUR
+        ][core]
+        return base + to, to_core
 
     def second_route(i, core):
-        position, base = i % FOUR, i - i % FOUR
-        if core == 0:
-            return (base, 0) if position == 1 else (i, 1)
-        return {2: (base + 1, 0), 3: (base + 1, 1)}.get(position, (i ^ 2, 0))
+        base = i - i % FOUR
+        to, to_core = [((0, 1), (2, 1)), ((0, 0), (3, 1)), ((3, 0), (1, 0)), ((2, 0), (1, 1))][
+            i % FOUR
+        ][core]
+        return base + to, to_core
 
     if routed:
         early = [

time: 24.6 us -> 24 us (0.976)
  starting transfers between devices: 5.79 us -> 5.24 us
    ppermute x4, starting transfers between devices: 5.79 us -> 5.24 us  [send(): return lax.ppermute(shard, ('loop', 'pair'), hops)]
where the time goes in v19:
time: 24 us; the launch traced here: 23.9 us
  Pallas kernels  18.5 us (77%)
  starting transfers between devices  5.24 us (22%)
    pallas_call x1, Pallas kernels, shards(): pl.pallas_call(functools.partial(last_stage, routed), name='last_stage',...  12.4 us
    ppermute x4, starting transfers between devices, send(): return lax.ppermute(shard, ('loop', 'pair'), hops)  5.24 us
    pallas_call x1, Pallas kernels, shards(): pl.pallas_call(local_stage, name='local_stage', out_shape=[state] * 3 + [...  4.31 us
    pallas_call x2, Pallas kernels, add_shards(): pl.pallas_call(functools.partial(add_stage, by_swap if routed else None),...  1.78 us
  transfers between devices with their start and end apart: 4, of which 1 were waited for; matrix products, arithmetic and copies ran while one was open for 0% of the time, Pallas kernels for 25%

profile of v19, /device:TPU:0, one launch (start us, length us, event | category | flops | bytes accessed | tf_op | source)
XLA Modules:
  0.0 23.9 jit_solution(763462929279799610)
XLA Ops:
  0.0 3.0 %collective-permute-start = (bf16[256,256]{1,0:T(8,128)(2,1)}, bf16[256,256]{1,0:T(8,128)(2,1)S(1)}, u32[]{:S(2)}, u32[]{:S(2)}) collective-permute-start(bf16[256,256]{1,0:T(8,128)(2,1)} %bitcast.3), channel_id=1, source_target_pairs={{0,4},{1,13},{4,5},{5,8},{8,12},{9,0},{12,9},{13,1},{2,6},{3,15},{... | collective-permute-start | bytes 393224 | tf_op jit(solution)/shard_map/ppermute | solution.py:276
  3.0 1.6 %collective-permute-start.1 = (bf16[256,256]{1,0:T(8,128)(2,1)}, bf16[256,256]{1,0:T(8,128)(2,1)S(1)}, u32[]{:S(2)}, u32[]{:S(2)}) collective-permute-start(bf16[256,256]{1,0:T(8,128)(2,1)} %bitcast.4), channel_id=1, source_target_pairs={{0,1},{1,9},{4,0},{5,13},{8,12},{9,4},{12,8},{13,5},{2,3},{3,11},{... | collective-permute-start | bytes 393224 | tf_op jit(solution)/shard_map/ppermute | solution.py:276
  4.6 4.3 %local_stage.1 = (f32[640,512]{1,0:T(8,128)S(1)}, f32[640,512]{1,0:T(8,128)S(1)}, f32[640,512]{1,0:T(8,128)S(1)}, bf16[640,512]{1,0:T(8,128)(2,1)S(1)}) custom-call(s32[8]{0:T(128)} %lengths_hbm.1, bf16[640,512]{1,0:T(8,128)(2,1)} %query_hbm.1, bf16[640,256]{1,0:T(8,128)(2,1)} %bitcast.2, bf16[256,256]{1,0:T(8,128)(2,1)} %bitcast.5), custom_call_target="tpu_custom_call" | custom-call | flops 1 | bytes 1 | tf_op jit(solution)/shard_map/local_stage/pallas_call | solution.py:311
  8.9 0.0 collective-permute-done.refs_4_.refs_6_
  8.9 0.1 collective-permute-start.2
  9.0 0.9 %add_stage.2 = (f32[640,512]{1,0:T(8,128)S(1)}, f32[640,512]{1,0:T(8,128)S(1)}) custom-call(bf16[640,512]{1,0:T(8,128)(2,1)S(1)} %get-tuple-element.17.refs_0_, f32[640,512]{1,0:T(8,128)S(1)} %get-tuple-element.19.refs_1_, f32[640,512]{1,0:T(8,128)S(1)} %get-tuple-element.20.refs_2_, f32[640,512]{1,0:T(8,128)S(1)} %get-tuple-element.21.refs_3_, ...), custom_call_target="tpu_custom_call" | custom-call | flops 1 | bytes 1 | tf_op jit(solution)/shard_map/add_stage/pallas_call | solution.py:330
  9.9 0.0 collective-permute-done.1.refs_8_
  9.9 0.6 %collective-permute-start.3 = (bf16[256,256]{1,0:T(8,128)(2,1)S(1)}, bf16[256,256]{1,0:T(8,128)(2,1)S(1)}, u32[]{:S(2)}, u32[]{:S(2)}) collective-permute-start(bf16[256,256]{1,0:T(8,128)(2,1)S(1)} %collective-permute-done.1.refs_8_), channel_id=1, source_target_pairs={{0,1},{1,0},{4,5},{5,4},{8,9},{9,8},{12,13},{13,12},{2,3},{3,2},{6... | collective-permute-start | bytes 393224 | tf_op jit(solution)/shard_map/ppermute | solution.py:276
  10.5 0.0 collective-permute-done.2.refs_4_.refs_7_
  10.5 0.9 %add_stage.3 = (f32[640,512]{1,0:T(8,128)S(1)}, f32[640,512]{1,0:T(8,128)S(1)}) custom-call(bf16[640,512]{1,0:T(8,128)(2,1)S(1)} %get-tuple-element.17.refs_0_, f32[640,512]{1,0:T(8,128)S(1)} %get-tuple-element.19.refs_1_, f32[640,512]{1,0:T(8,128)S(1)} %get-tuple-element.24.refs_2_, f32[640,512]{1,0:T(8,128)S(1)} %get-tuple-element.25.refs_3_, ...), custom_call_target="tpu_custom_call" | custom-call | flops 1 | bytes 1 | tf_op jit(solution)/shard_map/add_stage/pallas_call | solution.py:330
  11.4 0.1 collective-permute-done.3.refs_9_
  11.5 12.4 %last_stage.1 = bf16[640,512]{1,0:T(8,128)(2,1)} custom-call(bf16[640,512]{1,0:T(8,128)(2,1)S(1)} %get-tuple-element.17.refs_0_, f32[640,512]{1,0:T(8,128)S(1)} %get-tuple-element.19.refs_1_, f32[640,512]{1,0:T(8,128)S(1)} %get-tuple-element.20.refs_2_, f32[640,512]{1,0:T(8,128)S(1)} %get-tuple-element.21.refs_3_, f32[640,512]{1,0:T(8,128)S(1)} %get-tuple-element.26.refs_4_, ...), custom_call_target="tpu_custom_call" | custom-call | flops 1 | bytes 1 | tf_op jit(solution)/shard_map/last_stage/pallas_call | solution.py:352
Async XLA Ops:
  0.0 8.9 %collective-permute-start = (bf16[256,256]{1,0:T(8,128)(2,1)}, bf16[256,256]{1,0:T(8,128)(2,1)S(1)}, u32[]{:S(2)}, u32[]{:S(2)}) collective-permute-start(bf16[256,256]{1,0:T(8,128)(2,1)} %bitcast.3), channel_id=1, source_target_pairs={{0,4},{1,13},{4,5},{5,8},{8,12},{9,0},{12,9},{13,1},{2,6},{3,15},{... | collective-permute-start | bytes 393224 | tf_op jit(solution)/shard_map/ppermute | solution.py:276
  3.0 6.9 %collective-permute-start.1 = (bf16[256,256]{1,0:T(8,128)(2,1)}, bf16[256,256]{1,0:T(8,128)(2,1)S(1)}, u32[]{:S(2)}, u32[]{:S(2)}) collective-permute-start(bf16[256,256]{1,0:T(8,128)(2,1)} %bitcast.4), channel_id=1, source_target_pairs={{0,1},{1,9},{4,0},{5,13},{8,12},{9,4},{12,8},{13,5},{2,3},{3,11},{... | collective-permute-start | bytes 393224 | tf_op jit(solution)/shard_map/ppermute | solution.py:276
  8.9 1.6 %collective-permute-start.2 = (bf16[256,256]{1,0:T(8,128)(2,1)S(1)}, bf16[256,256]{1,0:T(8,128)(2,1)S(1)}, u32[]{:S(2)}, u32[]{:S(2)}) collective-permute-start(bf16[256,256]{1,0:T(8,128)(2,1)S(1)} %collective-permute-done.refs_4_.refs_6_), channel_id=1, source_target_pairs={{0,1},{1,0},{4,5},{5,4},{8,9},{9,8},{12,13},{13,12},{2,3},{3,2},{6... | collective-permute-start | bytes 393224 | tf_op jit(solution)/shard_map/ppermute | solution.py:276
  9.9 1.5 %collective-permute-start.3 = (bf16[256,256]{1,0:T(8,128)(2,1)S(1)}, bf16[256,256]{1,0:T(8,128)(2,1)S(1)}, u32[]{:S(2)}, u32[]{:S(2)}) collective-permute-start(bf16[256,256]{1,0:T(8,128)(2,1)S(1)} %collective-permute-done.1.refs_8_), channel_id=1, source_target_pairs={{0,1},{1,0},{4,5},{5,4},{8,9},{9,8},{12,13},{13,12},{2,3},{3,2},{6... | collective-permute-start | bytes 393224 | tf_op jit(solution)/shard_map/ppermute | solution.py:276

commit v20 on v19

--- a/solution.py
+++ b/solution.py
@@ -10,6 +10,7 @@
 
 HD = 128
 AG_DEV = 2
+MINLEN = 128
 MAXLEN = 320
 BLK = 128
 FOUR = 4
@@ -87,7 +88,7 @@
     window = BLK * ((MAXLEN + BLK - 2) // BLK) + BLK
     for block in range(blocks):
         stop = (block + 1) * BLK
-        start = max(0, stop - window)
+        start = max(0, stop - window, MINLEN // BLK * BLK if block * BLK >= MAXLEN else 0)
         rows = slice(block * BLK, stop)
         row_at = block * BLK + lax.broadcasted_iota(jnp.int32, (BLK, stop - start), 0)
         key_at = start + lax.broadcasted_iota(jnp.int32, (BLK, stop - start), 1)
@@ -271,8 +272,9 @@
         hops = []
         for i in range(loop_size):
             for core in range(2):
-                to, to_core = route(i, core)
-                hops.append((2 * i + core, 2 * to + to_core))
+                goal = route(i, core)
+                if goal is not None:
+                    hops.append((2 * i + core, 2 * goal[0] + goal[1]))
         return lax.ppermute(shard, ("loop", "pair"), hops)
 
     def first_route(i, core):
@@ -284,10 +286,10 @@
 
     def second_route(i, core):
         base = i - i % FOUR
-        to, to_core = [((0, 1), (2, 1)), ((0, 0), (3, 1)), ((3, 0), (1, 0)), ((2, 0), (1, 1))][
+        to, to_core = [((0, 1), (2, 1)), ((0, 0), (3, 1)), (None, (1, 0)), (None, (1, 1))][
             i % FOUR
-        ][core]
-        return base + to, to_core
+        ][core] or (None, None)
+        return None if to is None else (base + to, to_core)
 
     if routed:
         early = [

time: 24 us -> 26.1 us (1.088)
  starting transfers between devices: 5.24 us -> 7.14 us
    ppermute x4, starting transfers between devices: 5.24 us -> 7.14 us  [send(): return lax.ppermute(shard, ('loop', 'pair'), hops)]
  transfers between devices with their start and end apart: 4 -> 4, of which waited for: 1 -> 1; matrix products, arithmetic and copies ran while one was open for 0% -> 0% of each run, Pallas kernels for 25% -> 24%
where the time goes in v20:
time: 26.1 us; the launch traced here: 26 us
  Pallas kernels  18.7 us (72%)
  starting transfers between devices  7.14 us (27%)
    pallas_call x1, Pallas kernels, shards(): pl.pallas_call(functools.partial(last_stage, routed), name='last_stage',...  12.4 us
    ppermute x4, starting transfers between devices, send(): return lax.ppermute(shard, ('loop', 'pair'), hops)  7.14 us
    pallas_call x1, Pallas kernels, shards(): pl.pallas_call(local_stage, name='local_stage', out_shape=[state] * 3 + [...  4.5 us
    pallas_call x2, Pallas kernels, add_shards(): pl.pallas_call(functools.partial(add_stage, by_swap if routed else None),...  1.79 us
  transfers between devices with their start and end apart: 4, of which 1 were waited for; matrix products, arithmetic and copies ran while one was open for 0% of the time, Pallas kernels for 24%

profile of v20, /device:TPU:0, one launch (start us, length us, event | category | flops | bytes accessed | tf_op | source)
XLA Modules:
  0.0 26.0 jit_solution(3232257580238090183)
XLA Ops:
  0.0 3.0 %collective-permute-start = (bf16[256,256]{1,0:T(8,128)(2,1)}, bf16[256,256]{1,0:T(8,128)(2,1)S(1)}, u32[]{:S(2)}, u32[]{:S(2)}) collective-permute-start(bf16[256,256]{1,0:T(8,128)(2,1)} %bitcast.3), channel_id=1, source_target_pairs={{0,4},{1,13},{4,5},{5,8},{8,12},{9,0},{12,9},{13,1},{2,6},{3,15},{... | collective-permute-start | bytes 393224 | tf_op jit(solution)/shard_map/ppermute | solution.py:278
  3.0 3.5 %collective-permute-start.1 = (bf16[256,256]{1,0:T(8,128)(2,1)}, bf16[256,256]{1,0:T(8,128)(2,1)S(1)}, u32[]{:S(2)}, u32[]{:S(2)}) collective-permute-start(bf16[256,256]{1,0:T(8,128)(2,1)} %bitcast.4), channel_id=1, source_target_pairs={{0,1},{1,9},{4,0},{5,13},{9,4},{13,5},{2,3},{3,11},{6,2},{7,15},{1... | collective-permute-start | bytes 393224 | tf_op jit(solution)/shard_map/ppermute | solution.py:278
  6.5 4.5 %local_stage.1 = (f32[640,512]{1,0:T(8,128)S(1)}, f32[640,512]{1,0:T(8,128)S(1)}, f32[640,512]{1,0:T(8,128)S(1)}, bf16[640,512]{1,0:T(8,128)(2,1)S(1)}) custom-call(s32[8]{0:T(128)} %lengths_hbm.1, bf16[640,512]{1,0:T(8,128)(2,1)} %query_hbm.1, bf16[640,256]{1,0:T(8,128)(2,1)} %bitcast.2, bf16[256,256]{1,0:T(8,128)(2,1)} %bitcast.5), custom_call_target="tpu_custom_call" | custom-call | flops 1 | bytes 1 | tf_op jit(solution)/shard_map/local_stage/pallas_call | solution.py:313
  11.0 0.0 collective-permute-done.refs_4_.refs_6_
  11.0 0.1 collective-permute-start.2
  11.1 0.9 %add_stage.2 = (f32[640,512]{1,0:T(8,128)S(1)}, f32[640,512]{1,0:T(8,128)S(1)}) custom-call(bf16[640,512]{1,0:T(8,128)(2,1)S(1)} %get-tuple-element.17.refs_0_, f32[640,512]{1,0:T(8,128)S(1)} %get-tuple-element.19.refs_1_, f32[640,512]{1,0:T(8,128)S(1)} %get-tuple-element.20.refs_2_, f32[640,512]{1,0:T(8,128)S(1)} %get-tuple-element.21.refs_3_, ...), custom_call_target="tpu_custom_call" | custom-call | flops 1 | bytes 1 | tf_op jit(solution)/shard_map/add_stage/pallas_call | solution.py:332
  12.0 0.0 collective-permute-done.1.refs_8_
  12.0 0.6 %collective-permute-start.3 = (bf16[256,256]{1,0:T(8,128)(2,1)S(1)}, bf16[256,256]{1,0:T(8,128)(2,1)S(1)}, u32[]{:S(2)}, u32[]{:S(2)}) collective-permute-start(bf16[256,256]{1,0:T(8,128)(2,1)S(1)} %collective-permute-done.1.refs_8_), channel_id=1, source_target_pairs={{0,1},{1,0},{4,5},{5,4},{8,9},{9,8},{12,13},{13,12},{2,3},{3,2},{6... | collective-permute-start | bytes 393224 | tf_op jit(solution)/shard_map/ppermute | solution.py:278
  12.6 0.0 collective-permute-done.2.refs_4_.refs_7_
  12.6 0.9 %add_stage.3 = (f32[640,512]{1,0:T(8,128)S(1)}, f32[640,512]{1,0:T(8,128)S(1)}) custom-call(bf16[640,512]{1,0:T(8,128)(2,1)S(1)} %get-tuple-element.17.refs_0_, f32[640,512]{1,0:T(8,128)S(1)} %get-tuple-element.19.refs_1_, f32[640,512]{1,0:T(8,128)S(1)} %get-tuple-element.24.refs_2_, f32[640,512]{1,0:T(8,128)S(1)} %get-tuple-element.25.refs_3_, ...), custom_call_target="tpu_custom_call" | custom-call | flops 1 | bytes 1 | tf_op jit(solution)/shard_map/add_stage/pallas_call | solution.py:332
  13.5 0.1 collective-permute-done.3.refs_9_
  13.6 12.4 %last_stage.1 = bf16[640,512]{1,0:T(8,128)(2,1)} custom-call(bf16[640,512]{1,0:T(8,128)(2,1)S(1)} %get-tuple-element.17.refs_0_, f32[640,512]{1,0:T(8,128)S(1)} %get-tuple-element.19.refs_1_, f32[640,512]{1,0:T(8,128)S(1)} %get-tuple-element.20.refs_2_, f32[640,512]{1,0:T(8,128)S(1)} %get-tuple-element.21.refs_3_, f32[640,512]{1,0:T(8,128)S(1)} %get-tuple-element.26.refs_4_, ...), custom_call_target="tpu_custom_call" | custom-call | flops 1 | bytes 1 | tf_op jit(solution)/shard_map/last_stage/pallas_call | solution.py:354
Async XLA Ops:
  0.0 11.0 %collective-permute-start = (bf16[256,256]{1,0:T(8,128)(2,1)}, bf16[256,256]{1,0:T(8,128)(2,1)S(1)}, u32[]{:S(2)}, u32[]{:S(2)}) collective-permute-start(bf16[256,256]{1,0:T(8,128)(2,1)} %bitcast.3), channel_id=1, source_target_pairs={{0,4},{1,13},{4,5},{5,8},{8,12},{9,0},{12,9},{13,1},{2,6},{3,15},{... | collective-permute-start | bytes 393224 | tf_op jit(solution)/shard_map/ppermute | solution.py:278
  3.0 9.0 %collective-permute-start.1 = (bf16[256,256]{1,0:T(8,128)(2,1)}, bf16[256,256]{1,0:T(8,128)(2,1)S(1)}, u32[]{:S(2)}, u32[]{:S(2)}) collective-permute-start(bf16[256,256]{1,0:T(8,128)(2,1)} %bitcast.4), channel_id=1, source_target_pairs={{0,1},{1,9},{4,0},{5,13},{9,4},{13,5},{2,3},{3,11},{6,2},{7,15},{1... | collective-permute-start | bytes 393224 | tf_op jit(solution)/shard_map/ppermute | solution.py:278
  11.0 1.6 %collective-permute-start.2 = (bf16[256,256]{1,0:T(8,128)(2,1)S(1)}, bf16[256,256]{1,0:T(8,128)(2,1)S(1)}, u32[]{:S(2)}, u32[]{:S(2)}) collective-permute-start(bf16[256,256]{1,0:T(8,128)(2,1)S(1)} %collective-permute-done.refs_4_.refs_6_), channel_id=1, source_target_pairs={{0,1},{1,0},{4,5},{5,4},{8,9},{9,8},{12,13},{13,12},{2,3},{3,2},{6... | collective-permute-start | bytes 393224 | tf_op jit(solution)/shard_map/ppermute | solution.py:278
  12.0 1.6 %collective-permute-start.3 = (bf16[256,256]{1,0:T(8,128)(2,1)S(1)}, bf16[256,256]{1,0:T(8,128)(2,1)S(1)}, u32[]{:S(2)}, u32[]{:S(2)}) collective-permute-start(bf16[256,256]{1,0:T(8,128)(2,1)S(1)} %collective-permute-done.1.refs_8_), channel_id=1, source_target_pairs={{0,1},{1,0},{4,5},{5,4},{8,9},{9,8},{12,13},{13,12},{2,3},{3,2},{6... | collective-permute-start | bytes 393224 | tf_op jit(solution)/shard_map/ppermute | solution.py:278

commit v21 on v19

--- a/solution.py
+++ b/solution.py
@@ -182,22 +182,23 @@
         return pltpu.make_async_copy(out_ref.at[rows], out_hbm.at[rows], out_sems.at[index])
 
     def write(rows, total, weighted):
-        unstack(out_ref, rows, heads, (weighted / total).astype(jnp.bfloat16))
+        inverse = pl.reciprocal(total, approx=True)
+        inverse = inverse * (2.0 - total * inverse)
+        unstack(out_ref, rows, heads, (weighted * inverse).astype(jnp.bfloat16))
 
     def process(shard):
         trusted = [jnp.full((8, HD), True)]
+        key_rows, value_rows = shard[:, :HD], with_ones(shard[:, HD:])
 
         def start(rows):
-            return scores_of(stacked(query_ref, rows, heads), shard[:, :HD])
+            return scores_of(stacked(query_ref, rows, heads), key_rows)
 
         def finish(index, rows, scores):
             best = stacked(best_ref, rows, heads)
-            weights = jnp.exp2(scores - widen(best, scores.shape[1]))
-            lanes = sum(weights[:, i : i + HD] for i in range(0, scores.shape[1], HD))
-            total = stacked(total_ref, rows, heads) + jnp.sum(lanes, axis=1, keepdims=True)
-            weighted = stacked(sum_ref, rows, heads) + jnp.dot(
-                weights.astype(jnp.bfloat16), shard[:, HD:], preferred_element_type=jnp.float32
-            )
+            weights = jnp.exp2(scores - widen(best, scores.shape[1])).astype(jnp.bfloat16)
+            result = jnp.dot(weights, value_rows, preferred_element_type=jnp.float32)
+            total = stacked(total_ref, rows, heads) + result[:, HD:]
+            weighted = stacked(sum_ref, rows, heads) + result[:, :HD]
             good = (total < total_limit).reshape(total.shape[0] // 8, 8, HD)
             trusted[0] = trusted[0] & jnp.all(good, axis=0)
             write(rows, total, weighted)

time: 24 us -> 24.1 us (level)
  no operation moved by 1% of the time
where the time goes in v21:
time: 24.1 us; the launch traced here: 24 us
  Pallas kernels  18.6 us (77%)
  starting transfers between devices  5.24 us (22%)
    pallas_call x1, Pallas kernels, shards(): pl.pallas_call(functools.partial(last_stage, routed), name='last_stage',...  12.5 us
    ppermute x4, starting transfers between devices, send(): return lax.ppermute(shard, ('loop', 'pair'), hops)  5.24 us
    pallas_call x1, Pallas kernels, shards(): pl.pallas_call(local_stage, name='local_stage', out_shape=[state] * 3 + [...  4.31 us
    pallas_call x2, Pallas kernels, add_shards(): pl.pallas_call(functools.partial(add_stage, by_swap if routed else None),...  1.78 us
  transfers between devices with their start and end apart: 4, of which 1 were waited for; matrix products, arithmetic and copies ran while one was open for 0% of the time, Pallas kernels for 25%

profile of v21, /device:TPU:0, one launch (start us, length us, event | category | flops | bytes accessed | tf_op | source)
XLA Modules:
  0.0 24.0 jit_solution(15985366043305839527)
XLA Ops:
  0.0 3.0 %collective-permute-start = (bf16[256,256]{1,0:T(8,128)(2,1)}, bf16[256,256]{1,0:T(8,128)(2,1)S(1)}, u32[]{:S(2)}, u32[]{:S(2)}) collective-permute-start(bf16[256,256]{1,0:T(8,128)(2,1)} %bitcast.3), channel_id=1, source_target_pairs={{0,4},{1,13},{4,5},{5,8},{8,12},{9,0},{12,9},{13,1},{2,6},{3,15},{... | collective-permute-start | bytes 393224 | tf_op jit(solution)/shard_map/ppermute | solution.py:277
  3.0 1.6 %collective-permute-start.1 = (bf16[256,256]{1,0:T(8,128)(2,1)}, bf16[256,256]{1,0:T(8,128)(2,1)S(1)}, u32[]{:S(2)}, u32[]{:S(2)}) collective-permute-start(bf16[256,256]{1,0:T(8,128)(2,1)} %bitcast.4), channel_id=1, source_target_pairs={{0,1},{1,9},{4,0},{5,13},{8,12},{9,4},{12,8},{13,5},{2,3},{3,11},{... | collective-permute-start | bytes 393224 | tf_op jit(solution)/shard_map/ppermute | solution.py:277
  4.6 4.3 %local_stage.1 = (f32[640,512]{1,0:T(8,128)S(1)}, f32[640,512]{1,0:T(8,128)S(1)}, f32[640,512]{1,0:T(8,128)S(1)}, bf16[640,512]{1,0:T(8,128)(2,1)S(1)}) custom-call(s32[8]{0:T(128)} %lengths_hbm.1, bf16[640,512]{1,0:T(8,128)(2,1)} %query_hbm.1, bf16[640,256]{1,0:T(8,128)(2,1)} %bitcast.2, bf16[256,256]{1,0:T(8,128)(2,1)} %bitcast.5), custom_call_target="tpu_custom_call" | custom-call | flops 1 | bytes 1 | tf_op jit(solution)/shard_map/local_stage/pallas_call | solution.py:312
  8.9 0.0 collective-permute-done.refs_4_.refs_6_
  8.9 0.1 collective-permute-start.2
  9.0 0.9 %add_stage.2 = (f32[640,512]{1,0:T(8,128)S(1)}, f32[640,512]{1,0:T(8,128)S(1)}) custom-call(bf16[640,512]{1,0:T(8,128)(2,1)S(1)} %get-tuple-element.17.refs_0_, f32[640,512]{1,0:T(8,128)S(1)} %get-tuple-element.19.refs_1_, f32[640,512]{1,0:T(8,128)S(1)} %get-tuple-element.20.refs_2_, f32[640,512]{1,0:T(8,128)S(1)} %get-tuple-element.21.refs_3_, ...), custom_call_target="tpu_custom_call" | custom-call | flops 1 | bytes 1 | tf_op jit(solution)/shard_map/add_stage/pallas_call | solution.py:331
  9.9 0.0 collective-permute-done.1.refs_8_
  9.9 0.6 %collective-permute-start.3 = (bf16[256,256]{1,0:T(8,128)(2,1)S(1)}, bf16[256,256]{1,0:T(8,128)(2,1)S(1)}, u32[]{:S(2)}, u32[]{:S(2)}) collective-permute-start(bf16[256,256]{1,0:T(8,128)(2,1)S(1)} %collective-permute-done.1.refs_8_), channel_id=1, source_target_pairs={{0,1},{1,0},{4,5},{5,4},{8,9},{9,8},{12,13},{13,12},{2,3},{3,2},{6... | collective-permute-start | bytes 393224 | tf_op jit(solution)/shard_map/ppermute | solution.py:277
  10.5 0.0 collective-permute-done.2.refs_4_.refs_7_
  10.5 0.9 %add_stage.3 = (f32[640,512]{1,0:T(8,128)S(1)}, f32[640,512]{1,0:T(8,128)S(1)}) custom-call(bf16[640,512]{1,0:T(8,128)(2,1)S(1)} %get-tuple-element.17.refs_0_, f32[640,512]{1,0:T(8,128)S(1)} %get-tuple-element.19.refs_1_, f32[640,512]{1,0:T(8,128)S(1)} %get-tuple-element.24.refs_2_, f32[640,512]{1,0:T(8,128)S(1)} %get-tuple-element.25.refs_3_, ...), custom_call_target="tpu_custom_call" | custom-call | flops 1 | bytes 1 | tf_op jit(solution)/shard_map/add_stage/pallas_call | solution.py:331
  11.4 0.1 collective-permute-done.3.refs_9_
  11.5 12.5 %last_stage.1 = bf16[640,512]{1,0:T(8,128)(2,1)} custom-call(bf16[640,512]{1,0:T(8,128)(2,1)S(1)} %get-tuple-element.17.refs_0_, f32[640,512]{1,0:T(8,128)S(1)} %get-tuple-element.19.refs_1_, f32[640,512]{1,0:T(8,128)S(1)} %get-tuple-element.20.refs_2_, f32[640,512]{1,0:T(8,128)S(1)} %get-tuple-element.21.refs_3_, f32[640,512]{1,0:T(8,128)S(1)} %get-tuple-element.26.refs_4_, ...), custom_call_target="tpu_custom_call" | custom-call | flops 1 | bytes 1 | tf_op jit(solution)/shard_map/last_stage/pallas_call | solution.py:353
Async XLA Ops:
  0.0 8.9 %collective-permute-start = (bf16[256,256]{1,0:T(8,128)(2,1)}, bf16[256,256]{1,0:T(8,128)(2,1)S(1)}, u32[]{:S(2)}, u32[]{:S(2)}) collective-permute-start(bf16[256,256]{1,0:T(8,128)(2,1)} %bitcast.3), channel_id=1, source_target_pairs={{0,4},{1,13},{4,5},{5,8},{8,12},{9,0},{12,9},{13,1},{2,6},{3,15},{... | collective-permute-start | bytes 393224 | tf_op jit(solution)/shard_map/ppermute | solution.py:277
  3.0 6.9 %collective-permute-start.1 = (bf16[256,256]{1,0:T(8,128)(2,1)}, bf16[256,256]{1,0:T(8,128)(2,1)S(1)}, u32[]{:S(2)}, u32[]{:S(2)}) collective-permute-start(bf16[256,256]{1,0:T(8,128)(2,1)} %bitcast.4), channel_id=1, source_target_pairs={{0,1},{1,9},{4,0},{5,13},{8,12},{9,4},{12,8},{13,5},{2,3},{3,11},{... | collective-permute-start | bytes 393224 | tf_op jit(solution)/shard_map/ppermute | solution.py:277
  8.9 1.6 %collective-permute-start.2 = (bf16[256,256]{1,0:T(8,128)(2,1)S(1)}, bf16[256,256]{1,0:T(8,128)(2,1)S(1)}, u32[]{:S(2)}, u32[]{:S(2)}) collective-permute-start(bf16[256,256]{1,0:T(8,128)(2,1)S(1)} %collective-permute-done.refs_4_.refs_6_), channel_id=1, source_target_pairs={{0,1},{1,0},{4,5},{5,4},{8,9},{9,8},{12,13},{13,12},{2,3},{3,2},{6... | collective-permute-start | bytes 393224 | tf_op jit(solution)/shard_map/ppermute | solution.py:277
  9.9 1.5 %collective-permute-start.3 = (bf16[256,256]{1,0:T(8,128)(2,1)S(1)}, bf16[256,256]{1,0:T(8,128)(2,1)S(1)}, u32[]{:S(2)}, u32[]{:S(2)}) collective-permute-start(bf16[256,256]{1,0:T(8,128)(2,1)S(1)} %collective-permute-done.1.refs_8_), channel_id=1, source_target_pairs={{0,1},{1,0},{4,5},{5,4},{8,9},{9,8},{12,13},{13,12},{2,3},{3,2},{6... | collective-permute-start | bytes 393224 | tf_op jit(solution)/shard_map/ppermute | solution.py:277

commit v22 on v18

--- a/solution.py
+++ b/solution.py
@@ -47,11 +47,15 @@
     return jnp.concatenate([row_value] * (width // HD), axis=1)
 
 
+def place():
+    return lax.rem(lax.axis_index("loop"), FOUR), lax.axis_index("pair")
+
+
 def load_blocks(count):
     return [pl.ds(first, BLK) for first in range(0, count, BLK)]
 
 
-def load_stage(
+def load(
     lengths_hbm,
     query_hbm,
     suffix_hbm,
@@ -87,7 +91,25 @@
         copy.wait()
 
 
-def local_stage(query_ref, suffix_ref, own_ref, first_ref, best_ref, total_ref, sum_ref):
+def prelude_stage(*refs):
+    @pl.when(place()[0] == 0)
+    def ahead():
+        load(*refs)
+
+
+def local_stage(*refs):
+    sources, (best_ref, total_ref, sum_ref), loaded, scratch = (
+        refs[:4],
+        refs[8:11],
+        refs[11:15],
+        refs[15:],
+    )
+    query_ref, suffix_ref, own_ref, first_ref = loaded
+
+    @pl.when(place()[0] != 0)
+    def now():
+        load(*sources, *loaded, *scratch)
+
     slots = query_ref.shape[0]
     heads = query_ref.shape[1] // HD
     own_keys = own_ref[:, :HD]
@@ -140,10 +162,6 @@
     return [slice(first, first + step) for first in range(0, count, step)]
 
 
-def place():
-    return lax.rem(lax.axis_index("loop"), 2) == 1, lax.axis_index("pair")
-
-
 def penalty(is_there):
     return jnp.where(is_there, 0.0, empty_best)
 
@@ -157,8 +175,8 @@
     key_rows, value_rows = shard[:, :HD], with_ones(shard[:, HD:])
     extra = None
     if by_swap is not None:
-        is_odd, core = place()
-        extra = penalty(jnp.logical_not(is_odd) | (core == int(by_swap)))
+        position, core = place()
+        extra = penalty((position != 1) | (core == int(by_swap)))
 
     def start(rows):
         return scores_of(stacked(query_ref, rows, heads), key_rows)
@@ -185,29 +203,31 @@
     direct_ref, swapped_ref, out_hbm, out_ref, trusted_ref, out_sems = refs
     heads = query_ref.shape[1] // HD
     blocks = row_blocks(query_ref.shape[0], 80)
-    is_odd, core = place()
-    takes_both = is_odd & routed
+    position, core = place()
+    takes_both = (position == 1) & routed
+    is_direct = core == 0
 
     def out_copy(index, rows):
         return pltpu.make_async_copy(out_ref.at[rows], out_hbm.at[rows], out_sems.at[index])
 
     def write(rows, total, weighted):
-        unstack(out_ref, rows, heads, (weighted / total).astype(jnp.bfloat16))
+        inverse = pl.reciprocal(total, approx=True)
+        inverse = inverse * (2.0 - total * inverse)
+        unstack(out_ref, rows, heads, (weighted * inverse).astype(jnp.bfloat16))
 
     def process(shard):
         trusted = [jnp.full((8, HD), True)]
+        key_rows, value_rows = shard[:, :HD], with_ones(shard[:, HD:])
 
         def start(rows):
-            return scores_of(stacked(query_ref, rows, heads), shard[:, :HD])
+            return scores_of(stacked(query_ref, rows, heads), key_rows)
 
         def finish(index, rows, scores):
             best = stacked(best_ref, rows, heads)
-            weights = jnp.exp2(scores - widen(best, scores.shape[1]))
-            lanes = sum(weights[:, i : i + HD] for i in range(0, scores.shape[1], HD))
-            total = stacked(total_ref, rows, heads) + jnp.sum(lanes, axis=1, keepdims=True)
-            weighted = stacked(sum_ref, rows, heads) + jnp.dot(
-                weights.astype(jnp.bfloat16), shard[:, HD:], preferred_element_type=jnp.float32
-            )
+            weights = jnp.exp2(scores - widen(best, scores.shape[1])).astype(jnp.bfloat16)
+            result = jnp.dot(weights, value_rows, preferred_element_type=jnp.float32)
+            total = stacked(total_ref, rows, heads) + result[:, HD:]
+            weighted = stacked(sum_ref, rows, heads) + result[:, :HD]
             good = (total < total_limit).reshape(total.shape[0] // 8, 8, HD)
             trusted[0] = trusted[0] & jnp.all(good, axis=0)
             write(rows, total, weighted)
@@ -220,7 +240,7 @@
 
     @pl.when(jnp.logical_not(takes_both))
     def one_shard():
-        process(jnp.where(core == 0, direct_ref[...], swapped_ref[...]))
+        process(jnp.where(is_direct, direct_ref[...], swapped_ref[...]))
 
     @pl.when(takes_both)
     def two_shards():
@@ -232,12 +252,12 @@
         counted = [(ref, 0.0) for ref in earlier_refs]
         if routed:
             counted[-2:] = [
-                (ref, penalty(jnp.logical_not(is_odd) | (core == by_swap)))
+                (ref, penalty((position != 1) | (core == by_swap)))
                 for by_swap, ref in enumerate(earlier_refs[-2:])
             ]
         counted += [
-            (ref, penalty(takes_both | (core == by_swap)))
-            for by_swap, ref in enumerate([direct_ref, swapped_ref])
+            (direct_ref, penalty(takes_both | is_direct)),
+            (swapped_ref, penalty(takes_both | jnp.logical_not(is_direct))),
         ]
 
         def visit(index, unused):
@@ -275,6 +295,12 @@
     suffix = suffix_kv[:, 0, :]
     shard_rows = own.shape[0]
 
+    in_hbm = pl.BlockSpec(memory_space=pltpu.HBM)
+    in_vmem = pl.BlockSpec(memory_space=pltpu.VMEM)
+    state = jax.ShapeDtypeStruct((slots, width), jnp.float32)
+
+    cost = pl.CostEstimate(flops=1, bytes_accessed=1, transcendentals=0)
+
     routed = loop_size >= FOUR and loop_size & (loop_size - 1) == 0
 
     def send(shard, route):
@@ -286,47 +312,47 @@
         return lax.ppermute(shard, ("loop", "pair"), hops)
 
     def first_route(i, core):
-        if core == 1:
-            return (i ^ 2) & ~1, i & 1
-        return (i, 1) if i & 1 else (i + 1, 0)
+        base = i - i % FOUR
+        to, to_core = [((1, 0), (3, 1)), ((1, 1), (2, 0)), ((3, 0), (0, 0)), ((2, 1), (0, 1))][
+            i % FOUR
+        ][core]
+        return base + to, to_core
 
     def second_route(i, core):
-        if core == 1:
-            return (i ^ 2) | 1, i & 1
-        return (i - 1, 0) if i & 1 else (i, 1)
-
-    early = []
+        base = i - i % FOUR
+        to, to_core = [((0, 1), (2, 0)), ((0, 0), (3, 0)), ((2, 1), (1, 0)), ((3, 1), (1, 1))][
+            i % FOUR
+        ][core]
+        return base + to, to_core
+
+    hbm = [pltpu.with_memory_space_constraint(x, pltpu.HBM) for x in (lengths, queries, suffix, own)]
+    buffers = [
+        jax.ShapeDtypeStruct(queries.shape, queries.dtype),
+        jax.ShapeDtypeStruct(suffix.shape, suffix.dtype),
+        jax.ShapeDtypeStruct(own.shape, own.dtype),
+        jax.ShapeDtypeStruct((slots, HD), jnp.int32),
+    ]
+    load_scratch = [
+        pltpu.SMEM(lengths.shape, lengths.dtype),
+        pltpu.SemaphoreType.DMA((2 + 2 * len(load_blocks(slots)),)),
+    ]
+    loaded = pl.pallas_call(
+        prelude_stage,
+        name="prelude_stage",
+        out_shape=buffers,
+        in_specs=[in_hbm] * 4,
+        out_specs=[in_vmem] * 4,
+        scratch_shapes=load_scratch,
+        compiler_params=pltpu.CompilerParams(vmem_limit_bytes=8 * 2**20),
+        cost_estimate=cost,
+    )(*hbm)
+    own, loaded = lax.optimization_barrier((own, loaded))
     if routed:
         early = [
             send(own, lambda i, core, step=step: (i ^ (step + core), 1 - core))
             for step in range(FOUR, loop_size, 2)
         ]
         early.append(send(own, first_route))
-    in_hbm = pl.BlockSpec(memory_space=pltpu.HBM)
-    in_vmem = pl.BlockSpec(memory_space=pltpu.VMEM)
-    state = jax.ShapeDtypeStruct((slots, width), jnp.float32)
-
-    cost = pl.CostEstimate(flops=1, bytes_accessed=1, transcendentals=0)
-
-    queries, suffix, own, first = pl.pallas_call(
-        load_stage,
-        name="load_stage",
-        out_shape=[
-            jax.ShapeDtypeStruct(queries.shape, queries.dtype),
-            jax.ShapeDtypeStruct(suffix.shape, suffix.dtype),
-            jax.ShapeDtypeStruct(own.shape, own.dtype),
-            jax.ShapeDtypeStruct((slots, HD), jnp.int32),
-        ],
-        in_specs=[in_hbm] * 4,
-        out_specs=[in_vmem] * 4,
-        scratch_shapes=[
-            pltpu.SMEM(lengths.shape, lengths.dtype),
-            pltpu.SemaphoreType.DMA((2 + 2 * len(load_blocks(slots)),)),
-        ],
-        compiler_params=pltpu.CompilerParams(vmem_limit_bytes=8 * 2**20),
-        cost_estimate=cost,
-    )(*(pltpu.with_memory_space_constraint(x, pltpu.HBM) for x in (lengths, queries, suffix, own)))
-    if routed:
         final = send(own, second_route)
     else:
         early = [
@@ -334,15 +360,17 @@
             for step in range(1, loop_size)
         ]
         final = early.pop()
-    best, total, weighted = pl.pallas_call(
+    best, total, weighted, queries, *unused = pl.pallas_call(
         local_stage,
         name="local_stage",
-        out_shape=[state] * 3,
-        in_specs=[in_vmem] * 4,
-        out_specs=[in_vmem] * 3,
+        out_shape=[state] * 3 + buffers,
+        in_specs=[in_hbm] * 4 + [in_vmem] * 4,
+        out_specs=[in_vmem] * 7,
+        scratch_shapes=load_scratch,
+        input_output_aliases={4 + i: 3 + i for i in range(4)},
         compiler_params=pltpu.CompilerParams(vmem_limit_bytes=24 * 2**20),
         cost_estimate=cost,
-    )(queries, suffix, own, first)
+    )(*hbm, *loaded)
 
     def add_shards(total, weighted, shards_now, by_swap):
         if not shards_now:

time: 24.5 us -> 25.4 us (1.037)
  the two profiles are of different devices: /device:TPU:0 before, /device:TPU:3 now
where the time goes in v22:
time: 25.4 us; the launch traced here: 25.3 us
  Pallas kernels  18.7 us (74%)
  starting transfers between devices  5.39 us (21%)
  waiting for transfers between devices  1.15 us (5%)
    pallas_call x1, Pallas kernels, shards(): pl.pallas_call(functools.partial(last_stage, routed), name='last_stage',...  12.5 us
    ppermute x4, starting transfers between devices, send(): return lax.ppermute(shard, ('loop', 'pair'), hops)  5.39 us
    pallas_call x1, Pallas kernels, shards(): pl.pallas_call(local_stage, name='local_stage', out_shape=[state] * 3 + b...  3.03 us
    pallas_call x2, Pallas kernels, add_shards(): pl.pallas_call(functools.partial(add_stage, by_swap if routed else None),...  1.79 us
    pallas_call x1, Pallas kernels, shards(): pl.pallas_call(prelude_stage, name='prelude_stage', out_shape=buffers, in...  1.35 us
    ppermute x4, waiting for transfers between devices, send(): return lax.ppermute(shard, ('loop', 'pair'), hops)  1.15 us
  transfers between devices with their start and end apart: 4, of which 2 were waited for; matrix products, arithmetic and copies ran while one was open for 0% of the time, Pallas kernels for 19%

profile of v22, /device:TPU:3, one launch (start us, length us, event | category | flops | bytes accessed | tf_op | source)
XLA Modules:
  0.0 25.3 jit_solution(10348598846074298609)
XLA Ops:
  0.0 1.4 %prelude_stage.1 = (bf16[640,512]{1,0:T(8,128)(2,1)S(1)}, bf16[640,256]{1,0:T(8,128)(2,1)S(1)}, bf16[256,256]{1,0:T(8,128)(2,1)S(1)}, s32[640,128]{1,0:T(8,128)S(1)}) custom-call(s32[8]{0:T(128)} %refs_0_.3, bf16[640,512]{1,0:T(8,128)(2,1)} %refs_1_.3, bf16[640,256]{1,0:T(8,128)(2,1)} %bitcast.2, bf16[256,256]{1,0:T(8,128)(2,1)} %bitcast.4), custom_call_target="tpu_custom_call" | custom-call | flops 1 | bytes 1 | tf_op jit(solution)/shard_map/prelude_stage/pallas_call | solution.py:339
  1.4 2.1 %collective-permute-start = (bf16[256,256]{1,0:T(8,128)(2,1)}, bf16[256,256]{1,0:T(8,128)(2,1)S(1)}, u32[]{:S(2)}, u32[]{:S(2)}) collective-permute-start(bf16[256,256]{1,0:T(8,128)(2,1)} %bitcast.5), channel_id=1, source_target_pairs={{0,4},{1,13},{4,5},{5,8},{8,12},{9,0},{12,9},{13,1},{2,6},{3,15},{... | collective-permute-start | bytes 393224 | tf_op jit(solution)/shard_map/ppermute | solution.py:312
  3.5 1.1 %collective-permute-start.1 = (bf16[256,256]{1,0:T(8,128)(2,1)}, bf16[256,256]{1,0:T(8,128)(2,1)S(1)}, u32[]{:S(2)}, u32[]{:S(2)}) collective-permute-start(bf16[256,256]{1,0:T(8,128)(2,1)} %bitcast.6), channel_id=1, source_target_pairs={{0,1},{1,8},{4,0},{5,12},{8,9},{9,4},{12,13},{13,5},{2,3},{3,10},{... | collective-permute-start | bytes 393224 | tf_op jit(solution)/shard_map/ppermute | solution.py:312
  4.6 3.0 %local_stage.1 = (f32[640,512]{1,0:T(8,128)S(1)}, f32[640,512]{1,0:T(8,128)S(1)}, f32[640,512]{1,0:T(8,128)S(1)}, bf16[640,512]{1,0:T(8,128)(2,1)S(1)}, bf16[640...) custom-call(s32[8]{0:T(128)} %refs_0_.3, ...), custom_call_target="tpu_custom_call", output_to_operand_aliasing={{3}: (4, {}), {4}: (5, {}), {5}: (6, {}), {6}: (7, {})} | custom-call | flops 1 | bytes 1 | tf_op jit(solution)/shard_map/local_stage/pallas_call | solution.py:363
  7.7 0.7 %collective-permute-done.refs_4_.refs_6_ = bf16[256,256]{1,0:T(8,128)(2,1)S(1)} collective-permute-done((bf16[256,256]{1,0:T(8,128)(2,1)}, bf16[256,256]{1,0:T(8,128)(2,1)S(1)}, u32[]{:S(2)}, u32[]{:S(2)}) %collective-permute-start) | collective-permute-done | bytes 131104 | tf_op jit(solution)/shard_map/ppermute | solution.py:312
  8.4 2.1 %collective-permute-start.2 = (bf16[256,256]{1,0:T(8,128)(2,1)S(1)}, bf16[256,256]{1,0:T(8,128)(2,1)S(1)}, u32[]{:S(2)}, u32[]{:S(2)}) collective-permute-start(bf16[256,256]{1,0:T(8,128)(2,1)S(1)} %collective-permute-done.refs_4_.refs_6_), channel_id=1, source_target_pairs={{0,1},{1,0},{4,5},{5,4},{8,9},{9,8},{12,13},{13,12},{2,3},{3,2},{6... | collective-permute-start | bytes 393224 | tf_op jit(solution)/shard_map/ppermute | solution.py:312
  10.5 0.9 %add_stage.2 = (f32[640,512]{1,0:T(8,128)S(1)}, f32[640,512]{1,0:T(8,128)S(1)}) custom-call(bf16[640,512]{1,0:T(8,128)(2,1)S(1)} %get-tuple-element.34.refs_0_, f32[640,512]{1,0:T(8,128)S(1)} %get-tuple-element.37.refs_1_, f32[640,512]{1,0:T(8,128)S(1)} %get-tuple-element.38.refs_2_, f32[640,512]{1,0:T(8,128)S(1)} %get-tuple-element.39.refs_3_, ...), custom_call_target="tpu_custom_call" | custom-call | flops 1 | bytes 1 | tf_op jit(solution)/shard_map/add_stage/pallas_call | solution.py:378
  11.4 0.0 collective-permute-done.1.refs_8_
  11.4 0.1 collective-permute-start.3
  11.4 0.0 collective-permute-done.2.refs_4_.refs_7_
  11.5 0.9 %add_stage.3 = (f32[640,512]{1,0:T(8,128)S(1)}, f32[640,512]{1,0:T(8,128)S(1)}) custom-call(bf16[640,512]{1,0:T(8,128)(2,1)S(1)} %get-tuple-element.34.refs_0_, f32[640,512]{1,0:T(8,128)S(1)} %get-tuple-element.37.refs_1_, f32[640,512]{1,0:T(8,128)S(1)} %get-tuple-element.42.refs_2_, f32[640,512]{1,0:T(8,128)S(1)} %get-tuple-element.43.refs_3_, ...), custom_call_target="tpu_custom_call" | custom-call | flops 1 | bytes 1 | tf_op jit(solution)/shard_map/add_stage/pallas_call | solution.py:378
  12.4 0.4 %collective-permute-done.3.refs_9_ = bf16[256,256]{1,0:T(8,128)(2,1)S(1)} collective-permute-done((bf16[256,256]{1,0:T(8,128)(2,1)S(1)}, bf16[256,256]{1,0:T(8,128)(2,1)S(1)}, u32[]{:S(2)}, u32[]{:S(2)}) %collective-permute-start.3) | collective-permute-done | bytes 131104 | tf_op jit(solution)/shard_map/ppermute | solution.py:312
  12.8 12.5 %last_stage.1 = bf16[640,512]{1,0:T(8,128)(2,1)} custom-call(bf16[640,512]{1,0:T(8,128)(2,1)S(1)} %get-tuple-element.34.refs_0_, f32[640,512]{1,0:T(8,128)S(1)} %get-tuple-element.37.refs_1_, f32[640,512]{1,0:T(8,128)S(1)} %get-tuple-element.38.refs_2_, f32[640,512]{1,0:T(8,128)S(1)} %get-tuple-element.39.refs_3_, f32[640,512]{1,0:T(8,128)S(1)} %get-tuple-element.44.refs_4_, ...), custom_call_target="tpu_custom_call" | custom-call | flops 1 | bytes 1 | tf_op jit(solution)/shard_map/last_stage/pallas_call | solution.py:400
Async XLA Ops:
  1.4 7.0 %collective-permute-start = (bf16[256,256]{1,0:T(8,128)(2,1)}, bf16[256,256]{1,0:T(8,128)(2,1)S(1)}, u32[]{:S(2)}, u32[]{:S(2)}) collective-permute-start(bf16[256,256]{1,0:T(8,128)(2,1)} %bitcast.5), channel_id=1, source_target_pairs={{0,4},{1,13},{4,5},{5,8},{8,12},{9,0},{12,9},{13,1},{2,6},{3,15},{... | collective-permute-start | bytes 393224 | tf_op jit(solution)/shard_map/ppermute | solution.py:312
  3.5 7.9 %collective-permute-start.1 = (bf16[256,256]{1,0:T(8,128)(2,1)}, bf16[256,256]{1,0:T(8,128)(2,1)S(1)}, u32[]{:S(2)}, u32[]{:S(2)}) collective-permute-start(bf16[256,256]{1,0:T(8,128)(2,1)} %bitcast.6), channel_id=1, source_target_pairs={{0,1},{1,8},{4,0},{5,12},{8,9},{9,4},{12,13},{13,5},{2,3},{3,10},{... | collective-permute-start | bytes 393224 | tf_op jit(solution)/shard_map/ppermute | solution.py:312
  8.4 3.1 %collective-permute-start.2 = (bf16[256,256]{1,0:T(8,128)(2,1)S(1)}, bf16[256,256]{1,0:T(8,128)(2,1)S(1)}, u32[]{:S(2)}, u32[]{:S(2)}) collective-permute-start(bf16[256,256]{1,0:T(8,128)(2,1)S(1)} %collective-permute-done.refs_4_.refs_6_), channel_id=1, source_target_pairs={{0,1},{1,0},{4,5},{5,4},{8,9},{9,8},{12,13},{13,12},{2,3},{3,2},{6... | collective-permute-start | bytes 393224 | tf_op jit(solution)/shard_map/ppermute | solution.py:312
  11.4 1.4 %collective-permute-start.3 = (bf16[256,256]{1,0:T(8,128)(2,1)S(1)}, bf16[256,256]{1,0:T(8,128)(2,1)S(1)}, u32[]{:S(2)}, u32[]{:S(2)}) collective-permute-start(bf16[256,256]{1,0:T(8,128)(2,1)S(1)} %collective-permute-done.1.refs_8_), channel_id=1, source_target_pairs={{0,1},{1,0},{4,5},{5,4},{8,9},{9,8},{12,13},{13,12},{2,3},{3,2},{6... | collective-permute-start | bytes 393224 | tf_op jit(solution)/shard_map/ppermute | solution.py:312

commit v23 on v22

--- a/solution.py
+++ b/solution.py
@@ -92,7 +92,7 @@
 
 
 def prelude_stage(*refs):
-    @pl.when(place()[0] == 0)
+    @pl.when(is_first_chip())
     def ahead():
         load(*refs)
 
@@ -106,7 +106,7 @@
     )
     query_ref, suffix_ref, own_ref, first_ref = loaded
 
-    @pl.when(place()[0] != 0)
+    @pl.when(jnp.logical_not(is_first_chip()))
     def now():
         load(*sources, *loaded, *scratch)
 
@@ -162,6 +162,10 @@
     return [slice(first, first + step) for first in range(0, count, step)]
 
 
+def is_first_chip():
+    return lax.axis_index("groups") + lax.axis_index("loop") + lax.axis_index("heads") == 0
+
+
 def penalty(is_there):
     return jnp.where(is_there, 0.0, empty_best)
 
@@ -313,7 +317,7 @@
 
     def first_route(i, core):
         base = i - i % FOUR
-        to, to_core = [((1, 0), (3, 1)), ((1, 1), (2, 0)), ((3, 0), (0, 0)), ((2, 1), (0, 1))][
+        to, to_core = [((1, 0), (3, 1)), ((1, 1), (2, 1)), ((0, 0), (3, 0)), ((2, 0), (0, 1))][
             i % FOUR
         ][core]
         return base + to, to_core

time: 25.4 us -> 26.4 us (1.039)
  the two profiles are of different devices: /device:TPU:3 before, /device:TPU:0 now
where the time goes in v23:
time: 26.4 us; the launch traced here: 26.2 us
  Pallas kernels  18.6 us (70%)
  starting transfers between devices  4 us (15%)
  waiting for transfers between devices  3.51 us (13%)
    pallas_call x1, Pallas kernels, shards(): pl.pallas_call(functools.partial(last_stage, routed), name='last_stage',...  12.5 us
    ppermute x4, starting transfers between devices, send(): return lax.ppermute(shard, ('loop', 'pair'), hops)  4 us
    ppermute x4, waiting for transfers between devices, send(): return lax.ppermute(shard, ('loop', 'pair'), hops)  3.51 us
    pallas_call x1, Pallas kernels, shards(): pl.pallas_call(local_stage, name='local_stage', out_shape=[state] * 3 + b...  3.04 us
    pallas_call x2, Pallas kernels, add_shards(): pl.pallas_call(functools.partial(add_stage, by_swap if routed else None),...  1.78 us
    pallas_call x1, Pallas kernels, shards(): pl.pallas_call(prelude_stage, name='prelude_stage', out_shape=buffers, in...  1.35 us
  transfers between devices with their start and end apart: 4, of which 2 were waited for; matrix products, arithmetic and copies ran while one was open for 0% of the time, Pallas kernels for 18%

profile of v23, /device:TPU:0, one launch (start us, length us, event | category | flops | bytes accessed | tf_op | source)
XLA Modules:
  0.0 26.2 jit_solution(16576792259829541254)
XLA Ops:
  0.0 1.4 %prelude_stage.1 = (bf16[640,512]{1,0:T(8,128)(2,1)S(1)}, bf16[640,256]{1,0:T(8,128)(2,1)S(1)}, bf16[256,256]{1,0:T(8,128)(2,1)S(1)}, s32[640,128]{1,0:T(8,128)S(1)}) custom-call(s32[8]{0:T(128)} %refs_0_.3, bf16[640,512]{1,0:T(8,128)(2,1)} %refs_1_.3, bf16[640,256]{1,0:T(8,128)(2,1)} %bitcast.2, bf16[256,256]{1,0:T(8,128)(2,1)} %bitcast.4), custom_call_target="tpu_custom_call" | custom-call | flops 1 | bytes 1 | tf_op jit(solution)/shard_map/prelude_stage/pallas_call | solution.py:343
  1.4 1.8 %collective-permute-start = (bf16[256,256]{1,0:T(8,128)(2,1)}, bf16[256,256]{1,0:T(8,128)(2,1)S(1)}, u32[]{:S(2)}, u32[]{:S(2)}) collective-permute-start(bf16[256,256]{1,0:T(8,128)(2,1)} %bitcast.5), channel_id=1, source_target_pairs={{0,4},{1,13},{4,5},{5,9},{8,0},{9,12},{12,8},{13,1},{2,6},{3,15},{... | collective-permute-start | bytes 393224 | tf_op jit(solution)/shard_map/ppermute | solution.py:316
  3.2 1.6 %collective-permute-start.1 = (bf16[256,256]{1,0:T(8,128)(2,1)}, bf16[256,256]{1,0:T(8,128)(2,1)S(1)}, u32[]{:S(2)}, u32[]{:S(2)}) collective-permute-start(bf16[256,256]{1,0:T(8,128)(2,1)} %bitcast.6), channel_id=1, source_target_pairs={{0,1},{1,8},{4,0},{5,12},{8,9},{9,4},{12,13},{13,5},{2,3},{3,10},{... | collective-permute-start | bytes 393224 | tf_op jit(solution)/shard_map/ppermute | solution.py:316
  4.8 3.0 %local_stage.1 = (f32[640,512]{1,0:T(8,128)S(1)}, f32[640,512]{1,0:T(8,128)S(1)}, f32[640,512]{1,0:T(8,128)S(1)}, bf16[640,512]{1,0:T(8,128)(2,1)S(1)}, bf16[640...) custom-call(s32[8]{0:T(128)} %refs_0_.3, ...), custom_call_target="tpu_custom_call", output_to_operand_aliasing={{3}: (4, {}), {4}: (5, {}), {5}: (6, {}), {6}: (7, {})} | custom-call | flops 1 | bytes 1 | tf_op jit(solution)/shard_map/local_stage/pallas_call | solution.py:367
  7.8 3.4 %collective-permute-done.refs_4_.refs_6_ = bf16[256,256]{1,0:T(8,128)(2,1)S(1)} collective-permute-done((bf16[256,256]{1,0:T(8,128)(2,1)}, bf16[256,256]{1,0:T(8,128)(2,1)S(1)}, u32[]{:S(2)}, u32[]{:S(2)}) %collective-permute-start) | collective-permute-done | bytes 131104 | tf_op jit(solution)/shard_map/ppermute | solution.py:316
  11.2 0.0 collective-permute-start.2
  11.2 0.9 %add_stage.2 = (f32[640,512]{1,0:T(8,128)S(1)}, f32[640,512]{1,0:T(8,128)S(1)}) custom-call(bf16[640,512]{1,0:T(8,128)(2,1)S(1)} %get-tuple-element.34.refs_0_, f32[640,512]{1,0:T(8,128)S(1)} %get-tuple-element.37.refs_1_, f32[640,512]{1,0:T(8,128)S(1)} %get-tuple-element.38.refs_2_, f32[640,512]{1,0:T(8,128)S(1)} %get-tuple-element.39.refs_3_, ...), custom_call_target="tpu_custom_call" | custom-call | flops 1 | bytes 1 | tf_op jit(solution)/shard_map/add_stage/pallas_call | solution.py:382
  12.1 0.0 collective-permute-done.1.refs_8_
  12.2 0.6 %collective-permute-start.3 = (bf16[256,256]{1,0:T(8,128)(2,1)S(1)}, bf16[256,256]{1,0:T(8,128)(2,1)S(1)}, u32[]{:S(2)}, u32[]{:S(2)}) collective-permute-start(bf16[256,256]{1,0:T(8,128)(2,1)S(1)} %collective-permute-done.1.refs_8_), channel_id=1, source_target_pairs={{0,1},{1,0},{4,5},{5,4},{8,9},{9,8},{12,13},{13,12},{2,3},{3,2},{6... | collective-permute-start | bytes 393224 | tf_op jit(solution)/shard_map/ppermute | solution.py:316
  12.7 0.0 collective-permute-done.2.refs_4_.refs_7_
  12.7 0.9 %add_stage.3 = (f32[640,512]{1,0:T(8,128)S(1)}, f32[640,512]{1,0:T(8,128)S(1)}) custom-call(bf16[640,512]{1,0:T(8,128)(2,1)S(1)} %get-tuple-element.34.refs_0_, f32[640,512]{1,0:T(8,128)S(1)} %get-tuple-element.37.refs_1_, f32[640,512]{1,0:T(8,128)S(1)} %get-tuple-element.42.refs_2_, f32[640,512]{1,0:T(8,128)S(1)} %get-tuple-element.43.refs_3_, ...), custom_call_target="tpu_custom_call" | custom-call | flops 1 | bytes 1 | tf_op jit(solution)/shard_map/add_stage/pallas_call | solution.py:382
  13.6 0.1 collective-permute-done.3.refs_9_
  13.7 12.5 %last_stage.1 = bf16[640,512]{1,0:T(8,128)(2,1)} custom-call(bf16[640,512]{1,0:T(8,128)(2,1)S(1)} %get-tuple-element.34.refs_0_, f32[640,512]{1,0:T(8,128)S(1)} %get-tuple-element.37.refs_1_, f32[640,512]{1,0:T(8,128)S(1)} %get-tuple-element.38.refs_2_, f32[640,512]{1,0:T(8,128)S(1)} %get-tuple-element.39.refs_3_, f32[640,512]{1,0:T(8,128)S(1)} %get-tuple-element.44.refs_4_, ...), custom_call_target="tpu_custom_call" | custom-call | flops 1 | bytes 1 | tf_op jit(solution)/shard_map/last_stage/pallas_call | solution.py:404
Async XLA Ops:
  1.4 9.9 %collective-permute-start = (bf16[256,256]{1,0:T(8,128)(2,1)}, bf16[256,256]{1,0:T(8,128)(2,1)S(1)}, u32[]{:S(2)}, u32[]{:S(2)}) collective-permute-start(bf16[256,256]{1,0:T(8,128)(2,1)} %bitcast.5), channel_id=1, source_target_pairs={{0,4},{1,13},{4,5},{5,9},{8,0},{9,12},{12,8},{13,1},{2,6},{3,15},{... | collective-permute-start | bytes 393224 | tf_op jit(solution)/shard_map/ppermute | solution.py:316
  3.2 8.9 %collective-permute-start.1 = (bf16[256,256]{1,0:T(8,128)(2,1)}, bf16[256,256]{1,0:T(8,128)(2,1)S(1)}, u32[]{:S(2)}, u32[]{:S(2)}) collective-permute-start(bf16[256,256]{1,0:T(8,128)(2,1)} %bitcast.6), channel_id=1, source_target_pairs={{0,1},{1,8},{4,0},{5,12},{8,9},{9,4},{12,13},{13,5},{2,3},{3,10},{... | collective-permute-start | bytes 393224 | tf_op jit(solution)/shard_map/ppermute | solution.py:316
  11.2 1.5 %collective-permute-start.2 = (bf16[256,256]{1,0:T(8,128)(2,1)S(1)}, bf16[256,256]{1,0:T(8,128)(2,1)S(1)}, u32[]{:S(2)}, u32[]{:S(2)}) collective-permute-start(bf16[256,256]{1,0:T(8,128)(2,1)S(1)} %collective-permute-done.refs_4_.refs_6_), channel_id=1, source_target_pairs={{0,1},{1,0},{4,5},{5,4},{8,9},{9,8},{12,13},{13,12},{2,3},{3,2},{6... | collective-permute-start | bytes 393224 | tf_op jit(solution)/shard_map/ppermute | solution.py:316
  12.2 1.6 %collective-permute-start.3 = (bf16[256,256]{1,0:T(8,128)(2,1)S(1)}, bf16[256,256]{1,0:T(8,128)(2,1)S(1)}, u32[]{:S(2)}, u32[]{:S(2)}) collective-permute-start(bf16[256,256]{1,0:T(8,128)(2,1)S(1)} %collective-permute-done.1.refs_8_), channel_id=1, source_target_pairs={{0,1},{1,0},{4,5},{5,4},{8,9},{9,8},{12,13},{13,12},{2,3},{3,2},{6... | collective-permute-start | bytes 393224 | tf_op jit(solution)/shard_map/ppermute | solution.py:316

commit v24 on v23

--- a/solution.py
+++ b/solution.py
@@ -48,7 +48,7 @@
 
 
 def place():
-    return lax.rem(lax.axis_index("loop"), FOUR), lax.axis_index("pair")
+    return lax.rem(lax.axis_index("loop"), 2) == 1, lax.axis_index("pair")
 
 
 def load_blocks(count):
@@ -179,8 +179,8 @@
     key_rows, value_rows = shard[:, :HD], with_ones(shard[:, HD:])
     extra = None
     if by_swap is not None:
-        position, core = place()
-        extra = penalty((position != 1) | (core == int(by_swap)))
+        is_odd, core = place()
+        extra = penalty(jnp.logical_not(is_odd) | (core == int(by_swap)))
 
     def start(rows):
         return scores_of(stacked(query_ref, rows, heads), key_rows)
@@ -207,8 +207,8 @@
     direct_ref, swapped_ref, out_hbm, out_ref, trusted_ref, out_sems = refs
     heads = query_ref.shape[1] // HD
     blocks = row_blocks(query_ref.shape[0], 80)
-    position, core = place()
-    takes_both = (position == 1) & routed
+    is_odd, core = place()
+    takes_both = is_odd & routed
     is_direct = core == 0
 
     def out_copy(index, rows):
@@ -256,7 +256,7 @@
         counted = [(ref, 0.0) for ref in earlier_refs]
         if routed:
             counted[-2:] = [
-                (ref, penalty((position != 1) | (core == by_swap)))
+                (ref, penalty(jnp.logical_not(is_odd) | (core == by_swap)))
                 for by_swap, ref in enumerate(earlier_refs[-2:])
             ]
         counted += [
@@ -316,18 +316,14 @@
         return lax.ppermute(shard, ("loop", "pair"), hops)
 
     def first_route(i, core):
-        base = i - i % FOUR
-        to, to_core = [((1, 0), (3, 1)), ((1, 1), (2, 1)), ((0, 0), (3, 0)), ((2, 0), (0, 1))][
-            i % FOUR
-        ][core]
-        return base + to, to_core
+        if core == 1:
+            return (i ^ 2) & ~1, i & 1
+        return (i, 1) if i & 1 else (i + 1, 0)
 
     def second_route(i, core):
-        base = i - i % FOUR
-        to, to_core = [((0, 1), (2, 0)), ((0, 0), (3, 0)), ((2, 1), (1, 0)), ((3, 1), (1, 1))][
-            i % FOUR
-        ][core]
-        return base + to, to_core
+        if core == 1:
+            return (i ^ 2) | 1, 1 - i & 1
+        return (i - 1, 0) if i & 1 else (i, 1)
 
     hbm = [pltpu.with_memory_space_constraint(x, pltpu.HBM) for x in (lengths, queries, suffix, own)]
     buffers = [

time: 26.4 us -> 24.9 us (0.943)
  waiting for transfers between devices: 3.51 us -> 2.45 us
  starting transfers between devices: 4 us -> 3.55 us
    ppermute x4, waiting for transfers between devices: 3.51 us -> 2.45 us  [send(): return lax.ppermute(shard, ('loop', 'pair'), hops)]
    ppermute x4, starting transfers between devices: 4 us -> 3.55 us  [send(): return lax.ppermute(shard, ('loop', 'pair'), hops)]
  transfers between devices with their start and end apart: 4 -> 4, of which waited for: 2 -> 2; matrix products, arithmetic and copies ran while one was open for 0% -> 0% of each run, Pallas kernels for 18% -> 20%
where the time goes in v24:
time: 24.9 us; the launch traced here: 24.7 us
  Pallas kernels  18.7 us (75%)
  starting transfers between devices  3.55 us (14%)
  waiting for transfers between devices  2.45 us (10%)
    pallas_call x1, Pallas kernels, shards(): pl.pallas_call(functools.partial(last_stage, routed), name='last_stage',...  12.5 us
    ppermute x4, starting transfers between devices, send(): return lax.ppermute(shard, ('loop', 'pair'), hops)  3.55 us
    pallas_call x1, Pallas kernels, shards(): pl.pallas_call(local_stage, name='local_stage', out_shape=[state] * 3 + b...  3.04 us
    ppermute x4, waiting for transfers between devices, send(): return lax.ppermute(shard, ('loop', 'pair'), hops)  2.45 us
    pallas_call x2, Pallas kernels, add_shards(): pl.pallas_call(functools.partial(add_stage, by_swap if routed else None),...  1.78 us
    pallas_call x1, Pallas kernels, shards(): pl.pallas_call(prelude_stage, name='prelude_stage', out_shape=buffers, in...  1.35 us
  transfers between devices with their start and end apart: 4, of which 2 were waited for; matrix products, arithmetic and copies ran while one was open for 0% of the time, Pallas kernels for 20%

profile of v24, /device:TPU:0, one launch (start us, length us, event | category | flops | bytes accessed | tf_op | source)
XLA Modules:
  0.0 24.7 jit_solution(17412690279740894711)
XLA Ops:
  0.0 1.4 %prelude_stage.1 = (bf16[640,512]{1,0:T(8,128)(2,1)S(1)}, bf16[640,256]{1,0:T(8,128)(2,1)S(1)}, bf16[256,256]{1,0:T(8,128)(2,1)S(1)}, s32[640,128]{1,0:T(8,128)S(1)}) custom-call(s32[8]{0:T(128)} %refs_0_.3, bf16[640,512]{1,0:T(8,128)(2,1)} %refs_1_.3, bf16[640,256]{1,0:T(8,128)(2,1)} %bitcast.2, bf16[256,256]{1,0:T(8,128)(2,1)} %bitcast.4), custom_call_target="tpu_custom_call" | custom-call | flops 1 | bytes 1 | tf_op jit(solution)/shard_map/prelude_stage/pallas_call | solution.py:339
  1.4 1.8 %collective-permute-start = (bf16[256,256]{1,0:T(8,128)(2,1)}, bf16[256,256]{1,0:T(8,128)(2,1)S(1)}, u32[]{:S(2)}, u32[]{:S(2)}) collective-permute-start(bf16[256,256]{1,0:T(8,128)(2,1)} %bitcast.5), channel_id=1, source_target_pairs={{0,4},{1,8},{4,5},{5,9},{8,12},{9,0},{12,13},{13,1},{2,6},{3,10},{... | collective-permute-start | bytes 393224 | tf_op jit(solution)/shard_map/ppermute | solution.py:316
  3.2 1.1 %collective-permute-start.1 = (bf16[256,256]{1,0:T(8,128)(2,1)}, bf16[256,256]{1,0:T(8,128)(2,1)S(1)}, u32[]{:S(2)}, u32[]{:S(2)}) collective-permute-start(bf16[256,256]{1,0:T(8,128)(2,1)} %bitcast.6), channel_id=1, source_target_pairs={{0,1},{1,13},{4,0},{5,12},{8,9},{9,5},{12,8},{13,4},{2,3},{3,15},{... | collective-permute-start | bytes 393224 | tf_op jit(solution)/shard_map/ppermute | solution.py:316
  4.3 3.0 %local_stage.1 = (f32[640,512]{1,0:T(8,128)S(1)}, f32[640,512]{1,0:T(8,128)S(1)}, f32[640,512]{1,0:T(8,128)S(1)}, bf16[640,512]{1,0:T(8,128)(2,1)S(1)}, bf16[640...) custom-call(s32[8]{0:T(128)} %refs_0_.3, ...), custom_call_target="tpu_custom_call", output_to_operand_aliasing={{3}: (4, {}), {4}: (5, {}), {5}: (6, {}), {6}: (7, {})} | custom-call | flops 1 | bytes 1 | tf_op jit(solution)/shard_map/local_stage/pallas_call | solution.py:363
  7.4 2.4 %collective-permute-done.refs_4_.refs_6_ = bf16[256,256]{1,0:T(8,128)(2,1)S(1)} collective-permute-done((bf16[256,256]{1,0:T(8,128)(2,1)}, bf16[256,256]{1,0:T(8,128)(2,1)S(1)}, u32[]{:S(2)}, u32[]{:S(2)}) %collective-permute-start) | collective-permute-done | bytes 131104 | tf_op jit(solution)/shard_map/ppermute | solution.py:316
  9.7 0.0 collective-permute-start.2
  9.7 0.9 %add_stage.2 = (f32[640,512]{1,0:T(8,128)S(1)}, f32[640,512]{1,0:T(8,128)S(1)}) custom-call(bf16[640,512]{1,0:T(8,128)(2,1)S(1)} %get-tuple-element.34.refs_0_, f32[640,512]{1,0:T(8,128)S(1)} %get-tuple-element.37.refs_1_, f32[640,512]{1,0:T(8,128)S(1)} %get-tuple-element.38.refs_2_, f32[640,512]{1,0:T(8,128)S(1)} %get-tuple-element.39.refs_3_, ...), custom_call_target="tpu_custom_call" | custom-call | flops 1 | bytes 1 | tf_op jit(solution)/shard_map/add_stage/pallas_call | solution.py:378
  10.6 0.0 collective-permute-done.1.refs_8_
  10.6 0.6 %collective-permute-start.3 = (bf16[256,256]{1,0:T(8,128)(2,1)S(1)}, bf16[256,256]{1,0:T(8,128)(2,1)S(1)}, u32[]{:S(2)}, u32[]{:S(2)}) collective-permute-start(bf16[256,256]{1,0:T(8,128)(2,1)S(1)} %collective-permute-done.1.refs_8_), channel_id=1, source_target_pairs={{0,1},{1,0},{4,5},{5,4},{8,9},{9,8},{12,13},{13,12},{2,3},{3,2},{6... | collective-permute-start | bytes 393224 | tf_op jit(solution)/shard_map/ppermute | solution.py:316
  11.2 0.0 collective-permute-done.2.refs_4_.refs_7_
  11.2 0.9 %add_stage.3 = (f32[640,512]{1,0:T(8,128)S(1)}, f32[640,512]{1,0:T(8,128)S(1)}) custom-call(bf16[640,512]{1,0:T(8,128)(2,1)S(1)} %get-tuple-element.34.refs_0_, f32[640,512]{1,0:T(8,128)S(1)} %get-tuple-element.37.refs_1_, f32[640,512]{1,0:T(8,128)S(1)} %get-tuple-element.42.refs_2_, f32[640,512]{1,0:T(8,128)S(1)} %get-tuple-element.43.refs_3_, ...), custom_call_target="tpu_custom_call" | custom-call | flops 1 | bytes 1 | tf_op jit(solution)/shard_map/add_stage/pallas_call | solution.py:378
  12.1 0.1 collective-permute-done.3.refs_9_
  12.2 12.5 %last_stage.1 = bf16[640,512]{1,0:T(8,128)(2,1)} custom-call(bf16[640,512]{1,0:T(8,128)(2,1)S(1)} %get-tuple-element.34.refs_0_, f32[640,512]{1,0:T(8,128)S(1)} %get-tuple-element.37.refs_1_, f32[640,512]{1,0:T(8,128)S(1)} %get-tuple-element.38.refs_2_, f32[640,512]{1,0:T(8,128)S(1)} %get-tuple-element.39.refs_3_, f32[640,512]{1,0:T(8,128)S(1)} %get-tuple-element.44.refs_4_, ...), custom_call_target="tpu_custom_call" | custom-call | flops 1 | bytes 1 | tf_op jit(solution)/shard_map/last_stage/pallas_call | solution.py:400
Async XLA Ops:
  1.4 8.4 %collective-permute-start = (bf16[256,256]{1,0:T(8,128)(2,1)}, bf16[256,256]{1,0:T(8,128)(2,1)S(1)}, u32[]{:S(2)}, u32[]{:S(2)}) collective-permute-start(bf16[256,256]{1,0:T(8,128)(2,1)} %bitcast.5), channel_id=1, source_target_pairs={{0,4},{1,8},{4,5},{5,9},{8,12},{9,0},{12,13},{13,1},{2,6},{3,10},{... | collective-permute-start | bytes 393224 | tf_op jit(solution)/shard_map/ppermute | solution.py:316
  3.2 7.4 %collective-permute-start.1 = (bf16[256,256]{1,0:T(8,128)(2,1)}, bf16[256,256]{1,0:T(8,128)(2,1)S(1)}, u32[]{:S(2)}, u32[]{:S(2)}) collective-permute-start(bf16[256,256]{1,0:T(8,128)(2,1)} %bitcast.6), channel_id=1, source_target_pairs={{0,1},{1,13},{4,0},{5,12},{8,9},{9,5},{12,8},{13,4},{2,3},{3,15},{... | collective-permute-start | bytes 393224 | tf_op jit(solution)/shard_map/ppermute | solution.py:316
  9.7 1.5 %collective-permute-start.2 = (bf16[256,256]{1,0:T(8,128)(2,1)S(1)}, bf16[256,256]{1,0:T(8,128)(2,1)S(1)}, u32[]{:S(2)}, u32[]{:S(2)}) collective-permute-start(bf16[256,256]{1,0:T(8,128)(2,1)S(1)} %collective-permute-done.refs_4_.refs_6_), channel_id=1, source_target_pairs={{0,1},{1,0},{4,5},{5,4},{8,9},{9,8},{12,13},{13,12},{2,3},{3,2},{6... | collective-permute-start | bytes 393224 | tf_op jit(solution)/shard_map/ppermute | solution.py:316
  10.6 1.6 %collective-permute-start.3 = (bf16[256,256]{1,0:T(8,128)(2,1)S(1)}, bf16[256,256]{1,0:T(8,128)(2,1)S(1)}, u32[]{:S(2)}, u32[]{:S(2)}) collective-permute-start(bf16[256,256]{1,0:T(8,128)(2,1)S(1)} %collective-permute-done.1.refs_8_), channel_id=1, source_target_pairs={{0,1},{1,0},{4,5},{5,4},{8,9},{9,8},{12,13},{13,12},{2,3},{3,2},{6... | collective-permute-start | bytes 393224 | tf_op jit(solution)/shard_map/ppermute | solution.py:316

commit v25 on v24

--- a/solution.py
+++ b/solution.py
@@ -91,10 +91,25 @@
         copy.wait()
 
 
-def prelude_stage(*refs):
-    @pl.when(is_first_chip())
-    def ahead():
+def loads_first():
+    axes = ("groups", "loop", "heads")
+    return sum(lax.axis_index(axis) for axis in axes) == 0
+
+
+def loads_last():
+    return lax.rem(lax.axis_index("loop"), FOUR) == FOUR - 1
+
+
+def load_ahead_stage(*refs):
+    @pl.when(loads_first())
+    def load_now():
         load(*refs)
+
+
+def load_between_stage(*refs):
+    @pl.when(jnp.logical_not(loads_first() | loads_last()))
+    def load_now():
+        load(*refs[:4], *refs[8:])
 
 
 def local_stage(*refs):
@@ -106,8 +121,8 @@
     )
     query_ref, suffix_ref, own_ref, first_ref = loaded
 
-    @pl.when(jnp.logical_not(is_first_chip()))
-    def now():
+    @pl.when(loads_last() & jnp.logical_not(loads_first()))
+    def load_now():
         load(*sources, *loaded, *scratch)
 
     slots = query_ref.shape[0]
@@ -162,10 +177,6 @@
     return [slice(first, first + step) for first in range(0, count, step)]
 
 
-def is_first_chip():
-    return lax.axis_index("groups") + lax.axis_index("loop") + lax.axis_index("heads") == 0
-
-
 def penalty(is_there):
     return jnp.where(is_there, 0.0, empty_best)
 
@@ -337,8 +348,8 @@
         pltpu.SemaphoreType.DMA((2 + 2 * len(load_blocks(slots)),)),
     ]
     loaded = pl.pallas_call(
-        prelude_stage,
-        name="prelude_stage",
+        load_ahead_stage,
+        name="load_ahead_stage",
         out_shape=buffers,
         in_specs=[in_hbm] * 4,
         out_specs=[in_vmem] * 4,
@@ -353,6 +364,19 @@
             for step in range(FOUR, loop_size, 2)
         ]
         early.append(send(own, first_route))
+    loaded = pl.pallas_call(
+        load_between_stage,
+        name="load_between_stage",
+        out_shape=buffers,
+        in_specs=[in_hbm] * 4 + [in_vmem] * 4,
+        out_specs=[in_vmem] * 4,
+        scratch_shapes=load_scratch,
+        input_output_aliases={4 + i: i for i in range(4)},
+        compiler_params=pltpu.CompilerParams(vmem_limit_bytes=8 * 2**20),
+        cost_estimate=cost,
+    )(*hbm, *loaded)
+    own, loaded = lax.optimization_barrier((own, loaded))
+    if routed:
         final = send(own, second_route)
     else:
         early = [

time: 24.9 us -> 24.9 us (level)
    pallas_call x1 -> x2, Pallas kernels: 1.35 us -> 1.46 us  [the longest x1 1.35 us: shards(): pl.pallas_call(load_ahead_stage, name='load_ahead_stage', out_shape=buffe...]
where the time goes in v25:
time: 24.9 us; the launch traced here: 24.7 us
  Pallas kernels  18.8 us (76%)
  starting transfers between devices  3.6 us (14%)
  waiting for transfers between devices  2.26 us (9%)
    pallas_call x1, Pallas kernels, shards(): pl.pallas_call(functools.partial(last_stage, routed), name='last_stage',...  12.5 us
    ppermute x4, starting transfers between devices, send(): return lax.ppermute(shard, ('loop', 'pair'), hops)  3.6 us
    pallas_call x1, Pallas kernels, shards(): pl.pallas_call(local_stage, name='local_stage', out_shape=[state] * 3 + b...  3.03 us
    ppermute x4, waiting for transfers between devices, send(): return lax.ppermute(shard, ('loop', 'pair'), hops)  2.26 us
    pallas_call x2, Pallas kernels, add_shards(): pl.pallas_call(functools.partial(add_stage, by_swap if routed else None),...  1.79 us
    pallas_call x1, Pallas kernels, shards(): pl.pallas_call(load_ahead_stage, name='load_ahead_stage', out_shape=buffe...  1.35 us
  transfers between devices with their start and end apart: 4, of which 2 were waited for; matrix products, arithmetic and copies ran while one was open for 0% of the time, Pallas kernels for 20%

profile of v25, /device:TPU:0, one launch (start us, length us, event | category | flops | bytes accessed | tf_op | source)
XLA Modules:
  0.0 24.7 jit_solution(12747777363248171800)
XLA Ops:
  0.0 1.4 %load_ahead_stage.1 = (bf16[640,512]{1,0:T(8,128)(2,1)S(1)}, bf16[640,256]{1,0:T(8,128)(2,1)S(1)}, bf16[256,256]{1,0:T(8,128)(2,1)S(1)}, s32[640,128]{1,0:T(8,128)S(1)}) custom-call(s32[8]{0:T(128)} %refs_0_.5, bf16[640,512]{1,0:T(8,128)(2,1)} %refs_1_.5, bf16[640,256]{1,0:T(8,128)(2,1)} %bitcast.2, bf16[256,256]{1,0:T(8,128)(2,1)} %bitcast.5), custom_call_target="tpu_custom_call" | custom-call | flops 1 | bytes 1 | tf_op jit(solution)/shard_map/load_ahead_stage/pallas_call | solution.py:350
  1.4 0.0 copy-start
  1.4 1.8 %collective-permute-start = (bf16[256,256]{1,0:T(8,128)(2,1)}, bf16[256,256]{1,0:T(8,128)(2,1)S(1)}, u32[]{:S(2)}, u32[]{:S(2)}) collective-permute-start(bf16[256,256]{1,0:T(8,128)(2,1)} %bitcast.6), channel_id=1, source_target_pairs={{0,4},{1,8},{4,5},{5,9},{8,12},{9,0},{12,13},{13,1},{2,6},{3,10},{... | collective-permute-start | bytes 393224 | tf_op jit(solution)/shard_map/ppermute | solution.py:327
  3.2 0.1 load_between_stage.1
  3.3 0.0 copy-done
  3.3 1.2 %collective-permute-start.1 = (bf16[256,256]{1,0:T(8,128)(2,1)S(1)}, bf16[256,256]{1,0:T(8,128)(2,1)S(1)}, u32[]{:S(2)}, u32[]{:S(2)}) collective-permute-start(bf16[256,256]{1,0:T(8,128)(2,1)S(1)} %bitcast.9), channel_id=1, source_target_pairs={{0,1},{1,13},{4,0},{5,12},{8,9},{9,5},{12,8},{13,4},{2,3},{3,15},{... | collective-permute-start | bytes 393224 | tf_op jit(solution)/shard_map/ppermute | solution.py:327
  4.5 3.0 %local_stage.1 = (f32[640,512]{1,0:T(8,128)S(1)}, f32[640,512]{1,0:T(8,128)S(1)}, f32[640,512]{1,0:T(8,128)S(1)}, bf16[640,512]{1,0:T(8,128)(2,1)S(1)}, bf16[640...) custom-call(s32[8]{0:T(128)} %refs_0_.5, ...), custom_call_target="tpu_custom_call", output_to_operand_aliasing={{3}: (4, {}), {4}: (5, {}), {5}: (6, {}), {6}: (7, {})} | custom-call | flops 1 | bytes 1 | tf_op jit(solution)/shard_map/local_stage/pallas_call | solution.py:387
  7.6 2.2 %collective-permute-done.refs_4_.refs_6_ = bf16[256,256]{1,0:T(8,128)(2,1)S(1)} collective-permute-done((bf16[256,256]{1,0:T(8,128)(2,1)}, bf16[256,256]{1,0:T(8,128)(2,1)S(1)}, u32[]{:S(2)}, u32[]{:S(2)}) %collective-permute-start) | collective-permute-done | bytes 131104 | tf_op jit(solution)/shard_map/ppermute | solution.py:327
  9.7 0.0 collective-permute-start.2
  9.8 0.9 %add_stage.2 = (f32[640,512]{1,0:T(8,128)S(1)}, f32[640,512]{1,0:T(8,128)S(1)}) custom-call(bf16[640,512]{1,0:T(8,128)(2,1)S(1)} %get-tuple-element.52.refs_0_, f32[640,512]{1,0:T(8,128)S(1)} %get-tuple-element.54.refs_1_, f32[640,512]{1,0:T(8,128)S(1)} %get-tuple-element.55.refs_2_, f32[640,512]{1,0:T(8,128)S(1)} %get-tuple-element.56.refs_3_, ...), custom_call_target="tpu_custom_call" | custom-call | flops 1 | bytes 1 | tf_op jit(solution)/shard_map/add_stage/pallas_call | solution.py:402
  10.7 0.0 collective-permute-done.1.refs_8_
  10.7 0.6 %collective-permute-start.3 = (bf16[256,256]{1,0:T(8,128)(2,1)S(1)}, bf16[256,256]{1,0:T(8,128)(2,1)S(1)}, u32[]{:S(2)}, u32[]{:S(2)}) collective-permute-start(bf16[256,256]{1,0:T(8,128)(2,1)S(1)} %collective-permute-done.1.refs_8_), channel_id=1, source_target_pairs={{0,1},{1,0},{4,5},{5,4},{8,9},{9,8},{12,13},{13,12},{2,3},{3,2},{6... | collective-permute-start | bytes 393224 | tf_op jit(solution)/shard_map/ppermute | solution.py:327
  11.2 0.0 collective-permute-done.2.refs_4_.refs_7_
  11.2 0.9 %add_stage.3 = (f32[640,512]{1,0:T(8,128)S(1)}, f32[640,512]{1,0:T(8,128)S(1)}) custom-call(bf16[640,512]{1,0:T(8,128)(2,1)S(1)} %get-tuple-element.52.refs_0_, f32[640,512]{1,0:T(8,128)S(1)} %get-tuple-element.54.refs_1_, f32[640,512]{1,0:T(8,128)S(1)} %get-tuple-element.60.refs_2_, f32[640,512]{1,0:T(8,128)S(1)} %get-tuple-element.61.refs_3_, ...), custom_call_target="tpu_custom_call" | custom-call | flops 1 | bytes 1 | tf_op jit(solution)/shard_map/add_stage/pallas_call | solution.py:402
  12.1 0.1 collective-permute-done.3.refs_9_
  12.2 12.5 %last_stage.1 = bf16[640,512]{1,0:T(8,128)(2,1)} custom-call(bf16[640,512]{1,0:T(8,128)(2,1)S(1)} %get-tuple-element.52.refs_0_, f32[640,512]{1,0:T(8,128)S(1)} %get-tuple-element.54.refs_1_, f32[640,512]{1,0:T(8,128)S(1)} %get-tuple-element.55.refs_2_, f32[640,512]{1,0:T(8,128)S(1)} %get-tuple-element.56.refs_3_, f32[640,512]{1,0:T(8,128)S(1)} %get-tuple-element.62.refs_4_, ...), custom_call_target="tpu_custom_call" | custom-call | flops 1 | bytes 1 | tf_op jit(solution)/shard_map/last_stage/pallas_call | solution.py:424
Async XLA Ops:
  1.4 2.0 %copy-start = (bf16[256,1,256]{2,0,1:T(8,128)(2,1)S(1)}, bf16[256,1,256]{2,0,1:T(8,128)(2,1)}, u32[]{:S(2)}) copy-start(bf16[256,1,256]{2,0,1:T(8,128)(2,1)} %param.6) | copy-start | bytes 393220
  1.4 8.4 %collective-permute-start = (bf16[256,256]{1,0:T(8,128)(2,1)}, bf16[256,256]{1,0:T(8,128)(2,1)S(1)}, u32[]{:S(2)}, u32[]{:S(2)}) collective-permute-start(bf16[256,256]{1,0:T(8,128)(2,1)} %bitcast.6), channel_id=1, source_target_pairs={{0,4},{1,8},{4,5},{5,9},{8,12},{9,0},{12,13},{13,1},{2,6},{3,10},{... | collective-permute-start | bytes 393224 | tf_op jit(solution)/shard_map/ppermute | solution.py:327
  3.3 7.3 %collective-permute-start.1 = (bf16[256,256]{1,0:T(8,128)(2,1)S(1)}, bf16[256,256]{1,0:T(8,128)(2,1)S(1)}, u32[]{:S(2)}, u32[]{:S(2)}) collective-permute-start(bf16[256,256]{1,0:T(8,128)(2,1)S(1)} %bitcast.9), channel_id=1, source_target_pairs={{0,1},{1,13},{4,0},{5,12},{8,9},{9,5},{12,8},{13,4},{2,3},{3,15},{... | collective-permute-start | bytes 393224 | tf_op jit(solution)/shard_map/ppermute | solution.py:327
  9.7 1.5 %collective-permute-start.2 = (bf16[256,256]{1,0:T(8,128)(2,1)S(1)}, bf16[256,256]{1,0:T(8,128)(2,1)S(1)}, u32[]{:S(2)}, u32[]{:S(2)}) collective-permute-start(bf16[256,256]{1,0:T(8,128)(2,1)S(1)} %collective-permute-done.refs_4_.refs_6_), channel_id=1, source_target_pairs={{0,1},{1,0},{4,5},{5,4},{8,9},{9,8},{12,13},{13,12},{2,3},{3,2},{6... | collective-permute-start | bytes 393224 | tf_op jit(solution)/shard_map/ppermute | solution.py:327
  10.7 1.6 %collective-permute-start.3 = (bf16[256,256]{1,0:T(8,128)(2,1)S(1)}, bf16[256,256]{1,0:T(8,128)(2,1)S(1)}, u32[]{:S(2)}, u32[]{:S(2)}) collective-permute-start(bf16[256,256]{1,0:T(8,128)(2,1)S(1)} %collective-permute-done.1.refs_8_), channel_id=1, source_target_pairs={{0,1},{1,0},{4,5},{5,4},{8,9},{9,8},{12,13},{13,12},{2,3},{3,2},{6... | collective-permute-start | bytes 393224 | tf_op jit(solution)/shard_map/ppermute | solution.py:327

commit v26 on v24

--- a/solution.py
+++ b/solution.py
@@ -315,14 +315,17 @@
                 hops.append((2 * i + core, 2 * to + to_core))
         return lax.ppermute(shard, ("loop", "pair"), hops)
 
+    def far_core(i):
+        return 1 ^ (i & 1) ^ (i >> 1 & 1)
+
     def first_route(i, core):
         if core == 1:
-            return (i ^ 2) & ~1, i & 1
+            return (i ^ 2) & ~1, far_core(i)
         return (i, 1) if i & 1 else (i + 1, 0)
 
     def second_route(i, core):
         if core == 1:
-            return (i ^ 2) | 1, 1 - i & 1
+            return (i ^ 2) | 1, far_core(i)
         return (i - 1, 0) if i & 1 else (i, 1)
 
     hbm = [pltpu.with_memory_space_constraint(x, pltpu.HBM) for x in (lengths, queries, suffix, own)]

time: 24.9 us -> 24.7 us (level)
  starting transfers between devices: 3.55 us -> 2.98 us
  waiting for transfers between devices: 2.45 us -> 2.85 us
    ppermute x4, starting transfers between devices: 3.55 us -> 2.98 us  [send(): return lax.ppermute(shard, ('loop', 'pair'), hops)]
    ppermute x4, waiting for transfers between devices: 2.45 us -> 2.85 us  [send(): return lax.ppermute(shard, ('loop', 'pair'), hops)]
where the time goes in v26:
time: 24.7 us; the launch traced here: 24.5 us
  Pallas kernels  18.7 us (76%)
  starting transfers between devices  2.98 us (12%)
  waiting for transfers between devices  2.85 us (12%)
    pallas_call x1, Pallas kernels, shards(): pl.pallas_call(functools.partial(last_stage, routed), name='last_stage',...  12.5 us
    pallas_call x1, Pallas kernels, shards(): pl.pallas_call(local_stage, name='local_stage', out_shape=[state] * 3 + b...  3.03 us
    ppermute x4, starting transfers between devices, send(): return lax.ppermute(shard, ('loop', 'pair'), hops)  2.98 us
    ppermute x4, waiting for transfers between devices, send(): return lax.ppermute(shard, ('loop', 'pair'), hops)  2.85 us
    pallas_call x2, Pallas kernels, add_shards(): pl.pallas_call(functools.partial(add_stage, by_swap if routed else None),...  1.79 us
    pallas_call x1, Pallas kernels, shards(): pl.pallas_call(prelude_stage, name='prelude_stage', out_shape=buffers, in...  1.35 us
  transfers between devices with their start and end apart: 4, of which 2 were waited for; matrix products, arithmetic and copies ran while one was open for 0% of the time, Pallas kernels for 20%

profile of v26, /device:TPU:0, one launch (start us, length us, event | category | flops | bytes accessed | tf_op | source)
XLA Modules:
  0.0 24.5 jit_solution(9541736824619308690)
XLA Ops:
  0.0 1.4 %prelude_stage.1 = (bf16[640,512]{1,0:T(8,128)(2,1)S(1)}, bf16[640,256]{1,0:T(8,128)(2,1)S(1)}, bf16[256,256]{1,0:T(8,128)(2,1)S(1)}, s32[640,128]{1,0:T(8,128)S(1)}) custom-call(s32[8]{0:T(128)} %refs_0_.3, bf16[640,512]{1,0:T(8,128)(2,1)} %refs_1_.3, bf16[640,256]{1,0:T(8,128)(2,1)} %bitcast.2, bf16[256,256]{1,0:T(8,128)(2,1)} %bitcast.4), custom_call_target="tpu_custom_call" | custom-call | flops 1 | bytes 1 | tf_op jit(solution)/shard_map/prelude_stage/pallas_call | solution.py:342
  1.4 1.8 %collective-permute-start = (bf16[256,256]{1,0:T(8,128)(2,1)}, bf16[256,256]{1,0:T(8,128)(2,1)S(1)}, u32[]{:S(2)}, u32[]{:S(2)}) collective-permute-start(bf16[256,256]{1,0:T(8,128)(2,1)} %bitcast.5), channel_id=1, source_target_pairs={{0,4},{1,9},{4,5},{5,8},{8,12},{9,0},{12,13},{13,1},{2,6},{3,11},{... | collective-permute-start | bytes 393224 | tf_op jit(solution)/shard_map/ppermute | solution.py:316
  3.2 0.6 %collective-permute-start.1 = (bf16[256,256]{1,0:T(8,128)(2,1)}, bf16[256,256]{1,0:T(8,128)(2,1)S(1)}, u32[]{:S(2)}, u32[]{:S(2)}) collective-permute-start(bf16[256,256]{1,0:T(8,128)(2,1)} %bitcast.6), channel_id=1, source_target_pairs={{0,1},{1,13},{4,0},{5,12},{8,9},{9,4},{12,8},{13,5},{2,3},{3,15},{... | collective-permute-start | bytes 393224 | tf_op jit(solution)/shard_map/ppermute | solution.py:316
  3.8 3.0 %local_stage.1 = (f32[640,512]{1,0:T(8,128)S(1)}, f32[640,512]{1,0:T(8,128)S(1)}, f32[640,512]{1,0:T(8,128)S(1)}, bf16[640,512]{1,0:T(8,128)(2,1)S(1)}, bf16[640...) custom-call(s32[8]{0:T(128)} %refs_0_.3, ...), custom_call_target="tpu_custom_call", output_to_operand_aliasing={{3}: (4, {}), {4}: (5, {}), {5}: (6, {}), {6}: (7, {})} | custom-call | flops 1 | bytes 1 | tf_op jit(solution)/shard_map/local_stage/pallas_call | solution.py:366
  6.8 2.8 %collective-permute-done.refs_4_.refs_6_ = bf16[256,256]{1,0:T(8,128)(2,1)S(1)} collective-permute-done((bf16[256,256]{1,0:T(8,128)(2,1)}, bf16[256,256]{1,0:T(8,128)(2,1)S(1)}, u32[]{:S(2)}, u32[]{:S(2)}) %collective-permute-start) | collective-permute-done | bytes 131104 | tf_op jit(solution)/shard_map/ppermute | solution.py:316
  9.6 0.0 collective-permute-start.2
  9.6 0.9 %add_stage.2 = (f32[640,512]{1,0:T(8,128)S(1)}, f32[640,512]{1,0:T(8,128)S(1)}) custom-call(bf16[640,512]{1,0:T(8,128)(2,1)S(1)} %get-tuple-element.34.refs_0_, f32[640,512]{1,0:T(8,128)S(1)} %get-tuple-element.37.refs_1_, f32[640,512]{1,0:T(8,128)S(1)} %get-tuple-element.38.refs_2_, f32[640,512]{1,0:T(8,128)S(1)} %get-tuple-element.39.refs_3_, ...), custom_call_target="tpu_custom_call" | custom-call | flops 1 | bytes 1 | tf_op jit(solution)/shard_map/add_stage/pallas_call | solution.py:381
  10.5 0.0 collective-permute-done.1.refs_8_
  10.5 0.6 %collective-permute-start.3 = (bf16[256,256]{1,0:T(8,128)(2,1)S(1)}, bf16[256,256]{1,0:T(8,128)(2,1)S(1)}, u32[]{:S(2)}, u32[]{:S(2)}) collective-permute-start(bf16[256,256]{1,0:T(8,128)(2,1)S(1)} %collective-permute-done.1.refs_8_), channel_id=1, source_target_pairs={{0,1},{1,0},{4,5},{5,4},{8,9},{9,8},{12,13},{13,12},{2,3},{3,2},{6... | collective-permute-start | bytes 393224 | tf_op jit(solution)/shard_map/ppermute | solution.py:316
  11.1 0.0 collective-permute-done.2.refs_4_.refs_7_
  11.1 0.9 %add_stage.3 = (f32[640,512]{1,0:T(8,128)S(1)}, f32[640,512]{1,0:T(8,128)S(1)}) custom-call(bf16[640,512]{1,0:T(8,128)(2,1)S(1)} %get-tuple-element.34.refs_0_, f32[640,512]{1,0:T(8,128)S(1)} %get-tuple-element.37.refs_1_, f32[640,512]{1,0:T(8,128)S(1)} %get-tuple-element.42.refs_2_, f32[640,512]{1,0:T(8,128)S(1)} %get-tuple-element.43.refs_3_, ...), custom_call_target="tpu_custom_call" | custom-call | flops 1 | bytes 1 | tf_op jit(solution)/shard_map/add_stage/pallas_call | solution.py:381
  12.0 0.1 collective-permute-done.3.refs_9_
  12.1 12.5 %last_stage.1 = bf16[640,512]{1,0:T(8,128)(2,1)} custom-call(bf16[640,512]{1,0:T(8,128)(2,1)S(1)} %get-tuple-element.34.refs_0_, f32[640,512]{1,0:T(8,128)S(1)} %get-tuple-element.37.refs_1_, f32[640,512]{1,0:T(8,128)S(1)} %get-tuple-element.38.refs_2_, f32[640,512]{1,0:T(8,128)S(1)} %get-tuple-element.39.refs_3_, f32[640,512]{1,0:T(8,128)S(1)} %get-tuple-element.44.refs_4_, ...), custom_call_target="tpu_custom_call" | custom-call | flops 1 | bytes 1 | tf_op jit(solution)/shard_map/last_stage/pallas_call | solution.py:403
Async XLA Ops:
  1.4 8.2 %collective-permute-start = (bf16[256,256]{1,0:T(8,128)(2,1)}, bf16[256,256]{1,0:T(8,128)(2,1)S(1)}, u32[]{:S(2)}, u32[]{:S(2)}) collective-permute-start(bf16[256,256]{1,0:T(8,128)(2,1)} %bitcast.5), channel_id=1, source_target_pairs={{0,4},{1,9},{4,5},{5,8},{8,12},{9,0},{12,13},{13,1},{2,6},{3,11},{... | collective-permute-start | bytes 393224 | tf_op jit(solution)/shard_map/ppermute | solution.py:316
  3.2 7.3 %collective-permute-start.1 = (bf16[256,256]{1,0:T(8,128)(2,1)}, bf16[256,256]{1,0:T(8,128)(2,1)S(1)}, u32[]{:S(2)}, u32[]{:S(2)}) collective-permute-start(bf16[256,256]{1,0:T(8,128)(2,1)} %bitcast.6), channel_id=1, source_target_pairs={{0,1},{1,13},{4,0},{5,12},{8,9},{9,4},{12,8},{13,5},{2,3},{3,15},{... | collective-permute-start | bytes 393224 | tf_op jit(solution)/shard_map/ppermute | solution.py:316
  9.6 1.5 %collective-permute-start.2 = (bf16[256,256]{1,0:T(8,128)(2,1)S(1)}, bf16[256,256]{1,0:T(8,128)(2,1)S(1)}, u32[]{:S(2)}, u32[]{:S(2)}) collective-permute-start(bf16[256,256]{1,0:T(8,128)(2,1)S(1)} %collective-permute-done.refs_4_.refs_6_), channel_id=1, source_target_pairs={{0,1},{1,0},{4,5},{5,4},{8,9},{9,8},{12,13},{13,12},{2,3},{3,2},{6... | collective-permute-start | bytes 393224 | tf_op jit(solution)/shard_map/ppermute | solution.py:316
  10.5 1.6 %collective-permute-start.3 = (bf16[256,256]{1,0:T(8,128)(2,1)S(1)}, bf16[256,256]{1,0:T(8,128)(2,1)S(1)}, u32[]{:S(2)}, u32[]{:S(2)}) collective-permute-start(bf16[256,256]{1,0:T(8,128)(2,1)S(1)} %collective-permute-done.1.refs_8_), channel_id=1, source_target_pairs={{0,1},{1,0},{4,5},{5,4},{8,9},{9,8},{12,13},{13,12},{2,3},{3,2},{6... | collective-permute-start | bytes 393224 | tf_op jit(solution)/shard_map/ppermute | solution.py:316

commit v27 on v23

--- a/solution.py
+++ b/solution.py
@@ -209,7 +209,7 @@
     blocks = row_blocks(query_ref.shape[0], 80)
     position, core = place()
     takes_both = (position == 1) & routed
-    is_direct = core == 0
+    is_direct = core == jnp.where(position == 0, 0, 1)
 
     def out_copy(index, rows):
         return pltpu.make_async_copy(out_ref.at[rows], out_hbm.at[rows], out_sems.at[index])
@@ -317,14 +317,14 @@
 
     def first_route(i, core):
         base = i - i % FOUR
-        to, to_core = [((1, 0), (3, 1)), ((1, 1), (2, 1)), ((0, 0), (3, 0)), ((2, 0), (0, 1))][
+        to, to_core = [((1, 0), (3, 1)), ((1, 1), (2, 0)), ((3, 0), (0, 0)), ((2, 1), (0, 1))][
             i % FOUR
         ][core]
         return base + to, to_core
 
     def second_route(i, core):
         base = i - i % FOUR
-        to, to_core = [((0, 1), (2, 0)), ((0, 0), (3, 0)), ((2, 1), (1, 0)), ((3, 1), (1, 1))][
+        to, to_core = [((0, 1), (2, 1)), ((0, 0), (3, 1)), ((3, 0), (1, 0)), ((2, 0), (1, 1))][
             i % FOUR
         ][core]
         return base + to, to_core

time: 26.4 us -> 23.9 us (0.905)
  waiting for transfers between devices: 3.51 us -> 0.66 us
    ppermute x4, waiting for transfers between devices: 3.51 us -> 0.66 us  [send(): return lax.ppermute(shard, ('loop', 'pair'), hops)]
  transfers between devices with their start and end apart: 4 -> 4, of which waited for: 2 -> 3; matrix products, arithmetic and copies ran while one was open for 0% -> 0% of each run, Pallas kernels for 18% -> 20%
where the time goes in v27:
time: 23.9 us; the launch traced here: 23.6 us
  Pallas kernels  18.7 us (78%)
  starting transfers between devices  4.21 us (18%)
  waiting for transfers between devices  0.66 us (3%)
    pallas_call x1, Pallas kernels, shards(): pl.pallas_call(functools.partial(last_stage, routed), name='last_stage',...  12.5 us
    ppermute x4, starting transfers between devices, send(): return lax.ppermute(shard, ('loop', 'pair'), hops)  4.21 us
    pallas_call x1, Pallas kernels, shards(): pl.pallas_call(local_stage, name='local_stage', out_shape=[state] * 3 + b...  3.03 us
    pallas_call x2, Pallas kernels, add_shards(): pl.pallas_call(functools.partial(add_stage, by_swap if routed else None),...  1.79 us
    pallas_call x1, Pallas kernels, shards(): pl.pallas_call(prelude_stage, name='prelude_stage', out_shape=buffers, in...  1.35 us
    ppermute x4, waiting for transfers between devices, send(): return lax.ppermute(shard, ('loop', 'pair'), hops)  0.66 us
  transfers between devices with their start and end apart: 4, of which 3 were waited for; matrix products, arithmetic and copies ran while one was open for 0% of the time, Pallas kernels for 20%

profile of v27, /device:TPU:0, one launch (start us, length us, event | category | flops | bytes accessed | tf_op | source)
XLA Modules:
  0.0 23.6 jit_solution(10896376000092316210)
XLA Ops:
  0.0 1.4 %prelude_stage.1 = (bf16[640,512]{1,0:T(8,128)(2,1)S(1)}, bf16[640,256]{1,0:T(8,128)(2,1)S(1)}, bf16[256,256]{1,0:T(8,128)(2,1)S(1)}, s32[640,128]{1,0:T(8,128)S(1)}) custom-call(s32[8]{0:T(128)} %refs_0_.3, bf16[640,512]{1,0:T(8,128)(2,1)} %refs_1_.3, bf16[640,256]{1,0:T(8,128)(2,1)} %bitcast.2, bf16[256,256]{1,0:T(8,128)(2,1)} %bitcast.4), custom_call_target="tpu_custom_call" | custom-call | flops 1 | bytes 1 | tf_op jit(solution)/shard_map/prelude_stage/pallas_call | solution.py:343
  1.4 1.8 %collective-permute-start = (bf16[256,256]{1,0:T(8,128)(2,1)}, bf16[256,256]{1,0:T(8,128)(2,1)S(1)}, u32[]{:S(2)}, u32[]{:S(2)}) collective-permute-start(bf16[256,256]{1,0:T(8,128)(2,1)} %bitcast.5), channel_id=1, source_target_pairs={{0,4},{1,13},{4,5},{5,8},{8,12},{9,0},{12,9},{13,1},{2,6},{3,15},{... | collective-permute-start | bytes 393224 | tf_op jit(solution)/shard_map/ppermute | solution.py:316
  3.2 1.6 %collective-permute-start.1 = (bf16[256,256]{1,0:T(8,128)(2,1)}, bf16[256,256]{1,0:T(8,128)(2,1)S(1)}, u32[]{:S(2)}, u32[]{:S(2)}) collective-permute-start(bf16[256,256]{1,0:T(8,128)(2,1)} %bitcast.6), channel_id=1, source_target_pairs={{0,1},{1,9},{4,0},{5,13},{8,12},{9,4},{12,8},{13,5},{2,3},{3,11},{... | collective-permute-start | bytes 393224 | tf_op jit(solution)/shard_map/ppermute | solution.py:316
  4.8 3.0 %local_stage.1 = (f32[640,512]{1,0:T(8,128)S(1)}, f32[640,512]{1,0:T(8,128)S(1)}, f32[640,512]{1,0:T(8,128)S(1)}, bf16[640,512]{1,0:T(8,128)(2,1)S(1)}, bf16[640...) custom-call(s32[8]{0:T(128)} %refs_0_.3, ...), custom_call_target="tpu_custom_call", output_to_operand_aliasing={{3}: (4, {}), {4}: (5, {}), {5}: (6, {}), {6}: (7, {})} | custom-call | flops 1 | bytes 1 | tf_op jit(solution)/shard_map/local_stage/pallas_call | solution.py:367
  7.8 0.1 collective-permute-done.refs_4_.refs_6_
  7.9 0.8 %collective-permute-start.2 = (bf16[256,256]{1,0:T(8,128)(2,1)S(1)}, bf16[256,256]{1,0:T(8,128)(2,1)S(1)}, u32[]{:S(2)}, u32[]{:S(2)}) collective-permute-start(bf16[256,256]{1,0:T(8,128)(2,1)S(1)} %collective-permute-done.refs_4_.refs_6_), channel_id=1, source_target_pairs={{0,1},{1,0},{4,5},{5,4},{8,9},{9,8},{12,13},{13,12},{2,3},{3,2},{6... | collective-permute-start | bytes 393224 | tf_op jit(solution)/shard_map/ppermute | solution.py:316
  8.7 0.9 %add_stage.2 = (f32[640,512]{1,0:T(8,128)S(1)}, f32[640,512]{1,0:T(8,128)S(1)}) custom-call(bf16[640,512]{1,0:T(8,128)(2,1)S(1)} %get-tuple-element.34.refs_0_, f32[640,512]{1,0:T(8,128)S(1)} %get-tuple-element.37.refs_1_, f32[640,512]{1,0:T(8,128)S(1)} %get-tuple-element.38.refs_2_, f32[640,512]{1,0:T(8,128)S(1)} %get-tuple-element.39.refs_3_, ...), custom_call_target="tpu_custom_call" | custom-call | flops 1 | bytes 1 | tf_op jit(solution)/shard_map/add_stage/pallas_call | solution.py:382
  9.6 0.2 collective-permute-done.1.refs_8_
  9.7 0.0 collective-permute-start.3
  9.7 0.0 collective-permute-done.2.refs_4_.refs_7_
  9.7 0.9 %add_stage.3 = (f32[640,512]{1,0:T(8,128)S(1)}, f32[640,512]{1,0:T(8,128)S(1)}) custom-call(bf16[640,512]{1,0:T(8,128)(2,1)S(1)} %get-tuple-element.34.refs_0_, f32[640,512]{1,0:T(8,128)S(1)} %get-tuple-element.37.refs_1_, f32[640,512]{1,0:T(8,128)S(1)} %get-tuple-element.42.refs_2_, f32[640,512]{1,0:T(8,128)S(1)} %get-tuple-element.43.refs_3_, ...), custom_call_target="tpu_custom_call" | custom-call | flops 1 | bytes 1 | tf_op jit(solution)/shard_map/add_stage/pallas_call | solution.py:382
  10.6 0.4 %collective-permute-done.3.refs_9_ = bf16[256,256]{1,0:T(8,128)(2,1)S(1)} collective-permute-done((bf16[256,256]{1,0:T(8,128)(2,1)S(1)}, bf16[256,256]{1,0:T(8,128)(2,1)S(1)}, u32[]{:S(2)}, u32[]{:S(2)}) %collective-permute-start.3) | collective-permute-done | bytes 131104 | tf_op jit(solution)/shard_map/ppermute | solution.py:316
  11.1 12.5 %last_stage.1 = bf16[640,512]{1,0:T(8,128)(2,1)} custom-call(bf16[640,512]{1,0:T(8,128)(2,1)S(1)} %get-tuple-element.34.refs_0_, f32[640,512]{1,0:T(8,128)S(1)} %get-tuple-element.37.refs_1_, f32[640,512]{1,0:T(8,128)S(1)} %get-tuple-element.38.refs_2_, f32[640,512]{1,0:T(8,128)S(1)} %get-tuple-element.39.refs_3_, f32[640,512]{1,0:T(8,128)S(1)} %get-tuple-element.44.refs_4_, ...), custom_call_target="tpu_custom_call" | custom-call | flops 1 | bytes 1 | tf_op jit(solution)/shard_map/last_stage/pallas_call | solution.py:404
Async XLA Ops:
  1.4 6.5 %collective-permute-start = (bf16[256,256]{1,0:T(8,128)(2,1)}, bf16[256,256]{1,0:T(8,128)(2,1)S(1)}, u32[]{:S(2)}, u32[]{:S(2)}) collective-permute-start(bf16[256,256]{1,0:T(8,128)(2,1)} %bitcast.5), channel_id=1, source_target_pairs={{0,4},{1,13},{4,5},{5,8},{8,12},{9,0},{12,9},{13,1},{2,6},{3,15},{... | collective-permute-start | bytes 393224 | tf_op jit(solution)/shard_map/ppermute | solution.py:316
  3.2 6.5 %collective-permute-start.1 = (bf16[256,256]{1,0:T(8,128)(2,1)}, bf16[256,256]{1,0:T(8,128)(2,1)S(1)}, u32[]{:S(2)}, u32[]{:S(2)}) collective-permute-start(bf16[256,256]{1,0:T(8,128)(2,1)} %bitcast.6), channel_id=1, source_target_pairs={{0,1},{1,9},{4,0},{5,13},{8,12},{9,4},{12,8},{13,5},{2,3},{3,11},{... | collective-permute-start | bytes 393224 | tf_op jit(solution)/shard_map/ppermute | solution.py:316
  7.9 1.9 %collective-permute-start.2 = (bf16[256,256]{1,0:T(8,128)(2,1)S(1)}, bf16[256,256]{1,0:T(8,128)(2,1)S(1)}, u32[]{:S(2)}, u32[]{:S(2)}) collective-permute-start(bf16[256,256]{1,0:T(8,128)(2,1)S(1)} %collective-permute-done.refs_4_.refs_6_), channel_id=1, source_target_pairs={{0,1},{1,0},{4,5},{5,4},{8,9},{9,8},{12,13},{13,12},{2,3},{3,2},{6... | collective-permute-start | bytes 393224 | tf_op jit(solution)/shard_map/ppermute | solution.py:316
  9.7 1.3 %collective-permute-start.3 = (bf16[256,256]{1,0:T(8,128)(2,1)S(1)}, bf16[256,256]{1,0:T(8,128)(2,1)S(1)}, u32[]{:S(2)}, u32[]{:S(2)}) collective-permute-start(bf16[256,256]{1,0:T(8,128)(2,1)S(1)} %collective-permute-done.1.refs_8_), channel_id=1, source_target_pairs={{0,1},{1,0},{4,5},{5,4},{8,9},{9,8},{12,13},{13,12},{2,3},{3,2},{6... | collective-permute-start | bytes 393224 | tf_op jit(solution)/shard_map/ppermute | solution.py:316

commit v28 on v23

--- a/solution.py
+++ b/solution.py
@@ -48,7 +48,8 @@
 
 
 def place():
-    return lax.rem(lax.axis_index("loop"), FOUR), lax.axis_index("pair")
+    position = lax.rem(lax.axis_index("loop"), FOUR)
+    return (position == 1) | (position == 2), lax.axis_index("pair")
 
 
 def load_blocks(count):
@@ -179,8 +180,8 @@
     key_rows, value_rows = shard[:, :HD], with_ones(shard[:, HD:])
     extra = None
     if by_swap is not None:
-        position, core = place()
-        extra = penalty((position != 1) | (core == int(by_swap)))
+        is_middle, core = place()
+        extra = penalty(jnp.logical_not(is_middle) | (core == int(by_swap)))
 
     def start(rows):
         return scores_of(stacked(query_ref, rows, heads), key_rows)
@@ -207,8 +208,8 @@
     direct_ref, swapped_ref, out_hbm, out_ref, trusted_ref, out_sems = refs
     heads = query_ref.shape[1] // HD
     blocks = row_blocks(query_ref.shape[0], 80)
-    position, core = place()
-    takes_both = (position == 1) & routed
+    is_middle, core = place()
+    takes_both = is_middle & routed
     is_direct = core == 0
 
     def out_copy(index, rows):
@@ -256,7 +257,7 @@
         counted = [(ref, 0.0) for ref in earlier_refs]
         if routed:
             counted[-2:] = [
-                (ref, penalty((position != 1) | (core == by_swap)))
+                (ref, penalty(jnp.logical_not(is_middle) | (core == by_swap)))
                 for by_swap, ref in enumerate(earlier_refs[-2:])
             ]
         counted += [
@@ -317,14 +318,14 @@
 
     def first_route(i, core):
         base = i - i % FOUR
-        to, to_core = [((1, 0), (3, 1)), ((1, 1), (2, 1)), ((0, 0), (3, 0)), ((2, 0), (0, 1))][
+        to, to_core = [((1, 0), (3, 1)), ((1, 1), (3, 0)), ((2, 1), (0, 0)), ((2, 0), (0, 1))][
             i % FOUR
         ][core]
         return base + to, to_core
 
     def second_route(i, core):
         base = i - i % FOUR
-        to, to_core = [((0, 1), (2, 0)), ((0, 0), (3, 0)), ((2, 1), (1, 0)), ((3, 1), (1, 1))][
+        to, to_core = [((0, 1), (2, 1)), ((0, 0), (2, 0)), ((3, 0), (1, 0)), ((3, 1), (1, 1))][
             i % FOUR
         ][core]
         return base + to, to_core

time: 26.4 us -> 25 us (0.947)
  the two profiles are of different devices: /device:TPU:0 before, /device:TPU:21 now
where the time goes in v28:
time: 25 us; the launch traced here: 24.8 us
  Pallas kernels  19.3 us (77%)
  starting transfers between devices  5.4 us (22%)
    pallas_call x1, Pallas kernels, shards(): pl.pallas_call(functools.partial(last_stage, routed), name='last_stage',...  13.1 us
    ppermute x4, starting transfers between devices, send(): return lax.ppermute(shard, ('loop', 'pair'), hops)  5.4 us
    pallas_call x1, Pallas kernels, shards(): pl.pallas_call(local_stage, name='local_stage', out_shape=[state] * 3 + b...  4.28 us
    pallas_call x2, Pallas kernels, add_shards(): pl.pallas_call(functools.partial(add_stage, by_swap if routed else None),...  1.79 us
  transfers between devices with their start and end apart: 4, of which 1 were waited for; matrix products, arithmetic and copies ran while one was open for 0% of the time, Pallas kernels for 24%

profile of v28, /device:TPU:21, one launch (start us, length us, event | category | flops | bytes accessed | tf_op | source)
XLA Modules:
  0.0 24.8 jit_solution(12783483758711481252)
XLA Ops:
  0.0 0.1 prelude_stage.1
  0.1 0.7 %collective-permute-start = (bf16[256,256]{1,0:T(8,128)(2,1)}, bf16[256,256]{1,0:T(8,128)(2,1)S(1)}, u32[]{:S(2)}, u32[]{:S(2)}) collective-permute-start(bf16[256,256]{1,0:T(8,128)(2,1)} %bitcast.5), channel_id=1, source_target_pairs={{0,4},{1,13},{4,5},{5,12},{8,9},{9,0},{12,8},{13,1},{2,6},{3,15},{... | collective-permute-start | bytes 393224 | tf_op jit(solution)/shard_map/ppermute | solution.py:317
  0.8 0.2 collective-permute-start.1
  1.0 4.3 %local_stage.1 = (f32[640,512]{1,0:T(8,128)S(1)}, f32[640,512]{1,0:T(8,128)S(1)}, f32[640,512]{1,0:T(8,128)S(1)}, bf16[640,512]{1,0:T(8,128)(2,1)S(1)}, bf16[640...) custom-call(s32[8]{0:T(128)} %refs_0_.3, ...), custom_call_target="tpu_custom_call", output_to_operand_aliasing={{3}: (4, {}), {4}: (5, {}), {5}: (6, {}), {6}: (7, {})} | custom-call | flops 1 | bytes 1 | tf_op jit(solution)/shard_map/local_stage/pallas_call | solution.py:368
  5.3 0.0 collective-permute-done.refs_4_.refs_6_
  5.3 2.0 %collective-permute-start.2 = (bf16[256,256]{1,0:T(8,128)(2,1)S(1)}, bf16[256,256]{1,0:T(8,128)(2,1)S(1)}, u32[]{:S(2)}, u32[]{:S(2)}) collective-permute-start(bf16[256,256]{1,0:T(8,128)(2,1)S(1)} %collective-permute-done.refs_4_.refs_6_), channel_id=1, source_target_pairs={{0,1},{1,0},{4,5},{5,4},{8,9},{9,8},{12,13},{13,12},{2,3},{3,2},{6... | collective-permute-start | bytes 393224 | tf_op jit(solution)/shard_map/ppermute | solution.py:317
  7.2 0.9 %add_stage.2 = (f32[640,512]{1,0:T(8,128)S(1)}, f32[640,512]{1,0:T(8,128)S(1)}) custom-call(bf16[640,512]{1,0:T(8,128)(2,1)S(1)} %get-tuple-element.34.refs_0_, f32[640,512]{1,0:T(8,128)S(1)} %get-tuple-element.37.refs_1_, f32[640,512]{1,0:T(8,128)S(1)} %get-tuple-element.38.refs_2_, f32[640,512]{1,0:T(8,128)S(1)} %get-tuple-element.39.refs_3_, ...), custom_call_target="tpu_custom_call" | custom-call | flops 1 | bytes 1 | tf_op jit(solution)/shard_map/add_stage/pallas_call | solution.py:383
  8.1 0.0 collective-permute-done.1.refs_8_
  8.2 2.6 %collective-permute-start.3 = (bf16[256,256]{1,0:T(8,128)(2,1)S(1)}, bf16[256,256]{1,0:T(8,128)(2,1)S(1)}, u32[]{:S(2)}, u32[]{:S(2)}) collective-permute-start(bf16[256,256]{1,0:T(8,128)(2,1)S(1)} %collective-permute-done.1.refs_8_), channel_id=1, source_target_pairs={{0,1},{1,0},{4,5},{5,4},{8,9},{9,8},{12,13},{13,12},{2,3},{3,2},{6... | collective-permute-start | bytes 393224 | tf_op jit(solution)/shard_map/ppermute | solution.py:317
  10.7 0.0 collective-permute-done.2.refs_4_.refs_7_
  10.7 0.9 %add_stage.3 = (f32[640,512]{1,0:T(8,128)S(1)}, f32[640,512]{1,0:T(8,128)S(1)}) custom-call(bf16[640,512]{1,0:T(8,128)(2,1)S(1)} %get-tuple-element.34.refs_0_, f32[640,512]{1,0:T(8,128)S(1)} %get-tuple-element.37.refs_1_, f32[640,512]{1,0:T(8,128)S(1)} %get-tuple-element.42.refs_2_, f32[640,512]{1,0:T(8,128)S(1)} %get-tuple-element.43.refs_3_, ...), custom_call_target="tpu_custom_call" | custom-call | flops 1 | bytes 1 | tf_op jit(solution)/shard_map/add_stage/pallas_call | solution.py:383
  11.6 0.1 collective-permute-done.3.refs_9_
  11.7 13.1 %last_stage.1 = bf16[640,512]{1,0:T(8,128)(2,1)} custom-call(bf16[640,512]{1,0:T(8,128)(2,1)S(1)} %get-tuple-element.34.refs_0_, f32[640,512]{1,0:T(8,128)S(1)} %get-tuple-element.37.refs_1_, f32[640,512]{1,0:T(8,128)S(1)} %get-tuple-element.38.refs_2_, f32[640,512]{1,0:T(8,128)S(1)} %get-tuple-element.39.refs_3_, f32[640,512]{1,0:T(8,128)S(1)} %get-tuple-element.44.refs_4_, ...), custom_call_target="tpu_custom_call" | custom-call | flops 1 | bytes 1 | tf_op jit(solution)/shard_map/last_stage/pallas_call | solution.py:405
Async XLA Ops:
  0.1 5.2 %collective-permute-start = (bf16[256,256]{1,0:T(8,128)(2,1)}, bf16[256,256]{1,0:T(8,128)(2,1)S(1)}, u32[]{:S(2)}, u32[]{:S(2)}) collective-permute-start(bf16[256,256]{1,0:T(8,128)(2,1)} %bitcast.5), channel_id=1, source_target_pairs={{0,4},{1,13},{4,5},{5,12},{8,9},{9,0},{12,8},{13,1},{2,6},{3,15},{... | collective-permute-start | bytes 393224 | tf_op jit(solution)/shard_map/ppermute | solution.py:317
  0.8 7.4 %collective-permute-start.1 = (bf16[256,256]{1,0:T(8,128)(2,1)}, bf16[256,256]{1,0:T(8,128)(2,1)S(1)}, u32[]{:S(2)}, u32[]{:S(2)}) collective-permute-start(bf16[256,256]{1,0:T(8,128)(2,1)} %bitcast.6), channel_id=1, source_target_pairs={{0,1},{1,9},{4,0},{5,8},{8,12},{9,4},{12,13},{13,5},{2,3},{3,11},{... | collective-permute-start | bytes 393224 | tf_op jit(solution)/shard_map/ppermute | solution.py:317
  5.3 5.4 %collective-permute-start.2 = (bf16[256,256]{1,0:T(8,128)(2,1)S(1)}, bf16[256,256]{1,0:T(8,128)(2,1)S(1)}, u32[]{:S(2)}, u32[]{:S(2)}) collective-permute-start(bf16[256,256]{1,0:T(8,128)(2,1)S(1)} %collective-permute-done.refs_4_.refs_6_), channel_id=1, source_target_pairs={{0,1},{1,0},{4,5},{5,4},{8,9},{9,8},{12,13},{13,12},{2,3},{3,2},{6... | collective-permute-start | bytes 393224 | tf_op jit(solution)/shard_map/ppermute | solution.py:317
  8.2 3.6 %collective-permute-start.3 = (bf16[256,256]{1,0:T(8,128)(2,1)S(1)}, bf16[256,256]{1,0:T(8,128)(2,1)S(1)}, u32[]{:S(2)}, u32[]{:S(2)}) collective-permute-start(bf16[256,256]{1,0:T(8,128)(2,1)S(1)} %collective-permute-done.1.refs_8_), channel_id=1, source_target_pairs={{0,1},{1,0},{4,5},{5,4},{8,9},{9,8},{12,13},{13,12},{2,3},{3,2},{6... | collective-permute-start | bytes 393224 | tf_op jit(solution)/shard_map/ppermute | solution.py:317

commit v29 on v24

--- a/solution.py
+++ b/solution.py
@@ -1,4 +1,3 @@
-import functools
 import math
 
 import jax
@@ -45,10 +44,6 @@
 
 def widen(row_value, width):
     return jnp.concatenate([row_value] * (width // HD), axis=1)
-
-
-def place():
-    return lax.rem(lax.axis_index("loop"), 2) == 1, lax.axis_index("pair")
 
 
 def load_blocks(count):
@@ -166,34 +161,20 @@
     return lax.axis_index("groups") + lax.axis_index("loop") + lax.axis_index("heads") == 0
 
 
-def penalty(is_there):
-    return jnp.where(is_there, 0.0, empty_best)
-
-
-def add_stage(by_swap, *refs):
+def add_stage(*refs):
     query_ref, best_ref, total_ref, sum_ref = refs[:4]
     shard_refs = refs[4:-2]
     total_out, sum_out = refs[-2:]
     heads = query_ref.shape[1] // HD
     shard = jnp.concatenate([ref[...] for ref in shard_refs], axis=0)
     key_rows, value_rows = shard[:, :HD], with_ones(shard[:, HD:])
-    extra = None
-    if by_swap is not None:
-        is_odd, core = place()
-        extra = penalty(jnp.logical_not(is_odd) | (core == int(by_swap)))
 
     def start(rows):
         return scores_of(stacked(query_ref, rows, heads), key_rows)
 
     def finish(index, rows, scores):
         best = stacked(best_ref, rows, heads)
-        if extra is None:
-            points = widen(best, scores.shape[1])
-        else:
-            held = shard_refs[-1].shape[0]
-            points = [best] * ((scores.shape[1] - held) // HD) + [best + extra] * (held // HD)
-            points = jnp.concatenate(points, axis=1)
-        weights = jnp.exp2(scores - points).astype(jnp.bfloat16)
+        weights = jnp.exp2(scores - widen(best, scores.shape[1])).astype(jnp.bfloat16)
         result = jnp.dot(weights, value_rows, preferred_element_type=jnp.float32)
         unstack(total_out, rows, heads, stacked(total_ref, rows, heads) + result[:, HD:])
         unstack(sum_out, rows, heads, stacked(sum_ref, rows, heads) + result[:, :HD])
@@ -201,15 +182,15 @@
     staged(row_blocks(query_ref.shape[0], 80), start, finish)
 
 
-def last_stage(routed, *refs):
+def last_stage(*refs):
     query_ref, best_ref, old_total_ref, old_sum_ref, total_ref, sum_ref = refs[:6]
-    earlier_refs, refs = refs[6:-6], refs[-6:]
-    direct_ref, swapped_ref, out_hbm, out_ref, trusted_ref, out_sems = refs
+    earlier_refs, refs = refs[6:-5], refs[-5:]
+    direct_ref, swapped_ref, out_hbm, out_ref, out_sems = refs
     heads = query_ref.shape[1] // HD
     blocks = row_blocks(query_ref.shape[0], 80)
-    is_odd, core = place()
-    takes_both = is_odd & routed
-    is_direct = core == 0
+    position = lax.rem(lax.axis_index("loop"), FOUR)
+    is_direct = lax.axis_index("pair") == jnp.where(position == 2, 1, 0)
+    last_shard = jnp.where(is_direct, direct_ref[...], swapped_ref[...])
 
     def out_copy(index, rows):
         return pltpu.make_async_copy(out_ref.at[rows], out_hbm.at[rows], out_sems.at[index])
@@ -219,60 +200,40 @@
         inverse = inverse * (2.0 - total * inverse)
         unstack(out_ref, rows, heads, (weighted * inverse).astype(jnp.bfloat16))
 
-    def process(shard):
-        trusted = [jnp.full((8, HD), True)]
-        key_rows, value_rows = shard[:, :HD], with_ones(shard[:, HD:])
-
-        def start(rows):
-            return scores_of(stacked(query_ref, rows, heads), key_rows)
-
-        def finish(index, rows, scores):
-            best = stacked(best_ref, rows, heads)
-            weights = jnp.exp2(scores - widen(best, scores.shape[1])).astype(jnp.bfloat16)
-            result = jnp.dot(weights, value_rows, preferred_element_type=jnp.float32)
-            total = stacked(total_ref, rows, heads) + result[:, HD:]
-            weighted = stacked(sum_ref, rows, heads) + result[:, :HD]
-            good = (total < total_limit).reshape(total.shape[0] // 8, 8, HD)
-            trusted[0] = trusted[0] & jnp.all(good, axis=0)
-            write(rows, total, weighted)
-            out_copy(index, rows).start()
-
-        staged(blocks, start, finish)
-        trusted_ref[0] = jnp.all(trusted[0]).astype(jnp.int32)
-        for index, rows in enumerate(blocks):
-            out_copy(index, rows).wait()
-
-    @pl.when(jnp.logical_not(takes_both))
-    def one_shard():
-        process(jnp.where(is_direct, direct_ref[...], swapped_ref[...]))
-
-    @pl.when(takes_both)
-    def two_shards():
-        process(jnp.concatenate([direct_ref[...], swapped_ref[...]], axis=0))
-
-    @pl.when(trusted_ref[0] == 0)
+    trusted = [jnp.full((8, HD), True)]
+    key_rows, value_rows = last_shard[:, :HD], with_ones(last_shard[:, HD:])
+
+    def start(rows):
+        return scores_of(stacked(query_ref, rows, heads), key_rows)
+
+    def finish(index, rows, scores):
+        best = stacked(best_ref, rows, heads)
+        weights = jnp.exp2(scores - widen(best, scores.shape[1])).astype(jnp.bfloat16)
+        result = jnp.dot(weights, value_rows, preferred_element_type=jnp.float32)
+        total = stacked(total_ref, rows, heads) + result[:, HD:]
+        weighted = stacked(sum_ref, rows, heads) + result[:, :HD]
+        good = (total < total_limit).reshape(total.shape[0] // 8, 8, HD)
+        trusted[0] = trusted[0] & jnp.all(good, axis=0)
+        write(rows, total, weighted)
+        out_copy(index, rows).start()
+
+    staged(blocks, start, finish)
+    is_trusted = jnp.all(trusted[0])
+    for index, rows in enumerate(blocks):
+        out_copy(index, rows).wait()
+
+    @pl.when(jnp.logical_not(is_trusted))
     def exact_maximum():
         size = query_ref.shape[0] // len(blocks)
-        counted = [(ref, 0.0) for ref in earlier_refs]
-        if routed:
-            counted[-2:] = [
-                (ref, penalty(jnp.logical_not(is_odd) | (core == by_swap)))
-                for by_swap, ref in enumerate(earlier_refs[-2:])
-            ]
-        counted += [
-            (direct_ref, penalty(takes_both | is_direct)),
-            (swapped_ref, penalty(takes_both | jnp.logical_not(is_direct))),
-        ]
-
         def visit(index, unused):
             rows = pl.ds(pl.multiple_of(index * size, size), size)
             queries = stacked(query_ref, rows, heads)
             best = stacked(best_ref, rows, heads)
             weighted = stacked(old_sum_ref, rows, heads)
             total = stacked(old_total_ref, rows, heads)
-            for shard_ref, extra in counted:
-                key_rows, value_rows = shard_ref[:, :HD], with_ones(shard_ref[:, HD:])
-                scores = scores_of(queries, key_rows) - extra
+            for shard in [ref[...] for ref in earlier_refs] + [last_shard]:
+                key_rows, value_rows = shard[:, :HD], with_ones(shard[:, HD:])
+                scores = scores_of(queries, key_rows)
                 new_best = jnp.maximum(best, jnp.max(scores, axis=1, keepdims=True))
                 factor = jnp.exp2(best - new_best)
                 weights = jnp.exp2(scores - widen(new_best, scores.shape[1]))
@@ -315,15 +276,19 @@
                 hops.append((2 * i + core, 2 * to + to_core))
         return lax.ppermute(shard, ("loop", "pair"), hops)
 
-    def first_route(i, core):
-        if core == 1:
-            return (i ^ 2) & ~1, i & 1
-        return (i, 1) if i & 1 else (i + 1, 0)
-
-    def second_route(i, core):
-        if core == 1:
-            return (i ^ 2) | 1, 1 - i & 1
-        return (i - 1, 0) if i & 1 else (i, 1)
+    def routed_by(table):
+        def route(i, core):
+            to, to_core = table[i % FOUR][core]
+            return i - i % FOUR + to, to_core
+
+        return route
+
+    first_route = routed_by(
+        [((1, 1), (3, 1)), ((3, 0), (2, 0)), ((1, 0), (0, 0)), ((2, 1), (0, 1))]
+    )
+    second_route = routed_by(
+        [((0, 1), (2, 1)), ((1, 1), (0, 0)), ((3, 0), (2, 0)), ((3, 1), (1, 0))]
+    )
 
     hbm = [pltpu.with_memory_space_constraint(x, pltpu.HBM) for x in (lengths, queries, suffix, own)]
     buffers = [
@@ -372,11 +337,11 @@
         cost_estimate=cost,
     )(*hbm, *loaded)
 
-    def add_shards(total, weighted, shards_now, by_swap):
+    def add_shards(total, weighted, shards_now):
         if not shards_now:
             return total, weighted
         return pl.pallas_call(
-            functools.partial(add_stage, by_swap if routed else None),
+            add_stage,
             name="add_stage",
             out_shape=[state] * 2,
             in_specs=[in_vmem] * (4 + len(shards_now)),
@@ -390,22 +355,21 @@
 
     early, best = lax.optimization_barrier((early, best))
     early_swapped = [swapped(shard) for shard in early] if routed else []
-    new_total, new_weighted = add_shards(total, weighted, early, False)
+    new_total, new_weighted = add_shards(total, weighted, early)
     final, new_total = lax.optimization_barrier((final, new_total))
     final_swapped = swapped(final) if routed else final
-    new_total, new_weighted = add_shards(new_total, new_weighted, early_swapped, True)
+    new_total, new_weighted = add_shards(new_total, new_weighted, early_swapped)
     last_inputs = (queries, best, total, weighted, new_total, new_weighted)
     last_inputs += (*early[:-1], *early_swapped[:-1], *early[-1:], *early_swapped[-1:])
     last_inputs += (final, final_swapped)
     return pl.pallas_call(
-        functools.partial(last_stage, routed),
+        last_stage,
         name="last_stage",
         out_shape=jax.ShapeDtypeStruct((slots, width), jnp.bfloat16),
         in_specs=[in_vmem] * len(last_inputs),
         out_specs=in_hbm,
         scratch_shapes=[
             pltpu.VMEM((slots, width), jnp.bfloat16),
-            pltpu.SMEM((1,), jnp.int32),
             pltpu.SemaphoreType.DMA((len(row_blocks(slots, 80)),)),
         ],
         compiler_params=pltpu.CompilerParams(vmem_limit_bytes=32 * 2**20),

time: 24.9 us -> 24.4 us (0.980)
  the two profiles are of different devices: /device:TPU:0 before, /device:TPU:5 now
where the time goes in v29:
time: 24.4 us; the launch traced here: 24.3 us
  Pallas kernels  18 us (74%)
  starting transfers between devices  5.75 us (24%)
  waiting for transfers between devices  0.42 us (2%)
    pallas_call x1, Pallas kernels, shards(): pl.pallas_call(last_stage, name='last_stage', out_shape=jax.ShapeDtypeStr...  11.8 us
    ppermute x4, starting transfers between devices, send(): return lax.ppermute(shard, ('loop', 'pair'), hops)  5.75 us
    pallas_call x1, Pallas kernels, shards(): pl.pallas_call(local_stage, name='local_stage', out_shape=[state] * 3 + b...  4.28 us
    pallas_call x2, Pallas kernels, add_shards(): pl.pallas_call(add_stage, name='add_stage', out_shape=[state] * 2, in_spe...  1.81 us
  transfers between devices with their start and end apart: 4, of which 1 were waited for; matrix products, arithmetic and copies ran while one was open for 0% of the time, Pallas kernels for 25%

profile of v29, /device:TPU:5, one launch (start us, length us, event | category | flops | bytes accessed | tf_op | source)
XLA Modules:
  0.0 24.3 jit_solution(11825844870860355282)
XLA Ops:
  0.0 0.1 prelude_stage.1
  0.1 3.4 %collective-permute-start = (bf16[256,256]{1,0:T(8,128)(2,1)}, bf16[256,256]{1,0:T(8,128)(2,1)S(1)}, u32[]{:S(2)}, u32[]{:S(2)}) collective-permute-start(bf16[256,256]{1,0:T(8,128)(2,1)} %bitcast.5), channel_id=1, source_target_pairs={{0,5},{1,13},{4,12},{5,8},{8,4},{9,0},{12,9},{13,1},{2,7},{3,15},{... | collective-permute-start | bytes 393224 | tf_op jit(solution)/shard_map/ppermute | solution.py:277
  3.5 0.0 collective-permute-start.1
  3.5 4.3 %local_stage.1 = (f32[640,512]{1,0:T(8,128)S(1)}, f32[640,512]{1,0:T(8,128)S(1)}, f32[640,512]{1,0:T(8,128)S(1)}, bf16[640,512]{1,0:T(8,128)(2,1)S(1)}, bf16[640...) custom-call(s32[8]{0:T(128)} %refs_0_.3, ...), custom_call_target="tpu_custom_call", output_to_operand_aliasing={{3}: (4, {}), {4}: (5, {}), {5}: (6, {}), {6}: (7, {})} | custom-call | flops 1 | bytes 1 | tf_op jit(solution)/shard_map/local_stage/pallas_call | solution.py:328
  7.8 0.0 collective-permute-done.refs_4_.refs_6_
  7.8 2.3 %collective-permute-start.2 = (bf16[256,256]{1,0:T(8,128)(2,1)S(1)}, bf16[256,256]{1,0:T(8,128)(2,1)S(1)}, u32[]{:S(2)}, u32[]{:S(2)}) collective-permute-start(bf16[256,256]{1,0:T(8,128)(2,1)S(1)} %collective-permute-done.refs_4_.refs_6_), channel_id=1, source_target_pairs={{0,1},{1,0},{4,5},{5,4},{8,9},{9,8},{12,13},{13,12},{2,3},{3,2},{6... | collective-permute-start | bytes 393224 | tf_op jit(solution)/shard_map/ppermute | solution.py:277
  10.1 0.9 %add_stage.2 = (f32[640,512]{1,0:T(8,128)S(1)}, f32[640,512]{1,0:T(8,128)S(1)}) custom-call(bf16[640,512]{1,0:T(8,128)(2,1)S(1)} %get-tuple-element.34.refs_0_, f32[640,512]{1,0:T(8,128)S(1)} %get-tuple-element.37.refs_1_, f32[640,512]{1,0:T(8,128)S(1)} %get-tuple-element.38.refs_2_, f32[640,512]{1,0:T(8,128)S(1)} %get-tuple-element.39.refs_3_, ...), custom_call_target="tpu_custom_call" | custom-call | flops 1 | bytes 1 | tf_op jit(solution)/shard_map/add_stage/pallas_call | solution.py:343
  11.0 0.0 collective-permute-done.1.refs_8_
  11.0 0.1 collective-permute-start.3
  11.1 0.0 collective-permute-done.2.refs_4_.refs_7_
  11.1 0.9 %add_stage.3 = (f32[640,512]{1,0:T(8,128)S(1)}, f32[640,512]{1,0:T(8,128)S(1)}) custom-call(bf16[640,512]{1,0:T(8,128)(2,1)S(1)} %get-tuple-element.34.refs_0_, f32[640,512]{1,0:T(8,128)S(1)} %get-tuple-element.37.refs_1_, f32[640,512]{1,0:T(8,128)S(1)} %get-tuple-element.42.refs_2_, f32[640,512]{1,0:T(8,128)S(1)} %get-tuple-element.43.refs_3_, ...), custom_call_target="tpu_custom_call" | custom-call | flops 1 | bytes 1 | tf_op jit(solution)/shard_map/add_stage/pallas_call | solution.py:343
  12.0 0.4 %collective-permute-done.3.refs_9_ = bf16[256,256]{1,0:T(8,128)(2,1)S(1)} collective-permute-done((bf16[256,256]{1,0:T(8,128)(2,1)S(1)}, bf16[256,256]{1,0:T(8,128)(2,1)S(1)}, u32[]{:S(2)}, u32[]{:S(2)}) %collective-permute-start.3) | collective-permute-done | bytes 131104 | tf_op jit(solution)/shard_map/ppermute | solution.py:277
  12.4 11.8 %last_stage.1 = bf16[640,512]{1,0:T(8,128)(2,1)} custom-call(bf16[640,512]{1,0:T(8,128)(2,1)S(1)} %get-tuple-element.34.refs_0_, f32[640,512]{1,0:T(8,128)S(1)} %get-tuple-element.37.refs_1_, f32[640,512]{1,0:T(8,128)S(1)} %get-tuple-element.38.refs_2_, f32[640,512]{1,0:T(8,128)S(1)} %get-tuple-element.39.refs_3_, f32[640,512]{1,0:T(8,128)S(1)} %get-tuple-element.44.refs_4_, ...), custom_call_target="tpu_custom_call" | custom-call | flops 1 | bytes 1 | tf_op jit(solution)/shard_map/last_stage/pallas_call | solution.py:365
Async XLA Ops:
  0.1 7.7 %collective-permute-start = (bf16[256,256]{1,0:T(8,128)(2,1)}, bf16[256,256]{1,0:T(8,128)(2,1)S(1)}, u32[]{:S(2)}, u32[]{:S(2)}) collective-permute-start(bf16[256,256]{1,0:T(8,128)(2,1)} %bitcast.5), channel_id=1, source_target_pairs={{0,5},{1,13},{4,12},{5,8},{8,4},{9,0},{12,9},{13,1},{2,7},{3,15},{... | collective-permute-start | bytes 393224 | tf_op jit(solution)/shard_map/ppermute | solution.py:277
  3.5 7.5 %collective-permute-start.1 = (bf16[256,256]{1,0:T(8,128)(2,1)}, bf16[256,256]{1,0:T(8,128)(2,1)S(1)}, u32[]{:S(2)}, u32[]{:S(2)}) collective-permute-start(bf16[256,256]{1,0:T(8,128)(2,1)} %bitcast.6), channel_id=1, source_target_pairs={{0,1},{1,9},{4,5},{5,0},{8,12},{9,8},{12,13},{13,4},{2,3},{3,11},{... | collective-permute-start | bytes 393224 | tf_op jit(solution)/shard_map/ppermute | solution.py:277
  7.8 3.3 %collective-permute-start.2 = (bf16[256,256]{1,0:T(8,128)(2,1)S(1)}, bf16[256,256]{1,0:T(8,128)(2,1)S(1)}, u32[]{:S(2)}, u32[]{:S(2)}) collective-permute-start(bf16[256,256]{1,0:T(8,128)(2,1)S(1)} %collective-permute-done.refs_4_.refs_6_), channel_id=1, source_target_pairs={{0,1},{1,0},{4,5},{5,4},{8,9},{9,8},{12,13},{13,12},{2,3},{3,2},{6... | collective-permute-start | bytes 393224 | tf_op jit(solution)/shard_map/ppermute | solution.py:277
  11.0 1.4 %collective-permute-start.3 = (bf16[256,256]{1,0:T(8,128)(2,1)S(1)}, bf16[256,256]{1,0:T(8,128)(2,1)S(1)}, u32[]{:S(2)}, u32[]{:S(2)}) collective-permute-start(bf16[256,256]{1,0:T(8,128)(2,1)S(1)} %collective-permute-done.1.refs_8_), channel_id=1, source_target_pairs={{0,1},{1,0},{4,5},{5,4},{8,9},{9,8},{12,13},{13,12},{2,3},{3,2},{6... | collective-permute-start | bytes 393224 | tf_op jit(solution)/shard_map/ppermute | solution.py:277

commit v30 on v27

--- a/solution.py
+++ b/solution.py
@@ -198,7 +198,7 @@
         unstack(total_out, rows, heads, stacked(total_ref, rows, heads) + result[:, HD:])
         unstack(sum_out, rows, heads, stacked(sum_ref, rows, heads) + result[:, :HD])
 
-    staged(row_blocks(query_ref.shape[0], 80), start, finish)
+    staged(row_blocks(query_ref.shape[0], 160), start, finish)
 
 
 def last_stage(routed, *refs):
@@ -206,7 +206,7 @@
     earlier_refs, refs = refs[6:-6], refs[-6:]
     direct_ref, swapped_ref, out_hbm, out_ref, trusted_ref, out_sems = refs
     heads = query_ref.shape[1] // HD
-    blocks = row_blocks(query_ref.shape[0], 80)
+    blocks = row_blocks(query_ref.shape[0], 160)
     position, core = place()
     takes_both = (position == 1) & routed
     is_direct = core == jnp.where(position == 0, 0, 1)
@@ -410,7 +410,7 @@
         scratch_shapes=[
             pltpu.VMEM((slots, width), jnp.bfloat16),
             pltpu.SMEM((1,), jnp.int32),
-            pltpu.SemaphoreType.DMA((len(row_blocks(slots, 80)),)),
+            pltpu.SemaphoreType.DMA((len(row_blocks(slots, 160)),)),
         ],
         compiler_params=pltpu.CompilerParams(vmem_limit_bytes=32 * 2**20),
         cost_estimate=cost,

time: 23.9 us -> 20.2 us (0.85)
  Pallas kernels: 18.7 us -> 15 us
    pallas_call x1, Pallas kernels: 12.5 us -> 8.8 us  [shards(): pl.pallas_call(functools.partial(last_stage, routed), name='last_stage',...]
  transfers between devices with their start and end apart: 4 -> 4, of which waited for: 3 -> 3; matrix products, arithmetic and copies ran while one was open for 0% -> 0% of each run, Pallas kernels for 20% -> 24%
where the time goes in v30:
time: 20.2 us; the launch traced here: 19.9 us
  Pallas kernels  15 us (74%)
  starting transfers between devices  4.21 us (21%)
  waiting for transfers between devices  0.63 us (3%)
    pallas_call x1, Pallas kernels, shards(): pl.pallas_call(functools.partial(last_stage, routed), name='last_stage',...  8.8 us
    ppermute x4, starting transfers between devices, send(): return lax.ppermute(shard, ('loop', 'pair'), hops)  4.21 us
    pallas_call x1, Pallas kernels, shards(): pl.pallas_call(local_stage, name='local_stage', out_shape=[state] * 3 + b...  3.03 us
    pallas_call x2, Pallas kernels, add_shards(): pl.pallas_call(functools.partial(add_stage, by_swap if routed else None),...  1.82 us
    pallas_call x1, Pallas kernels, shards(): pl.pallas_call(prelude_stage, name='prelude_stage', out_shape=buffers, in...  1.35 us
    ppermute x4, waiting for transfers between devices, send(): return lax.ppermute(shard, ('loop', 'pair'), hops)  0.63 us
  transfers between devices with their start and end apart: 4, of which 3 were waited for; matrix products, arithmetic and copies ran while one was open for 0% of the time, Pallas kernels for 24%

profile of v30, /device:TPU:0, one launch (start us, length us, event | category | flops | bytes accessed | tf_op | source)
XLA Modules:
  0.0 19.9 jit_solution(3088355545184725573)
XLA Ops:
  0.0 1.4 %prelude_stage.1 = (bf16[640,512]{1,0:T(8,128)(2,1)S(1)}, bf16[640,256]{1,0:T(8,128)(2,1)S(1)}, bf16[256,256]{1,0:T(8,128)(2,1)S(1)}, s32[640,128]{1,0:T(8,128)S(1)}) custom-call(s32[8]{0:T(128)} %refs_0_.3, bf16[640,512]{1,0:T(8,128)(2,1)} %refs_1_.3, bf16[640,256]{1,0:T(8,128)(2,1)} %bitcast.2, bf16[256,256]{1,0:T(8,128)(2,1)} %bitcast.4), custom_call_target="tpu_custom_call" | custom-call | flops 1 | bytes 1 | tf_op jit(solution)/shard_map/prelude_stage/pallas_call | solution.py:343
  1.4 1.8 %collective-permute-start = (bf16[256,256]{1,0:T(8,128)(2,1)}, bf16[256,256]{1,0:T(8,128)(2,1)S(1)}, u32[]{:S(2)}, u32[]{:S(2)}) collective-permute-start(bf16[256,256]{1,0:T(8,128)(2,1)} %bitcast.5), channel_id=1, source_target_pairs={{0,4},{1,13},{4,5},{5,8},{8,12},{9,0},{12,9},{13,1},{2,6},{3,15},{... | collective-permute-start | bytes 393224 | tf_op jit(solution)/shard_map/ppermute | solution.py:316
  3.2 1.6 %collective-permute-start.1 = (bf16[256,256]{1,0:T(8,128)(2,1)}, bf16[256,256]{1,0:T(8,128)(2,1)S(1)}, u32[]{:S(2)}, u32[]{:S(2)}) collective-permute-start(bf16[256,256]{1,0:T(8,128)(2,1)} %bitcast.6), channel_id=1, source_target_pairs={{0,1},{1,9},{4,0},{5,13},{8,12},{9,4},{12,8},{13,5},{2,3},{3,11},{... | collective-permute-start | bytes 393224 | tf_op jit(solution)/shard_map/ppermute | solution.py:316
  4.8 3.0 %local_stage.1 = (f32[640,512]{1,0:T(8,128)S(1)}, f32[640,512]{1,0:T(8,128)S(1)}, f32[640,512]{1,0:T(8,128)S(1)}, bf16[640,512]{1,0:T(8,128)(2,1)S(1)}, bf16[640...) custom-call(s32[8]{0:T(128)} %refs_0_.3, ...), custom_call_target="tpu_custom_call", output_to_operand_aliasing={{3}: (4, {}), {4}: (5, {}), {5}: (6, {}), {6}: (7, {})} | custom-call | flops 1 | bytes 1 | tf_op jit(solution)/shard_map/local_stage/pallas_call | solution.py:367
  7.8 0.1 collective-permute-done.refs_4_.refs_6_
  7.9 0.8 %collective-permute-start.2 = (bf16[256,256]{1,0:T(8,128)(2,1)S(1)}, bf16[256,256]{1,0:T(8,128)(2,1)S(1)}, u32[]{:S(2)}, u32[]{:S(2)}) collective-permute-start(bf16[256,256]{1,0:T(8,128)(2,1)S(1)} %collective-permute-done.refs_4_.refs_6_), channel_id=1, source_target_pairs={{0,1},{1,0},{4,5},{5,4},{8,9},{9,8},{12,13},{13,12},{2,3},{3,2},{6... | collective-permute-start | bytes 393224 | tf_op jit(solution)/shard_map/ppermute | solution.py:316
  8.7 0.9 %add_stage.2 = (f32[640,512]{1,0:T(8,128)S(1)}, f32[640,512]{1,0:T(8,128)S(1)}) custom-call(bf16[640,512]{1,0:T(8,128)(2,1)S(1)} %get-tuple-element.34.refs_0_, f32[640,512]{1,0:T(8,128)S(1)} %get-tuple-element.37.refs_1_, f32[640,512]{1,0:T(8,128)S(1)} %get-tuple-element.38.refs_2_, f32[640,512]{1,0:T(8,128)S(1)} %get-tuple-element.39.refs_3_, ...), custom_call_target="tpu_custom_call" | custom-call | flops 1 | bytes 1 | tf_op jit(solution)/shard_map/add_stage/pallas_call | solution.py:382
  9.6 0.1 collective-permute-done.1.refs_8_
  9.7 0.0 collective-permute-start.3
  9.7 0.0 collective-permute-done.2.refs_4_.refs_7_
  9.7 0.9 %add_stage.3 = (f32[640,512]{1,0:T(8,128)S(1)}, f32[640,512]{1,0:T(8,128)S(1)}) custom-call(bf16[640,512]{1,0:T(8,128)(2,1)S(1)} %get-tuple-element.34.refs_0_, f32[640,512]{1,0:T(8,128)S(1)} %get-tuple-element.37.refs_1_, f32[640,512]{1,0:T(8,128)S(1)} %get-tuple-element.42.refs_2_, f32[640,512]{1,0:T(8,128)S(1)} %get-tuple-element.43.refs_3_, ...), custom_call_target="tpu_custom_call" | custom-call | flops 1 | bytes 1 | tf_op jit(solution)/shard_map/add_stage/pallas_call | solution.py:382
  10.7 0.4 %collective-permute-done.3.refs_9_ = bf16[256,256]{1,0:T(8,128)(2,1)S(1)} collective-permute-done((bf16[256,256]{1,0:T(8,128)(2,1)S(1)}, bf16[256,256]{1,0:T(8,128)(2,1)S(1)}, u32[]{:S(2)}, u32[]{:S(2)}) %collective-permute-start.3) | collective-permute-done | bytes 131104 | tf_op jit(solution)/shard_map/ppermute | solution.py:316
  11.1 8.8 %last_stage.1 = bf16[640,512]{1,0:T(8,128)(2,1)} custom-call(bf16[640,512]{1,0:T(8,128)(2,1)S(1)} %get-tuple-element.34.refs_0_, f32[640,512]{1,0:T(8,128)S(1)} %get-tuple-element.37.refs_1_, f32[640,512]{1,0:T(8,128)S(1)} %get-tuple-element.38.refs_2_, f32[640,512]{1,0:T(8,128)S(1)} %get-tuple-element.39.refs_3_, f32[640,512]{1,0:T(8,128)S(1)} %get-tuple-element.44.refs_4_, ...), custom_call_target="tpu_custom_call" | custom-call | flops 1 | bytes 1 | tf_op jit(solution)/shard_map/last_stage/pallas_call | solution.py:404
Async XLA Ops:
  1.4 6.5 %collective-permute-start = (bf16[256,256]{1,0:T(8,128)(2,1)}, bf16[256,256]{1,0:T(8,128)(2,1)S(1)}, u32[]{:S(2)}, u32[]{:S(2)}) collective-permute-start(bf16[256,256]{1,0:T(8,128)(2,1)} %bitcast.5), channel_id=1, source_target_pairs={{0,4},{1,13},{4,5},{5,8},{8,12},{9,0},{12,9},{13,1},{2,6},{3,15},{... | collective-permute-start | bytes 393224 | tf_op jit(solution)/shard_map/ppermute | solution.py:316
  3.2 6.5 %collective-permute-start.1 = (bf16[256,256]{1,0:T(8,128)(2,1)}, bf16[256,256]{1,0:T(8,128)(2,1)S(1)}, u32[]{:S(2)}, u32[]{:S(2)}) collective-permute-start(bf16[256,256]{1,0:T(8,128)(2,1)} %bitcast.6), channel_id=1, source_target_pairs={{0,1},{1,9},{4,0},{5,13},{8,12},{9,4},{12,8},{13,5},{2,3},{3,11},{... | collective-permute-start | bytes 393224 | tf_op jit(solution)/shard_map/ppermute | solution.py:316
  7.9 1.9 %collective-permute-start.2 = (bf16[256,256]{1,0:T(8,128)(2,1)S(1)}, bf16[256,256]{1,0:T(8,128)(2,1)S(1)}, u32[]{:S(2)}, u32[]{:S(2)}) collective-permute-start(bf16[256,256]{1,0:T(8,128)(2,1)S(1)} %collective-permute-done.refs_4_.refs_6_), channel_id=1, source_target_pairs={{0,1},{1,0},{4,5},{5,4},{8,9},{9,8},{12,13},{13,12},{2,3},{3,2},{6... | collective-permute-start | bytes 393224 | tf_op jit(solution)/shard_map/ppermute | solution.py:316
  9.7 1.3 %collective-permute-start.3 = (bf16[256,256]{1,0:T(8,128)(2,1)S(1)}, bf16[256,256]{1,0:T(8,128)(2,1)S(1)}, u32[]{:S(2)}, u32[]{:S(2)}) collective-permute-start(bf16[256,256]{1,0:T(8,128)(2,1)S(1)} %collective-permute-done.1.refs_8_), channel_id=1, source_target_pairs={{0,1},{1,0},{4,5},{5,4},{8,9},{9,8},{12,13},{13,12},{2,3},{3,2},{6... | collective-permute-start | bytes 393224 | tf_op jit(solution)/shard_map/ppermute | solution.py:316

commit v31 on v27

--- a/solution.py
+++ b/solution.py
@@ -317,7 +317,7 @@
 
     def first_route(i, core):
         base = i - i % FOUR
-        to, to_core = [((1, 0), (3, 1)), ((1, 1), (2, 0)), ((3, 0), (0, 0)), ((2, 1), (0, 1))][
+        to, to_core = [((1, 0), (3, 1)), ((1, 1), (2, 1)), ((3, 0), (0, 0)), ((2, 0), (0, 1))][
             i % FOUR
         ][core]
         return base + to, to_core

time: 23.9 us -> 23.9 us (level)
  starting transfers between devices: 4.21 us -> 3.55 us
  waiting for transfers between devices: 0.66 us -> 1.31 us
    ppermute x4, starting transfers between devices: 4.21 us -> 3.55 us  [send(): return lax.ppermute(shard, ('loop', 'pair'), hops)]
    ppermute x4, waiting for transfers between devices: 0.66 us -> 1.31 us  [send(): return lax.ppermute(shard, ('loop', 'pair'), hops)]
where the time goes in v31:
time: 23.9 us; the launch traced here: 23.6 us
  Pallas kernels  18.7 us (78%)
  starting transfers between devices  3.55 us (15%)
  waiting for transfers between devices  1.31 us (5%)
    pallas_call x1, Pallas kernels, shards(): pl.pallas_call(functools.partial(last_stage, routed), name='last_stage',...  12.5 us
    ppermute x4, starting transfers between devices, send(): return lax.ppermute(shard, ('loop', 'pair'), hops)  3.55 us
    pallas_call x1, Pallas kernels, shards(): pl.pallas_call(local_stage, name='local_stage', out_shape=[state] * 3 + b...  3.04 us
    pallas_call x2, Pallas kernels, add_shards(): pl.pallas_call(functools.partial(add_stage, by_swap if routed else None),...  1.79 us
    pallas_call x1, Pallas kernels, shards(): pl.pallas_call(prelude_stage, name='prelude_stage', out_shape=buffers, in...  1.35 us
    ppermute x4, waiting for transfers between devices, send(): return lax.ppermute(shard, ('loop', 'pair'), hops)  1.31 us
  transfers between devices with their start and end apart: 4, of which 3 were waited for; matrix products, arithmetic and copies ran while one was open for 0% of the time, Pallas kernels for 20%

profile of v31, /device:TPU:0, one launch (start us, length us, event | category | flops | bytes accessed | tf_op | source)
XLA Modules:
  0.0 23.6 jit_solution(3959848640185287790)
XLA Ops:
  0.0 1.4 %prelude_stage.1 = (bf16[640,512]{1,0:T(8,128)(2,1)S(1)}, bf16[640,256]{1,0:T(8,128)(2,1)S(1)}, bf16[256,256]{1,0:T(8,128)(2,1)S(1)}, s32[640,128]{1,0:T(8,128)S(1)}) custom-call(s32[8]{0:T(128)} %refs_0_.3, bf16[640,512]{1,0:T(8,128)(2,1)} %refs_1_.3, bf16[640,256]{1,0:T(8,128)(2,1)} %bitcast.2, bf16[256,256]{1,0:T(8,128)(2,1)} %bitcast.4), custom_call_target="tpu_custom_call" | custom-call | flops 1 | bytes 1 | tf_op jit(solution)/shard_map/prelude_stage/pallas_call | solution.py:343
  1.4 1.8 %collective-permute-start = (bf16[256,256]{1,0:T(8,128)(2,1)}, bf16[256,256]{1,0:T(8,128)(2,1)S(1)}, u32[]{:S(2)}, u32[]{:S(2)}) collective-permute-start(bf16[256,256]{1,0:T(8,128)(2,1)} %bitcast.5), channel_id=1, source_target_pairs={{0,4},{1,13},{4,5},{5,9},{8,12},{9,0},{12,8},{13,1},{2,6},{3,15},{... | collective-permute-start | bytes 393224 | tf_op jit(solution)/shard_map/ppermute | solution.py:316
  3.2 1.6 %collective-permute-start.1 = (bf16[256,256]{1,0:T(8,128)(2,1)}, bf16[256,256]{1,0:T(8,128)(2,1)S(1)}, u32[]{:S(2)}, u32[]{:S(2)}) collective-permute-start(bf16[256,256]{1,0:T(8,128)(2,1)} %bitcast.6), channel_id=1, source_target_pairs={{0,1},{1,9},{4,0},{5,13},{8,12},{9,4},{12,8},{13,5},{2,3},{3,11},{... | collective-permute-start | bytes 393224 | tf_op jit(solution)/shard_map/ppermute | solution.py:316
  4.8 3.0 %local_stage.1 = (f32[640,512]{1,0:T(8,128)S(1)}, f32[640,512]{1,0:T(8,128)S(1)}, f32[640,512]{1,0:T(8,128)S(1)}, bf16[640,512]{1,0:T(8,128)(2,1)S(1)}, bf16[640...) custom-call(s32[8]{0:T(128)} %refs_0_.3, ...), custom_call_target="tpu_custom_call", output_to_operand_aliasing={{3}: (4, {}), {4}: (5, {}), {5}: (6, {}), {6}: (7, {})} | custom-call | flops 1 | bytes 1 | tf_op jit(solution)/shard_map/local_stage/pallas_call | solution.py:367
  7.8 0.6 %collective-permute-done.refs_4_.refs_6_ = bf16[256,256]{1,0:T(8,128)(2,1)S(1)} collective-permute-done((bf16[256,256]{1,0:T(8,128)(2,1)}, bf16[256,256]{1,0:T(8,128)(2,1)S(1)}, u32[]{:S(2)}, u32[]{:S(2)}) %collective-permute-start) | collective-permute-done | bytes 131104 | tf_op jit(solution)/shard_map/ppermute | solution.py:316
  8.4 0.0 collective-permute-start.2
  8.4 0.9 %add_stage.2 = (f32[640,512]{1,0:T(8,128)S(1)}, f32[640,512]{1,0:T(8,128)S(1)}) custom-call(bf16[640,512]{1,0:T(8,128)(2,1)S(1)} %get-tuple-element.34.refs_0_, f32[640,512]{1,0:T(8,128)S(1)} %get-tuple-element.37.refs_1_, f32[640,512]{1,0:T(8,128)S(1)} %get-tuple-element.38.refs_2_, f32[640,512]{1,0:T(8,128)S(1)} %get-tuple-element.39.refs_3_, ...), custom_call_target="tpu_custom_call" | custom-call | flops 1 | bytes 1 | tf_op jit(solution)/shard_map/add_stage/pallas_call | solution.py:382
  9.3 0.4 %collective-permute-done.1.refs_8_ = bf16[256,256]{1,0:T(8,128)(2,1)S(1)} collective-permute-done((bf16[256,256]{1,0:T(8,128)(2,1)}, bf16[256,256]{1,0:T(8,128)(2,1)S(1)}, u32[]{:S(2)}, u32[]{:S(2)}) %collective-permute-start.1) | collective-permute-done | bytes 131104 | tf_op jit(solution)/shard_map/ppermute | solution.py:316
  9.7 0.1 collective-permute-start.3
  9.9 0.0 collective-permute-done.2.refs_4_.refs_7_
  9.9 0.9 %add_stage.3 = (f32[640,512]{1,0:T(8,128)S(1)}, f32[640,512]{1,0:T(8,128)S(1)}) custom-call(bf16[640,512]{1,0:T(8,128)(2,1)S(1)} %get-tuple-element.34.refs_0_, f32[640,512]{1,0:T(8,128)S(1)} %get-tuple-element.37.refs_1_, f32[640,512]{1,0:T(8,128)S(1)} %get-tuple-element.42.refs_2_, f32[640,512]{1,0:T(8,128)S(1)} %get-tuple-element.43.refs_3_, ...), custom_call_target="tpu_custom_call" | custom-call | flops 1 | bytes 1 | tf_op jit(solution)/shard_map/add_stage/pallas_call | solution.py:382
  10.8 0.3 %collective-permute-done.3.refs_9_ = bf16[256,256]{1,0:T(8,128)(2,1)S(1)} collective-permute-done((bf16[256,256]{1,0:T(8,128)(2,1)S(1)}, bf16[256,256]{1,0:T(8,128)(2,1)S(1)}, u32[]{:S(2)}, u32[]{:S(2)}) %collective-permute-start.3) | collective-permute-done | bytes 131104 | tf_op jit(solution)/shard_map/ppermute | solution.py:316
  11.1 12.5 %last_stage.1 = bf16[640,512]{1,0:T(8,128)(2,1)} custom-call(bf16[640,512]{1,0:T(8,128)(2,1)S(1)} %get-tuple-element.34.refs_0_, f32[640,512]{1,0:T(8,128)S(1)} %get-tuple-element.37.refs_1_, f32[640,512]{1,0:T(8,128)S(1)} %get-tuple-element.38.refs_2_, f32[640,512]{1,0:T(8,128)S(1)} %get-tuple-element.39.refs_3_, f32[640,512]{1,0:T(8,128)S(1)} %get-tuple-element.44.refs_4_, ...), custom_call_target="tpu_custom_call" | custom-call | flops 1 | bytes 1 | tf_op jit(solution)/shard_map/last_stage/pallas_call | solution.py:404
Async XLA Ops:
  1.4 7.0 %collective-permute-start = (bf16[256,256]{1,0:T(8,128)(2,1)}, bf16[256,256]{1,0:T(8,128)(2,1)S(1)}, u32[]{:S(2)}, u32[]{:S(2)}) collective-permute-start(bf16[256,256]{1,0:T(8,128)(2,1)} %bitcast.5), channel_id=1, source_target_pairs={{0,4},{1,13},{4,5},{5,9},{8,12},{9,0},{12,8},{13,1},{2,6},{3,15},{... | collective-permute-start | bytes 393224 | tf_op jit(solution)/shard_map/ppermute | solution.py:316
  3.2 6.5 %collective-permute-start.1 = (bf16[256,256]{1,0:T(8,128)(2,1)}, bf16[256,256]{1,0:T(8,128)(2,1)S(1)}, u32[]{:S(2)}, u32[]{:S(2)}) collective-permute-start(bf16[256,256]{1,0:T(8,128)(2,1)} %bitcast.6), channel_id=1, source_target_pairs={{0,1},{1,9},{4,0},{5,13},{8,12},{9,4},{12,8},{13,5},{2,3},{3,11},{... | collective-permute-start | bytes 393224 | tf_op jit(solution)/shard_map/ppermute | solution.py:316
  8.4 1.5 %collective-permute-start.2 = (bf16[256,256]{1,0:T(8,128)(2,1)S(1)}, bf16[256,256]{1,0:T(8,128)(2,1)S(1)}, u32[]{:S(2)}, u32[]{:S(2)}) collective-permute-start(bf16[256,256]{1,0:T(8,128)(2,1)S(1)} %collective-permute-done.refs_4_.refs_6_), channel_id=1, source_target_pairs={{0,1},{1,0},{4,5},{5,4},{8,9},{9,8},{12,13},{13,12},{2,3},{3,2},{6... | collective-permute-start | bytes 393224 | tf_op jit(solution)/shard_map/ppermute | solution.py:316
  9.7 1.3 %collective-permute-start.3 = (bf16[256,256]{1,0:T(8,128)(2,1)S(1)}, bf16[256,256]{1,0:T(8,128)(2,1)S(1)}, u32[]{:S(2)}, u32[]{:S(2)}) collective-permute-start(bf16[256,256]{1,0:T(8,128)(2,1)S(1)} %collective-permute-done.1.refs_8_), channel_id=1, source_target_pairs={{0,1},{1,0},{4,5},{5,4},{8,9},{9,8},{12,13},{13,12},{2,3},{3,2},{6... | collective-permute-start | bytes 393224 | tf_op jit(solution)/shard_map/ppermute | solution.py:316

commit v32 on v31

--- a/solution.py
+++ b/solution.py
@@ -180,7 +180,7 @@
     extra = None
     if by_swap is not None:
         position, core = place()
-        extra = penalty((position != 1) | (core == int(by_swap)))
+        extra = penalty((position == 0) | (core == int(by_swap)))
 
     def start(rows):
         return scores_of(stacked(query_ref, rows, heads), key_rows)
@@ -208,8 +208,8 @@
     heads = query_ref.shape[1] // HD
     blocks = row_blocks(query_ref.shape[0], 80)
     position, core = place()
-    takes_both = (position == 1) & routed
-    is_direct = core == jnp.where(position == 0, 0, 1)
+    takes_both = (position != 0) & routed
+    is_direct = core == 0
 
     def out_copy(index, rows):
         return pltpu.make_async_copy(out_ref.at[rows], out_hbm.at[rows], out_sems.at[index])
@@ -256,7 +256,7 @@
         counted = [(ref, 0.0) for ref in earlier_refs]
         if routed:
             counted[-2:] = [
-                (ref, penalty((position != 1) | (core == by_swap)))
+                (ref, penalty((position == 0) | (core == by_swap)))
                 for by_swap, ref in enumerate(earlier_refs[-2:])
             ]
         counted += [
@@ -317,7 +317,7 @@
 
     def first_route(i, core):
         base = i - i % FOUR
-        to, to_core = [((1, 0), (3, 1)), ((1, 1), (2, 1)), ((3, 0), (0, 0)), ((2, 0), (0, 1))][
+        to, to_core = [((1, 0), (3, 0)), ((1, 1), (2, 0)), ((2, 1), (0, 0)), ((3, 1), (0, 1))][
             i % FOUR
         ][core]
         return base + to, to_core

time: 23.9 us -> 23.9 us (level)
  waiting for transfers between devices: 1.31 us -> 0.6 us
  starting transfers between devices: 3.55 us -> 4.26 us
    ppermute x4, waiting for transfers between devices: 1.31 us -> 0.6 us  [send(): return lax.ppermute(shard, ('loop', 'pair'), hops)]
    ppermute x4, starting transfers between devices: 3.55 us -> 4.26 us  [send(): return lax.ppermute(shard, ('loop', 'pair'), hops)]
  transfers between devices with their start and end apart: 4 -> 4, of which waited for: 3 -> 2; matrix products, arithmetic and copies ran while one was open for 0% -> 0% of each run, Pallas kernels for 20% -> 20%
where the time goes in v32:
time: 23.9 us; the launch traced here: 23.6 us
  Pallas kernels  18.7 us (78%)
  starting transfers between devices  4.26 us (18%)
  waiting for transfers between devices  0.6 us (3%)
    pallas_call x1, Pallas kernels, shards(): pl.pallas_call(functools.partial(last_stage, routed), name='last_stage',...  12.5 us
    ppermute x4, starting transfers between devices, send(): return lax.ppermute(shard, ('loop', 'pair'), hops)  4.26 us
    pallas_call x1, Pallas kernels, shards(): pl.pallas_call(local_stage, name='local_stage', out_shape=[state] * 3 + b...  3.03 us
    pallas_call x2, Pallas kernels, add_shards(): pl.pallas_call(functools.partial(add_stage, by_swap if routed else None),...  1.79 us
    pallas_call x1, Pallas kernels, shards(): pl.pallas_call(prelude_stage, name='prelude_stage', out_shape=buffers, in...  1.35 us
    ppermute x4, waiting for transfers between devices, send(): return lax.ppermute(shard, ('loop', 'pair'), hops)  0.6 us
  transfers between devices with their start and end apart: 4, of which 2 were waited for; matrix products, arithmetic and copies ran while one was open for 0% of the time, Pallas kernels for 20%

profile of v32, /device:TPU:0, one launch (start us, length us, event | category | flops | bytes accessed | tf_op | source)
XLA Modules:
  0.0 23.6 jit_solution(2667936499723297489)
XLA Ops:
  0.0 1.4 %prelude_stage.1 = (bf16[640,512]{1,0:T(8,128)(2,1)S(1)}, bf16[640,256]{1,0:T(8,128)(2,1)S(1)}, bf16[256,256]{1,0:T(8,128)(2,1)S(1)}, s32[640,128]{1,0:T(8,128)S(1)}) custom-call(s32[8]{0:T(128)} %refs_0_.3, bf16[640,512]{1,0:T(8,128)(2,1)} %refs_1_.3, bf16[640,256]{1,0:T(8,128)(2,1)} %bitcast.2, bf16[256,256]{1,0:T(8,128)(2,1)} %bitcast.4), custom_call_target="tpu_custom_call" | custom-call | flops 1 | bytes 1 | tf_op jit(solution)/shard_map/prelude_stage/pallas_call | solution.py:343
  1.4 1.8 %collective-permute-start = (bf16[256,256]{1,0:T(8,128)(2,1)}, bf16[256,256]{1,0:T(8,128)(2,1)S(1)}, u32[]{:S(2)}, u32[]{:S(2)}) collective-permute-start(bf16[256,256]{1,0:T(8,128)(2,1)} %bitcast.5), channel_id=1, source_target_pairs={{0,4},{1,12},{4,5},{5,8},{8,9},{9,0},{12,13},{13,1},{2,6},{3,14},{... | collective-permute-start | bytes 393224 | tf_op jit(solution)/shard_map/ppermute | solution.py:316
  3.2 2.1 %collective-permute-start.1 = (bf16[256,256]{1,0:T(8,128)(2,1)}, bf16[256,256]{1,0:T(8,128)(2,1)S(1)}, u32[]{:S(2)}, u32[]{:S(2)}) collective-permute-start(bf16[256,256]{1,0:T(8,128)(2,1)} %bitcast.6), channel_id=1, source_target_pairs={{0,1},{1,9},{4,0},{5,13},{8,12},{9,4},{12,8},{13,5},{2,3},{3,11},{... | collective-permute-start | bytes 393224 | tf_op jit(solution)/shard_map/ppermute | solution.py:316
  5.3 3.0 %local_stage.1 = (f32[640,512]{1,0:T(8,128)S(1)}, f32[640,512]{1,0:T(8,128)S(1)}, f32[640,512]{1,0:T(8,128)S(1)}, bf16[640,512]{1,0:T(8,128)(2,1)S(1)}, bf16[640...) custom-call(s32[8]{0:T(128)} %refs_0_.3, ...), custom_call_target="tpu_custom_call", output_to_operand_aliasing={{3}: (4, {}), {4}: (5, {}), {5}: (6, {}), {6}: (7, {})} | custom-call | flops 1 | bytes 1 | tf_op jit(solution)/shard_map/local_stage/pallas_call | solution.py:367
  8.4 0.0 collective-permute-done.refs_4_.refs_6_
  8.4 0.1 collective-permute-start.2
  8.5 0.9 %add_stage.2 = (f32[640,512]{1,0:T(8,128)S(1)}, f32[640,512]{1,0:T(8,128)S(1)}) custom-call(bf16[640,512]{1,0:T(8,128)(2,1)S(1)} %get-tuple-element.34.refs_0_, f32[640,512]{1,0:T(8,128)S(1)} %get-tuple-element.37.refs_1_, f32[640,512]{1,0:T(8,128)S(1)} %get-tuple-element.38.refs_2_, f32[640,512]{1,0:T(8,128)S(1)} %get-tuple-element.39.refs_3_, ...), custom_call_target="tpu_custom_call" | custom-call | flops 1 | bytes 1 | tf_op jit(solution)/shard_map/add_stage/pallas_call | solution.py:382
  9.4 0.4 %collective-permute-done.1.refs_8_ = bf16[256,256]{1,0:T(8,128)(2,1)S(1)} collective-permute-done((bf16[256,256]{1,0:T(8,128)(2,1)}, bf16[256,256]{1,0:T(8,128)(2,1)S(1)}, u32[]{:S(2)}, u32[]{:S(2)}) %collective-permute-start.1) | collective-permute-done | bytes 131104 | tf_op jit(solution)/shard_map/ppermute | solution.py:316
  9.7 0.2 collective-permute-start.3
  9.9 0.0 collective-permute-done.2.refs_4_.refs_7_
  9.9 0.9 %add_stage.3 = (f32[640,512]{1,0:T(8,128)S(1)}, f32[640,512]{1,0:T(8,128)S(1)}) custom-call(bf16[640,512]{1,0:T(8,128)(2,1)S(1)} %get-tuple-element.34.refs_0_, f32[640,512]{1,0:T(8,128)S(1)} %get-tuple-element.37.refs_1_, f32[640,512]{1,0:T(8,128)S(1)} %get-tuple-element.42.refs_2_, f32[640,512]{1,0:T(8,128)S(1)} %get-tuple-element.43.refs_3_, ...), custom_call_target="tpu_custom_call" | custom-call | flops 1 | bytes 1 | tf_op jit(solution)/shard_map/add_stage/pallas_call | solution.py:382
  10.8 0.2 %collective-permute-done.3.refs_9_ = bf16[256,256]{1,0:T(8,128)(2,1)S(1)} collective-permute-done((bf16[256,256]{1,0:T(8,128)(2,1)S(1)}, bf16[256,256]{1,0:T(8,128)(2,1)S(1)}, u32[]{:S(2)}, u32[]{:S(2)}) %collective-permute-start.3) | collective-permute-done | bytes 131104 | tf_op jit(solution)/shard_map/ppermute | solution.py:316
  11.1 12.5 %last_stage.1 = bf16[640,512]{1,0:T(8,128)(2,1)} custom-call(bf16[640,512]{1,0:T(8,128)(2,1)S(1)} %get-tuple-element.34.refs_0_, f32[640,512]{1,0:T(8,128)S(1)} %get-tuple-element.37.refs_1_, f32[640,512]{1,0:T(8,128)S(1)} %get-tuple-element.38.refs_2_, f32[640,512]{1,0:T(8,128)S(1)} %get-tuple-element.39.refs_3_, f32[640,512]{1,0:T(8,128)S(1)} %get-tuple-element.44.refs_4_, ...), custom_call_target="tpu_custom_call" | custom-call | flops 1 | bytes 1 | tf_op jit(solution)/shard_map/last_stage/pallas_call | solution.py:404
Async XLA Ops:
  1.4 7.0 %collective-permute-start = (bf16[256,256]{1,0:T(8,128)(2,1)}, bf16[256,256]{1,0:T(8,128)(2,1)S(1)}, u32[]{:S(2)}, u32[]{:S(2)}) collective-permute-start(bf16[256,256]{1,0:T(8,128)(2,1)} %bitcast.5), channel_id=1, source_target_pairs={{0,4},{1,12},{4,5},{5,8},{8,9},{9,0},{12,13},{13,1},{2,6},{3,14},{... | collective-permute-start | bytes 393224 | tf_op jit(solution)/shard_map/ppermute | solution.py:316
  3.2 6.5 %collective-permute-start.1 = (bf16[256,256]{1,0:T(8,128)(2,1)}, bf16[256,256]{1,0:T(8,128)(2,1)S(1)}, u32[]{:S(2)}, u32[]{:S(2)}) collective-permute-start(bf16[256,256]{1,0:T(8,128)(2,1)} %bitcast.6), channel_id=1, source_target_pairs={{0,1},{1,9},{4,0},{5,13},{8,12},{9,4},{12,8},{13,5},{2,3},{3,11},{... | collective-permute-start | bytes 393224 | tf_op jit(solution)/shard_map/ppermute | solution.py:316
  8.4 1.6 %collective-permute-start.2 = (bf16[256,256]{1,0:T(8,128)(2,1)S(1)}, bf16[256,256]{1,0:T(8,128)(2,1)S(1)}, u32[]{:S(2)}, u32[]{:S(2)}) collective-permute-start(bf16[256,256]{1,0:T(8,128)(2,1)S(1)} %collective-permute-done.refs_4_.refs_6_), channel_id=1, source_target_pairs={{0,1},{1,0},{4,5},{5,4},{8,9},{9,8},{12,13},{13,12},{2,3},{3,2},{6... | collective-permute-start | bytes 393224 | tf_op jit(solution)/shard_map/ppermute | solution.py:316
  9.7 1.3 %collective-permute-start.3 = (bf16[256,256]{1,0:T(8,128)(2,1)S(1)}, bf16[256,256]{1,0:T(8,128)(2,1)S(1)}, u32[]{:S(2)}, u32[]{:S(2)}) collective-permute-start(bf16[256,256]{1,0:T(8,128)(2,1)S(1)} %collective-permute-done.1.refs_8_), channel_id=1, source_target_pairs={{0,1},{1,0},{4,5},{5,4},{8,9},{9,8},{12,13},{13,12},{2,3},{3,2},{6... | collective-permute-start | bytes 393224 | tf_op jit(solution)/shard_map/ppermute | solution.py:316

commit v33 on v32

--- a/solution.py
+++ b/solution.py
@@ -317,14 +317,14 @@
 
     def first_route(i, core):
         base = i - i % FOUR
-        to, to_core = [((1, 0), (3, 0)), ((1, 1), (2, 0)), ((2, 1), (0, 0)), ((3, 1), (0, 1))][
+        to, to_core = [((1, 0), (2, 0)), ((1, 1), (3, 0)), ((2, 1), (0, 0)), ((3, 1), (0, 1))][
             i % FOUR
         ][core]
         return base + to, to_core
 
     def second_route(i, core):
         base = i - i % FOUR
-        to, to_core = [((0, 1), (2, 1)), ((0, 0), (3, 1)), ((3, 0), (1, 0)), ((2, 0), (1, 1))][
+        to, to_core = [((0, 1), (3, 1)), ((0, 0), (2, 1)), ((3, 0), (1, 0)), ((2, 0), (1, 1))][
             i % FOUR
         ][core]
         return base + to, to_core

time: 23.9 us -> 24.6 us (1.029)
  the two profiles are of different devices: /device:TPU:0 before, /device:TPU:25 now
where the time goes in v33:
time: 24.6 us; the launch traced here: 24.5 us
  Pallas kernels  19.3 us (78%)
  starting transfers between devices  4.72 us (19%)
  waiting for transfers between devices  0.43 us (2%)
    pallas_call x1, Pallas kernels, shards(): pl.pallas_call(functools.partial(last_stage, routed), name='last_stage',...  13.1 us
    ppermute x4, starting transfers between devices, send(): return lax.ppermute(shard, ('loop', 'pair'), hops)  4.72 us
    pallas_call x1, Pallas kernels, shards(): pl.pallas_call(local_stage, name='local_stage', out_shape=[state] * 3 + b...  4.28 us
    pallas_call x2, Pallas kernels, add_shards(): pl.pallas_call(functools.partial(add_stage, by_swap if routed else None),...  1.79 us
  transfers between devices with their start and end apart: 4, of which 1 were waited for; matrix products, arithmetic and copies ran while one was open for 0% of the time, Pallas kernels for 25%

profile of v33, /device:TPU:25, one launch (start us, length us, event | category | flops | bytes accessed | tf_op | source)
XLA Modules:
  0.0 24.5 jit_solution(15740804393021986971)
XLA Ops:
  0.0 0.1 prelude_stage.1
  0.1 0.4 %collective-permute-start = (bf16[256,256]{1,0:T(8,128)(2,1)}, bf16[256,256]{1,0:T(8,128)(2,1)S(1)}, u32[]{:S(2)}, u32[]{:S(2)}) collective-permute-start(bf16[256,256]{1,0:T(8,128)(2,1)} %bitcast.5), channel_id=1, source_target_pairs={{0,4},{1,8},{4,5},{5,12},{8,9},{9,0},{12,13},{13,1},{2,6},{3,10},{... | collective-permute-start | bytes 393224 | tf_op jit(solution)/shard_map/ppermute | solution.py:316
  0.5 2.6 %collective-permute-start.1 = (bf16[256,256]{1,0:T(8,128)(2,1)}, bf16[256,256]{1,0:T(8,128)(2,1)S(1)}, u32[]{:S(2)}, u32[]{:S(2)}) collective-permute-start(bf16[256,256]{1,0:T(8,128)(2,1)} %bitcast.6), channel_id=1, source_target_pairs={{0,1},{1,13},{4,0},{5,9},{8,12},{9,4},{12,8},{13,5},{2,3},{3,15},{... | collective-permute-start | bytes 393224 | tf_op jit(solution)/shard_map/ppermute | solution.py:316
  3.1 4.3 %local_stage.1 = (f32[640,512]{1,0:T(8,128)S(1)}, f32[640,512]{1,0:T(8,128)S(1)}, f32[640,512]{1,0:T(8,128)S(1)}, bf16[640,512]{1,0:T(8,128)(2,1)S(1)}, bf16[640...) custom-call(s32[8]{0:T(128)} %refs_0_.3, ...), custom_call_target="tpu_custom_call", output_to_operand_aliasing={{3}: (4, {}), {4}: (5, {}), {5}: (6, {}), {6}: (7, {})} | custom-call | flops 1 | bytes 1 | tf_op jit(solution)/shard_map/local_stage/pallas_call | solution.py:367
  7.4 0.0 collective-permute-done.refs_4_.refs_6_
  7.4 1.7 %collective-permute-start.2 = (bf16[256,256]{1,0:T(8,128)(2,1)S(1)}, bf16[256,256]{1,0:T(8,128)(2,1)S(1)}, u32[]{:S(2)}, u32[]{:S(2)}) collective-permute-start(bf16[256,256]{1,0:T(8,128)(2,1)S(1)} %collective-permute-done.refs_4_.refs_6_), channel_id=1, source_target_pairs={{0,1},{1,0},{4,5},{5,4},{8,9},{9,8},{12,13},{13,12},{2,3},{3,2},{6... | collective-permute-start | bytes 393224 | tf_op jit(solution)/shard_map/ppermute | solution.py:316
  9.1 0.9 %add_stage.2 = (f32[640,512]{1,0:T(8,128)S(1)}, f32[640,512]{1,0:T(8,128)S(1)}) custom-call(bf16[640,512]{1,0:T(8,128)(2,1)S(1)} %get-tuple-element.34.refs_0_, f32[640,512]{1,0:T(8,128)S(1)} %get-tuple-element.37.refs_1_, f32[640,512]{1,0:T(8,128)S(1)} %get-tuple-element.38.refs_2_, f32[640,512]{1,0:T(8,128)S(1)} %get-tuple-element.39.refs_3_, ...), custom_call_target="tpu_custom_call" | custom-call | flops 1 | bytes 1 | tf_op jit(solution)/shard_map/add_stage/pallas_call | solution.py:382
  10.0 0.0 collective-permute-done.1.refs_8_
  10.0 0.1 collective-permute-start.3
  10.1 0.0 collective-permute-done.2.refs_4_.refs_7_
  10.1 0.9 %add_stage.3 = (f32[640,512]{1,0:T(8,128)S(1)}, f32[640,512]{1,0:T(8,128)S(1)}) custom-call(bf16[640,512]{1,0:T(8,128)(2,1)S(1)} %get-tuple-element.34.refs_0_, f32[640,512]{1,0:T(8,128)S(1)} %get-tuple-element.37.refs_1_, f32[640,512]{1,0:T(8,128)S(1)} %get-tuple-element.42.refs_2_, f32[640,512]{1,0:T(8,128)S(1)} %get-tuple-element.43.refs_3_, ...), custom_call_target="tpu_custom_call" | custom-call | flops 1 | bytes 1 | tf_op jit(solution)/shard_map/add_stage/pallas_call | solution.py:382
  11.0 0.4 %collective-permute-done.3.refs_9_ = bf16[256,256]{1,0:T(8,128)(2,1)S(1)} collective-permute-done((bf16[256,256]{1,0:T(8,128)(2,1)S(1)}, bf16[256,256]{1,0:T(8,128)(2,1)S(1)}, u32[]{:S(2)}, u32[]{:S(2)}) %collective-permute-start.3) | collective-permute-done | bytes 131104 | tf_op jit(solution)/shard_map/ppermute | solution.py:316
  11.4 13.1 %last_stage.1 = bf16[640,512]{1,0:T(8,128)(2,1)} custom-call(bf16[640,512]{1,0:T(8,128)(2,1)S(1)} %get-tuple-element.34.refs_0_, f32[640,512]{1,0:T(8,128)S(1)} %get-tuple-element.37.refs_1_, f32[640,512]{1,0:T(8,128)S(1)} %get-tuple-element.38.refs_2_, f32[640,512]{1,0:T(8,128)S(1)} %get-tuple-element.39.refs_3_, f32[640,512]{1,0:T(8,128)S(1)} %get-tuple-element.44.refs_4_, ...), custom_call_target="tpu_custom_call" | custom-call | flops 1 | bytes 1 | tf_op jit(solution)/shard_map/last_stage/pallas_call | solution.py:404
Async XLA Ops:
  0.1 7.3 %collective-permute-start = (bf16[256,256]{1,0:T(8,128)(2,1)}, bf16[256,256]{1,0:T(8,128)(2,1)S(1)}, u32[]{:S(2)}, u32[]{:S(2)}) collective-permute-start(bf16[256,256]{1,0:T(8,128)(2,1)} %bitcast.5), channel_id=1, source_target_pairs={{0,4},{1,8},{4,5},{5,12},{8,9},{9,0},{12,13},{13,1},{2,6},{3,10},{... | collective-permute-start | bytes 393224 | tf_op jit(solution)/shard_map/ppermute | solution.py:316
  0.5 9.4 %collective-permute-start.1 = (bf16[256,256]{1,0:T(8,128)(2,1)}, bf16[256,256]{1,0:T(8,128)(2,1)S(1)}, u32[]{:S(2)}, u32[]{:S(2)}) collective-permute-start(bf16[256,256]{1,0:T(8,128)(2,1)} %bitcast.6), channel_id=1, source_target_pairs={{0,1},{1,13},{4,0},{5,9},{8,12},{9,4},{12,8},{13,5},{2,3},{3,15},{... | collective-permute-start | bytes 393224 | tf_op jit(solution)/shard_map/ppermute | solution.py:316
  7.4 2.7 %collective-permute-start.2 = (bf16[256,256]{1,0:T(8,128)(2,1)S(1)}, bf16[256,256]{1,0:T(8,128)(2,1)S(1)}, u32[]{:S(2)}, u32[]{:S(2)}) collective-permute-start(bf16[256,256]{1,0:T(8,128)(2,1)S(1)} %collective-permute-done.refs_4_.refs_6_), channel_id=1, source_target_pairs={{0,1},{1,0},{4,5},{5,4},{8,9},{9,8},{12,13},{13,12},{2,3},{3,2},{6... | collective-permute-start | bytes 393224 | tf_op jit(solution)/shard_map/ppermute | solution.py:316
  10.0 1.4 %collective-permute-start.3 = (bf16[256,256]{1,0:T(8,128)(2,1)S(1)}, bf16[256,256]{1,0:T(8,128)(2,1)S(1)}, u32[]{:S(2)}, u32[]{:S(2)}) collective-permute-start(bf16[256,256]{1,0:T(8,128)(2,1)S(1)} %collective-permute-done.1.refs_8_), channel_id=1, source_target_pairs={{0,1},{1,0},{4,5},{5,4},{8,9},{9,8},{12,13},{13,12},{2,3},{3,2},{6... | collective-permute-start | bytes 393224 | tf_op jit(solution)/shard_map/ppermute | solution.py:316

commit v34 on v27

--- a/solution.py
+++ b/solution.py
@@ -75,8 +75,8 @@
         pltpu.make_async_copy(source, target, sems.at[i])
         for i, (source, target) in enumerate(pairs)
     ]
-    for copy in copies:
-        copy.start()
+    for i, copy in enumerate(copies):
+        copy.start(priority=i % 2)
     copies[0].wait()
     slots = query_ref.shape[0]
     position = lax.axis_index("loop")
@@ -235,7 +235,7 @@
             good = (total < total_limit).reshape(total.shape[0] // 8, 8, HD)
             trusted[0] = trusted[0] & jnp.all(good, axis=0)
             write(rows, total, weighted)
-            out_copy(index, rows).start()
+            out_copy(index, rows).start(priority=index % 2)
 
         staged(blocks, start, finish)
         trusted_ref[0] = jnp.all(trusted[0]).astype(jnp.int32)

time: 23.9 us -> 24 us (level)
  transfers between devices with their start and end apart: 4 -> 4, of which waited for: 3 -> 2; matrix products, arithmetic and copies ran while one was open for 0% -> 0% of each run, Pallas kernels for 20% -> 20%
where the time goes in v34:
time: 24 us; the launch traced here: 23.7 us
  Pallas kernels  18.7 us (78%)
  starting transfers between devices  4.36 us (18%)
  waiting for transfers between devices  0.52 us (2%)
    pallas_call x1, Pallas kernels, shards(): pl.pallas_call(functools.partial(last_stage, routed), name='last_stage',...  12.5 us
    ppermute x4, starting transfers between devices, send(): return lax.ppermute(shard, ('loop', 'pair'), hops)  4.36 us
    pallas_call x1, Pallas kernels, shards(): pl.pallas_call(local_stage, name='local_stage', out_shape=[state] * 3 + b...  3.03 us
    pallas_call x2, Pallas kernels, add_shards(): pl.pallas_call(functools.partial(add_stage, by_swap if routed else None),...  1.79 us
    pallas_call x1, Pallas kernels, shards(): pl.pallas_call(prelude_stage, name='prelude_stage', out_shape=buffers, in...  1.45 us
    ppermute x4, waiting for transfers between devices, send(): return lax.ppermute(shard, ('loop', 'pair'), hops)  0.52 us
  transfers between devices with their start and end apart: 4, of which 2 were waited for; matrix products, arithmetic and copies ran while one was open for 0% of the time, Pallas kernels for 20%

profile of v34, /device:TPU:0, one launch (start us, length us, event | category | flops | bytes accessed | tf_op | source)
XLA Modules:
  0.0 23.7 jit_solution(6849374796325885719)
XLA Ops:
  0.0 1.4 %prelude_stage.1 = (bf16[640,512]{1,0:T(8,128)(2,1)S(1)}, bf16[640,256]{1,0:T(8,128)(2,1)S(1)}, bf16[256,256]{1,0:T(8,128)(2,1)S(1)}, s32[640,128]{1,0:T(8,128)S(1)}) custom-call(s32[8]{0:T(128)} %refs_0_.3, bf16[640,512]{1,0:T(8,128)(2,1)} %refs_1_.3, bf16[640,256]{1,0:T(8,128)(2,1)} %bitcast.2, bf16[256,256]{1,0:T(8,128)(2,1)} %bitcast.4), custom_call_target="tpu_custom_call" | custom-call | flops 1 | bytes 1 | tf_op jit(solution)/shard_map/prelude_stage/pallas_call | solution.py:343
  1.5 1.7 %collective-permute-start = (bf16[256,256]{1,0:T(8,128)(2,1)}, bf16[256,256]{1,0:T(8,128)(2,1)S(1)}, u32[]{:S(2)}, u32[]{:S(2)}) collective-permute-start(bf16[256,256]{1,0:T(8,128)(2,1)} %bitcast.5), channel_id=1, source_target_pairs={{0,4},{1,13},{4,5},{5,8},{8,12},{9,0},{12,9},{13,1},{2,6},{3,15},{... | collective-permute-start | bytes 393224 | tf_op jit(solution)/shard_map/ppermute | solution.py:316
  3.2 1.6 %collective-permute-start.1 = (bf16[256,256]{1,0:T(8,128)(2,1)}, bf16[256,256]{1,0:T(8,128)(2,1)S(1)}, u32[]{:S(2)}, u32[]{:S(2)}) collective-permute-start(bf16[256,256]{1,0:T(8,128)(2,1)} %bitcast.6), channel_id=1, source_target_pairs={{0,1},{1,9},{4,0},{5,13},{8,12},{9,4},{12,8},{13,5},{2,3},{3,11},{... | collective-permute-start | bytes 393224 | tf_op jit(solution)/shard_map/ppermute | solution.py:316
  4.8 3.0 %local_stage.1 = (f32[640,512]{1,0:T(8,128)S(1)}, f32[640,512]{1,0:T(8,128)S(1)}, f32[640,512]{1,0:T(8,128)S(1)}, bf16[640,512]{1,0:T(8,128)(2,1)S(1)}, bf16[640...) custom-call(s32[8]{0:T(128)} %refs_0_.3, ...), custom_call_target="tpu_custom_call", output_to_operand_aliasing={{3}: (4, {}), {4}: (5, {}), {5}: (6, {}), {6}: (7, {})} | custom-call | flops 1 | bytes 1 | tf_op jit(solution)/shard_map/local_stage/pallas_call | solution.py:367
  7.8 0.0 collective-permute-done.refs_4_.refs_6_
  7.9 1.0 %collective-permute-start.2 = (bf16[256,256]{1,0:T(8,128)(2,1)S(1)}, bf16[256,256]{1,0:T(8,128)(2,1)S(1)}, u32[]{:S(2)}, u32[]{:S(2)}) collective-permute-start(bf16[256,256]{1,0:T(8,128)(2,1)S(1)} %collective-permute-done.refs_4_.refs_6_), channel_id=1, source_target_pairs={{0,1},{1,0},{4,5},{5,4},{8,9},{9,8},{12,13},{13,12},{2,3},{3,2},{6... | collective-permute-start | bytes 393224 | tf_op jit(solution)/shard_map/ppermute | solution.py:316
  8.9 0.9 %add_stage.2 = (f32[640,512]{1,0:T(8,128)S(1)}, f32[640,512]{1,0:T(8,128)S(1)}) custom-call(bf16[640,512]{1,0:T(8,128)(2,1)S(1)} %get-tuple-element.34.refs_0_, f32[640,512]{1,0:T(8,128)S(1)} %get-tuple-element.37.refs_1_, f32[640,512]{1,0:T(8,128)S(1)} %get-tuple-element.38.refs_2_, f32[640,512]{1,0:T(8,128)S(1)} %get-tuple-element.39.refs_3_, ...), custom_call_target="tpu_custom_call" | custom-call | flops 1 | bytes 1 | tf_op jit(solution)/shard_map/add_stage/pallas_call | solution.py:382
  9.8 0.1 collective-permute-done.1.refs_8_
  9.8 0.0 collective-permute-start.3
  9.9 0.0 collective-permute-done.2.refs_4_.refs_7_
  9.9 0.9 %add_stage.3 = (f32[640,512]{1,0:T(8,128)S(1)}, f32[640,512]{1,0:T(8,128)S(1)}) custom-call(bf16[640,512]{1,0:T(8,128)(2,1)S(1)} %get-tuple-element.34.refs_0_, f32[640,512]{1,0:T(8,128)S(1)} %get-tuple-element.37.refs_1_, f32[640,512]{1,0:T(8,128)S(1)} %get-tuple-element.42.refs_2_, f32[640,512]{1,0:T(8,128)S(1)} %get-tuple-element.43.refs_3_, ...), custom_call_target="tpu_custom_call" | custom-call | flops 1 | bytes 1 | tf_op jit(solution)/shard_map/add_stage/pallas_call | solution.py:382
  10.8 0.4 %collective-permute-done.3.refs_9_ = bf16[256,256]{1,0:T(8,128)(2,1)S(1)} collective-permute-done((bf16[256,256]{1,0:T(8,128)(2,1)S(1)}, bf16[256,256]{1,0:T(8,128)(2,1)S(1)}, u32[]{:S(2)}, u32[]{:S(2)}) %collective-permute-start.3) | collective-permute-done | bytes 131104 | tf_op jit(solution)/shard_map/ppermute | solution.py:316
  11.2 12.5 %last_stage.1 = bf16[640,512]{1,0:T(8,128)(2,1)} custom-call(bf16[640,512]{1,0:T(8,128)(2,1)S(1)} %get-tuple-element.34.refs_0_, f32[640,512]{1,0:T(8,128)S(1)} %get-tuple-element.37.refs_1_, f32[640,512]{1,0:T(8,128)S(1)} %get-tuple-element.38.refs_2_, f32[640,512]{1,0:T(8,128)S(1)} %get-tuple-element.39.refs_3_, f32[640,512]{1,0:T(8,128)S(1)} %get-tuple-element.44.refs_4_, ...), custom_call_target="tpu_custom_call" | custom-call | flops 1 | bytes 1 | tf_op jit(solution)/shard_map/last_stage/pallas_call | solution.py:404
Async XLA Ops:
  1.5 6.4 %collective-permute-start = (bf16[256,256]{1,0:T(8,128)(2,1)}, bf16[256,256]{1,0:T(8,128)(2,1)S(1)}, u32[]{:S(2)}, u32[]{:S(2)}) collective-permute-start(bf16[256,256]{1,0:T(8,128)(2,1)} %bitcast.5), channel_id=1, source_target_pairs={{0,4},{1,13},{4,5},{5,8},{8,12},{9,0},{12,9},{13,1},{2,6},{3,15},{... | collective-permute-start | bytes 393224 | tf_op jit(solution)/shard_map/ppermute | solution.py:316
  3.2 6.6 %collective-permute-start.1 = (bf16[256,256]{1,0:T(8,128)(2,1)}, bf16[256,256]{1,0:T(8,128)(2,1)S(1)}, u32[]{:S(2)}, u32[]{:S(2)}) collective-permute-start(bf16[256,256]{1,0:T(8,128)(2,1)} %bitcast.6), channel_id=1, source_target_pairs={{0,1},{1,9},{4,0},{5,13},{8,12},{9,4},{12,8},{13,5},{2,3},{3,11},{... | collective-permute-start | bytes 393224 | tf_op jit(solution)/shard_map/ppermute | solution.py:316
  7.9 2.0 %collective-permute-start.2 = (bf16[256,256]{1,0:T(8,128)(2,1)S(1)}, bf16[256,256]{1,0:T(8,128)(2,1)S(1)}, u32[]{:S(2)}, u32[]{:S(2)}) collective-permute-start(bf16[256,256]{1,0:T(8,128)(2,1)S(1)} %collective-permute-done.refs_4_.refs_6_), channel_id=1, source_target_pairs={{0,1},{1,0},{4,5},{5,4},{8,9},{9,8},{12,13},{13,12},{2,3},{3,2},{6... | collective-permute-start | bytes 393224 | tf_op jit(solution)/shard_map/ppermute | solution.py:316
  9.8 1.4 %collective-permute-start.3 = (bf16[256,256]{1,0:T(8,128)(2,1)S(1)}, bf16[256,256]{1,0:T(8,128)(2,1)S(1)}, u32[]{:S(2)}, u32[]{:S(2)}) collective-permute-start(bf16[256,256]{1,0:T(8,128)(2,1)S(1)} %collective-permute-done.1.refs_8_), channel_id=1, source_target_pairs={{0,1},{1,0},{4,5},{5,4},{8,9},{9,8},{12,13},{13,12},{2,3},{3,2},{6... | collective-permute-start | bytes 393224 | tf_op jit(solution)/shard_map/ppermute | solution.py:316
